TPU v7x, 32 devices: a whole 2x2x4 slice. The times are simulated.
32 devices in a mesh: mp: 2 (over x), dp: 4 (over z), outer: 4 (over y, core).
Axes of the slice: x: 2, y: 2, z: 4, core: 2. Of those that a mesh axis runs over, the one named last changes fastest.
Arguments:
- inputs: bfloat16 [16, 2560, 1024], P(('dp', 'outer'), 'mp'), may hold values from -6 to 6
- cotangent: bfloat16 [16, 2560, 1024], P(('dp', 'outer'), 'mp'), may hold values from -6 to 6
- lengths: int32 [16, 12], P(('dp', 'outer')), may hold values from 1 to 1280, 2560 in all within a row
- project_master: float32 [1024, 16, 192], P('dp', 'mp'), may hold values from -0.1875 to 0.1875
- project_first: float32 [1024, 16, 192], P('dp', 'mp'), may hold values from -0.0007324219 to 0.0007324219
- project_second: float32 [1024, 16, 192], P('dp', 'mp'), may hold values from 1.0490417e-08 to 4.196167e-08
- mixing_master: float32 [16, 64, 1024], P('mp', None, 'dp'), may hold values from -1 to 1
- mixing_first: float32 [16, 64, 1024], P('mp', None, 'dp'), may hold values from -0.00010681152 to 0.00010681152
- mixing_second: float32 [16, 64, 1024], P('mp', None, 'dp'), may hold values from 2.384186e-10 to 9.536744e-10
- expand_master: float32 [1024, 4096], P('dp', 'mp'), may hold values from -0.1875 to 0.1875
- expand_first: float32 [1024, 4096], P('dp', 'mp'), may hold values from -0.00021362305 to 0.00021362305
- expand_second: float32 [1024, 4096], P('dp', 'mp'), may hold values from 9.536744e-10 to 3.8146974e-09
- shrink_master: float32 [4096, 1024], P('mp', 'dp'), may hold values from -0.09375 to 0.09375
- shrink_first: float32 [4096, 1024], P('mp', 'dp'), may hold values from -0.0004272461 to 0.0004272461
- shrink_second: float32 [4096, 1024], P('mp', 'dp'), may hold values from 3.8146974e-09 to 1.525879e-08
- norm_master: float32 [2, 1024], P(None, 'dp'), may hold values from -0.5 to 1.5, as said below
- norm_first: float32 [2, 1024], P(None, 'dp'), may hold values from -0.0014648438 to 0.0014648438
- norm_second: float32 [2, 1024], P(None, 'dp'), may hold values from 4.053116e-08 to 1.6212464e-07
Outputs:
- block_out: bfloat16 [16, 2560, 1024], P(('dp', 'outer'), 'mp')
- input_grad: float32 [16, 2560, 1024], P(('dp', 'outer'), 'mp')
- project_next: float32 [1024, 16, 192], P('dp', 'mp')
- project_mean: float32 [1024, 16, 192], P('dp', 'mp')
- project_square: float32 [1024, 16, 192], P('dp', 'mp')
- project_copy: bfloat16 [1024, 16, 192], P('dp', 'mp')
- mixing_next: float32 [16, 64, 1024], P('mp', None, 'dp')
- mixing_mean: float32 [16, 64, 1024], P('mp', None, 'dp')
- mixing_square: float32 [16, 64, 1024], P('mp', None, 'dp')
- mixing_copy: bfloat16 [16, 64, 1024], P('mp', None, 'dp')
- expand_next: float32 [1024, 4096], P('dp', 'mp')
- expand_mean: float32 [1024, 4096], P('dp', 'mp')
- expand_square: float32 [1024, 4096], P('dp', 'mp')
- expand_copy: bfloat16 [1024, 4096], P('dp', 'mp')
- shrink_next: float32 [4096, 1024], P('mp', 'dp')
- shrink_mean: float32 [4096, 1024], P('mp', 'dp')
- shrink_square: float32 [4096, 1024], P('mp', 'dp')
- shrink_copy: bfloat16 [4096, 1024], P('mp', 'dp')
- norm_next: float32 [2, 1024], P(None, 'dp')
- norm_mean: float32 [2, 1024], P(None, 'dp')
- norm_square: float32 [2, 1024], P(None, 'dp')
- norm_copy: bfloat16 [2, 1024], P(None, 'dp')
- grad_norm: float32 [], replicated
Inputs may be any that keep to these rules, and one draw needn't show every extreme that they name: Each row's lengths sum to 2560 and the longest is 1280. `norm_master`: row 0 holds gains, row 1 biases.
All inputs are finite; a program needn't handle non-finite values.
Results may differ from a plain program's by a relative error of at most 0.003.
The roundings to bfloat16 on the way count: a program that leaves them out, or rounds other values in their place, can miss the bound.
Values may be sent and summed in bfloat16 or wider, within the bound.
A program may use at most 448 MiB of HBM per device.

v0:
```python
from functools import partial
import math

import jax
import jax.numpy as jnp
from jax import lax
from jax.sharding import PartitionSpec as P

D = 1024
HD = 64
ROT = 32
FF = 4096
QB = 512
STEP = 10


norm_epsilon = 1e-05
beta_one = 0.9
beta_two = 0.95
adam_epsilon = 1e-08
decay_rate = 0.1
clip_level = 1.0
masked_value = -1e30


def layout(sizes_row, count):
    ends = jnp.cumsum(sizes_row)
    places = jnp.arange(count, dtype=jnp.int32)
    passed = (ends[None, :] <= places[:, None]).astype(jnp.int32)
    segment = jnp.sum(passed, axis=1)
    begins = jnp.sum(passed * sizes_row[None, :], axis=1)
    return (segment, places - begins)


def rotary(vectors, places, direction):
    half_rot = ROT // 2
    counter = jnp.arange(half_rot, dtype=jnp.float32)
    frequency = jnp.exp(counter * (-2.0 * math.log(10000.0) / ROT))
    angles = places.astype(jnp.float32)[:, None] * frequency[None, :] * direction
    cosine = jnp.cos(angles)[:, None, :]
    sine = jnp.sin(angles)[:, None, :]
    first = vectors[..., :half_rot]
    second = vectors[..., half_rot:ROT]
    return jnp.concatenate(
        [first * cosine - second * sine, second * cosine + first * sine, vectors[..., ROT:]],
        axis=-1,
    )


def layer_norm(rows_in, gain, bias):
    mean = jnp.mean(rows_in, axis=1, keepdims=True)
    centred = rows_in - mean
    spread = jnp.mean(centred * centred, axis=1, keepdims=True)
    normed = centred * lax.rsqrt(spread + norm_epsilon)
    return normed * gain + bias


def adam_update(master, first, second, gradient, rate, decay):
    first_new = beta_one * first + (1.0 - beta_one) * gradient
    second_new = beta_two * second + (1.0 - beta_two) * gradient * gradient
    first_hat = first_new / (1.0 - beta_one**STEP)
    second_hat = second_new / (1.0 - beta_two**STEP)
    master_new = master - rate * (
        first_hat / (jnp.sqrt(second_hat) + adam_epsilon) + decay * master
    )
    return (master_new, first_new, second_new, master_new.astype(jnp.bfloat16))


def local(
    inputs,
    cotangent,
    lengths,
    project_master,
    project_first,
    project_second,
    mixing_master,
    mixing_first,
    mixing_second,
    expand_master,
    expand_first,
    expand_second,
    shrink_master,
    shrink_first,
    shrink_second,
    norm_master,
    norm_first,
    norm_second,
):
    project_weight, mixing_weight, expand_weight, shrink_weight, norm_weight = (
        lax.all_gather(project_master.astype(jnp.bfloat16), "dp", axis=0, tiled=True),
        lax.all_gather(mixing_master.astype(jnp.bfloat16), "dp", axis=2, tiled=True),
        lax.all_gather(expand_master.astype(jnp.bfloat16), "dp", axis=0, tiled=True),
        lax.all_gather(shrink_master.astype(jnp.bfloat16), "dp", axis=1, tiled=True),
        lax.all_gather(norm_master.astype(jnp.bfloat16), "dp", axis=1, tiled=True),
    )
    gain = norm_weight[0].astype(jnp.float32)
    bias = norm_weight[1].astype(jnp.float32)
    rows_local = inputs[0].astype(jnp.float32)
    shaped, norm_pull = jax.vjp(layer_norm, rows_local, gain, bias)
    hidden_local = shaped.astype(jnp.bfloat16)
    hidden = lax.all_gather(hidden_local, "mp", axis=0, tiled=True)
    count = hidden.shape[0]
    blocks = count // QB
    segment, places = layout(lengths[0], count)
    index = jnp.arange(count, dtype=jnp.int32)
    heads_here = project_weight.shape[1]
    scale = HD ** (-0.5)
    project_flat = project_weight.reshape(project_weight.shape[0], heads_here * 3 * HD)
    projected = jnp.dot(hidden, project_flat, preferred_element_type=jnp.float32).reshape(
        count, heads_here, 3 * HD
    )
    query = rotary(projected[..., :HD], places, 1.0).astype(jnp.bfloat16)
    keys = rotary(projected[..., HD : 2 * HD], places, 1.0).astype(jnp.bfloat16)
    values = projected[..., 2 * HD :].astype(jnp.bfloat16)

    def block_scores(block_query, block_segment, block_index):
        raw = jnp.einsum("qhd,khd->hqk", block_query, keys, preferred_element_type=jnp.float32)
        allowed = (block_segment[:, None] == segment[None, :]) & (
            index[None, :] <= block_index[:, None]
        )
        return jnp.where(allowed[None], raw * scale, masked_value)

    def forward_block(items):
        block_query, block_segment, block_index = items
        masked = block_scores(block_query, block_segment, block_index)
        top = jnp.max(masked, axis=2, keepdims=True)
        shifted = jnp.exp(masked - top)
        total = jnp.sum(shifted, axis=2, keepdims=True)
        shares = (shifted / total).astype(jnp.bfloat16)
        mixed_block = jnp.einsum("hqk,khd->qhd", shares, values, preferred_element_type=jnp.float32)
        return (mixed_block.astype(jnp.bfloat16), top + jnp.log(total))

    blocked_query = query.reshape(blocks, QB, heads_here, HD)
    blocked_segment = segment.reshape(blocks, QB)
    blocked_index = index.reshape(blocks, QB)
    mixed_parts, log_totals = lax.map(
        forward_block, (blocked_query, blocked_segment, blocked_index)
    )
    mixed = mixed_parts.reshape(count, heads_here, HD)
    mixed_flat = mixed.reshape(count, heads_here * HD)
    mixing_flat = mixing_weight.reshape(heads_here * HD, mixing_weight.shape[2])
    lifted = jnp.dot(hidden, expand_weight, preferred_element_type=jnp.float32)
    activated = jax.nn.gelu(lifted, approximate=True).astype(jnp.bfloat16)
    branch = lax.psum_scatter(
        jnp.dot(mixed_flat, mixing_flat, preferred_element_type=jnp.float32)
        + jnp.dot(activated, shrink_weight, preferred_element_type=jnp.float32),
        "mp",
        scatter_dimension=0,
        tiled=True,
    )
    block_out = (rows_local + branch).astype(jnp.bfloat16)[None]
    back_local = cotangent[0].astype(jnp.float32)
    back_rows = lax.all_gather(cotangent[0], "mp", axis=0, tiled=True)
    shrink_gradient = jnp.einsum(
        "tf,td->fd", activated, back_rows, preferred_element_type=jnp.float32
    )
    active_grad = jnp.einsum(
        "td,fd->tf", back_rows, shrink_weight, preferred_element_type=jnp.float32
    )
    gelu_pull = jax.vjp(partial(jax.nn.gelu, approximate=True), lifted)[1]
    lifted_grad = gelu_pull(active_grad)[0].astype(jnp.bfloat16)
    expand_gradient = jnp.einsum(
        "td,tf->df", hidden, lifted_grad, preferred_element_type=jnp.float32
    )
    mixing_gradient = jnp.einsum(
        "the,td->hed", mixed, back_rows, preferred_element_type=jnp.float32
    )
    mixed_grad = jnp.einsum(
        "td,hed->the", back_rows, mixing_weight, preferred_element_type=jnp.float32
    ).astype(jnp.bfloat16)

    def backward_block(carry, items):
        key_sum, value_sum = carry
        block_query, block_segment, block_index, block_total, block_grad = items
        masked = block_scores(block_query, block_segment, block_index)
        shares = jnp.exp(masked - block_total)
        share_grad = jnp.einsum(
            "qhd,khd->hqk", block_grad, values, preferred_element_type=jnp.float32
        )
        inner = jnp.sum(shares * share_grad, axis=2, keepdims=True)
        score_grad = (shares * (share_grad - inner)).astype(jnp.bfloat16)
        query_part = (
            jnp.einsum("hqk,khd->qhd", score_grad, keys, preferred_element_type=jnp.float32) * scale
        )
        key_sum = (
            key_sum
            + jnp.einsum(
                "hqk,qhd->khd", score_grad, block_query, preferred_element_type=jnp.float32
            )
            * scale
        )
        value_sum = value_sum + jnp.einsum(
            "hqk,qhd->khd",
            shares.astype(jnp.bfloat16),
            block_grad,
            preferred_element_type=jnp.float32,
        )
        return ((key_sum, value_sum), query_part)

    zero_keys = jnp.zeros((count, heads_here, HD), jnp.float32)
    (key_grad, value_grad), query_parts = lax.scan(
        backward_block,
        (zero_keys, zero_keys),
        (
            blocked_query,
            blocked_segment,
            blocked_index,
            log_totals,
            mixed_grad.reshape(blocks, QB, heads_here, HD),
        ),
    )
    query_grad = query_parts.reshape(count, heads_here, HD)
    projected_grad = jnp.concatenate(
        [rotary(query_grad, places, -1.0), rotary(key_grad, places, -1.0), value_grad], axis=-1
    ).astype(jnp.bfloat16)
    projected_flat = projected_grad.reshape(count, heads_here * 3 * HD)
    project_gradient = jnp.einsum(
        "td,te->de", hidden, projected_flat, preferred_element_type=jnp.float32
    ).reshape(project_weight.shape)
    hidden_grad = lax.psum_scatter(
        jnp.einsum("te,de->td", projected_flat, project_flat, preferred_element_type=jnp.float32)
        + jnp.einsum("tf,df->td", lifted_grad, expand_weight, preferred_element_type=jnp.float32),
        "mp",
        scatter_dimension=0,
        tiled=True,
    )
    rows_grad, gain_grad, bias_grad = norm_pull(hidden_grad)
    input_grad = (back_local + rows_grad)[None]
    norm_part = jnp.stack([gain_grad, bias_grad])
    project_gradient, mixing_gradient, expand_gradient, shrink_gradient, norm_piece = (
        lax.psum_scatter(project_gradient, "dp", scatter_dimension=0, tiled=True),
        lax.psum_scatter(mixing_gradient, "dp", scatter_dimension=2, tiled=True),
        lax.psum_scatter(expand_gradient, "dp", scatter_dimension=0, tiled=True),
        lax.psum_scatter(shrink_gradient, "dp", scatter_dimension=1, tiled=True),
        lax.psum_scatter(norm_part, "dp", scatter_dimension=1, tiled=True),
    )
    project_gradient, mixing_gradient, expand_gradient, shrink_gradient, norm_piece = lax.psum(
        (project_gradient, mixing_gradient, expand_gradient, shrink_gradient, norm_piece), "outer"
    )
    norm_gradient = lax.psum(norm_piece, "mp")
    head_first = (lax.axis_index("mp") == 0).astype(jnp.float32)
    own_square = (
        jnp.sum(project_gradient * project_gradient)
        + jnp.sum(mixing_gradient * mixing_gradient)
        + jnp.sum(expand_gradient * expand_gradient)
        + jnp.sum(shrink_gradient * shrink_gradient)
        + head_first * jnp.sum(norm_gradient * norm_gradient)
    )
    total_square = lax.psum(own_square, ("mp", "dp"))
    grad_norm = jnp.sqrt(total_square)
    factor = clip_level / jnp.maximum(grad_norm, clip_level)
    project_out = adam_update(
        project_master,
        project_first,
        project_second,
        factor * project_gradient,
        D ** (-0.5),
        decay_rate,
    )
    mixing_out = adam_update(
        mixing_master,
        mixing_first,
        mixing_second,
        factor * mixing_gradient,
        (D // 32) ** (-0.5),
        decay_rate,
    )
    expand_out = adam_update(
        expand_master,
        expand_first,
        expand_second,
        factor * expand_gradient,
        D ** (-0.5),
        decay_rate,
    )
    shrink_out = adam_update(
        shrink_master,
        shrink_first,
        shrink_second,
        factor * shrink_gradient,
        FF ** (-0.5),
        decay_rate,
    )
    norm_out = adam_update(norm_master, norm_first, norm_second, factor * norm_gradient, 0.3, 0.0)
    return (
        block_out,
        input_grad,
        project_out[0],
        project_out[1],
        project_out[2],
        project_out[3],
        mixing_out[0],
        mixing_out[1],
        mixing_out[2],
        mixing_out[3],
        expand_out[0],
        expand_out[1],
        expand_out[2],
        expand_out[3],
        shrink_out[0],
        shrink_out[1],
        shrink_out[2],
        shrink_out[3],
        norm_out[0],
        norm_out[1],
        norm_out[2],
        norm_out[3],
        grad_norm,
    )


def solution(mesh):
    in_specs = (
        P(("dp", "outer"), "mp", None),
        P(("dp", "outer"), "mp", None),
        P(("dp", "outer"), None),
        P("dp", "mp", None),
        P("dp", "mp", None),
        P("dp", "mp", None),
        P("mp", None, "dp"),
        P("mp", None, "dp"),
        P("mp", None, "dp"),
        P("dp", "mp"),
        P("dp", "mp"),
        P("dp", "mp"),
        P("mp", "dp"),
        P("mp", "dp"),
        P("mp", "dp"),
        P(None, "dp"),
        P(None, "dp"),
        P(None, "dp"),
    )
    out_specs = (
        P(("dp", "outer"), "mp", None),
        P(("dp", "outer"), "mp", None),
        P("dp", "mp", None),
        P("dp", "mp", None),
        P("dp", "mp", None),
        P("dp", "mp", None),
        P("mp", None, "dp"),
        P("mp", None, "dp"),
        P("mp", None, "dp"),
        P("mp", None, "dp"),
        P("dp", "mp"),
        P("dp", "mp"),
        P("dp", "mp"),
        P("dp", "mp"),
        P("mp", "dp"),
        P("mp", "dp"),
        P("mp", "dp"),
        P("mp", "dp"),
        P(None, "dp"),
        P(None, "dp"),
        P(None, "dp"),
        P(None, "dp"),
        P(),
    )
    return jax.shard_map(local, mesh=mesh, in_specs=in_specs, out_specs=out_specs, check_vma=False)
```

profile of v0, /device:TPU:0, one launch (start us, length us, event | category | flops | bytes accessed | tf_op | source)
XLA Modules:
  0.0 2159.8 jit_solution(3821488995930234038)
XLA Ops:
  37.9 38.4 %all-gather.10.cloned.1.call-done = bf16[1024,8,192]{0,2,1:T(8,128)(2,1)} async-done(((bf16[256,8,192]{0,2,1:T(8,128)(2,1)}), bf16[1024,8,192]{0,2,1:T(8,128)(2,1)}) %all-gather.10.cloned.1.call-update) | async-done | bytes 3145744 | tf_op jit(solution)/shard_map/all_gather | solution.py:90
  76.3 68.9 %all-gather.8.cloned.1.call-done = bf16[2560,1024]{1,0:T(8,128)(2,1)} async-done(((bf16[1280,1024]{1,0:T(8,128)(2,1)}), bf16[2560,1024]{1,0:T(8,128)(2,1)}) %all-gather.8.cloned.1.call-update) | async-done | bytes 5242896 | tf_op jit(solution)/shard_map/all_gather | solution.py:101
  180.0 291.2 %while.28 = (s32[]{:T(128)}, bf16[5,512,8,64]{1,3,2,0:T(8,128)(2,1)}, f32[5,8,512,1]{2,1,3,0:T(8,128)S(1)}, s32[5,512]{1,0:T(8,128)S(1)}, s32[2560]{0:T(1024)S(1...) while((s32[]{:T(128)}, ...), condition=%wide.region_8.9_spmd.clone, body=%wide.region_5.8_spmd.clone.sunk | while | flops 2814373888 | bytes 148003984 | solution.py:136
  182.1 19.7 fusion.144
  201.7 18.8 fusion.145
  220.5 18.6 fusion.146
  240.7 19.6 fusion.144
  260.3 18.9 fusion.145
  279.2 18.8 fusion.146
  299.5 18.6 fusion.144
  318.1 18.8 fusion.145
  336.9 19.0 fusion.146
  357.4 18.8 fusion.144
  376.1 18.9 fusion.145
  395.1 18.6 fusion.146
  415.2 18.6 fusion.144
  433.8 18.8 fusion.145
  452.7 18.6 fusion.146
  479.6 754.0 %while.29 = (s32[]{:T(128)}, f32[2560,8,64]{0,2,1:T(8,128)}, f32[2560,8,64]{0,2,1:T(8,128)}, f32[5,512,8,64]{1,0,3,2:T(8,128)}, bf16[5,512,8,64]{1,3,2,0:T(8,128...) while((s32[]{:T(128)}, f32[2560,8,64]{0,2,1:T(8,128)}, ...), condition=%wide.region_12.13_spmd.clone, body=%wide.region_10.12_spmd.clone.sunk | while | flops 6816002048 | bytes 353476736 | solution.py:201
  499.1 30.1 %multiply_reduce_fusion.7 = (f32[8,512]{1,0:T(8,128)S(1)}, f32[8,512,2560]{2,1,0:T(8,128)}) fusion(f32[8,512,2560]{2,1,0:T(8,128)} %fusion.156, f32[8,512]{1,0:T(8,128)S(1)} %dynamic-slice_bitcast_fusion.2, bf16[2560,8,64]{0,2,1:T(8,128)(2,1)S(1)} %get-tuple-element.591, bf16[5,512,8,64]{1,3,2,0:T(8,128)(2,1)} %get-tuple-element.587, ...), kind=kOutput, calls=%fused_computation.23.clone.1 | convolution fusion | flops 1394601984 | bytes 88375808 | tf_op jit(solution)/shard_map/while/body/eval_jaxpr/qhd,khd->hqk/dot_general | solution.py:117
  529.2 34.2 %multiply_convert_fusion.5 = bf16[8,512,2560]{2,1,0:T(8,128)(2,1)} fusion(f32[8,512,2560]{2,1,0:T(8,128)} %get-tuple-element.523, f32[8,512,2560]{2,1,0:T(8,128)} %fusion.156, f32[8,512]{1,0:T(8,128)S(1)} %get-tuple-element.524), kind=kLoop, calls=%fused_computation.22.clone.1 | loop fusion | flops 31457280 | bytes 104873984 | tf_op jit(solution)/shard_map/while/body/eval_jaxpr/convert_element_type | solution.py:181
  575.9 21.9 %dynamic_update_slice.22 = f32[5,512,8,64]{1,0,3,2:T(8,128)} dynamic-update-slice(f32[5,512,8,64]{1,0,3,2:T(8,128)} %get-tuple-element.572, f32[1,512,8,64]{1,0,3,2:T(1,128)} %copy.86, s32[]{:T(128)} %get-tuple-element.569, s32[]{:T(128)} %constant.54.clone.1..sunk, s32[]{:T(128)} %constant.54.clone.1..sunk, s32[]{:T(128)} %constant.54.clone.1..sunk) | dynamic-update-slice | bytes 2097156 | tf_op jit(solution)/shard_map/while/body/jit(dynamic_update_index_in_dim)/dynamic_update_slice | solution.py:201
  647.5 30.0 %multiply_reduce_fusion.7 = (f32[8,512]{1,0:T(8,128)S(1)}, f32[8,512,2560]{2,1,0:T(8,128)}) fusion(f32[8,512,2560]{2,1,0:T(8,128)} %fusion.156, f32[8,512]{1,0:T(8,128)S(1)} %dynamic-slice_bitcast_fusion.2, bf16[2560,8,64]{0,2,1:T(8,128)(2,1)S(1)} %get-tuple-element.591, bf16[5,512,8,64]{1,3,2,0:T(8,128)(2,1)} %get-tuple-element.587, ...), kind=kOutput, calls=%fused_computation.23.clone.1 | convolution fusion | flops 1394601984 | bytes 88375808 | tf_op jit(solution)/shard_map/while/body/eval_jaxpr/qhd,khd->hqk/dot_general | solution.py:117
  677.5 34.2 %multiply_convert_fusion.5 = bf16[8,512,2560]{2,1,0:T(8,128)(2,1)} fusion(f32[8,512,2560]{2,1,0:T(8,128)} %get-tuple-element.523, f32[8,512,2560]{2,1,0:T(8,128)} %fusion.156, f32[8,512]{1,0:T(8,128)S(1)} %get-tuple-element.524), kind=kLoop, calls=%fused_computation.22.clone.1 | loop fusion | flops 31457280 | bytes 104873984 | tf_op jit(solution)/shard_map/while/body/eval_jaxpr/convert_element_type | solution.py:181
  724.3 21.9 %dynamic_update_slice.22 = f32[5,512,8,64]{1,0,3,2:T(8,128)} dynamic-update-slice(f32[5,512,8,64]{1,0,3,2:T(8,128)} %get-tuple-element.572, f32[1,512,8,64]{1,0,3,2:T(1,128)} %copy.86, s32[]{:T(128)} %get-tuple-element.569, s32[]{:T(128)} %constant.54.clone.1..sunk, s32[]{:T(128)} %constant.54.clone.1..sunk, s32[]{:T(128)} %constant.54.clone.1..sunk) | dynamic-update-slice | bytes 2097156 | tf_op jit(solution)/shard_map/while/body/jit(dynamic_update_index_in_dim)/dynamic_update_slice | solution.py:201
  760.8 18.7 bitcast_add_fusion.6
  798.8 30.0 %multiply_reduce_fusion.7 = (f32[8,512]{1,0:T(8,128)S(1)}, f32[8,512,2560]{2,1,0:T(8,128)}) fusion(f32[8,512,2560]{2,1,0:T(8,128)} %fusion.156, f32[8,512]{1,0:T(8,128)S(1)} %dynamic-slice_bitcast_fusion.2, bf16[2560,8,64]{0,2,1:T(8,128)(2,1)S(1)} %get-tuple-element.591, bf16[5,512,8,64]{1,3,2,0:T(8,128)(2,1)} %get-tuple-element.587, ...), kind=kOutput, calls=%fused_computation.23.clone.1 | convolution fusion | flops 1394601984 | bytes 88375808 | tf_op jit(solution)/shard_map/while/body/eval_jaxpr/qhd,khd->hqk/dot_general | solution.py:117
  828.8 34.2 %multiply_convert_fusion.5 = bf16[8,512,2560]{2,1,0:T(8,128)(2,1)} fusion(f32[8,512,2560]{2,1,0:T(8,128)} %get-tuple-element.523, f32[8,512,2560]{2,1,0:T(8,128)} %fusion.156, f32[8,512]{1,0:T(8,128)S(1)} %get-tuple-element.524), kind=kLoop, calls=%fused_computation.22.clone.1 | loop fusion | flops 31457280 | bytes 104873984 | tf_op jit(solution)/shard_map/while/body/eval_jaxpr/convert_element_type | solution.py:181
  875.6 21.9 %dynamic_update_slice.22 = f32[5,512,8,64]{1,0,3,2:T(8,128)} dynamic-update-slice(f32[5,512,8,64]{1,0,3,2:T(8,128)} %get-tuple-element.572, f32[1,512,8,64]{1,0,3,2:T(1,128)} %copy.86, s32[]{:T(128)} %get-tuple-element.569, s32[]{:T(128)} %constant.54.clone.1..sunk, s32[]{:T(128)} %constant.54.clone.1..sunk, s32[]{:T(128)} %constant.54.clone.1..sunk) | dynamic-update-slice | bytes 2097156 | tf_op jit(solution)/shard_map/while/body/jit(dynamic_update_index_in_dim)/dynamic_update_slice | solution.py:201
  912.2 18.7 bitcast_add_fusion.6
  950.1 30.1 %multiply_reduce_fusion.7 = (f32[8,512]{1,0:T(8,128)S(1)}, f32[8,512,2560]{2,1,0:T(8,128)}) fusion(f32[8,512,2560]{2,1,0:T(8,128)} %fusion.156, f32[8,512]{1,0:T(8,128)S(1)} %dynamic-slice_bitcast_fusion.2, bf16[2560,8,64]{0,2,1:T(8,128)(2,1)S(1)} %get-tuple-element.591, bf16[5,512,8,64]{1,3,2,0:T(8,128)(2,1)} %get-tuple-element.587, ...), kind=kOutput, calls=%fused_computation.23.clone.1 | convolution fusion | flops 1394601984 | bytes 88375808 | tf_op jit(solution)/shard_map/while/body/eval_jaxpr/qhd,khd->hqk/dot_general | solution.py:117
  980.2 34.2 %multiply_convert_fusion.5 = bf16[8,512,2560]{2,1,0:T(8,128)(2,1)} fusion(f32[8,512,2560]{2,1,0:T(8,128)} %get-tuple-element.523, f32[8,512,2560]{2,1,0:T(8,128)} %fusion.156, f32[8,512]{1,0:T(8,128)S(1)} %get-tuple-element.524), kind=kLoop, calls=%fused_computation.22.clone.1 | loop fusion | flops 31457280 | bytes 104873984 | tf_op jit(solution)/shard_map/while/body/eval_jaxpr/convert_element_type | solution.py:181
  1026.9 21.9 %dynamic_update_slice.22 = f32[5,512,8,64]{1,0,3,2:T(8,128)} dynamic-update-slice(f32[5,512,8,64]{1,0,3,2:T(8,128)} %get-tuple-element.572, f32[1,512,8,64]{1,0,3,2:T(1,128)} %copy.86, s32[]{:T(128)} %get-tuple-element.569, s32[]{:T(128)} %constant.54.clone.1..sunk, s32[]{:T(128)} %constant.54.clone.1..sunk, s32[]{:T(128)} %constant.54.clone.1..sunk) | dynamic-update-slice | bytes 2097156 | tf_op jit(solution)/shard_map/while/body/jit(dynamic_update_index_in_dim)/dynamic_update_slice | solution.py:201
  1063.5 18.7 bitcast_add_fusion.6
  1101.5 30.0 %multiply_reduce_fusion.7 = (f32[8,512]{1,0:T(8,128)S(1)}, f32[8,512,2560]{2,1,0:T(8,128)}) fusion(f32[8,512,2560]{2,1,0:T(8,128)} %fusion.156, f32[8,512]{1,0:T(8,128)S(1)} %dynamic-slice_bitcast_fusion.2, bf16[2560,8,64]{0,2,1:T(8,128)(2,1)S(1)} %get-tuple-element.591, bf16[5,512,8,64]{1,3,2,0:T(8,128)(2,1)} %get-tuple-element.587, ...), kind=kOutput, calls=%fused_computation.23.clone.1 | convolution fusion | flops 1394601984 | bytes 88375808 | tf_op jit(solution)/shard_map/while/body/eval_jaxpr/qhd,khd->hqk/dot_general | solution.py:117
  1131.5 34.2 %multiply_convert_fusion.5 = bf16[8,512,2560]{2,1,0:T(8,128)(2,1)} fusion(f32[8,512,2560]{2,1,0:T(8,128)} %get-tuple-element.523, f32[8,512,2560]{2,1,0:T(8,128)} %fusion.156, f32[8,512]{1,0:T(8,128)S(1)} %get-tuple-element.524), kind=kLoop, calls=%fused_computation.22.clone.1 | loop fusion | flops 31457280 | bytes 104873984 | tf_op jit(solution)/shard_map/while/body/eval_jaxpr/convert_element_type | solution.py:181
  1178.2 21.9 %dynamic_update_slice.22 = f32[5,512,8,64]{1,0,3,2:T(8,128)} dynamic-update-slice(f32[5,512,8,64]{1,0,3,2:T(8,128)} %get-tuple-element.572, f32[1,512,8,64]{1,0,3,2:T(1,128)} %copy.86, s32[]{:T(128)} %get-tuple-element.569, s32[]{:T(128)} %constant.54.clone.1..sunk, s32[]{:T(128)} %constant.54.clone.1..sunk, s32[]{:T(128)} %constant.54.clone.1..sunk) | dynamic-update-slice | bytes 2097156 | tf_op jit(solution)/shard_map/while/body/jit(dynamic_update_index_in_dim)/dynamic_update_slice | solution.py:201
  1214.8 18.7 bitcast_add_fusion.6
  1280.1 18.5 fusion.99
  1298.6 27.0 %fusion.42 = bf16[2560,2048]{1,0:T(8,128)(2,1)S(1)} fusion(f32[2560,2048]{1,0:T(8,128)} %fusion.99, bf16[2048,1024]{1,0:T(8,128)(2,1)} %all-gather.16.cloned.1.call-done, bf16[1,2560,1024]{2,1,0:T(8,128)(2,1)} %all-gather.18.cloned.1.call-done), kind=kOutput, calls=%fused_computation.57 | convolution fusion | flops 10842275840 | bytes 40894464 | tf_op jit(solution)/shard_map/td,fd->tf/dot_general | solution.py:157
  1345.5 21.1 fusion.65
  1413.7 147.5 %reduce-scatter.18.cloned.1.call-done = f32[256,2048]{1,0:T(8,128)} async-done(((f32[1024,2048]{1,0:T(8,128)}), f32[256,2048]{1,0:T(8,128)}) %reduce-scatter.18.cloned.1.call-update) | async-done | bytes 2097168 | tf_op jit(solution)/shard_map/reduce_scatter | solution.py:233
  1561.3 147.6 %reduce-scatter.20.cloned.1.call-done = f32[2048,256]{1,0:T(8,128)} async-done(((f32[2048,1024]{1,0:T(8,128)}), f32[2048,256]{1,0:T(8,128)}) %reduce-scatter.20.cloned.1.call-update) | async-done | bytes 2097168 | tf_op jit(solution)/shard_map/reduce_scatter | solution.py:234
  1720.0 113.8 %reduce-scatter.12.cloned.1.call-done = f32[1280,1024]{1,0:T(8,128)} async-done(((f32[2560,1024]{1,0:T(8,128)}), f32[1280,1024]{1,0:T(8,128)}) %reduce-scatter.12.cloned.1.call-update) | async-done | bytes 5242896 | tf_op jit(solution)/shard_map/reduce_scatter | solution.py:220
  1842.6 22.4 %convolution_add_fusion = f32[2560,1024]{1,0:T(8,128)} fusion(f32[2560,1024]{1,0:T(8,128)} %fusion.98, bf16[2048,1024]{1,0:T(8,128)(2,1)} %all-gather.16.cloned.1.call-done, f32[2560,2048]{1,0:T(8,128)} %fusion.99), kind=kOutput, calls=%fused_computation.71 | convolution fusion | flops 10787225600 | bytes 46137344 | tf_op jit(solution)/shard_map/dot_general | solution.py:146
  1865.0 91.6 %all-reduce.3.cloned.1.call-done = (f32[256,8,192]{0,2,1:T(8,128)}, f32[8,64,256]{2,1,0:T(8,128)}, f32[256,2048]{1,0:T(8,128)}, f32[2048,256]{1,0:T(8,128)}) async-done(((f32[256,8,192]{0,2,1:T(8,128)}, f32[8,64,256]{2,1,0:T(8,128)}, f32[256,2048]{1,0:T(8,128)}, f32[2048,256]{1,0:T(8,128)}), (f32[256,8,192]{0,2,1:T(8,128)}, f32[8,64,256]{2,1,0:T(8,128)}, f32[256,2048]{1,0:T(8,128)}, ...) | async-done | bytes 6291472 | tf_op jit(solution)/shard_map/psum | solution.py:237
  1994.3 109.7 %reduce-scatter.10.cloned.1.call-done = f32[1280,1024]{1,0:T(8,128)} async-done(((f32[2560,1024]{1,0:T(8,128)}), f32[1280,1024]{1,0:T(8,128)}) %reduce-scatter.10.cloned.1.call-update) | async-done | bytes 5242896 | tf_op jit(solution)/shard_map/reduce_scatter | solution.py:144
  2111.9 21.1 psum.55
  (262 shorter events, 522.7 us)
Async XLA Ops:
  7.2 18.2 copy-start.2
  7.2 69.1 %all-gather.10.cloned.1.call-start = ((), (), s32[]{:S(2)}) async-start(), calls=%async_computation.8 | async-start | bytes 3932160 | tf_op jit(solution)/shard_map/all_gather | solution.py:90
  9.8 135.4 %all-gather.8.cloned.1.call-start = ((), (), s32[]{:S(2)}) async-start(), calls=%async_computation.7 | async-start | bytes 7864320 | tf_op jit(solution)/shard_map/all_gather | solution.py:101
  29.8 441.5 %all-gather.12.cloned.1.call-start = ((), (), s32[]{:S(2)}) async-start(), calls=%async_computation.9 | async-start | bytes 1310720 | tf_op jit(solution)/shard_map/all_gather | solution.py:91
  30.6 5.0 copy-start.36
  30.6 440.7 %all-gather.18.cloned.1.call-start = ((), (), s32[]{:S(2)}) async-start(), calls=%async_computation.18 | async-start | bytes 7864320 | tf_op jit(solution)/shard_map/all_gather | solution.py:153
  31.2 1248.9 %all-gather.14.cloned.1.call-start = ((), (), s32[]{:S(2)}) async-start(), calls=%async_computation.10 | async-start | bytes 5242880 | tf_op jit(solution)/shard_map/all_gather | solution.py:92
  34.0 1264.6 %all-gather.16.cloned.1.call-start = ((), (), s32[]{:S(2)}) async-start(), calls=%async_computation.11 | async-start | bytes 5242880 | tf_op jit(solution)/shard_map/all_gather | solution.py:93
  35.1 1360.8 %reduce-scatter.16.cloned.1.call-start = ((), (), s32[]{:S(2)}) async-start(), calls=%async_computation.15 | async-start | bytes 2621440 | tf_op jit(solution)/shard_map/reduce_scatter | solution.py:232
  201.7 18.8 copy-start.1
  260.3 18.9 copy-start.1
  318.1 18.8 copy-start.1
  376.1 18.9 copy-start.1
  433.8 18.8 copy-start.1
  1233.7 10.9 copy-start.11
  1233.7 10.9 copy-start.12
  1233.7 15.6 slice-start.4
  1242.5 6.8 slice-start.5
  1253.6 12.3 slice-start
  1256.7 157.0 %reduce-scatter.14.cloned.1.call-start = ((), (), s32[]{:S(2)}) async-start(), calls=%async_computation.14 | async-start | bytes 7864320 | tf_op jit(solution)/shard_map/reduce_scatter | solution.py:231
  1256.8 9.1 slice-start.1
  1262.5 5.2 slice-start.2
  1280.0 281.3 %reduce-scatter.18.cloned.1.call-start = ((), (), s32[]{:S(2)}) async-start(), calls=%async_computation.16 | async-start | bytes 10485760 | tf_op jit(solution)/shard_map/reduce_scatter | solution.py:233
  1345.4 363.4 %reduce-scatter.20.cloned.1.call-start = ((), (), s32[]{:S(2)}) async-start(), calls=%async_computation.17 | async-start | bytes 10485760 | tf_op jit(solution)/shard_map/reduce_scatter | solution.py:234
  1366.6 15.8 copy-start.37
  1366.6 467.2 %reduce-scatter.12.cloned.1.call-start = ((), (), s32[]{:S(2)}) async-start(), calls=%async_computation.13 | async-start | bytes 15728640 | tf_op jit(solution)/shard_map/reduce_scatter | solution.py:220
  1395.8 560.8 %all-reduce.3.cloned.1.call-start = ((), (), s32[]{:S(2)}) async-start(), calls=%async_computation.20 | async-start | bytes 12582912 | tf_op jit(solution)/shard_map/psum | solution.py:237
  1708.8 272.5 %reduce-scatter.22.cloned.1.call-start = ((), (), s32[]{:S(2)}) async-start(), calls=%async_computation.19 | async-start | bytes 655360
  1709.1 5.1 copy-start.38
  1714.2 119.6 %copy-start.3 = (bf16[1,1280,1024]{2,1,0:T(8,128)(2,1)S(1)}, bf16[1,1280,1024]{2,1,0:T(8,128)(2,1)}, u32[]{:S(2)}) copy-start(bf16[1,1280,1024]{2,1,0:T(8,128)(2,1)} %param.22) | copy-start | bytes 7864324
  1714.2 119.6 %copy-start.25 = (f32[1280]{0:T(1024)S(1)}, f32[1280]{0:T(1024)}, u32[]{:S(2)}) copy-start(f32[1280]{0:T(1024)} %copy-done.24) | copy-start | bytes 15364
  1714.2 119.6 %copy-start.30 = (f32[1,1024]{1,0:T(1,128)S(1)}, f32[1,1024]{1,0:T(1,128)}, u32[]{:S(2)}) copy-start(f32[1,1024]{1,0:T(1,128)} %copy-done.29) | copy-start | bytes 12292
  1720.0 117.4 %copy-start.32 = (f32[1280]{0:T(1024)S(1)}, f32[1280]{0:T(1024)}, u32[]{:S(2)}) copy-start(f32[1280]{0:T(1024)} %copy-done.31) | copy-start | bytes 15364
  1720.0 117.5 %copy-start.28 = (f32[1280]{0:T(1024)S(1)}, f32[1280]{0:T(1024)}, u32[]{:S(2)}) copy-start(f32[1280]{0:T(1024)} %copy-done.27) | copy-start | bytes 15364
  1842.1 261.9 %reduce-scatter.10.cloned.1.call-start = ((), (), s32[]{:S(2)}) async-start(), calls=%async_computation.12 | async-start | bytes 15728640 | tf_op jit(solution)/shard_map/reduce_scatter | solution.py:144
  1994.2 139.5 %copy-start.33 = (f32[2,256]{1,0:T(2,128)S(1)}, f32[2,256]{1,0:T(2,128)}, u32[]{:S(2)}) copy-start(f32[2,256]{1,0:T(2,128)} %param.37) | copy-start | bytes 6148
  1994.2 139.5 %copy-start.34 = (f32[2,256]{1,0:T(2,128)S(1)}, f32[2,256]{1,0:T(2,128)}, u32[]{:S(2)}) copy-start(f32[2,256]{1,0:T(2,128)} %param.38) | copy-start | bytes 6148
  1994.2 139.5 %copy-start.35 = (f32[2,256]{1,0:T(2,128)S(1)}, f32[2,256]{1,0:T(2,128)}, u32[]{:S(2)}) copy-start(f32[2,256]{1,0:T(2,128)} %param.39) | copy-start | bytes 6148
  2134.4 7.6 copy-start.7
  2134.4 7.6 copy-start.8
  2134.4 7.6 copy-start.15
  2134.4 7.7 copy-start.16
  2142.1 4.6 copy-start.18
  2142.1 4.6 copy-start.19
  2142.1 6.0 copy-start.9
  2142.1 6.0 copy-start.10
  2142.1 6.0 copy-start.20
  2142.1 6.5 copy-start.21
  (16 other events, 48.0 us)
Sparse Core Ops, SparseCore 0:
  10.2 66.1 all-gather.9
  78.4 66.7 all-gather.7
  147.4 30.1 all-gather.11
  179.0 66.8 all-gather.17
  247.9 80.7 all-gather.13
  330.7 79.0 all-gather.15
  1256.8 44.3 reduce-scatter.15
  1303.6 110.0 reduce-scatter.13
  1416.2 144.9 reduce-scatter.17
  1563.6 145.1 reduce-scatter.19
  1711.2 122.5 reduce-scatter.11
  1836.4 120.1 all-reduce.2
  1959.6 21.7 reduce-scatter.21
  1983.6 120.3 reduce-scatter.9
where the time goes:
time: 2170 us; the launch traced here: 2160 us
  matrix products  821 us (38%)
  waiting for transfers between devices  749 us (35%)
  other arithmetic  352 us (16%)
  local copies, waits for them, and re-layouts  171 us (8%)
  blocking collectives  44.4 us (2%)
    dot_general x10, matrix products, block_scores(): jnp.einsum('qhd,khd->hqk', block_query, keys, preferred_element_type=jnp....  245 us
    convert_element_type x5, other arithmetic, backward_block(): score_grad = (shares * (share_grad - inner)).astype(jnp.bfloat16)  171 us
    reduce_scatter x1, waiting for transfers between devices, local(): lax.psum_scatter(shrink_gradient, 'dp', scatter_dimension=1, tiled=True)  148 us
    reduce_scatter x1, waiting for transfers between devices, local(): lax.psum_scatter(expand_gradient, 'dp', scatter_dimension=0, tiled=True)  148 us
    dynamic_update_slice x10, local copies, waits for them, and re-layouts, local(): lax.scan(backward_block, (zero_keys, zero_keys), (blocked_query, blocked_...  120 us
    reduce_scatter x1, waiting for transfers between devices, local(): lax.psum_scatter(jnp.einsum('te,de->td', projected_flat, project_flat, pr...  114 us
    reduce_scatter x1, waiting for transfers between devices, local(): lax.psum_scatter(jnp.dot(mixed_flat, mixing_flat, preferred_element_type=...  110 us
    reduce_sum x5, other arithmetic, forward_block(): total = jnp.sum(shifted, axis=2, keepdims=True)  94.1 us
  transfers between devices with their start and end apart: 14, of which 9 were waited for; matrix products, arithmetic and copies ran while one was open for 60% of the time, Pallas kernels for 0%

commit v1 on v0

--- a/solution.py
+++ b/solution.py
@@ -4,13 +4,14 @@
 import jax
 import jax.numpy as jnp
 from jax import lax
+from jax.experimental import pallas as pl
+from jax.experimental.pallas import tpu as pltpu
 from jax.sharding import PartitionSpec as P
 
 D = 1024
 HD = 64
 ROT = 32
 FF = 4096
-QB = 512
 STEP = 10
 
 
@@ -24,27 +25,164 @@
 
 
 def layout(sizes_row, count):
-    ends = jnp.cumsum(sizes_row)
-    places = jnp.arange(count, dtype=jnp.int32)
-    passed = (ends[None, :] <= places[:, None]).astype(jnp.int32)
-    segment = jnp.sum(passed, axis=1)
-    begins = jnp.sum(passed * sizes_row[None, :], axis=1)
-    return (segment, places - begins)
-
-
-def rotary(vectors, places, direction):
+    number = jnp.arange(sizes_row.shape[0], dtype=jnp.int32)
+    ends = jnp.sum(jnp.where(number[None, :] <= number[:, None], sizes_row[None, :], 0), axis=1)
+    tokens = jnp.arange(count, dtype=jnp.int32)
+    passed = (ends[:, None] <= tokens[None, :]).astype(jnp.int32)
+    begins = jnp.sum(passed * sizes_row[:, None], axis=0)
+    return (begins, tokens - begins)
+
+
+def turns(places):
     half_rot = ROT // 2
     counter = jnp.arange(half_rot, dtype=jnp.float32)
     frequency = jnp.exp(counter * (-2.0 * math.log(10000.0) / ROT))
-    angles = places.astype(jnp.float32)[:, None] * frequency[None, :] * direction
-    cosine = jnp.cos(angles)[:, None, :]
-    sine = jnp.sin(angles)[:, None, :]
-    first = vectors[..., :half_rot]
-    second = vectors[..., half_rot:ROT]
-    return jnp.concatenate(
-        [first * cosine - second * sine, second * cosine + first * sine, vectors[..., ROT:]],
-        axis=-1,
-    )
+    angles = places.astype(jnp.float32)[None, :] * frequency[:, None]
+    return jnp.cos(angles), jnp.sin(angles)
+
+
+BQ = 256
+BK = 256
+
+def attend_kernel(together, first_block, proj_ref, back_ref, start_ref, cos_ref, sin_ref,
+                  mixed_ref, grad_ref, q_ref, kt_ref, vt_ref, k_ref, v_ref, dk_ref, dv_ref,
+                  shifted_ref, share_grad_ref, top_ref):
+    count = proj_ref.shape[1]
+    half = ROT // 2
+    cosine, sine = cos_ref[...], sin_ref[...]
+    scale = HD ** (-0.5)
+    for h in range(together):
+        base = h * 3 * HD
+        def turned(at):
+            a = proj_ref[at:at + half]
+            b = proj_ref[at + half:at + ROT]
+            return jnp.concatenate(
+                [a * cosine - b * sine, b * cosine + a * sine, proj_ref[at + ROT:at + HD]], axis=0
+            ).astype(jnp.bfloat16)
+        q_ref[h] = (turned(base).astype(jnp.float32) * scale).astype(jnp.bfloat16)
+        keys = turned(base + HD)
+        values = proj_ref[base + 2 * HD:base + 3 * HD].astype(jnp.bfloat16)
+        kt_ref[h] = keys
+        vt_ref[h] = values
+        k_ref[h] = keys.T
+        v_ref[h] = values.T
+    dk_ref[...] = jnp.zeros_like(dk_ref)
+    dv_ref[...] = jnp.zeros_like(dv_ref)
+    key_at = lax.broadcasted_iota(jnp.int32, (BK, BQ), 0)
+    query_at = lax.broadcasted_iota(jnp.int32, (1, BQ), 1)
+    nt = (((1,), (1,)), ((), ()))
+
+    def query_block(i, _):
+        columns = pl.ds(pl.multiple_of(i * BQ, BQ), BQ)
+        start = start_ref[:, columns]
+        own = query_at + i * BQ
+        lowest = first_block[i]
+        queries = [q_ref[h, :, columns] for h in range(together)]
+        backs = [back_ref[h * HD:(h + 1) * HD, columns] for h in range(together)]
+
+        def scores(j, carry):
+            rows = pl.ds(pl.multiple_of(j * BK, BK), BK)
+            allowed = (key_at >= start - j * BK) & (key_at <= own - j * BK)
+            out = []
+            for h in range(together):
+                top, total, inner = carry[h]
+                raw = jnp.dot(k_ref[h, rows, :], queries[h], preferred_element_type=jnp.float32)
+                share_grad = jnp.dot(v_ref[h, rows, :], backs[h], preferred_element_type=jnp.float32)
+                masked = jnp.where(allowed, raw, masked_value)
+                here = jnp.max(masked, axis=0, keepdims=True)
+                shifted = jnp.exp(masked - here)
+                shifted_ref[h, j] = shifted
+                share_grad_ref[h, j] = share_grad
+                top_ref[h, j] = here
+                new = jnp.maximum(top, here)
+                old_by, here_by = jnp.exp(top - new), jnp.exp(here - new)
+                total = total * old_by + jnp.sum(shifted, axis=0, keepdims=True) * here_by
+                inner = inner * old_by + jnp.sum(shifted * share_grad, axis=0, keepdims=True) * here_by
+                out.append((new, total, inner))
+            return tuple(out)
+
+        zero = jnp.zeros((1, BQ), jnp.float32)
+        empty = (jnp.full((1, BQ), masked_value, jnp.float32), zero, zero)
+        stats = lax.fori_loop(lowest, i + 1, scores, (empty,) * together)
+        inverse = [1.0 / s[1] for s in stats]
+        inners = [s[2] * r for s, r in zip(stats, inverse)]
+
+        def sums(j, carry):
+            rows = pl.ds(pl.multiple_of(j * BK, BK), BK)
+            out = []
+            for h in range(together):
+                mixed, dq = carry[h]
+                by = jnp.exp(top_ref[h, j] - stats[h][0]) * inverse[h]
+                probs = shifted_ref[h, j] * by
+                shares = probs.astype(jnp.bfloat16)
+                score_grad = (probs * (share_grad_ref[h, j] - inners[h])).astype(jnp.bfloat16)
+                mixed = mixed + jnp.dot(vt_ref[h, :, rows], shares, preferred_element_type=jnp.float32)
+                dq = dq + jnp.dot(kt_ref[h, :, rows], score_grad, preferred_element_type=jnp.float32)
+                dv_ref[h, :, rows] += lax.dot_general(backs[h], shares, nt, preferred_element_type=jnp.float32)
+                dk_ref[h, :, rows] += lax.dot_general(queries[h], score_grad, nt, preferred_element_type=jnp.float32)
+                out.append((mixed, dq))
+            return tuple(out)
+
+        nothing = jnp.zeros((HD, BQ), jnp.float32)
+        results = lax.fori_loop(lowest, i + 1, sums, ((nothing, nothing),) * together)
+        cos_here, sin_here = cos_ref[:, columns], sin_ref[:, columns]
+        for h in range(together):
+            mixed, dq = results[h]
+            mixed_ref[h * HD:(h + 1) * HD, columns] = mixed.astype(jnp.bfloat16)
+            dq = dq * scale
+            a, b = dq[:half], dq[half:ROT]
+            grad_ref[h * 3 * HD:h * 3 * HD + HD, columns] = jnp.concatenate(
+                [a * cos_here + b * sin_here, b * cos_here - a * sin_here, dq[ROT:]], axis=0
+            ).astype(jnp.bfloat16)
+        return 0
+
+    lax.fori_loop(0, count // BQ, query_block, 0)
+    for h in range(together):
+        base = h * 3 * HD + HD
+        a, b = dk_ref[h, :half], dk_ref[h, half:ROT]
+        grad_ref[base:base + HD] = jnp.concatenate(
+            [a * cosine + b * sine, b * cosine - a * sine, dk_ref[h, ROT:]], axis=0
+        ).astype(jnp.bfloat16)
+        grad_ref[base + HD:base + 2 * HD] = dv_ref[h].astype(jnp.bfloat16)
+
+
+def attend(projected, back, start, cosine, sine):
+    heads = back.shape[0] // HD
+    count = back.shape[1]
+    together = 2 if heads % 2 == 0 else 1
+    blocks = count // BK
+    first_block = start[0, ::BQ] // BK
+    half = ROT // 2
+    whole = lambda rows: pl.BlockSpec((rows, count), lambda g, *_: (0, 0))
+    mine = lambda rows: pl.BlockSpec((rows, count), lambda g, *_: (g, 0))
+    pairs = heads * blocks * (blocks + 1) // 4
+    return pl.pallas_call(
+        partial(attend_kernel, together),
+        grid_spec=pltpu.PrefetchScalarGridSpec(
+            num_scalar_prefetch=1,
+            grid=(heads // together,),
+            in_specs=[mine(together * 3 * HD), mine(together * HD), whole(1), whole(half), whole(half)],
+            out_specs=[mine(together * HD), mine(together * 3 * HD)],
+            scratch_shapes=[
+                pltpu.VMEM((together, HD, count), jnp.bfloat16),
+                pltpu.VMEM((together, HD, count), jnp.bfloat16),
+                pltpu.VMEM((together, HD, count), jnp.bfloat16),
+                pltpu.VMEM((together, count, HD), jnp.bfloat16),
+                pltpu.VMEM((together, count, HD), jnp.bfloat16),
+                pltpu.VMEM((together, HD, count), jnp.float32),
+                pltpu.VMEM((together, HD, count), jnp.float32),
+                pltpu.VMEM((together, blocks, BK, BQ), jnp.float32),
+                pltpu.VMEM((together, blocks, BK, BQ), jnp.float32),
+                pltpu.VMEM((together, blocks, 1, BQ), jnp.float32),
+            ],
+        ),
+        out_shape=[
+            jax.ShapeDtypeStruct((heads * HD, count), jnp.bfloat16),
+            jax.ShapeDtypeStruct((heads * 3 * HD, count), jnp.bfloat16),
+        ],
+        compiler_params=pltpu.CompilerParams(vmem_limit_bytes=48 * 2**20),
+        cost_estimate=pl.CostEstimate(flops=pairs * 12 * BK * BQ * HD, bytes_accessed=heads * count * HD * 22, transcendentals=pairs * BK * BQ),
+    )(first_block, projected, back, start, cosine, sine)
 
 
 def layer_norm(rows_in, gain, bias):
@@ -100,49 +238,21 @@
     hidden_local = shaped.astype(jnp.bfloat16)
     hidden = lax.all_gather(hidden_local, "mp", axis=0, tiled=True)
     count = hidden.shape[0]
-    blocks = count // QB
-    segment, places = layout(lengths[0], count)
-    index = jnp.arange(count, dtype=jnp.int32)
+    begins, places = layout(lengths[0], count)
+    cosine, sine = turns(places)
     heads_here = project_weight.shape[1]
-    scale = HD ** (-0.5)
     project_flat = project_weight.reshape(project_weight.shape[0], heads_here * 3 * HD)
-    projected = jnp.dot(hidden, project_flat, preferred_element_type=jnp.float32).reshape(
-        count, heads_here, 3 * HD
-    )
-    query = rotary(projected[..., :HD], places, 1.0).astype(jnp.bfloat16)
-    keys = rotary(projected[..., HD : 2 * HD], places, 1.0).astype(jnp.bfloat16)
-    values = projected[..., 2 * HD :].astype(jnp.bfloat16)
-
-    def block_scores(block_query, block_segment, block_index):
-        raw = jnp.einsum("qhd,khd->hqk", block_query, keys, preferred_element_type=jnp.float32)
-        allowed = (block_segment[:, None] == segment[None, :]) & (
-            index[None, :] <= block_index[:, None]
-        )
-        return jnp.where(allowed[None], raw * scale, masked_value)
-
-    def forward_block(items):
-        block_query, block_segment, block_index = items
-        masked = block_scores(block_query, block_segment, block_index)
-        top = jnp.max(masked, axis=2, keepdims=True)
-        shifted = jnp.exp(masked - top)
-        total = jnp.sum(shifted, axis=2, keepdims=True)
-        shares = (shifted / total).astype(jnp.bfloat16)
-        mixed_block = jnp.einsum("hqk,khd->qhd", shares, values, preferred_element_type=jnp.float32)
-        return (mixed_block.astype(jnp.bfloat16), top + jnp.log(total))
-
-    blocked_query = query.reshape(blocks, QB, heads_here, HD)
-    blocked_segment = segment.reshape(blocks, QB)
-    blocked_index = index.reshape(blocks, QB)
-    mixed_parts, log_totals = lax.map(
-        forward_block, (blocked_query, blocked_segment, blocked_index)
-    )
-    mixed = mixed_parts.reshape(count, heads_here, HD)
-    mixed_flat = mixed.reshape(count, heads_here * HD)
     mixing_flat = mixing_weight.reshape(heads_here * HD, mixing_weight.shape[2])
+    back_rows = lax.all_gather(cotangent[0], "mp", axis=0, tiled=True)
+    projected = jnp.einsum("td,de->et", hidden, project_flat, preferred_element_type=jnp.float32)
+    mixed_back = jnp.einsum(
+        "td,fd->ft", back_rows, mixing_flat, preferred_element_type=jnp.float32
+    ).astype(jnp.bfloat16)
+    mixed, projected_grad = attend(projected, mixed_back, begins[None, :], cosine, sine)
     lifted = jnp.dot(hidden, expand_weight, preferred_element_type=jnp.float32)
     activated = jax.nn.gelu(lifted, approximate=True).astype(jnp.bfloat16)
     branch = lax.psum_scatter(
-        jnp.dot(mixed_flat, mixing_flat, preferred_element_type=jnp.float32)
+        jnp.einsum("ft,fd->td", mixed, mixing_flat, preferred_element_type=jnp.float32)
         + jnp.dot(activated, shrink_weight, preferred_element_type=jnp.float32),
         "mp",
         scatter_dimension=0,
@@ -150,7 +260,6 @@
     )
     block_out = (rows_local + branch).astype(jnp.bfloat16)[None]
     back_local = cotangent[0].astype(jnp.float32)
-    back_rows = lax.all_gather(cotangent[0], "mp", axis=0, tiled=True)
     shrink_gradient = jnp.einsum(
         "tf,td->fd", activated, back_rows, preferred_element_type=jnp.float32
     )
@@ -163,62 +272,13 @@
         "td,tf->df", hidden, lifted_grad, preferred_element_type=jnp.float32
     )
     mixing_gradient = jnp.einsum(
-        "the,td->hed", mixed, back_rows, preferred_element_type=jnp.float32
-    )
-    mixed_grad = jnp.einsum(
-        "td,hed->the", back_rows, mixing_weight, preferred_element_type=jnp.float32
-    ).astype(jnp.bfloat16)
-
-    def backward_block(carry, items):
-        key_sum, value_sum = carry
-        block_query, block_segment, block_index, block_total, block_grad = items
-        masked = block_scores(block_query, block_segment, block_index)
-        shares = jnp.exp(masked - block_total)
-        share_grad = jnp.einsum(
-            "qhd,khd->hqk", block_grad, values, preferred_element_type=jnp.float32
-        )
-        inner = jnp.sum(shares * share_grad, axis=2, keepdims=True)
-        score_grad = (shares * (share_grad - inner)).astype(jnp.bfloat16)
-        query_part = (
-            jnp.einsum("hqk,khd->qhd", score_grad, keys, preferred_element_type=jnp.float32) * scale
-        )
-        key_sum = (
-            key_sum
-            + jnp.einsum(
-                "hqk,qhd->khd", score_grad, block_query, preferred_element_type=jnp.float32
-            )
-            * scale
-        )
-        value_sum = value_sum + jnp.einsum(
-            "hqk,qhd->khd",
-            shares.astype(jnp.bfloat16),
-            block_grad,
-            preferred_element_type=jnp.float32,
-        )
-        return ((key_sum, value_sum), query_part)
-
-    zero_keys = jnp.zeros((count, heads_here, HD), jnp.float32)
-    (key_grad, value_grad), query_parts = lax.scan(
-        backward_block,
-        (zero_keys, zero_keys),
-        (
-            blocked_query,
-            blocked_segment,
-            blocked_index,
-            log_totals,
-            mixed_grad.reshape(blocks, QB, heads_here, HD),
-        ),
-    )
-    query_grad = query_parts.reshape(count, heads_here, HD)
-    projected_grad = jnp.concatenate(
-        [rotary(query_grad, places, -1.0), rotary(key_grad, places, -1.0), value_grad], axis=-1
-    ).astype(jnp.bfloat16)
-    projected_flat = projected_grad.reshape(count, heads_here * 3 * HD)
+        "ft,td->fd", mixed, back_rows, preferred_element_type=jnp.float32
+    ).reshape(mixing_weight.shape)
     project_gradient = jnp.einsum(
-        "td,te->de", hidden, projected_flat, preferred_element_type=jnp.float32
+        "td,et->de", hidden, projected_grad, preferred_element_type=jnp.float32
     ).reshape(project_weight.shape)
     hidden_grad = lax.psum_scatter(
-        jnp.einsum("te,de->td", projected_flat, project_flat, preferred_element_type=jnp.float32)
+        jnp.einsum("et,de->td", projected_grad, project_flat, preferred_element_type=jnp.float32)
         + jnp.einsum("tf,df->td", lifted_grad, expand_weight, preferred_element_type=jnp.float32),
         "mp",
         scatter_dimension=0,

time: 2170 us -> 1320 us (0.61)
  matrix products: 821 us -> 183 us
  other arithmetic: 352 us -> 56.8 us
  local copies, waits for them, and re-layouts: 171 us -> 11.6 us
  waiting for transfers between devices: 749 us -> 894 us
  Pallas kernels: 0 us -> 105 us
    dot_general x41 -> x6, matrix products: 700 us -> 59 us  [the longest x1 14.6 us: local(): jnp.einsum('td,de->et', hidden, project_flat, preferred_element_type=jnp....]
    convert_element_type x6 -> x1, other arithmetic: 171 us -> 0.01 us  [turns(): angles = places.astype(jnp.float32)[None, :] * frequency[:, None]]
    dynamic_update_slice x10 -> x0, local copies, waits for them, and re-layouts: 120 us -> none  [local(): lax.scan(backward_block, (zero_keys, zero_keys), (blocked_query, blocked_...]
    pallas_call x0 -> x1, Pallas kernels: none -> 105 us  [attend(): pl.pallas_call(partial(attend_kernel, together), grid_spec=pltpu.Prefetch...]
    reduce_sum x6 -> x2, other arithmetic: 94.3 us -> 0.23 us  [the longest x1 0.11 us: layout(): jnp.sum(jnp.where(number[None, :] <= number[:, None], sizes_row[None, :],...]
    all_gather x1, waiting for transfers between devices: 0.01 us -> 68.4 us  [local(): back_rows = lax.all_gather(cotangent[0], 'mp', axis=0, tiled=True)]
    reduce_scatter x1, waiting for transfers between devices: 17.8 us -> 53.2 us  [local(): lax.psum_scatter(project_gradient, 'dp', scatter_dimension=0, tiled=True)]
  transfers between devices with their start and end apart: 14 -> 14, of which waited for: 9 -> 12; matrix products, arithmetic and copies ran while one was open for 60% -> 16% of each run, Pallas kernels for 0% -> 8%
where the time goes in v1:
time: 1320 us
  waiting for transfers between devices  894 us (68%)
  matrix products  183 us (14%)
  Pallas kernels  105 us (8%)
  other arithmetic  56.8 us (4%)
  blocking collectives  44.3 us (3%)
  between operations  19.6 us (1%)
    reduce_scatter x1, waiting for transfers between devices, local(): lax.psum_scatter(shrink_gradient, 'dp', scatter_dimension=1, tiled=True)  148 us
    reduce_scatter x1, waiting for transfers between devices, local(): lax.psum_scatter(expand_gradient, 'dp', scatter_dimension=0, tiled=True)  148 us
    reduce_scatter x1, waiting for transfers between devices, local(): lax.psum_scatter(jnp.einsum('et,de->td', projected_grad, project_flat, pr...  118 us
    reduce_scatter x1, waiting for transfers between devices, local(): lax.psum_scatter(jnp.einsum('ft,fd->td', mixed, mixing_flat, preferred_el...  110 us
    pallas_call x1, Pallas kernels, attend(): pl.pallas_call(partial(attend_kernel, together), grid_spec=pltpu.Prefetch...  105 us
    psum x1, waiting for transfers between devices, local(): lax.psum((project_gradient, mixing_gradient, expand_gradient, shrink_grad...  91.3 us
    all_gather x1, waiting for transfers between devices, local(): hidden = lax.all_gather(hidden_local, 'mp', axis=0, tiled=True)  68.8 us
    all_gather x1, waiting for transfers between devices, local(): back_rows = lax.all_gather(cotangent[0], 'mp', axis=0, tiled=True)  68.4 us
  transfers between devices with their start and end apart: 14, of which 12 were waited for; matrix products, arithmetic and copies ran while one was open for 16% of the time, Pallas kernels for 8%

profile of v1, /device:TPU:0, one launch (start us, length us, event | category | flops | bytes accessed | tf_op | source)
XLA Modules:
  0.0 1316.1 jit_solution(6984593864470039084)
XLA Ops:
  7.3 1.9 convert_element_type.72
  10.0 2.4 convert_element_type.71
  12.5 12.7 all_gather.21
  27.1 2.3 fusion.16
  29.5 2.9 convert_element_type.75
  32.4 1.1 convert_element_type.77
  34.9 8.2 all-gather.12.cloned.1.call-done
  43.1 68.4 %all-gather.18.cloned.1.call-done = bf16[1,2560,1024]{2,1,0:T(8,128)(2,1)} async-done(((bf16[1,1280,1024]{2,1,0:T(8,128)(2,1)}), bf16[1,2560,1024]{2,1,0:T(8,128)(2,1)}) %all-gather.18.cloned.1.call-update) | async-done | bytes 5242896 | tf_op jit(solution)/shard_map/all_gather | solution.py:246
  111.5 5.7 fusion.29.back_ref
  117.3 59.9 %all-gather.10.cloned.1.call-done = bf16[1024,8,192]{0,2,1:T(8,128)(2,1)} async-done(((bf16[256,8,192]{0,2,1:T(8,128)(2,1)}), bf16[1024,8,192]{0,2,1:T(8,128)(2,1)}) %all-gather.10.cloned.1.call-update) | async-done | bytes 3145744 | tf_op jit(solution)/shard_map/all_gather | solution.py:228
  177.1 68.8 %all-gather.8.cloned.1.call-done = bf16[2560,1024]{1,0:T(8,128)(2,1)} async-done(((bf16[1280,1024]{1,0:T(8,128)(2,1)}), bf16[2560,1024]{1,0:T(8,128)(2,1)}) %all-gather.8.cloned.1.call-update) | async-done | bytes 5242896 | tf_op jit(solution)/shard_map/all_gather | solution.py:239
  245.9 14.6 %convolution_bitcast_fusion.proj_ref = f32[1536,2560]{1,0:T(8,128)} fusion(bf16[2560,1024]{1,0:T(8,128)(2,1)} %all-gather.8.cloned.1.call-done, bf16[1024,1536]{0,1:T(8,128)(2,1)} %bitcast.108), kind=kOutput, calls=%fused_computation.10 | convolution fusion | flops 8053063680 | bytes 24117248 | tf_op jit(solution)/shard_map/td,de->et/dot_general | solution.py:247
  260.4 105.3 %shard_map.353 = (bf16[512,2560]{1,0:T(8,128)(2,1)S(1)}, bf16[1536,2560]{1,0:T(8,128)(2,1)}) custom-call(s32[10]{0:T(128)S(1)} %and_select_fusion.first_block, f32[1536,2560]{1,0:T(8,128)} %convolution_bitcast_fusion.proj_ref, bf16[512,2560]{1,0:T(8,128)(2,1)S(1)} %fusion.29.back_ref, s32[1,2560]{1,0:T(1,128)S(1)} %broadcast_in_dim.42.start_ref, ...), custom_call_target="tpu_custom_call" | custom-call | flops 11072962560 | bytes 28835840 | tf_op jit(solution)/shard_map/pallas_call | solution.py:159
  365.8 4.2 fusion.24
  370.6 13.8 %fusion.54 = f32[1024,1536]{0,1:T(8,128)} fusion(bf16[1536,2560]{1,0:T(8,128)(2,1)} %get-tuple-element.26, bf16[2560,1024]{1,0:T(8,128)(2,1)} %all-gather.8.cloned.1.call-done), kind=kOutput, calls=%fused_computation.97 | convolution fusion | flops 8053063680 | bytes 19398656 | tf_op jit(solution)/shard_map/td,et->de/dot_general | solution.py:277
  384.5 18.2 %fusion.51 = f32[2560,2048]{1,0:T(8,128)} fusion(bf16[2560,1024]{1,0:T(8,128)(2,1)} %all-gather.8.cloned.1.call-done, bf16[1024,2048]{1,0:T(8,128)(2,1)} %all-gather.14.cloned.1.call-done), kind=kOutput, calls=%fused_computation.94 | convolution fusion | flops 10737418240 | bytes 30408704 | tf_op jit(solution)/shard_map/dot_general | solution.py:252
  402.7 8.7 all-gather.16.cloned.1.call-done
  411.4 26.9 %fusion.6 = bf16[2560,2048]{1,0:T(8,128)(2,1)S(1)} fusion(f32[2560,2048]{1,0:T(8,128)} %fusion.51, bf16[2048,1024]{1,0:T(8,128)(2,1)} %all-gather.16.cloned.1.call-done, bf16[1,2560,1024]{2,1,0:T(8,128)(2,1)} %all-gather.18.cloned.1.call-done), kind=kOutput, calls=%fused_computation.8 | convolution fusion | flops 10842275840 | bytes 40894464 | tf_op jit(solution)/shard_map/td,fd->tf/dot_general | solution.py:266
  438.4 4.0 copy-done.31
  442.4 15.9 %fusion.53 = f32[1024,2048]{1,0:T(8,128)} fusion(bf16[2560,1024]{1,0:T(8,128)(2,1)} %all-gather.8.cloned.1.call-done, bf16[2560,2048]{1,0:T(8,128)(2,1)S(1)} %fusion.6), kind=kOutput, calls=%fused_computation.96 | convolution fusion | flops 10737418240 | bytes 24117248 | tf_op jit(solution)/shard_map/td,tf->df/dot_general | solution.py:271
  458.3 22.2 %fusion.22 = f32[2048,1024]{1,0:T(8,128)} fusion(bf16[1,2560,1024]{2,1,0:T(8,128)(2,1)} %all-gather.18.cloned.1.call-done, f32[2560,2048]{1,0:T(8,128)} %fusion.51), kind=kOutput, calls=%fused_computation.32 | convolution fusion | flops 10784604160 | bytes 34603008 | tf_op jit(solution)/shard_map/tf,td->fd/dot_general | solution.py:263
  480.6 1.8 copy-done.30
  482.4 13.5 %fusion.52 = f32[2560,1024]{1,0:T(8,128)} fusion(bf16[1536,2560]{1,0:T(8,128)(2,1)} %get-tuple-element.26, bf16[1024,1536]{0,1:T(8,128)(2,1)S(1)} %bitcast.109), kind=kOutput, calls=%fused_computation.95 | convolution fusion | flops 8053063680 | bytes 21495808 | tf_op jit(solution)/shard_map/et,de->td/dot_general | solution.py:281
  495.9 18.1 %convolution_add_fusion = f32[2560,1024]{1,0:T(8,128)} fusion(f32[2560,1024]{1,0:T(8,128)} %fusion.52, bf16[2560,2048]{1,0:T(8,128)(2,1)} %copy-done.31, bf16[1024,2048]{1,0:T(8,128)(2,1)S(1)} %copy-done.29), kind=kOutput, calls=%fused_computation.20 | convolution fusion | flops 10740039680 | bytes 35651584 | tf_op jit(solution)/shard_map/tf,df->td/dot_general | solution.py:282
  514.1 53.2 %reduce-scatter.14.cloned.1.call-done = f32[256,8,192]{0,2,1:T(8,128)} async-done(((f32[1024,8,192]{0,2,1:T(8,128)}), f32[256,8,192]{0,2,1:T(8,128)}) %reduce-scatter.14.cloned.1.call-update) | async-done | bytes 1572880 | tf_op jit(solution)/shard_map/reduce_scatter | solution.py:291
  567.3 147.5 %reduce-scatter.18.cloned.1.call-done = f32[256,2048]{1,0:T(8,128)} async-done(((f32[1024,2048]{1,0:T(8,128)}), f32[256,2048]{1,0:T(8,128)}) %reduce-scatter.18.cloned.1.call-update) | async-done | bytes 2097168 | tf_op jit(solution)/shard_map/reduce_scatter | solution.py:293
  714.8 147.5 %reduce-scatter.20.cloned.1.call-done = f32[2048,256]{1,0:T(8,128)} async-done(((f32[2048,1024]{1,0:T(8,128)}), f32[2048,256]{1,0:T(8,128)}) %reduce-scatter.20.cloned.1.call-update) | async-done | bytes 2097168 | tf_op jit(solution)/shard_map/reduce_scatter | solution.py:294
  862.4 7.2 fusion.50
  869.6 117.7 %reduce-scatter.12.cloned.1.call-done = f32[1280,1024]{1,0:T(8,128)} async-done(((f32[2560,1024]{1,0:T(8,128)}), f32[1280,1024]{1,0:T(8,128)}) %reduce-scatter.12.cloned.1.call-update) | async-done | bytes 5242896 | tf_op jit(solution)/shard_map/reduce_scatter | solution.py:280
  987.4 4.4 fusion.19
  992.1 3.1 fusion.17
  996.4 22.5 %convolution_add_fusion.1 = f32[2560,1024]{1,0:T(8,128)} fusion(f32[2560,1024]{1,0:T(8,128)} %fusion.50, bf16[2048,1024]{1,0:T(8,128)(2,1)} %all-gather.16.cloned.1.call-done, f32[2560,2048]{1,0:T(8,128)} %fusion.51), kind=kOutput, calls=%fused_computation.21 | convolution fusion | flops 10787225600 | bytes 46137344 | tf_op jit(solution)/shard_map/dot_general | solution.py:256
  1018.9 91.3 %all-reduce.3.cloned.1.call-done = (f32[256,8,192]{0,2,1:T(8,128)}, f32[8,64,256]{2,1,0:T(8,128)}, f32[256,2048]{1,0:T(8,128)}, f32[2048,256]{1,0:T(8,128)}) async-done(((f32[256,8,192]{0,2,1:T(8,128)}, f32[8,64,256]{2,1,0:T(8,128)}, f32[256,2048]{1,0:T(8,128)}, f32[2048,256]{1,0:T(8,128)}), (f32[256,8,192]{0,2,1:T(8,128)}, f32[8,64,256]{2,1,0:T(8,128)}, f32[256,2048]{1,0:T(8,128)}, ...) | async-done | bytes 6291472 | tf_op jit(solution)/shard_map/psum | solution.py:297
  1110.2 1.8 multiply_reduce_fusion.3
  1111.9 2.4 multiply_reduce_fusion.2
  1115.7 2.7 multiply_reduce_fusion.1
  1119.0 2.7 multiply_reduce_fusion
  1122.5 12.4 reduce-scatter.22.cloned.1.call-done
  1135.9 5.6 psum.53
  1141.5 5.0 psum.54
  1147.8 109.7 %reduce-scatter.10.cloned.1.call-done = f32[1280,1024]{1,0:T(8,128)} async-done(((f32[2560,1024]{1,0:T(8,128)}), f32[1280,1024]{1,0:T(8,128)}) %reduce-scatter.10.cloned.1.call-update) | async-done | bytes 5242896 | tf_op jit(solution)/shard_map/reduce_scatter | solution.py:254
  1257.5 8.0 fusion.21
  1265.6 21.0 %psum.55 = f32[]{:T(128)} all-reduce(f32[]{:T(128)S(6)} %add.178), channel_id=1, replica_groups=mesh['mp'=2,'dp'=4,'outer'=4] {'mp','dp'}, use_global_device_ids=true, to_apply=%region_26.27 | all-reduce | flops 1 | bytes 8 | tf_op jit(solution)/shard_map/psum | solution.py:309
  1287.9 2.8 fusion.46
  1290.8 6.3 fusion.48
  1298.0 4.3 fusion.42
  1302.3 1.1 copy-done.12
  1304.0 4.2 fusion.44
  (112 shorter events, 10.4 us)
Async XLA Ops:
  7.2 5.3 copy-start.23
  7.2 18.0 %copy-start.2 = (bf16[1,1280,1024]{2,1,0:T(8,128)(2,1)S(1)}, bf16[1,1280,1024]{2,1,0:T(8,128)(2,1)}, u32[]{:S(2)}) copy-start(bf16[1,1280,1024]{2,1,0:T(8,128)(2,1)} %param.18) | copy-start | bytes 7864324
  7.2 35.9 %all-gather.12.cloned.1.call-start = ((), (), s32[]{:S(2)}) async-start(), calls=%async_computation.9 | async-start | bytes 1310720 | tf_op jit(solution)/shard_map/all_gather | solution.py:229
  9.2 102.3 %all-gather.18.cloned.1.call-start = ((), (), s32[]{:S(2)}) async-start(), calls=%async_computation.18 | async-start | bytes 7864320 | tf_op jit(solution)/shard_map/all_gather | solution.py:246
  10.0 167.2 %all-gather.10.cloned.1.call-start = ((), (), s32[]{:S(2)}) async-start(), calls=%async_computation.8 | async-start | bytes 3932160 | tf_op jit(solution)/shard_map/all_gather | solution.py:228
  12.4 233.5 %all-gather.8.cloned.1.call-start = ((), (), s32[]{:S(2)}) async-start(), calls=%async_computation.7 | async-start | bytes 7864320 | tf_op jit(solution)/shard_map/all_gather | solution.py:239
  25.2 1.3 copy-start.19
  25.7 0.9 copy-start.15
  26.5 0.6 copy-start.21
  26.5 0.6 copy-start.17
  29.4 3.0 copy-start.5
  29.4 4.5 copy-start.27
  29.5 355.0 %all-gather.14.cloned.1.call-start = ((), (), s32[]{:S(2)}) async-start(), calls=%async_computation.10 | async-start | bytes 5242880 | tf_op jit(solution)/shard_map/all_gather | solution.py:230
  32.4 379.0 %all-gather.16.cloned.1.call-start = ((), (), s32[]{:S(2)}) async-start(), calls=%async_computation.11 | async-start | bytes 5242880 | tf_op jit(solution)/shard_map/all_gather | solution.py:231
  33.5 480.6 %reduce-scatter.16.cloned.1.call-start = ((), (), s32[]{:S(2)}) async-start(), calls=%async_computation.15 | async-start | bytes 2621440 | tf_op jit(solution)/shard_map/reduce_scatter | solution.py:292
  260.4 105.3 %copy-start.28 = (bf16[1,2560,1024]{2,1,0:T(8,128)(2,1)S(1)}, bf16[1,2560,1024]{2,1,0:T(8,128)(2,1)}, u32[]{:S(2)}) copy-start(bf16[1,2560,1024]{2,1,0:T(8,128)(2,1)} %all-gather.18.cloned.1.call-done) | copy-start | bytes 15728644
  365.8 4.2 copy-start
  370.0 197.3 %reduce-scatter.14.cloned.1.call-start = ((), (), s32[]{:S(2)}) async-start(), calls=%async_computation.14 | async-start | bytes 7864320 | tf_op jit(solution)/shard_map/reduce_scatter | solution.py:291
  384.4 330.3 %reduce-scatter.18.cloned.1.call-start = ((), (), s32[]{:S(2)}) async-start(), calls=%async_computation.16 | async-start | bytes 10485760 | tf_op jit(solution)/shard_map/reduce_scatter | solution.py:293
  438.4 4.0 copy-start.31
  458.3 404.1 %reduce-scatter.20.cloned.1.call-start = ((), (), s32[]{:S(2)}) async-start(), calls=%async_computation.17 | async-start | bytes 10485760 | tf_op jit(solution)/shard_map/reduce_scatter | solution.py:294
  480.5 1.9 copy-start.30
  480.6 506.8 %reduce-scatter.12.cloned.1.call-start = ((), (), s32[]{:S(2)}) async-start(), calls=%async_computation.13 | async-start | bytes 15728640 | tf_op jit(solution)/shard_map/reduce_scatter | solution.py:280
  482.4 13.5 %copy-start.29 = (bf16[1024,2048]{1,0:T(8,128)(2,1)S(1)}, bf16[1024,2048]{1,0:T(8,128)(2,1)}, u32[]{:S(2)}) copy-start(bf16[1024,2048]{1,0:T(8,128)(2,1)} %all-gather.14.cloned.1.call-done) | copy-start | bytes 12582916
  514.0 348.4 %copy-start.1 = (bf16[512,2560]{1,0:T(8,128)(2,1)S(1)}, bf16[512,2560]{1,0:T(8,128)(2,1)}, u32[]{:S(2)}) copy-start(bf16[512,2560]{1,0:T(8,128)(2,1)} %copy-done) | copy-start | bytes 7864324
  514.0 596.1 %all-reduce.3.cloned.1.call-start = ((), (), s32[]{:S(2)}) async-start(), calls=%async_computation.20 | async-start | bytes 12582912 | tf_op jit(solution)/shard_map/psum | solution.py:297
  862.4 125.0 %copy-start.16 = (f32[1280]{0:T(1024)S(1)}, f32[1280]{0:T(1024)}, u32[]{:S(2)}) copy-start(f32[1280]{0:T(1024)} %copy-done.15) | copy-start | bytes 15364
  862.4 125.0 %copy-start.20 = (f32[1,1024]{1,0:T(1,128)S(1)}, f32[1,1024]{1,0:T(1,128)}, u32[]{:S(2)}) copy-start(f32[1,1024]{1,0:T(1,128)} %copy-done.19) | copy-start | bytes 12292
  862.4 272.5 %reduce-scatter.22.cloned.1.call-start = ((), (), s32[]{:S(2)}) async-start(), calls=%async_computation.19 | async-start | bytes 655360
  869.6 122.2 %copy-start.22 = (f32[1280]{0:T(1024)S(1)}, f32[1280]{0:T(1024)}, u32[]{:S(2)}) copy-start(f32[1280]{0:T(1024)} %copy-done.21) | copy-start | bytes 15364
  869.6 122.2 %copy-start.3 = (bf16[1,1280,1024]{2,1,0:T(8,128)(2,1)S(1)}, bf16[1,1280,1024]{2,1,0:T(8,128)(2,1)}, u32[]{:S(2)}) copy-start(bf16[1,1280,1024]{2,1,0:T(8,128)(2,1)} %param.18) | copy-start | bytes 7864324
  869.6 122.2 %copy-start.18 = (f32[1280]{0:T(1024)S(1)}, f32[1280]{0:T(1024)}, u32[]{:S(2)}) copy-start(f32[1280]{0:T(1024)} %copy-done.17) | copy-start | bytes 15364
  987.4 4.8 copy-start.4
  996.3 261.2 %reduce-scatter.10.cloned.1.call-start = ((), (), s32[]{:S(2)}) async-start(), calls=%async_computation.12 | async-start | bytes 15728640 | tf_op jit(solution)/shard_map/reduce_scatter | solution.py:254
  1147.8 139.5 %copy-start.24 = (f32[2,256]{1,0:T(2,128)S(1)}, f32[2,256]{1,0:T(2,128)}, u32[]{:S(2)}) copy-start(f32[2,256]{1,0:T(2,128)} %param.33) | copy-start | bytes 6148
  1147.8 139.5 %copy-start.25 = (f32[2,256]{1,0:T(2,128)S(1)}, f32[2,256]{1,0:T(2,128)}, u32[]{:S(2)}) copy-start(f32[2,256]{1,0:T(2,128)} %param.34) | copy-start | bytes 6148
  1147.8 139.5 %copy-start.26 = (f32[2,256]{1,0:T(2,128)S(1)}, f32[2,256]{1,0:T(2,128)}, u32[]{:S(2)}) copy-start(f32[2,256]{1,0:T(2,128)} %param.35) | copy-start | bytes 6148
  1147.8 140.1 %copy-start.14 = (f32[8,64,256]{2,1,0:T(8,128)S(1)}, f32[8,64,256]{2,1,0:T(8,128)}, u32[]{:S(2)}) copy-start(f32[8,64,256]{2,1,0:T(8,128)} %param.24) | copy-start | bytes 1572868
  1290.8 6.3 copy-start.6
  1290.8 6.3 copy-start.9
  1290.8 6.3 copy-start.10
  1290.8 7.3 copy-start.11
  1298.0 4.3 copy-start.7
  1298.0 4.3 copy-start.8
  1298.0 5.4 copy-start.12
  1298.0 6.0 copy-start.13
Sparse Core Ops, SparseCore 0:
  10.2 32.8 all-gather.11
  44.6 66.8 all-gather.17
  113.7 63.4 all-gather.9
  179.1 66.7 all-gather.7
  247.9 80.7 all-gather.13
  330.7 80.7 all-gather.15
  414.3 40.4 reduce-scatter.15
  457.2 110.0 reduce-scatter.13
  569.7 144.9 reduce-scatter.17
  717.1 145.1 reduce-scatter.19
  864.7 122.5 reduce-scatter.11
  990.0 120.1 all-reduce.2
  1113.1 21.7 reduce-scatter.21
  1137.1 120.3 reduce-scatter.9

commit v2 on v1

v2 whole, which is shorter than its diff:
```python
from functools import partial
import math

import jax
import jax.numpy as jnp
from jax import lax
from jax.experimental import pallas as pl
from jax.experimental.pallas import tpu as pltpu
from jax.sharding import PartitionSpec as P

D = 1024
HD = 64
ROT = 32
FF = 4096
STEP = 10


norm_epsilon = 1e-05
beta_one = 0.9
beta_two = 0.95
adam_epsilon = 1e-08
decay_rate = 0.1
clip_level = 1.0
masked_value = -1e30


def layout(sizes_row, count):
    number = jnp.arange(sizes_row.shape[0], dtype=jnp.int32)
    ends = jnp.sum(jnp.where(number[None, :] <= number[:, None], sizes_row[None, :], 0), axis=1)
    tokens = jnp.arange(count, dtype=jnp.int32)
    passed = (ends[:, None] <= tokens[None, :]).astype(jnp.int32)
    begins = jnp.sum(passed * sizes_row[:, None], axis=0)
    return (begins, tokens - begins)


def turns(places):
    half_rot = ROT // 2
    counter = jnp.arange(half_rot, dtype=jnp.float32)
    frequency = jnp.exp(counter * (-2.0 * math.log(10000.0) / ROT))
    angles = places.astype(jnp.float32)[None, :] * frequency[:, None]
    return jnp.cos(angles), jnp.sin(angles)


BQ = 256
BK = 256


def attend_kernel(together, parts, *refs):
    facts = refs[0]
    projected_refs = refs[1 : 1 + parts]
    back_refs = refs[1 + parts : 1 + 2 * parts]
    start_ref, cos_ref, sin_ref = refs[1 + 2 * parts : 4 + 2 * parts]
    mixed_refs = refs[4 + 2 * parts : 4 + 3 * parts]
    grad_refs = refs[4 + 3 * parts : 4 + 4 * parts]
    (
        query_ref,
        key_columns_ref,
        value_columns_ref,
        key_ref,
        value_ref,
        back_ref,
        query_grad_ref,
        key_grad_ref,
        value_grad_ref,
        shifted_ref,
        share_grad_ref,
        top_ref,
    ) = refs[4 + 4 * parts :]
    width = projected_refs[0].shape[1]
    count = width * parts
    blocks = count // BQ
    turn = facts[blocks]
    half = ROT // 2
    scale = HD ** (-0.5)
    nt = (((1,), (1,)), ((), ()))

    def place_of(part):
        if parts == 1:
            return pl.ds(0, width)
        block = lax.rem(part * (blocks // parts) + blocks - turn, blocks)
        return pl.ds(pl.multiple_of(block * BQ, BQ), width)

    for part in range(parts):
        columns = slice(part * width, (part + 1) * width)
        cosine, sine = cos_ref[:, place_of(part)], sin_ref[:, place_of(part)]
        projected_ref = projected_refs[part]

        def turned(at):
            first = projected_ref[at : at + half]
            second = projected_ref[at + half : at + ROT]
            return jnp.concatenate(
                [
                    first * cosine - second * sine,
                    second * cosine + first * sine,
                    projected_ref[at + ROT : at + HD],
                ],
                axis=0,
            ).astype(jnp.bfloat16)

        for h in range(together):
            base = h * 3 * HD
            query_ref[h, :, columns] = (turned(base).astype(jnp.float32) * scale).astype(
                jnp.bfloat16
            )
            keys = turned(base + HD)
            values = projected_ref[base + 2 * HD : base + 3 * HD].astype(jnp.bfloat16)
            key_columns_ref[h, :, columns] = keys
            value_columns_ref[h, :, columns] = values
            key_ref[h, columns] = keys.T
            value_ref[h, columns] = values.T
            back_ref[h, :, columns] = back_refs[part][h * HD : (h + 1) * HD]
    key_grad_ref[...] = jnp.zeros_like(key_grad_ref)
    value_grad_ref[...] = jnp.zeros_like(value_grad_ref)
    key_at = lax.broadcasted_iota(jnp.int32, (BK, BQ), 0)
    query_at = lax.broadcasted_iota(jnp.int32, (1, BQ), 1)

    def stored(block):
        if parts == 1:
            return pl.ds(pl.multiple_of(block * BQ, BQ), BQ)
        return pl.ds(pl.multiple_of(lax.rem(block + turn, blocks) * BQ, BQ), BQ)

    def query_block(i, _):
        columns = stored(i)
        start = start_ref[:, pl.ds(pl.multiple_of(i * BQ, BQ), BQ)]
        own = query_at + i * BQ
        lowest = facts[i]
        queries = [query_ref[h, :, columns] for h in range(together)]
        backs = [back_ref[h, :, columns] for h in range(together)]

        def scores(j, carry):
            rows = stored(j)
            allowed = (key_at >= start - j * BK) & (key_at <= own - j * BK)
            out = []
            for h in range(together):
                top, total, inner = carry[h]
                raw = jnp.dot(key_ref[h, rows, :], queries[h], preferred_element_type=jnp.float32)
                share_grad = jnp.dot(
                    value_ref[h, rows, :], backs[h], preferred_element_type=jnp.float32
                )
                masked = jnp.where(allowed, raw, masked_value)
                here = jnp.max(masked, axis=0, keepdims=True)
                shifted = jnp.exp(masked - here)
                shifted_ref[h, j] = shifted
                share_grad_ref[h, j] = share_grad
                top_ref[h, j] = here
                new = jnp.maximum(top, here)
                old_by, here_by = jnp.exp(top - new), jnp.exp(here - new)
                total = total * old_by + jnp.sum(shifted, axis=0, keepdims=True) * here_by
                inner = (
                    inner * old_by
                    + jnp.sum(shifted * share_grad, axis=0, keepdims=True) * here_by
                )
                out.append((new, total, inner))
            return tuple(out)

        zero = jnp.zeros((1, BQ), jnp.float32)
        empty = (jnp.full((1, BQ), masked_value, jnp.float32), zero, zero)
        stats = lax.fori_loop(lowest, i + 1, scores, (empty,) * together)
        inverse = [1.0 / s[1] for s in stats]
        inners = [s[2] * r for s, r in zip(stats, inverse)]

        def sums(j, carry):
            rows = stored(j)
            out = []
            for h in range(together):
                mixed, query_grad = carry[h]
                by = jnp.exp(top_ref[h, j] - stats[h][0]) * inverse[h]
                probs = shifted_ref[h, j] * by
                shares = probs.astype(jnp.bfloat16)
                score_grad = (probs * (share_grad_ref[h, j] - inners[h])).astype(jnp.bfloat16)
                mixed = mixed + jnp.dot(
                    value_columns_ref[h, :, rows], shares, preferred_element_type=jnp.float32
                )
                query_grad = query_grad + jnp.dot(
                    key_columns_ref[h, :, rows], score_grad, preferred_element_type=jnp.float32
                )
                value_grad_ref[h, :, rows] += lax.dot_general(
                    backs[h], shares, nt, preferred_element_type=jnp.float32
                )
                key_grad_ref[h, :, rows] += lax.dot_general(
                    queries[h], score_grad, nt, preferred_element_type=jnp.float32
                )
                out.append((mixed, query_grad))
            return tuple(out)

        nothing = jnp.zeros((HD, BQ), jnp.float32)
        results = lax.fori_loop(lowest, i + 1, sums, ((nothing, nothing),) * together)
        for h in range(together):
            back_ref[h, :, columns] = results[h][0].astype(jnp.bfloat16)
            query_grad_ref[h, :, columns] = results[h][1] * scale
        return 0

    lax.fori_loop(0, blocks, query_block, 0)
    for part in range(parts):
        columns = slice(part * width, (part + 1) * width)
        cosine, sine = cos_ref[:, place_of(part)], sin_ref[:, place_of(part)]

        def turned_back(ref, h):
            first, second = ref[h, :half, columns], ref[h, half:ROT, columns]
            return jnp.concatenate(
                [
                    first * cosine + second * sine,
                    second * cosine - first * sine,
                    ref[h, ROT:, columns],
                ],
                axis=0,
            ).astype(jnp.bfloat16)

        for h in range(together):
            base = h * 3 * HD
            mixed_refs[part][h * HD : (h + 1) * HD] = back_ref[h, :, columns]
            grad_refs[part][base : base + HD] = turned_back(query_grad_ref, h)
            grad_refs[part][base + HD : base + 2 * HD] = turned_back(key_grad_ref, h)
            grad_refs[part][base + 2 * HD : base + 3 * HD] = value_grad_ref[h, :, columns].astype(
                jnp.bfloat16
            )


def attend(projected, back, begins, cosine, sine, offset):
    parts = len(projected)
    heads = back[0].shape[0] // HD
    width = back[0].shape[1]
    count = begins.shape[0]
    together = 2 if heads % 2 == 0 else 1
    blocks = count // BK
    half = ROT // 2
    turn = jnp.asarray(offset * ((blocks // parts) if parts > 1 else 0), jnp.int32)
    facts = jnp.concatenate([begins[::BQ] // BK, turn[None]])
    whole = lambda rows: pl.BlockSpec((rows, count), lambda g, *_: (0, 0))
    mine = lambda rows: pl.BlockSpec((rows, width), lambda g, *_: (g, 0))
    pairs = heads * blocks * 3
    results = pl.pallas_call(
        partial(attend_kernel, together, parts),
        grid_spec=pltpu.PrefetchScalarGridSpec(
            num_scalar_prefetch=1,
            grid=(heads // together,),
            in_specs=[mine(together * 3 * HD)] * parts
            + [mine(together * HD)] * parts
            + [whole(1), whole(half), whole(half)],
            out_specs=[mine(together * HD)] * parts + [mine(together * 3 * HD)] * parts,
            scratch_shapes=[
                pltpu.VMEM((together, HD, count), jnp.bfloat16),
                pltpu.VMEM((together, HD, count), jnp.bfloat16),
                pltpu.VMEM((together, HD, count), jnp.bfloat16),
                pltpu.VMEM((together, count, HD), jnp.bfloat16),
                pltpu.VMEM((together, count, HD), jnp.bfloat16),
                pltpu.VMEM((together, HD, count), jnp.bfloat16),
                pltpu.VMEM((together, HD, count), jnp.float32),
                pltpu.VMEM((together, HD, count), jnp.float32),
                pltpu.VMEM((together, HD, count), jnp.float32),
                pltpu.VMEM((together, blocks, BK, BQ), jnp.float32),
                pltpu.VMEM((together, blocks, BK, BQ), jnp.float32),
                pltpu.VMEM((together, blocks, 1, BQ), jnp.float32),
            ],
        ),
        out_shape=[jax.ShapeDtypeStruct((heads * HD, width), jnp.bfloat16)] * parts
        + [jax.ShapeDtypeStruct((heads * 3 * HD, width), jnp.bfloat16)] * parts,
        compiler_params=pltpu.CompilerParams(vmem_limit_bytes=48 * 2**20),
        cost_estimate=pl.CostEstimate(
            flops=pairs * 12 * BK * BQ * 256,
            bytes_accessed=heads * count * HD * 22,
            transcendentals=pairs * BK * BQ,
        ),
    )(facts, *projected, *back, begins[None, :], cosine, sine)
    return results[:parts], results[parts:]


def layer_norm(rows_in, gain, bias):
    mean = jnp.mean(rows_in, axis=1, keepdims=True)
    centred = rows_in - mean
    spread = jnp.mean(centred * centred, axis=1, keepdims=True)
    normed = centred * lax.rsqrt(spread + norm_epsilon)
    return normed * gain + bias


def adam_update(master, first, second, gradient, rate, decay):
    first_new = beta_one * first + (1.0 - beta_one) * gradient
    second_new = beta_two * second + (1.0 - beta_two) * gradient * gradient
    first_hat = first_new / (1.0 - beta_one**STEP)
    second_hat = second_new / (1.0 - beta_two**STEP)
    master_new = master - rate * (
        first_hat / (jnp.sqrt(second_hat) + adam_epsilon) + decay * master
    )
    return (master_new, first_new, second_new, master_new.astype(jnp.bfloat16))


def product(pattern, left, right):
    return jnp.einsum(pattern, left, right, preferred_element_type=jnp.float32)


def gelu_both(lifted, active_grad):
    activated, pull = jax.vjp(partial(jax.nn.gelu, approximate=True), lifted)
    return pull(active_grad)[0].astype(jnp.bfloat16)


def gelu(lifted):
    return jax.nn.gelu(lifted, approximate=True).astype(jnp.bfloat16)


def swap(array, axis, bit):
    size = lax.axis_size(axis)
    return lax.ppermute(array, axis, [(i, i ^ bit) for i in range(size)])


def ordered(index, mine, other, axis):
    return jnp.where(
        index == 0,
        jnp.concatenate([mine, other], axis=axis),
        jnp.concatenate([other, mine], axis=axis),
    )


class Paired:
    def __init__(self):
        outer = lax.axis_index("outer")
        self.far, self.near = outer // 2, outer % 2
        self.place = lax.axis_index("dp")
        self.deep = lax.axis_size("dp")

    def gather(self, master, cut, depth):
        half = master.shape[cut] // 2
        own = lax.dynamic_slice_in_dim(master, self.near * half, half, cut).astype(jnp.bfloat16)
        own = lax.all_gather(own, "dp", axis=depth, tiled=True)
        return jnp.concatenate([own, swap(own, "outer", 1)], axis=cut)

    def total(self, own, sibling, cut, depth):
        own = own + swap(sibling, "outer", 1)
        half = own.shape[cut] // 2
        keep = lax.dynamic_slice_in_dim(own, self.far * half, half, cut)
        send = lax.dynamic_slice_in_dim(own, (1 - self.far) * half, half, cut)
        keep = keep + swap(send.astype(jnp.bfloat16), "outer", 2).astype(jnp.float32)
        piece = keep.shape[depth] // self.deep

        def part(at):
            return lax.dynamic_slice_in_dim(keep, at * piece, piece, depth)

        result = part(self.place)
        for step in range(1, self.deep):
            target = lax.rem(self.place + step, self.deep)
            pairs = [(i, (i + step) % self.deep) for i in range(self.deep)]
            result = result + lax.ppermute(
                part(target).astype(jnp.bfloat16), "dp", pairs
            ).astype(jnp.float32)
        return result

    def spread(self, share, cut):
        pair = ordered(self.far, share, swap(share, "outer", 2), cut)
        return ordered(self.near, pair, swap(pair, "outer", 1), cut)


def local(
    inputs,
    cotangent,
    lengths,
    project_master,
    project_first,
    project_second,
    mixing_master,
    mixing_first,
    mixing_second,
    expand_master,
    expand_first,
    expand_second,
    shrink_master,
    shrink_first,
    shrink_second,
    norm_master,
    norm_first,
    norm_second,
):
    split, deep = lax.axis_size("mp"), lax.axis_size("dp")
    heads_here = project_master.shape[1]
    width = inputs.shape[1]
    paired = (
        split == 2
        and lax.axis_size("outer") == 4
        and heads_here % 4 == 0
        and width % BQ == 0
    )
    position = lax.axis_index("mp")
    count = width * split
    norm_weight = lax.all_gather(norm_master.astype(jnp.bfloat16), "dp", axis=1, tiled=True)
    gain = norm_weight[0].astype(jnp.float32)
    bias = norm_weight[1].astype(jnp.float32)
    project_flat = project_master.reshape(project_master.shape[0], heads_here * 3 * HD)
    mixing_flat = mixing_master.reshape(heads_here * HD, mixing_master.shape[2])
    masters = (project_flat, mixing_flat, expand_master, shrink_master)
    cuts, depths = (1, 0, 1, 0), (0, 1, 0, 1)
    rows_local = inputs[0].astype(jnp.float32)
    shaped, norm_pull = jax.vjp(layer_norm, rows_local, gain, bias)
    hidden_local = shaped.astype(jnp.bfloat16)
    begins, places = layout(lengths[0], count)
    cosine, sine = turns(places)
    if paired:
        plan = Paired()
        expand, shrink, mixing, project = (
            plan.gather(masters[k], cuts[k], depths[k]) for k in (2, 3, 1, 0)
        )
        backs = [cotangent[0], swap(cotangent[0], "mp", 1)]
        hiddens = [hidden_local, swap(hidden_local, "mp", 1)]
    else:
        project, mixing, expand, shrink = (
            lax.all_gather(master.astype(jnp.bfloat16), "dp", axis=depth, tiled=True)
            for master, depth in zip(masters, depths)
        )
        backs = [lax.all_gather(cotangent[0], "mp", axis=0, tiled=True)]
        hiddens = [lax.all_gather(hidden_local, "mp", axis=0, tiled=True)]

    def over_tokens(pattern, lefts, rights):
        return sum(product(pattern, left, right) for left, right in zip(lefts, rights))

    def weight_sum(pattern, lefts, rights, cut, depth):
        if not paired:
            term = over_tokens(pattern, lefts, rights)
            term = lax.psum_scatter(term, "dp", scatter_dimension=depth, tiled=True)
            return lax.psum(term, "outer")
        sources = rights if cut == 1 else lefts
        axis = 0 if pattern.split(",")[cut].index("t") == 1 else 1
        half = sources[0].shape[axis] // 2

        def term(near):
            chosen = [
                lax.slice_in_dim(v, near * half, (near + 1) * half, axis=axis) for v in sources
            ]
            return (
                over_tokens(pattern, lefts, chosen)
                if cut == 1
                else over_tokens(pattern, chosen, rights)
            )

        sibling = term(1)
        return plan.total(term(0), sibling, cut, depth)

    lifteds = [product("td,df->tf", hidden, expand) for hidden in hiddens]
    activated = [gelu(lifted) for lifted in lifteds]
    active_grads = [product("td,fd->tf", back, shrink) for back in backs]
    lifted_grads = [gelu_both(a, b) for a, b in zip(lifteds, active_grads)]
    shrink_sum = weight_sum("tf,td->fd", activated, backs, 0, 1)
    expand_sum = weight_sum("td,tf->df", hiddens, lifted_grads, 1, 0)
    projected = [product("td,de->et", hidden, project) for hidden in hiddens]
    mixed_backs = [product("td,fd->ft", back, mixing).astype(jnp.bfloat16) for back in backs]
    mixed, projected_grads = attend(projected, mixed_backs, begins, cosine, sine, position)
    mixing_sum = weight_sum("ft,td->fd", mixed, backs, 0, 1)
    project_sum = weight_sum("td,et->de", hiddens, projected_grads, 1, 0)
    hidden_grads = [
        product("et,de->td", a, project) + product("tf,df->td", b, expand)
        for a, b in zip(projected_grads, lifted_grads)
    ]
    branches = [
        product("ft,fd->td", a, mixing) + product("tf,fd->td", b, shrink)
        for a, b in zip(mixed, activated)
    ]

    def over_positions(terms):
        if paired:
            other = swap(terms[1].astype(jnp.bfloat16), "mp", 1)
            return terms[0] + other.astype(jnp.float32)
        return lax.psum_scatter(terms[0], "mp", scatter_dimension=0, tiled=True)

    rows_grad, gain_grad, bias_grad = norm_pull(over_positions(hidden_grads))
    input_grad = (cotangent[0].astype(jnp.float32) + rows_grad)[None]
    block_out = (rows_local + over_positions(branches)).astype(jnp.bfloat16)[None]
    sums = (project_sum, mixing_sum, expand_sum, shrink_sum)
    own_square = sum(jnp.sum(v * v) for v in sums)
    everywhere = ("mp", "dp", "outer")
    if not paired:
        own_square = own_square / lax.axis_size("outer")
    norm_all = lax.psum(
        jnp.concatenate([gain_grad, bias_grad, jnp.full((128,), own_square)]), everywhere
    )
    norm_full = norm_all[: 2 * D].reshape(2, D)
    grad_norm = jnp.sqrt(norm_all[2 * D] + jnp.sum(norm_full * norm_full))
    factor = clip_level / jnp.maximum(grad_norm, clip_level)
    norm_gradient = lax.dynamic_slice_in_dim(
        norm_full, lax.axis_index("dp") * (D // deep), D // deep, 1
    )
    gradients = [
        (plan.spread(v, cut) if paired else v).reshape(master.shape)
        for v, cut, master in zip(
            sums, cuts, (project_master, mixing_master, expand_master, shrink_master)
        )
    ]
    states = (
        (project_master, project_first, project_second, D ** (-0.5)),
        (mixing_master, mixing_first, mixing_second, (D // 32) ** (-0.5)),
        (expand_master, expand_first, expand_second, D ** (-0.5)),
        (shrink_master, shrink_first, shrink_second, FF ** (-0.5)),
    )
    results = [block_out, input_grad]
    for (master, first, second, rate), gradient in zip(states, gradients):
        results += adam_update(master, first, second, factor * gradient, rate, decay_rate)
    results += adam_update(norm_master, norm_first, norm_second, factor * norm_gradient, 0.3, 0.0)
    return (*results, grad_norm)


def solution(mesh):
    in_specs = (
        P(("dp", "outer"), "mp", None),
        P(("dp", "outer"), "mp", None),
        P(("dp", "outer"), None),
        P("dp", "mp", None),
        P("dp", "mp", None),
        P("dp", "mp", None),
        P("mp", None, "dp"),
        P("mp", None, "dp"),
        P("mp", None, "dp"),
        P("dp", "mp"),
        P("dp", "mp"),
        P("dp", "mp"),
        P("mp", "dp"),
        P("mp", "dp"),
        P("mp", "dp"),
        P(None, "dp"),
        P(None, "dp"),
        P(None, "dp"),
    )
    out_specs = (
        P(("dp", "outer"), "mp", None),
        P(("dp", "outer"), "mp", None),
        P("dp", "mp", None),
        P("dp", "mp", None),
        P("dp", "mp", None),
        P("dp", "mp", None),
        P("mp", None, "dp"),
        P("mp", None, "dp"),
        P("mp", None, "dp"),
        P("mp", None, "dp"),
        P("dp", "mp"),
        P("dp", "mp"),
        P("dp", "mp"),
        P("dp", "mp"),
        P("mp", "dp"),
        P("mp", "dp"),
        P("mp", "dp"),
        P("mp", "dp"),
        P(None, "dp"),
        P(None, "dp"),
        P(None, "dp"),
        P(None, "dp"),
        P(),
    )
    return jax.shard_map(local, mesh=mesh, in_specs=in_specs, out_specs=out_specs, check_vma=False)
```

time: 1320 us -> 722 us (0.55)
  waiting for transfers between devices: 894 us -> 144 us
  starting transfers between devices: 1.39 us -> 40.5 us
  matrix products: 183 us -> 215 us
  local copies, waits for them, and re-layouts: 11.6 us -> 42 us
  blocking collectives: 44.3 us -> 74.3 us
  other arithmetic: 56.8 us -> 74.2 us
    reduce_scatter x6 -> x0, waiting for transfers between devices: 576 us -> none  [the longest x1 148 us: local(): lax.psum_scatter(shrink_gradient, 'dp', scatter_dimension=1, tiled=True)]
    all_gather x6 -> x3, waiting for transfers between devices: 214 us -> 8.9 us  [gather(): own = lax.all_gather(own, 'dp', axis=depth, tiled=True)]
    ppermute x0 -> x36, waiting for transfers between devices: none -> 135 us  [the longest x24 106 us: swap(): return lax.ppermute(array, axis, [(i, i ^ bit) for i in range(size)])]
    psum x1 -> x0, waiting for transfers between devices: 91.3 us -> none  [local(): lax.psum((project_gradient, mixing_gradient, expand_gradient, shrink_grad...]
    ppermute x0 -> x36, starting transfers between devices: none -> 40.4 us  [the longest x12 21.9 us: total(): lax.ppermute(part(target).astype(jnp.bfloat16), 'dp', pairs)]
    dot_general x12 -> x32, matrix products: 183 us -> 215 us  [product(): return jnp.einsum(pattern, left, right, preferred_element_type=jnp.float32)]
    all_gather x0 -> x1, blocking collectives: none -> 20.9 us  [gather(): own = lax.all_gather(own, 'dp', axis=depth, tiled=True)]
    add x0 -> x7, other arithmetic: none -> 20.8 us  [the longest x3 15.4 us: total(): own = own + swap(sibling, 'outer', 1)]
  transfers between devices with their start and end apart: 14 -> 39, of which waited for: 12 -> 11; matrix products, arithmetic and copies ran while one was open for 16% -> 44% of each run, Pallas kernels for 8% -> 15%
where the time goes in v2:
time: 722 us; the launch traced here: 717 us
  matrix products  215 us (30%)
  waiting for transfers between devices  144 us (20%)
  Pallas kernels  107 us (15%)
  blocking collectives  74.3 us (10%)
  other arithmetic  74.2 us (10%)
  local copies, waits for them, and re-layouts  42 us (6%)
  starting transfers between devices  40.5 us (6%)
  between operations  20 us (3%)
    dot_general x32, matrix products, product(): return jnp.einsum(pattern, left, right, preferred_element_type=jnp.float32)  215 us
    pallas_call x1, Pallas kernels, attend(): pl.pallas_call(partial(attend_kernel, together, parts), grid_spec=pltpu.P...  107 us
    ppermute x24, waiting for transfers between devices, swap(): return lax.ppermute(array, axis, [(i, i ^ bit) for i in range(size)])  106 us
    psum x1, blocking collectives, local(): lax.psum(jnp.concatenate([gain_grad, bias_grad, jnp.full((128,), own_squa...  40.7 us
    ppermute x12, waiting for transfers between devices, total(): lax.ppermute(part(target).astype(jnp.bfloat16), 'dp', pairs)  29.7 us
    unnamed x117, local copies, waits for them, and re-layouts  25.8 us
    ppermute x12, starting transfers between devices, total(): lax.ppermute(part(target).astype(jnp.bfloat16), 'dp', pairs)  21.9 us
    convert_element_type x5, other arithmetic, adam_update(): return (master_new, first_new, second_new, master_new.astype(jnp.bfloat16))  21.2 us
  transfers between devices with their start and end apart: 39, of which 11 were waited for; matrix products, arithmetic and copies ran while one was open for 44% of the time, Pallas kernels for 15%

profile of v2, /device:TPU:0, one launch (start us, length us, event | category | flops | bytes accessed | tf_op | source)
XLA Modules:
  0.0 716.8 jit_solution(5997249839860279535)
XLA Ops:
  12.3 12.7 %all_gather.16 = bf16[2,1024]{1,0:T(2,128)(2,1)S(1)} all-gather(bf16[2,256]{1,0:T(2,128)(2,1)S(1)} %convert_element_type.186), channel_id=1, replica_groups=mesh['mp'=2,'dp'=4,'outer'=4] {'dp'}, dimensions={1}, use_global_device_ids=true | all-gather | bytes 5120 | tf_op jit(solution)/shard_map/all_gather | solution.py:382
  33.8 20.9 %all_gather.17 = bf16[256,1024]{1,0:T(8,128)(2,1)} all-gather(bf16[256,256]{1,0:T(8,128)(2,1)S(1)} %dynamic-slice_convert_fusion.16), channel_id=1, replica_groups=mesh['mp'=2,'dp'=4,'outer'=4] {'dp'}, dimensions={1}, use_global_device_ids=true | all-gather | bytes 655360 | tf_op jit(solution)/shard_map/all_gather | solution.py:323
  66.7 3.9 convolution_convert_fusion.1.refs_3_
  71.9 69.9 %collective-permute-done.3 = bf16[1280,1024]{1,0:T(8,128)(2,1)} collective-permute-done((bf16[1280,1024]{1,0:T(8,128)(2,1)}, bf16[1280,1024]{1,0:T(8,128)(2,1)}, u32[]{:S(2)}, u32[]{:S(2)}) %collective-permute-start.3) | collective-permute-done | bytes 2621472 | tf_op jit(solution)/shard_map/ppermute | solution.py:302
  141.7 3.6 convolution_convert_fusion.refs_4_
  145.5 7.0 all-gather.8.cloned.1.call-done
  159.1 9.3 %fusion.104.refs_1_ = f32[1536,1280]{1,0:T(8,128)} fusion(bf16[1024,1536]{0,1:T(8,128)(2,1)S(1)} %constant_dynamic-update-slice_fusion, bf16[1280,1024]{1,0:T(8,128)(2,1)} %fusion.29), kind=kOutput, calls=%fused_computation.203 | convolution fusion | flops 4026531840 | bytes 13631488 | tf_op jit(solution)/shard_map/td,de->et/dot_general | solution.py:288
  168.4 8.1 %fusion.105.refs_2_ = f32[1536,1280]{1,0:T(8,128)} fusion(bf16[1024,1536]{0,1:T(8,128)(2,1)S(1)} %constant_dynamic-update-slice_fusion, bf16[1280,1024]{1,0:T(8,128)(2,1)} %collective-permute-done.1), kind=kOutput, calls=%fused_computation.204 | convolution fusion | flops 4026531840 | bytes 13631488 | tf_op jit(solution)/shard_map/td,de->et/dot_general | solution.py:288
  176.6 106.6 %shard_map.353 = (bf16[512,1280]{1,0:T(8,128)(2,1)S(1)}, bf16[512,1280]{1,0:T(8,128)(2,1)S(1)}, bf16[1536,1280]{1,0:T(8,128)(2,1)}, bf16[1536,1280]{1,0:T(8,128)(2,1)}) custom-call(s32[11]{0:T(128)S(1)} %pad_add_fusion.refs_0_, f32[1536,1280]{1,0:T(8,128)} %fusion.104.refs_1_, f32[1536,1280]{1,0:T(8,128)} %fusion.105.refs_2_, ...), custom_call_target="tpu_custom_call" | custom-call | flops 48318382080 | bytes 28835840 | tf_op jit(solution)/shard_map/pallas_call | solution.py:232
  283.2 10.2 %fusion.109 = f32[1280,1024]{1,0:T(8,128)} fusion(bf16[1536,1280]{1,0:T(8,128)(2,1)} %get-tuple-element.29, bf16[1024,1536]{0,1:T(8,128)(2,1)} %copy-done.26), kind=kOutput, calls=%fused_computation.208 | convolution fusion | flops 4026531840 | bytes 12320768 | tf_op jit(solution)/shard_map/et,de->td/dot_general | solution.py:288
  293.4 3.9 fusion.57
  303.1 5.6 fusion.69
  308.7 5.8 fusion.61
  314.5 3.8 fusion.106
  318.5 5.8 fusion.59
  334.8 11.7 %multiply_convert_fusion.1 = (bf16[1280,2048]{1,0:T(8,128)(2,1)S(1)}, f32[1280,2048]{1,0:T(8,128)}) fusion(bf16[1280,1024]{1,0:T(8,128)(2,1)} %fusion.29, bf16[1024,2048]{1,0:T(8,128)(2,1)S(1)} %constant_dynamic-update-slice_fusion.4), kind=kOutput, calls=%fused_computation.29 | convolution fusion | flops 5392302080 | bytes 22544384 | tf_op jit(solution)/shard_map/td,df->tf/dot_general | solution.py:288
  346.7 16.4 %fusion.6 = bf16[1280,2048]{1,0:T(8,128)(2,1)S(1)} fusion(f32[1280,2048]{1,0:T(8,128)} %get-tuple-element.133, bf16[2048,1024]{1,0:T(8,128)(2,1)S(1)} %constant_dynamic-update-slice_fusion.6, bf16[1,1280,1024]{2,1,0:T(8,128)(2,1)} %param.19), kind=kOutput, calls=%fused_computation.10 | convolution fusion | flops 5421137920 | bytes 22544384 | tf_op jit(solution)/shard_map/td,fd->tf/dot_general | solution.py:288
  363.1 7.4 %fusion.110 = f32[1280,1024]{1,0:T(8,128)} fusion(bf16[1280,2048]{1,0:T(8,128)(2,1)S(1)} %fusion.6, bf16[1024,2048]{1,0:T(8,128)(2,1)S(1)} %constant_dynamic-update-slice_fusion.4), kind=kOutput, calls=%fused_computation.209 | convolution fusion | flops 5368709120 | bytes 14680064 | tf_op jit(solution)/shard_map/tf,df->td/dot_general | solution.py:288
  370.5 6.3 fusion.45
  376.8 6.6 fusion.49
  383.3 6.2 fusion.37
  389.5 6.2 fusion.41
  395.8 11.7 %multiply_convert_fusion = (bf16[1280,2048]{1,0:T(8,128)(2,1)S(1)}, f32[1280,2048]{1,0:T(8,128)}) fusion(bf16[1280,1024]{1,0:T(8,128)(2,1)} %collective-permute-done.1, bf16[1024,2048]{1,0:T(8,128)(2,1)S(1)} %constant_dynamic-update-slice_fusion.4), kind=kOutput, calls=%fused_computation.28 | convolution fusion | flops 5392302080 | bytes 22544384 | tf_op jit(solution)/shard_map/td,df->tf/dot_general | solution.py:288
  407.5 16.5 %fusion.13 = bf16[1280,2048]{1,0:T(8,128)(2,1)S(1)} fusion(f32[1280,2048]{1,0:T(8,128)} %get-tuple-element.131, bf16[2048,1024]{1,0:T(8,128)(2,1)S(1)} %constant_dynamic-update-slice_fusion.6, bf16[1280,1024]{1,0:T(8,128)(2,1)} %collective-permute-done.3), kind=kOutput, calls=%fused_computation.17 | convolution fusion | flops 5421137920 | bytes 22544384 | tf_op jit(solution)/shard_map/td,fd->tf/dot_general | solution.py:288
  424.0 7.5 %fusion.111 = f32[1280,1024]{1,0:T(8,128)} fusion(bf16[1280,2048]{1,0:T(8,128)(2,1)S(1)} %fusion.13, bf16[1024,2048]{1,0:T(8,128)(2,1)S(1)} %constant_dynamic-update-slice_fusion.4), kind=kOutput, calls=%fused_computation.210 | convolution fusion | flops 5368709120 | bytes 14680064 | tf_op jit(solution)/shard_map/tf,df->td/dot_general | solution.py:288
  431.5 7.3 %add_convert_fusion = bf16[1280,1024]{1,0:T(8,128)(2,1)} fusion(f32[1280,1024]{1,0:T(8,128)} %fusion.111, bf16[1536,1280]{1,0:T(8,128)(2,1)S(1)} %copy-done.41, bf16[1024,1536]{0,1:T(8,128)(2,1)S(1)} %copy-done.27), kind=kOutput, calls=%fused_computation.49 | convolution fusion | flops 4029153280 | bytes 14942208 | tf_op jit(solution)/shard_map/et,de->td/dot_general | solution.py:288
  440.4 5.7 fusion.108
  446.1 6.2 fusion.63
  452.4 6.5 fusion.47
  458.9 6.6 fusion.66
  465.5 5.7 fusion.107
  471.2 6.4 fusion.39
  495.4 15.9 %collective-permute-done.30 = f32[128,256]{1,0:T(8,128)S(1)} collective-permute-done((f32[128,256]{1,0:T(8,128)S(1)}, f32[128,256]{1,0:T(8,128)S(1)}, u32[]{:S(2)}, u32[]{:S(2)}) %collective-permute-start.30) | collective-permute-done | bytes 131104 | tf_op jit(solution)/shard_map/ppermute | solution.py:302
  514.7 4.4 fusion.32
  523.0 7.3 %collective-permute-done.11 = bf16[256,384]{0,1:T(8,128)(2,1)S(1)} collective-permute-done((bf16[256,384]{0,1:T(8,128)(2,1)S(1)}, bf16[256,384]{0,1:T(8,128)(2,1)S(1)}, u32[]{:S(2)}, u32[]{:S(2)}) %collective-permute-start.11) | collective-permute-done | bytes 196640 | tf_op jit(solution)/shard_map/ppermute | solution.py:341
  534.0 6.3 add_add_fusion.2
  542.6 6.1 add_add_fusion.1
  551.0 17.8 %collective-permute-done.6 = bf16[1280,1024]{1,0:T(8,128)(2,1)} collective-permute-done((bf16[1280,1024]{1,0:T(8,128)(2,1)}, bf16[1280,1024]{1,0:T(8,128)(2,1)}, u32[]{:S(2)}, u32[]{:S(2)}) %collective-permute-start.6) | collective-permute-done | bytes 2621472 | tf_op jit(solution)/shard_map/ppermute | solution.py:302
  568.8 6.8 add_bitcast_fusion
  587.5 5.6 collective-permute-start.27
  593.1 5.1 collective-permute-start.25
  600.6 16.0 %collective-permute-done.21 = bf16[256,512]{0,1:T(8,128)(2,1)S(1)} collective-permute-done((bf16[256,512]{0,1:T(8,128)(2,1)S(1)}, bf16[256,512]{0,1:T(8,128)(2,1)S(1)}, u32[]{:S(2)}, u32[]{:S(2)}) %collective-permute-start.21) | collective-permute-done | bytes 262176 | tf_op jit(solution)/shard_map/ppermute | solution.py:341
  617.9 3.5 collective-permute-start.32
  621.4 4.6 collective-permute-done.26
  628.1 40.7 %psum.7 = f32[2176]{0:T(1024)S(1)} all-reduce(f32[2176]{0:T(1024)S(1)} %pad_maximum_fusion), channel_id=1, replica_groups=mesh['mp'=2,'dp'=4,'outer'=4] {'mp','dp','outer'}, use_global_device_ids=true, to_apply=%region_12.13 | all-reduce | flops 2176 | bytes 17408 | tf_op jit(solution)/shard_map/psum | solution.py:468
  678.0 6.3 fusion.101
  687.9 5.6 fusion.97
  703.0 5.9 fusion.95
  (253 shorter events, 120.8 us)
Async XLA Ops:
  7.2 51.6 %all-gather.4.cloned.1.call-start = ((), (), s32[]{:S(2)}) async-start(), calls=%async_computation | async-start | bytes 1966080 | tf_op jit(solution)/shard_map/all_gather | solution.py:323
  9.4 136.0 %all-gather.6.cloned.1.call-start = ((), (), s32[]{:S(2)}) async-start(), calls=%async_computation.1 | async-start | bytes 2621440 | tf_op jit(solution)/shard_map/all_gather | solution.py:323
  11.5 140.9 %all-gather.8.cloned.1.call-start = ((), (), s32[]{:S(2)}) async-start(), calls=%async_computation.2 | async-start | bytes 2621440 | tf_op jit(solution)/shard_map/all_gather | solution.py:323
  26.3 28.4 %copy-start.39 = (s32[1,12]{1,0:T(1,128)S(1)}, s32[1,12]{1,0:T(1,128)}, u32[]{:S(2)}) copy-start(s32[1,12]{1,0:T(1,128)} %param.20) | copy-start | bytes 148
  28.7 30.1 %copy-start.12 = (f32[256,2048]{1,0:T(8,128)S(1)}, f32[256,2048]{1,0:T(8,128)}, u32[]{:S(2)}) copy-start(f32[256,2048]{1,0:T(8,128)} %param.27) | copy-start | bytes 6291460
  28.7 139.8 %collective-permute-start.1 = (bf16[1280,1024]{1,0:T(8,128)(2,1)}, bf16[1280,1024]{1,0:T(8,128)(2,1)}, u32[]{:S(2)}, u32[]{:S(2)}) collective-permute-start(bf16[1280,1024]{1,0:T(8,128)(2,1)} %fusion.29), channel_id=1, source_target_pairs={{0,16},{16,0},{1,17},{17,1},{2,18},{18,2},{3,19},{19,3},{4,20},{20... | collective-permute-start | bytes 7864328 | tf_op jit(solution)/shard_map/ppermute | solution.py:302
  30.2 111.5 %collective-permute-start.3 = (bf16[1280,1024]{1,0:T(8,128)(2,1)}, bf16[1280,1024]{1,0:T(8,128)(2,1)}, u32[]{:S(2)}, u32[]{:S(2)}) collective-permute-start(bf16[1280,1024]{1,0:T(8,128)(2,1)} %bitcast.7), channel_id=1, source_target_pairs={{0,16},{16,0},{1,17},{17,1},{2,18},{18,2},{3,19},{19,3},{4,20},{20... | collective-permute-start | bytes 7864328 | tf_op jit(solution)/shard_map/ppermute | solution.py:302
  54.8 10.8 %collective-permute-start.2 = (bf16[256,1024]{1,0:T(8,128)(2,1)}, bf16[256,1024]{1,0:T(8,128)(2,1)}, u32[]{:S(2)}, u32[]{:S(2)}) collective-permute-start(bf16[256,1024]{1,0:T(8,128)(2,1)} %all_gather.17), channel_id=1, source_target_pairs={{0,1},{1,0},{2,3},{3,2},{4,5},{5,4},{6,7},{7,6},{8,9},{9,8},{10,11... | collective-permute-start | bytes 1572872 | tf_op jit(solution)/shard_map/ppermute | solution.py:302
  58.8 97.0 %collective-permute-start = (bf16[1024,768]{0,1:T(8,128)(2,1)}, bf16[1024,768]{0,1:T(8,128)(2,1)}, u32[]{:S(2)}, u32[]{:S(2)}) collective-permute-start(bf16[1024,768]{0,1:T(8,128)(2,1)} %all-gather.4.cloned.1.call-done), channel_id=1, source_target_pairs={{0,1},{1,0},{2,3},{3,2},{4,5},{5,4},{6,7},{7,6},{8,9},{9,8},{10,11... | collective-permute-start | bytes 4718600 | tf_op jit(solution)/shard_map/ppermute | solution.py:302
  145.4 187.6 %collective-permute-start.4 = (bf16[1024,1024]{1,0:T(8,128)(2,1)}, bf16[1024,1024]{1,0:T(8,128)(2,1)}, u32[]{:S(2)}, u32[]{:S(2)}) collective-permute-start(bf16[1024,1024]{1,0:T(8,128)(2,1)} %all-gather.6.cloned.1.call-done), channel_id=1, source_target_pairs={{0,1},{1,0},{2,3},{3,2},{4,5},{5,4},{6,7},{7,6},{8,9},{9,8},{10,11... | collective-permute-start | bytes 6291464 | tf_op jit(solution)/shard_map/ppermute | solution.py:302
  152.4 194.1 %collective-permute-start.5 = (bf16[1024,1024]{1,0:T(8,128)(2,1)}, bf16[1024,1024]{1,0:T(8,128)(2,1)S(1)}, u32[]{:S(2)}, u32[]{:S(2)}) collective-permute-start(bf16[1024,1024]{1,0:T(8,128)(2,1)} %all-gather.8.cloned.1.call-done), channel_id=1, source_target_pairs={{0,1},{1,0},{2,3},{3,2},{4,5},{5,4},{6,7},{7,6},{8,9},{9,8},{10,11... | collective-permute-start | bytes 6291464 | tf_op jit(solution)/shard_map/ppermute | solution.py:302
  283.2 43.7 %copy-start = (bf16[512,1280]{1,0:T(8,128)(2,1)}, bf16[512,1280]{1,0:T(8,128)(2,1)S(1)}, u32[]{:S(2)}) copy-start(bf16[512,1280]{1,0:T(8,128)(2,1)S(1)} %get-tuple-element.28) | copy-start | bytes 3932164
  302.7 24.2 %collective-permute-start.13 = (f32[256,1024]{1,0:T(8,128)S(1)}, f32[256,1024]{1,0:T(8,128)S(1)}, u32[]{:S(2)}, u32[]{:S(2)}) collective-permute-start(f32[256,1024]{1,0:T(8,128)S(1)} %convolution_add_fusion), channel_id=1, source_target_pairs={{0,1},{1,0},{2,3},{3,2},{4,5},{5,4},{6,7},{7,6},{8,9},{9,8},{10,11... | collective-permute-start | bytes 3145736 | tf_op jit(solution)/shard_map/ppermute | solution.py:302
  318.3 164.2 %collective-permute-start.8 = (f32[1024,768]{0,1:T(8,128)}, f32[1024,768]{0,1:T(8,128)}, u32[]{:S(2)}, u32[]{:S(2)}) collective-permute-start(f32[1024,768]{0,1:T(8,128)} %fusion.69), channel_id=1, source_target_pairs={{0,1},{1,0},{2,3},{3,2},{4,5},{5,4},{6,7},{7,6},{8,9},{9,8},{10,11... | collective-permute-start | bytes 9437192 | tf_op jit(solution)/shard_map/ppermute | solution.py:302
  331.4 146.2 %collective-permute-start.14 = (bf16[128,1024]{1,0:T(8,128)(2,1)}, bf16[128,1024]{1,0:T(8,128)(2,1)}, u32[]{:S(2)}, u32[]{:S(2)}) collective-permute-start(bf16[128,1024]{1,0:T(8,128)(2,1)} %dynamic-slice_convert_fusion.12), channel_id=1, source_target_pairs={{0,2},{1,3},{2,0},{3,1},{4,6},{5,7},{6,4},{7,5},{8,10},{9,11},{10,... | collective-permute-start | bytes 786440 | tf_op jit(solution)/shard_map/ppermute | solution.py:302
  346.5 43.0 %copy-start.46 = (bf16[1280,2048]{1,0:T(8,128)(2,1)}, bf16[1280,2048]{1,0:T(8,128)(2,1)S(1)}, u32[]{:S(2)}) copy-start(bf16[1280,2048]{1,0:T(8,128)(2,1)S(1)} %get-tuple-element.132) | copy-start | bytes 15728644
  407.4 51.4 %copy-start.42 = (bf16[1280,2048]{1,0:T(8,128)(2,1)}, bf16[1280,2048]{1,0:T(8,128)(2,1)S(1)}, u32[]{:S(2)}) copy-start(bf16[1280,2048]{1,0:T(8,128)(2,1)S(1)} %get-tuple-element.130) | copy-start | bytes 15728644
  438.9 75.7 %collective-permute-start.7 = (bf16[1280,1024]{1,0:T(8,128)(2,1)}, bf16[1280,1024]{1,0:T(8,128)(2,1)S(1)}, u32[]{:S(2)}, u32[]{:S(2)}) collective-permute-start(bf16[1280,1024]{1,0:T(8,128)(2,1)} %add_convert_fusion), channel_id=1, source_target_pairs={{0,16},{16,0},{1,17},{17,1},{2,18},{18,2},{3,19},{19,3},{4,20},{20... | collective-permute-start | bytes 7864328 | tf_op jit(solution)/shard_map/ppermute | solution.py:302
  452.4 81.6 %collective-permute-start.18 = (f32[1024,1024]{0,1:T(8,128)}, f32[1024,1024]{0,1:T(8,128)}, u32[]{:S(2)}, u32[]{:S(2)}) collective-permute-start(f32[1024,1024]{0,1:T(8,128)} %fusion.63), channel_id=1, source_target_pairs={{0,1},{1,0},{2,3},{3,2},{4,5},{5,4},{6,7},{7,6},{8,9},{9,8},{10,11... | collective-permute-start | bytes 12582920 | tf_op jit(solution)/shard_map/ppermute | solution.py:302
  478.6 9.0 %collective-permute-start.17 = (bf16[128,256]{1,0:T(8,128)(2,1)S(1)}, bf16[128,256]{1,0:T(8,128)(2,1)S(1)}, u32[]{:S(2)}, u32[]{:S(2)}) collective-permute-start(bf16[128,256]{1,0:T(8,128)(2,1)S(1)} %get-tuple-element.122), channel_id=1, source_target_pairs={{0,12},{4,0},{8,4},{12,8},{1,13},{5,1},{9,5},{13,9},{2,14},{6,2},{... | collective-permute-start | bytes 196616 | tf_op jit(solution)/shard_map/ppermute | solution.py:341
  481.1 8.4 %collective-permute-start.16 = (bf16[128,256]{1,0:T(8,128)(2,1)S(1)}, bf16[128,256]{1,0:T(8,128)(2,1)S(1)}, u32[]{:S(2)}, u32[]{:S(2)}) collective-permute-start(bf16[128,256]{1,0:T(8,128)(2,1)S(1)} %get-tuple-element.123), channel_id=1, source_target_pairs={{0,8},{4,12},{8,0},{12,4},{1,9},{5,13},{9,1},{13,5},{2,10},{6,14},... | collective-permute-start | bytes 196616 | tf_op jit(solution)/shard_map/ppermute | solution.py:341
  482.5 8.4 %collective-permute-start.15 = (bf16[128,256]{1,0:T(8,128)(2,1)S(1)}, bf16[128,256]{1,0:T(8,128)(2,1)S(1)}, u32[]{:S(2)}, u32[]{:S(2)}) collective-permute-start(bf16[128,256]{1,0:T(8,128)(2,1)S(1)} %get-tuple-element.121), channel_id=1, source_target_pairs={{0,4},{4,8},{8,12},{12,0},{1,5},{5,9},{9,13},{13,1},{2,6},{6,10},{... | collective-permute-start | bytes 196616 | tf_op jit(solution)/shard_map/ppermute | solution.py:341
  487.6 54.9 %collective-permute-start.23 = (f32[1024,1024]{1,0:T(8,128)}, f32[1024,1024]{1,0:T(8,128)}, u32[]{:S(2)}, u32[]{:S(2)}) collective-permute-start(f32[1024,1024]{1,0:T(8,128)} %fusion.66), channel_id=1, source_target_pairs={{0,1},{1,0},{2,3},{3,2},{4,5},{5,4},{6,7},{7,6},{8,9},{9,8},{10,11... | collective-permute-start | bytes 12582920 | tf_op jit(solution)/shard_map/ppermute | solution.py:302
  489.5 23.1 %collective-permute-start.9 = (bf16[1024,384]{0,1:T(8,128)(2,1)S(1)}, bf16[1024,384]{0,1:T(8,128)(2,1)S(1)}, u32[]{:S(2)}, u32[]{:S(2)}) collective-permute-start(bf16[1024,384]{0,1:T(8,128)(2,1)S(1)} %dynamic-slice_convert_fusion.2), channel_id=1, source_target_pairs={{0,2},{1,3},{2,0},{3,1},{4,6},{5,7},{6,4},{7,5},{8,10},{9,11},{10,... | collective-permute-start | bytes 2359304 | tf_op jit(solution)/shard_map/ppermute | solution.py:302
  491.6 19.6 %collective-permute-start.30 = (f32[128,256]{1,0:T(8,128)S(1)}, f32[128,256]{1,0:T(8,128)S(1)}, u32[]{:S(2)}, u32[]{:S(2)}) collective-permute-start(f32[128,256]{1,0:T(8,128)S(1)} %get-tuple-element.105), channel_id=1, source_target_pairs={{0,2},{1,3},{2,0},{3,1},{4,6},{5,7},{6,4},{7,5},{8,10},{9,11},{10,... | collective-permute-start | bytes 393224 | tf_op jit(solution)/shard_map/ppermute | solution.py:302
  511.2 57.6 %collective-permute-start.6 = (bf16[1280,1024]{1,0:T(8,128)(2,1)}, bf16[1280,1024]{1,0:T(8,128)(2,1)}, u32[]{:S(2)}, u32[]{:S(2)}) collective-permute-start(bf16[1280,1024]{1,0:T(8,128)(2,1)} %add_convert_fusion.1), channel_id=1, source_target_pairs={{0,16},{16,0},{1,17},{17,1},{2,18},{18,2},{3,19},{19,3},{4,20},{20... | collective-permute-start | bytes 7864328 | tf_op jit(solution)/shard_map/ppermute | solution.py:302
  513.0 9.3 %collective-permute-start.12 = (bf16[256,384]{0,1:T(8,128)(2,1)S(1)}, bf16[256,384]{0,1:T(8,128)(2,1)S(1)}, u32[]{:S(2)}, u32[]{:S(2)}) collective-permute-start(bf16[256,384]{0,1:T(8,128)(2,1)S(1)} %get-tuple-element.119), channel_id=1, source_target_pairs={{0,12},{4,0},{8,4},{12,8},{1,13},{5,1},{9,5},{13,9},{2,14},{6,2},{... | collective-permute-start | bytes 589832 | tf_op jit(solution)/shard_map/ppermute | solution.py:341
  514.6 15.7 %collective-permute-start.11 = (bf16[256,384]{0,1:T(8,128)(2,1)S(1)}, bf16[256,384]{0,1:T(8,128)(2,1)S(1)}, u32[]{:S(2)}, u32[]{:S(2)}) collective-permute-start(bf16[256,384]{0,1:T(8,128)(2,1)S(1)} %get-tuple-element.120), channel_id=1, source_target_pairs={{0,8},{4,12},{8,0},{12,4},{1,9},{5,13},{9,1},{13,5},{2,10},{6,14},... | collective-permute-start | bytes 589832 | tf_op jit(solution)/shard_map/ppermute | solution.py:341
  522.3 8.0 %collective-permute-start.10 = (bf16[256,384]{0,1:T(8,128)(2,1)S(1)}, bf16[256,384]{0,1:T(8,128)(2,1)S(1)}, u32[]{:S(2)}, u32[]{:S(2)}) collective-permute-start(bf16[256,384]{0,1:T(8,128)(2,1)S(1)} %get-tuple-element.118), channel_id=1, source_target_pairs={{0,4},{4,8},{8,12},{12,0},{1,5},{5,9},{9,13},{13,1},{2,6},{6,10},{... | collective-permute-start | bytes 589832 | tf_op jit(solution)/shard_map/ppermute | solution.py:341
  531.7 45.2 %collective-permute-start.28 = (f32[256,384]{0,1:T(8,128)}, f32[256,384]{0,1:T(8,128)}, u32[]{:S(2)}, u32[]{:S(2)}) collective-permute-start(f32[256,384]{0,1:T(8,128)} %get-tuple-element.107), channel_id=1, source_target_pairs={{0,2},{1,3},{2,0},{3,1},{4,6},{5,7},{6,4},{7,5},{8,10},{9,11},{10,... | collective-permute-start | bytes 1179656 | tf_op jit(solution)/shard_map/ppermute | solution.py:302
  534.0 34.8 %slice-start = ((s8[5242880]{0:T(1024)(128)(4,1)}), s8[4194304]{0:T(1024)(128)(4,1)S(1)}, s32[]{:S(2)}) async-start(s8[5242880]{0:T(1024)(128)(4,1)} %bitcast.135), calls=%async_computation.3 | async-start | bytes 8388608
  541.6 27.3 %slice-start.1 = ((s8[5242880]{0:T(1024)(128)(4,1)}), s8[1048576]{0:T(1024)(128)(4,1)S(1)}, s32[]{:S(2)}) async-start(s8[5242880]{0:T(1024)(128)(4,1)} %bitcast.135), calls=%async_computation.4 | async-start | bytes 2097152
  541.6 36.8 %collective-permute-start.19 = (bf16[1024,512]{0,1:T(8,128)(2,1)}, bf16[1024,512]{0,1:T(8,128)(2,1)}, u32[]{:S(2)}, u32[]{:S(2)}) collective-permute-start(bf16[1024,512]{0,1:T(8,128)(2,1)} %dynamic-slice_convert_fusion.1), channel_id=1, source_target_pairs={{0,2},{1,3},{2,0},{3,1},{4,6},{5,7},{6,4},{7,5},{8,10},{9,11},{10,... | collective-permute-start | bytes 3145736 | tf_op jit(solution)/shard_map/ppermute | solution.py:302
  548.7 26.9 %copy-start.4 = (f32[1024,1024]{1,0:T(8,128)}, f32[1024,1024]{1,0:T(8,128)S(1)}, u32[]{:S(2)}) copy-start(f32[1024,1024]{1,0:T(8,128)S(1)} %add_add_fusion.1) | copy-start | bytes 12582916
  550.0 35.7 %collective-permute-start.24 = (bf16[512,1024]{1,0:T(8,128)(2,1)}, bf16[512,1024]{1,0:T(8,128)(2,1)}, u32[]{:S(2)}, u32[]{:S(2)}) collective-permute-start(bf16[512,1024]{1,0:T(8,128)(2,1)} %dynamic-slice_convert_fusion), channel_id=1, source_target_pairs={{0,2},{1,3},{2,0},{3,1},{4,6},{5,7},{6,4},{7,5},{8,10},{9,11},{10,... | collective-permute-start | bytes 3145736 | tf_op jit(solution)/shard_map/ppermute | solution.py:302
  580.9 12.2 %collective-permute-start.22 = (bf16[256,512]{0,1:T(8,128)(2,1)S(1)}, bf16[256,512]{0,1:T(8,128)(2,1)S(1)}, u32[]{:S(2)}, u32[]{:S(2)}) collective-permute-start(bf16[256,512]{0,1:T(8,128)(2,1)S(1)} %get-tuple-element.116), channel_id=1, source_target_pairs={{0,12},{4,0},{8,4},{12,8},{1,13},{5,1},{9,5},{13,9},{2,14},{6,2},{... | collective-permute-start | bytes 786440 | tf_op jit(solution)/shard_map/ppermute | solution.py:341
  583.3 33.3 %collective-permute-start.21 = (bf16[256,512]{0,1:T(8,128)(2,1)S(1)}, bf16[256,512]{0,1:T(8,128)(2,1)S(1)}, u32[]{:S(2)}, u32[]{:S(2)}) collective-permute-start(bf16[256,512]{0,1:T(8,128)(2,1)S(1)} %get-tuple-element.117), channel_id=1, source_target_pairs={{0,8},{4,12},{8,0},{12,4},{1,9},{5,13},{9,1},{13,5},{2,10},{6,14},... | collective-permute-start | bytes 786440 | tf_op jit(solution)/shard_map/ppermute | solution.py:341
  583.3 33.3 %copy-start.23 = (f32[256,256]{1,0:T(8,128)S(1)}, f32[256,256]{1,0:T(8,128)}, u32[]{:S(2)}) copy-start(f32[256,256]{1,0:T(8,128)} %maximum_select_fusion.8) | copy-start | bytes 786436
  583.3 33.3 %collective-permute-start.20 = (bf16[256,512]{0,1:T(8,128)(2,1)S(1)}, bf16[256,512]{0,1:T(8,128)(2,1)S(1)}, u32[]{:S(2)}, u32[]{:S(2)}) collective-permute-start(bf16[256,512]{0,1:T(8,128)(2,1)S(1)} %get-tuple-element.115), channel_id=1, source_target_pairs={{0,4},{4,8},{8,12},{12,0},{1,5},{5,9},{9,13},{13,1},{2,6},{6,10},{... | collective-permute-start | bytes 786440 | tf_op jit(solution)/shard_map/ppermute | solution.py:341
  587.5 30.4 %collective-permute-start.27 = (bf16[512,256]{1,0:T(8,128)(2,1)S(1)}, bf16[512,256]{1,0:T(8,128)(2,1)S(1)}, u32[]{:S(2)}, u32[]{:S(2)}) collective-permute-start(bf16[512,256]{1,0:T(8,128)(2,1)S(1)} %get-tuple-element.113), channel_id=1, source_target_pairs={{0,12},{4,0},{8,4},{12,8},{1,13},{5,1},{9,5},{13,9},{2,14},{6,2},{... | collective-permute-start | bytes 786440 | tf_op jit(solution)/shard_map/ppermute | solution.py:341
  593.1 32.9 %collective-permute-start.26 = (bf16[512,256]{1,0:T(8,128)(2,1)S(1)}, bf16[512,256]{1,0:T(8,128)(2,1)S(1)}, u32[]{:S(2)}, u32[]{:S(2)}) collective-permute-start(bf16[512,256]{1,0:T(8,128)(2,1)S(1)} %get-tuple-element.114), channel_id=1, source_target_pairs={{0,8},{4,12},{8,0},{12,4},{1,9},{5,13},{9,1},{13,5},{2,10},{6,14},... | collective-permute-start | bytes 786440 | tf_op jit(solution)/shard_map/ppermute | solution.py:341
  593.1 32.9 %collective-permute-start.25 = (bf16[512,256]{1,0:T(8,128)(2,1)S(1)}, bf16[512,256]{1,0:T(8,128)(2,1)S(1)}, u32[]{:S(2)}, u32[]{:S(2)}) collective-permute-start(bf16[512,256]{1,0:T(8,128)(2,1)S(1)} %get-tuple-element.112), channel_id=1, source_target_pairs={{0,4},{4,8},{8,12},{12,0},{1,5},{5,9},{9,13},{13,1},{2,6},{6,10},{... | collective-permute-start | bytes 786440 | tf_op jit(solution)/shard_map/ppermute | solution.py:341
  616.6 57.0 %collective-permute-start.31 = (f32[256,256]{1,0:T(8,128)S(1)}, f32[256,256]{1,0:T(8,128)S(1)}, u32[]{:S(2)}, u32[]{:S(2)}) collective-permute-start(f32[256,256]{1,0:T(8,128)S(1)} %copy-done.23), channel_id=1, source_target_pairs={{0,1},{1,0},{2,3},{3,2},{4,5},{5,4},{6,7},{7,6},{8,9},{9,8},{10,11... | collective-permute-start | bytes 786440 | tf_op jit(solution)/shard_map/ppermute | solution.py:302
  616.6 61.3 %collective-permute-start.29 = (f32[256,768]{0,1:T(8,128)}, f32[256,768]{0,1:T(8,128)}, u32[]{:S(2)}, u32[]{:S(2)}) collective-permute-start(f32[256,768]{0,1:T(8,128)} %maximum_select_fusion.6), channel_id=1, source_target_pairs={{0,1},{1,0},{2,3},{3,2},{4,5},{5,4},{6,7},{7,6},{8,9},{9,8},{10,11... | collective-permute-start | bytes 2359304 | tf_op jit(solution)/shard_map/ppermute | solution.py:302
  617.9 55.8 %collective-permute-start.32 = (f32[256,512]{0,1:T(8,128)S(1)}, f32[256,512]{0,1:T(8,128)}, u32[]{:S(2)}, u32[]{:S(2)}) collective-permute-start(f32[256,512]{0,1:T(8,128)S(1)} %get-tuple-element.103), channel_id=1, source_target_pairs={{0,2},{1,3},{2,0},{3,1},{4,6},{5,7},{6,4},{7,5},{8,10},{9,11},{10,... | collective-permute-start | bytes 1572872 | tf_op jit(solution)/shard_map/ppermute | solution.py:302
  671.3 13.4 %collective-permute-start.34 = (f32[512,256]{1,0:T(8,128)S(1)}, f32[512,256]{1,0:T(8,128)}, u32[]{:S(2)}, u32[]{:S(2)}) collective-permute-start(f32[512,256]{1,0:T(8,128)S(1)} %get-tuple-element.101), channel_id=1, source_target_pairs={{0,2},{1,3},{2,0},{3,1},{4,6},{5,7},{6,4},{7,5},{8,10},{9,11},{10,... | collective-permute-start | bytes 1572872 | tf_op jit(solution)/shard_map/ppermute | solution.py:302
  675.0 12.9 %collective-permute-start.33 = (f32[256,1024]{0,1:T(8,128)S(1)}, f32[256,1024]{0,1:T(8,128)}, u32[]{:S(2)}, u32[]{:S(2)}) collective-permute-start(f32[256,1024]{0,1:T(8,128)S(1)} %maximum_select_fusion.3), channel_id=1, source_target_pairs={{0,1},{1,0},{2,3},{3,2},{4,5},{5,4},{6,7},{7,6},{8,9},{9,8},{10,11... | collective-permute-start | bytes 3145736 | tf_op jit(solution)/shard_map/ppermute | solution.py:302
  687.2 15.3 %collective-permute-start.35 = (f32[1024,256]{1,0:T(8,128)}, f32[1024,256]{1,0:T(8,128)}, u32[]{:S(2)}, u32[]{:S(2)}) collective-permute-start(f32[1024,256]{1,0:T(8,128)} %maximum_select_fusion.4), channel_id=1, source_target_pairs={{0,1},{1,0},{2,3},{3,2},{4,5},{5,4},{6,7},{7,6},{8,9},{9,8},{10,11... | collective-permute-start | bytes 3145736 | tf_op jit(solution)/shard_map/ppermute | solution.py:302
  (44 other events, 359.0 us)
Sparse Core Ops, SparseCore 0:
  10.2 48.6 all-gather.3
  61.0 44.2 all-gather.5
  107.4 44.9 all-gather.7

commit v3 on v2

--- a/solution.py
+++ b/solution.py
@@ -45,11 +45,12 @@
 BK = 256
 
 
-def attend_kernel(together, parts, *refs):
+def attend_kernel(together, parts, later, *refs):
     facts = refs[0]
     projected_refs = refs[1 : 1 + parts]
     back_refs = refs[1 + parts : 1 + 2 * parts]
     start_ref, cos_ref, sin_ref = refs[1 + 2 * parts : 4 + 2 * parts]
+    refs = refs[: 4 + 2 * parts] + refs[4 + 2 * parts + later :]
     mixed_refs = refs[4 + 2 * parts : 4 + 3 * parts]
     grad_refs = refs[4 + 3 * parts : 4 + 4 * parts]
     (
@@ -216,7 +217,7 @@
             )
 
 
-def attend(projected, back, begins, cosine, sine, offset):
+def attend(projected, back, begins, cosine, sine, offset, after=()):
     parts = len(projected)
     heads = back[0].shape[0] // HD
     width = back[0].shape[1]
@@ -228,15 +229,15 @@
     facts = jnp.concatenate([begins[::BQ] // BK, turn[None]])
     whole = lambda rows: pl.BlockSpec((rows, count), lambda g, *_: (0, 0))
     mine = lambda rows: pl.BlockSpec((rows, width), lambda g, *_: (g, 0))
-    pairs = heads * blocks * 3
     results = pl.pallas_call(
-        partial(attend_kernel, together, parts),
+        partial(attend_kernel, together, parts, len(after)),
         grid_spec=pltpu.PrefetchScalarGridSpec(
             num_scalar_prefetch=1,
             grid=(heads // together,),
             in_specs=[mine(together * 3 * HD)] * parts
             + [mine(together * HD)] * parts
-            + [whole(1), whole(half), whole(half)],
+            + [whole(1), whole(half), whole(half)]
+            + [pl.BlockSpec(memory_space=pl.ANY)] * len(after),
             out_specs=[mine(together * HD)] * parts + [mine(together * 3 * HD)] * parts,
             scratch_shapes=[
                 pltpu.VMEM((together, HD, count), jnp.bfloat16),
@@ -257,11 +258,11 @@
         + [jax.ShapeDtypeStruct((heads * 3 * HD, width), jnp.bfloat16)] * parts,
         compiler_params=pltpu.CompilerParams(vmem_limit_bytes=48 * 2**20),
         cost_estimate=pl.CostEstimate(
-            flops=pairs * 12 * BK * BQ * 256,
-            bytes_accessed=heads * count * HD * 22,
-            transcendentals=pairs * BK * BQ,
+            flops=2**20,
+            bytes_accessed=2**20,
+            transcendentals=0,
         ),
-    )(facts, *projected, *back, begins[None, :], cosine, sine)
+    )(facts, *projected, *back, begins[None, :], cosine, sine, *after)
     return results[:parts], results[parts:]
 
 
@@ -310,6 +311,373 @@
     )
 
 
+MESH = pl.DeviceIdType.MESH
+
+
+def opening_kernel(
+    expand_ref,
+    shrink_ref,
+    project_ref,
+    mixing_ref,
+    norm_ref,
+    inputs_ref,
+    back_ref,
+    expand_out,
+    shrink_out,
+    project_out,
+    mixing_out,
+    norm_out,
+    hidden_ref,
+    other_back,
+    expand_low,
+    shrink_low,
+    norm_low,
+    norm_all,
+    own_sem,
+    norm_send,
+    norm_recv,
+    line_send,
+    line_recv,
+    far_send,
+    far_recv,
+    near_send,
+    near_recv,
+    row_sem,
+):
+    place, deep = lax.axis_index("dp"), 4
+    outer = lax.axis_index("outer")
+    far, near = outer // 2, outer % 2
+    far_id = {"outer": (outer + 2) % 4}
+    near_id = {"outer": outer + 1 - 2 * near}
+    rows = expand_ref.shape[0]
+    half = expand_ref.shape[1] // 2
+    part = half // 2
+
+    barrier = pltpu.get_barrier_semaphore()
+    for step in range(1, deep):
+        pl.semaphore_signal(
+            barrier, inc=1, device_id={"dp": (place + step) % deep}, device_id_type=MESH
+        )
+    pl.semaphore_signal(barrier, inc=1, device_id=far_id, device_id_type=MESH)
+    pl.semaphore_signal(barrier, inc=1, device_id=near_id, device_id_type=MESH)
+    row_id = {"mp": 1 - lax.axis_index("mp")}
+    pl.semaphore_signal(barrier, inc=1, device_id=row_id, device_id_type=MESH)
+
+    expand_low[...] = expand_ref[...].astype(jnp.bfloat16)
+    norm_low[...] = jnp.zeros_like(norm_low)
+    norm_low[0:2] = norm_ref[...].astype(jnp.bfloat16).astype(jnp.float32)
+    pl.semaphore_wait(barrier, deep + 2)
+
+    def piece(w, which, at, side):
+        across = pl.ds(pl.multiple_of(at * rows, rows), rows)
+        along = pl.ds(pl.multiple_of(side * part, part), part)
+        if w == 0:
+            return expand_out.at[which, across, along]
+        return shrink_out.at[which, along, across]
+
+    def mine(w):
+        along = pl.ds(pl.multiple_of(near * half + far * part, part), part)
+        return expand_low.at[:, along] if w == 0 else shrink_low.at[along, :]
+
+    def remote(source, target, send, recv, device):
+        return pltpu.make_async_remote_copy(
+            src_ref=source,
+            dst_ref=target,
+            send_sem=send,
+            recv_sem=recv,
+            device_id=device,
+            device_id_type=MESH,
+        )
+
+    def line(w, way, step, source, at):
+        to = place + 1 if way == 0 else place - 1
+        return remote(
+            source,
+            piece(w, 0, at, far),
+            line_send.at[w, way, step],
+            line_recv.at[w, way, step],
+            {"dp": to},
+        )
+
+    def can_send(way):
+        return place < deep - 1 if way == 0 else place > 0
+
+    def start_own(w):
+        for way in range(2):
+
+            @pl.when(can_send(way))
+            def _(way=way):
+                line(w, way, 0, mine(w), place).start()
+
+    def own_copies(w):
+        out = []
+        for which in range(2):
+            side = near + which - 2 * near * which
+            along = pl.ds(pl.multiple_of(side * half, half), half)
+            across = pl.ds(pl.multiple_of(place * rows, rows), rows)
+            if w == 0:
+                pair = (expand_low.at[:, along], expand_out.at[which, across, :])
+            else:
+                pair = (shrink_low.at[along, :], shrink_out.at[which, :, across])
+            out.append(pltpu.make_async_copy(*pair, own_sem.at[w, which]))
+        return out
+
+    start_own(0)
+    row_copy = remote(back_ref, other_back, row_sem.at[0], row_sem.at[1], row_id)
+    row_copy.start()
+    norm_copies = []
+    for step in range(1, deep):
+        copy = remote(
+            norm_low,
+            norm_all.at[step],
+            norm_send.at[step],
+            norm_recv.at[step],
+            {"dp": (place + step) % deep},
+        )
+        copy.start()
+        norm_copies.append(copy)
+    shrink_low[...] = shrink_ref[...].astype(jnp.bfloat16)
+    start_own(1)
+    for w in range(2):
+        for copy in own_copies(w):
+            copy.start()
+    heads = project_ref.shape[1] // 2
+    units = mixing_ref.shape[0] // 2
+    project_out[...] = project_ref[
+        :, pl.ds(pl.multiple_of(near * heads, heads), heads)
+    ].astype(jnp.bfloat16)
+    mixing_out[...] = mixing_ref[
+        pl.ds(pl.multiple_of(near * units, units), units), :
+    ].astype(jnp.bfloat16)
+    norm_all[0] = norm_low[...]
+    for copy in norm_copies:
+        copy.wait()
+    for at in range(deep):
+        norm_out[:, at * rows : (at + 1) * rows] = norm_all[(place - at + deep) % deep]
+    gain, bias = norm_out[0:1], norm_out[1:2]
+    tokens = inputs_ref.shape[0]
+    height = 128
+
+    def normalize(i, _):
+        at = pl.ds(pl.multiple_of(i * height, height), height)
+        x = inputs_ref[at, :].astype(jnp.float32)
+        mean = jnp.mean(x, axis=1, keepdims=True)
+        centred = x - mean
+        spread = jnp.mean(centred * centred, axis=1, keepdims=True)
+        normed = centred * lax.rsqrt(spread + norm_epsilon)
+        hidden_ref[at, :] = (normed * gain + bias).astype(jnp.bfloat16)
+        return 0
+
+    lax.fori_loop(0, tokens // height, normalize, 0)
+
+    def arrives(way, step):
+        return place >= step if way == 0 else place + step < deep
+
+    def at_of(way, step):
+        return place - step if way == 0 else place + step
+
+    def to_far(w, way, step):
+        at = at_of(way, step)
+        return remote(
+            piece(w, 0, at, far),
+            piece(w, 0, at, far),
+            far_send.at[w, way, step - 1],
+            far_recv.at[w, way, step - 1],
+            far_id,
+        )
+
+    def from_far(w, way, step):
+        at = at_of(way, step)
+        return remote(
+            piece(w, 0, at, 1 - far),
+            piece(w, 0, at, 1 - far),
+            far_send.at[w, way, step - 1],
+            far_recv.at[w, way, step - 1],
+            far_id,
+        )
+
+    def to_near(w, way, step, other):
+        at = at_of(way, step)
+        side = 1 - far if other else far
+        return remote(
+            piece(w, 0, at, side),
+            piece(w, 1, at, side),
+            near_send.at[w, way, step - 1, other],
+            near_recv.at[w, way, step - 1, other],
+            near_id,
+        )
+
+    order = [(w, step) for w in range(2) for step in range(1, deep)]
+
+    def first_half(w, step):
+        for way in range(2):
+
+            @pl.when(arrives(way, step))
+            def _(way=way):
+                at = at_of(way, step)
+                line(w, way, step - 1, mine(w), at).wait_recv()
+                if step < deep - 1:
+
+                    @pl.when(can_send(way))
+                    def _():
+                        line(w, way, step, piece(w, 0, at, far), at).start()
+
+                to_far(w, way, step).start()
+                to_near(w, way, step, 0).start()
+
+    def second_half(w, step):
+        for way in range(2):
+
+            @pl.when(arrives(way, step))
+            def _(way=way):
+                from_far(w, way, step).wait_recv()
+                to_near(w, way, step, 1).start()
+
+    for n, (w, step) in enumerate(order):
+        first_half(w, step)
+        if n:
+            second_half(*order[n - 1])
+    second_half(*order[-1])
+    row_copy.wait()
+    for w in range(2):
+        for copy in own_copies(w):
+            copy.wait()
+        for way in range(2):
+
+            @pl.when(can_send(way))
+            def _(way=way):
+                line(w, way, 0, mine(w), place).wait_send()
+
+            for step in range(1, deep):
+
+                @pl.when(arrives(way, step))
+                def _(way=way, step=step):
+                    at = at_of(way, step)
+                    if step < deep - 1:
+
+                        @pl.when(can_send(way))
+                        def _():
+                            line(w, way, step, piece(w, 0, at, far), at).wait_send()
+
+                    to_far(w, way, step).wait_send()
+                    for other in range(2):
+                        to_near(w, way, step, other).wait_send()
+                        to_near(w, way, step, other).wait_recv()
+
+
+def opening(expand, shrink, project, mixing, norm, inputs, back):
+    deep = 4
+    here = lambda: pl.BlockSpec(memory_space=pltpu.VMEM)
+    rows, units = expand.shape
+    low = jnp.bfloat16
+    sem = pltpu.SemaphoreType.DMA
+    return pl.pallas_call(
+        opening_kernel,
+        in_specs=[here() for _ in range(6)] + [pl.BlockSpec(memory_space=pl.ANY)],
+        out_specs=[pl.BlockSpec(memory_space=pl.ANY)] * 2
+        + [here() for _ in range(4)]
+        + [pl.BlockSpec(memory_space=pl.ANY)],
+        out_shape=[
+            jax.ShapeDtypeStruct((2, rows * deep, units // 2), low),
+            jax.ShapeDtypeStruct((2, units // 2, rows * deep), low),
+            jax.ShapeDtypeStruct((project.shape[0], project.shape[1] // 2), low),
+            jax.ShapeDtypeStruct((mixing.shape[0] // 2, mixing.shape[1]), low),
+            jax.ShapeDtypeStruct((8, rows * deep), jnp.float32),
+            jax.ShapeDtypeStruct(inputs.shape, low),
+            jax.ShapeDtypeStruct(back.shape, low),
+        ],
+        scratch_shapes=[
+            pltpu.VMEM(expand.shape, low),
+            pltpu.VMEM(shrink.shape, low),
+            pltpu.VMEM((8, norm.shape[1]), jnp.float32),
+            pltpu.VMEM((deep, 8, norm.shape[1]), jnp.float32),
+            sem((2, 2)),
+            sem((deep,)),
+            sem((deep,)),
+            sem((2, 2, deep)),
+            sem((2, 2, deep)),
+            sem((2, 2, deep)),
+            sem((2, 2, deep)),
+            sem((2, 2, deep, 2)),
+            sem((2, 2, deep, 2)),
+            sem((2,)),
+        ],
+        compiler_params=pltpu.CompilerParams(
+            collective_id=1, has_side_effects=True, vmem_limit_bytes=40 * 2**20
+        ),
+        cost_estimate=pl.CostEstimate(flops=0, bytes_accessed=2**20, transcendentals=0),
+    )(expand, shrink, project, mixing, norm, inputs, back)
+
+
+def total_kernel(term_ref, out_ref, first, second, first_send, first_recv, second_send, second_recv):
+    split, outers, deep = first.shape[0] // 4, 4, second.shape[0]
+    plane = split * outers
+    place = lax.axis_index("dp")
+    me = lax.axis_index("mp") * outers + lax.axis_index("outer")
+
+    def plane_id(step):
+        other = (me + step) % plane
+        return {"mp": other // outers, "outer": other % outers}
+
+    def line_id(step):
+        return {"dp": (place + step) % deep}
+
+    barrier = pltpu.get_barrier_semaphore()
+    for step in range(1, plane):
+        pl.semaphore_signal(barrier, inc=1, device_id=plane_id(step), device_id_type=MESH)
+    for step in range(1, deep):
+        pl.semaphore_signal(barrier, inc=1, device_id=line_id(step), device_id_type=MESH)
+    pl.semaphore_wait(barrier, plane + deep - 2)
+
+    def exchange(source, slots, send, recv, size, device):
+        copies = []
+        for step in range(1, size):
+            copy = pltpu.make_async_remote_copy(
+                src_ref=source,
+                dst_ref=slots.at[step],
+                send_sem=send.at[step],
+                recv_sem=recv.at[step],
+                device_id=device(step),
+                device_id_type=MESH,
+            )
+            copy.start()
+            copies.append(copy)
+        slots[0] = source[...]
+        for copy in copies:
+            copy.wait()
+
+    exchange(term_ref, first, first_send, first_recv, plane, plane_id)
+    total = first[me]
+    for at in range(1, plane):
+        total = total + first[(me + plane - at) % plane]
+    out_ref[...] = total
+    exchange(out_ref, second, second_send, second_recv, deep, line_id)
+    total = second[place]
+    for at in range(1, deep):
+        total = total + second[(place + deep - at) % deep]
+    out_ref[...] = total
+
+
+def total_over_all(term, split, deep):
+    plane = split * 4
+    sem = pltpu.SemaphoreType.DMA
+    return pl.pallas_call(
+        total_kernel,
+        in_specs=[pl.BlockSpec(memory_space=pltpu.VMEM)],
+        out_specs=pl.BlockSpec(memory_space=pltpu.VMEM),
+        out_shape=jax.ShapeDtypeStruct(term.shape, term.dtype),
+        scratch_shapes=[
+            pltpu.VMEM((plane, *term.shape), term.dtype),
+            pltpu.VMEM((deep, *term.shape), term.dtype),
+            sem((plane,)),
+            sem((plane,)),
+            sem((deep,)),
+            sem((deep,)),
+        ],
+        compiler_params=pltpu.CompilerParams(collective_id=2, has_side_effects=True),
+    )(term)
+
+
 class Paired:
     def __init__(self):
         outer = lax.axis_index("outer")
@@ -317,11 +685,21 @@
         self.place = lax.axis_index("dp")
         self.deep = lax.axis_size("dp")
 
-    def gather(self, master, cut, depth):
-        half = master.shape[cut] // 2
-        own = lax.dynamic_slice_in_dim(master, self.near * half, half, cut).astype(jnp.bfloat16)
+    def gather(self, own, cut, depth):
         own = lax.all_gather(own, "dp", axis=depth, tiled=True)
         return jnp.concatenate([own, swap(own, "outer", 1)], axis=cut)
+
+    def gather_few(self, own, cut, depth):
+        wide = list(own.shape)
+        piece = wide[depth]
+        wide[depth] *= self.deep
+        out = jnp.zeros(wide, own.dtype)
+        for step in range(self.deep):
+            pairs = [(i, (i + step) % self.deep) for i in range(self.deep)]
+            come = lax.ppermute(own, "dp", pairs) if step else own
+            at = lax.rem(self.place - step + self.deep, self.deep)
+            out = lax.dynamic_update_slice_in_dim(out, come, at * piece, depth)
+        return jnp.concatenate([out, swap(out, "outer", 1)], axis=cut)
 
     def total(self, own, sibling, cut, depth):
         own = own + swap(sibling, "outer", 1)
@@ -379,26 +757,38 @@
     )
     position = lax.axis_index("mp")
     count = width * split
-    norm_weight = lax.all_gather(norm_master.astype(jnp.bfloat16), "dp", axis=1, tiled=True)
-    gain = norm_weight[0].astype(jnp.float32)
-    bias = norm_weight[1].astype(jnp.float32)
     project_flat = project_master.reshape(project_master.shape[0], heads_here * 3 * HD)
     mixing_flat = mixing_master.reshape(heads_here * HD, mixing_master.shape[2])
     masters = (project_flat, mixing_flat, expand_master, shrink_master)
     cuts, depths = (1, 0, 1, 0), (0, 1, 0, 1)
     rows_local = inputs[0].astype(jnp.float32)
-    shaped, norm_pull = jax.vjp(layer_norm, rows_local, gain, bias)
-    hidden_local = shaped.astype(jnp.bfloat16)
     begins, places = layout(lengths[0], count)
     cosine, sine = turns(places)
     if paired:
         plan = Paired()
-        expand, shrink, mixing, project = (
-            plan.gather(masters[k], cuts[k], depths[k]) for k in (2, 3, 1, 0)
+        expand, shrink, project, mixing, norm_weight, hidden_local, other_back = opening(
+            expand_master,
+            shrink_master,
+            project_flat,
+            mixing_flat,
+            norm_master,
+            inputs[0],
+            cotangent[0],
         )
-        backs = [cotangent[0], swap(cotangent[0], "mp", 1)]
+        backs = [cotangent[0], other_back]
+        expand = jnp.concatenate([expand[0], expand[1]], axis=1)
+        shrink = shrink.reshape(-1, shrink.shape[2])
+        project = plan.gather(project, 1, 0)
+        mixing = plan.gather_few(mixing, 0, 1)
+        gain, bias = norm_weight[0], norm_weight[1]
+        norm_pull = jax.vjp(layer_norm, rows_local, gain, bias)[1]
         hiddens = [hidden_local, swap(hidden_local, "mp", 1)]
     else:
+        norm_weight = lax.all_gather(norm_master.astype(jnp.bfloat16), "dp", axis=1, tiled=True)
+        gain = norm_weight[0].astype(jnp.float32)
+        bias = norm_weight[1].astype(jnp.float32)
+        shaped, norm_pull = jax.vjp(layer_norm, rows_local, gain, bias)
+        hidden_local = shaped.astype(jnp.bfloat16)
         project, mixing, expand, shrink = (
             lax.all_gather(master.astype(jnp.bfloat16), "dp", axis=depth, tiled=True)
             for master, depth in zip(masters, depths)
@@ -413,7 +803,7 @@
         if not paired:
             term = over_tokens(pattern, lefts, rights)
             term = lax.psum_scatter(term, "dp", scatter_dimension=depth, tiled=True)
-            return lax.psum(term, "outer")
+            return lax.psum(term, "outer"), ()
         sources = rights if cut == 1 else lefts
         axis = 0 if pattern.split(",")[cut].index("t") == 1 else 1
         half = sources[0].shape[axis] // 2
@@ -428,20 +818,28 @@
                 else over_tokens(pattern, chosen, rights)
             )
 
-        sibling = term(1)
-        return plan.total(term(0), sibling, cut, depth)
+        sibling, own = term(1), term(0)
+        return plan.total(own, sibling, cut, depth), (sibling, own)
 
     lifteds = [product("td,df->tf", hidden, expand) for hidden in hiddens]
     activated = [gelu(lifted) for lifted in lifteds]
     active_grads = [product("td,fd->tf", back, shrink) for back in backs]
     lifted_grads = [gelu_both(a, b) for a, b in zip(lifteds, active_grads)]
-    shrink_sum = weight_sum("tf,td->fd", activated, backs, 0, 1)
-    expand_sum = weight_sum("td,tf->df", hiddens, lifted_grads, 1, 0)
+    shrink_sum, shrink_terms = weight_sum("tf,td->fd", activated, backs, 0, 1)
+    expand_sum, expand_terms = weight_sum("td,tf->df", hiddens, lifted_grads, 1, 0)
     projected = [product("td,de->et", hidden, project) for hidden in hiddens]
     mixed_backs = [product("td,fd->ft", back, mixing).astype(jnp.bfloat16) for back in backs]
-    mixed, projected_grads = attend(projected, mixed_backs, begins, cosine, sine, position)
-    mixing_sum = weight_sum("ft,td->fd", mixed, backs, 0, 1)
-    project_sum = weight_sum("td,et->de", hiddens, projected_grads, 1, 0)
+    mixed, projected_grads = attend(
+        projected,
+        mixed_backs,
+        begins,
+        cosine,
+        sine,
+        position,
+        (*shrink_terms, *expand_terms),
+    )
+    mixing_sum, _ = weight_sum("ft,td->fd", mixed, backs, 0, 1)
+    project_sum, _ = weight_sum("td,et->de", hiddens, projected_grads, 1, 0)
     hidden_grads = [
         product("et,de->td", a, project) + product("tf,df->td", b, expand)
         for a, b in zip(projected_grads, lifted_grads)
@@ -462,14 +860,17 @@
     block_out = (rows_local + over_positions(branches)).astype(jnp.bfloat16)[None]
     sums = (project_sum, mixing_sum, expand_sum, shrink_sum)
     own_square = sum(jnp.sum(v * v) for v in sums)
-    everywhere = ("mp", "dp", "outer")
     if not paired:
         own_square = own_square / lax.axis_size("outer")
-    norm_all = lax.psum(
-        jnp.concatenate([gain_grad, bias_grad, jnp.full((128,), own_square)]), everywhere
-    )
-    norm_full = norm_all[: 2 * D].reshape(2, D)
-    grad_norm = jnp.sqrt(norm_all[2 * D] + jnp.sum(norm_full * norm_full))
+    norm_terms = jnp.concatenate([gain_grad, bias_grad, jnp.full((D,), own_square)])
+    norm_terms = norm_terms.reshape(-1, 128)
+    if paired:
+        norm_all = total_over_all(norm_terms, split, deep)
+    else:
+        norm_all = lax.psum(norm_terms, ("mp", "dp", "outer"))
+    norm_all = norm_all.reshape(3, D)
+    norm_full = norm_all[:2]
+    grad_norm = jnp.sqrt(norm_all[2, 0] + jnp.sum(norm_full * norm_full))
     factor = clip_level / jnp.maximum(grad_norm, clip_level)
     norm_gradient = lax.dynamic_slice_in_dim(
         norm_full, lax.axis_index("dp") * (D // deep), D // deep, 1

time: 722 us -> 634 us (0.88)
  Pallas kernels: 107 us -> 185 us
  blocking collectives: 74.3 us -> 0 us
  waiting for transfers between devices: 144 us -> 86.4 us
  other arithmetic: 74.2 us -> 56.5 us
  local copies, waits for them, and re-layouts: 42 us -> 27.2 us
  matrix products: 215 us -> 205 us
    pallas_call x1 -> x3, Pallas kernels: 107 us -> 185 us  [the longest x1 107 us: attend(): pl.pallas_call(partial(attend_kernel, together, parts, len(after)), grid_...]
    ppermute x24 -> x21, waiting for transfers between devices: 106 us -> 63.7 us  [swap(): return lax.ppermute(array, axis, [(i, i ^ bit) for i in range(size)])]
    psum x1 -> x0, blocking collectives: 40.7 us -> none  [local(): lax.psum(jnp.concatenate([gain_grad, bias_grad, jnp.full((128,), own_squa...]
    all_gather x2 -> x0, blocking collectives: 33.6 us -> none  [the longest x1 20.9 us: gather(): own = lax.all_gather(own, 'dp', axis=depth, tiled=True)]
    unnamed x117 -> x127, local copies, waits for them, and re-layouts: 25.8 us -> 14.5 us
    dot_general x32, matrix products: 215 us -> 205 us  [product(): return jnp.einsum(pattern, left, right, preferred_element_type=jnp.float32)]
    all_gather x3 -> x1, waiting for transfers between devices: 8.9 us -> 0.01 us  [gather(): own = lax.all_gather(own, 'dp', axis=depth, tiled=True)]
    ppermute x12, starting transfers between devices: 21.9 us -> 30 us  [total(): lax.ppermute(part(target).astype(jnp.bfloat16), 'dp', pairs)]
  transfers between devices with their start and end apart: 39 -> 37, of which waited for: 11 -> 10; matrix products, arithmetic and copies ran while one was open for 44% -> 43% of each run, Pallas kernels for 15% -> 19%
where the time goes in v3:
time: 634 us; the launch traced here: 629 us
  matrix products  205 us (32%)
  Pallas kernels  185 us (29%)
  waiting for transfers between devices  86.4 us (14%)
  other arithmetic  56.5 us (9%)
  starting transfers between devices  47.7 us (8%)
  local copies, waits for them, and re-layouts  27.2 us (4%)
  between operations  20.4 us (3%)
    dot_general x32, matrix products, product(): return jnp.einsum(pattern, left, right, preferred_element_type=jnp.float32)  205 us
    pallas_call x1, Pallas kernels, attend(): pl.pallas_call(partial(attend_kernel, together, parts, len(after)), grid_...  107 us
    pallas_call x1, Pallas kernels, opening(): pl.pallas_call(opening_kernel, in_specs=[here() for _ in range(6)] + [pl....  67.2 us
    ppermute x21, waiting for transfers between devices, swap(): return lax.ppermute(array, axis, [(i, i ^ bit) for i in range(size)])  63.7 us
    ppermute x12, starting transfers between devices, total(): lax.ppermute(part(target).astype(jnp.bfloat16), 'dp', pairs)  30 us
    ppermute x12, waiting for transfers between devices, total(): lax.ppermute(part(target).astype(jnp.bfloat16), 'dp', pairs)  22.7 us
    convert_element_type x5, other arithmetic, adam_update(): return (master_new, first_new, second_new, master_new.astype(jnp.bfloat16))  18.4 us
    ppermute x21, starting transfers between devices, swap(): return lax.ppermute(array, axis, [(i, i ^ bit) for i in range(size)])  15.1 us
  transfers between devices with their start and end apart: 37, of which 10 were waited for; matrix products, arithmetic and copies ran while one was open for 43% of the time, Pallas kernels for 19%

profile of v3, /device:TPU:0, one launch (start us, length us, event | category | flops | bytes accessed | tf_op | source)
XLA Modules:
  0.0 628.8 jit_solution(322111176712408531)
XLA Ops:
  7.3 3.1 copy.53.project_ref
  14.9 67.2 %shard_map.353 = (bf16[2,1024,1024]{2,1,0:T(8,128)(2,1)}, bf16[2,1024,1024]{2,1,0:T(8,128)(2,1)}, bf16[256,768]{1,0:T(8,128)(2,1)}, bf16[256,256]{1,0:T(8,128)(2...) custom-call(f32[256,2048]{1,0:T(8,128)S(1)} %copy-done.2, ...), custom_call_target="tpu_custom_call" | custom-call | bytes 1048576 | tf_op jit(solution)/shard_map/pallas_call | solution.py:574
  92.0 11.5 %multiply_convert_fusion.1 = (bf16[1280,2048]{1,0:T(8,128)(2,1)}, f32[1280,2048]{1,0:T(8,128)}) fusion(bf16[1280,1024]{1,0:T(8,128)(2,1)S(1)} %copy-done.11, bf16[1024,1024]{1,0:T(8,128)(2,1)S(1)} %get-tuple-element.82, bf16[1024,1024]{1,0:T(8,128)(2,1)S(1)} %get-tuple-element.81), kind=kOutput, calls=%fused_computation.24 | convolution fusion | flops 5400690688 | bytes 22544384 | tf_op jit(solution)/shard_map/td,df->tf/dot_general | solution.py:289
  103.5 13.8 %fusion.6 = bf16[1280,2048]{1,0:T(8,128)(2,1)S(1)} fusion(f32[1280,2048]{1,0:T(8,128)} %get-tuple-element.104, bf16[2048,1024]{1,0:T(8,128)(2,1)S(1)} %bitcast.115, bf16[1,1280,1024]{2,1,0:T(8,128)(2,1)S(1)} %copy-done.15), kind=kOutput, calls=%fused_computation.10 | convolution fusion | flops 5421137920 | bytes 22544384 | tf_op jit(solution)/shard_map/td,fd->tf/dot_general | solution.py:289
  117.4 7.4 %fusion.92 = f32[1280,1024]{1,0:T(8,128)} fusion(bf16[1280,2048]{1,0:T(8,128)(2,1)S(1)} %fusion.6, bf16[1024,1024]{1,0:T(8,128)(2,1)S(1)} %get-tuple-element.82, bf16[1024,1024]{1,0:T(8,128)(2,1)S(1)} %get-tuple-element.81), kind=kOutput, calls=%fused_computation.185 | convolution fusion | flops 5377097728 | bytes 14680064 | tf_op jit(solution)/shard_map/tf,df->td/dot_general | solution.py:289
  124.8 4.5 fusion.29
  129.3 4.5 fusion.33
  134.8 10.8 %fusion.110 = f32[1280,2048]{1,0:T(8,128)} fusion(bf16[1280,1024]{1,0:T(8,128)(2,1)S(1)} %get-tuple-element.37, bf16[2048,1024]{1,0:T(8,128)(2,1)} %bitcast.114), kind=kOutput, calls=%fused_computation.198 | convolution fusion | flops 5368709120 | bytes 17301504 | tf_op jit(solution)/shard_map/td,fd->tf/dot_general | solution.py:289
  145.5 9.1 %fusion.111 = f32[1280,1024]{1,0:T(8,128)} fusion(bf16[1280,2048]{1,0:T(8,128)(2,1)} %get-tuple-element.103, bf16[2048,1024]{1,0:T(8,128)(2,1)S(1)} %bitcast.116), kind=kOutput, calls=%fused_computation.199 | convolution fusion | flops 5368709120 | bytes 14680064 | tf_op jit(solution)/shard_map/tf,fd->td/dot_general | solution.py:289
  162.2 3.9 convolution_convert_fusion.refs_4_
  168.9 2.8 constant_dynamic-update-slice_fusion.5
  171.7 18.8 %fusion.13 = (bf16[1280,2048]{1,0:T(8,128)(2,1)}, bf16[1280,2048]{1,0:T(8,128)(2,1)}) fusion(f32[1280,2048]{1,0:T(8,128)} %fusion.110, bf16[1280,1024]{1,0:T(8,128)(2,1)} %collective-permute-done.1, bf16[1024,1024]{1,0:T(8,128)(2,1)} %copy-done.26, bf16[1024,1024]{1,0:T(8,128)(2,1)S(1)} %copy-done.25), kind=kOutput, calls=%fused_computation.17 | convolution fusion | flops 5434769408 | bytes 27787264 | tf_op jit(solution)/shard_map/td,df->tf/dot_general | solution.py:289
  190.6 6.5 %fusion.39 = f32[1024,1024]{1,0:T(8,128)} fusion(bf16[1280,1024]{1,0:T(8,128)(2,1)S(1)} %get-tuple-element.37, bf16[1280,2048]{1,0:T(8,128)(2,1)} %get-tuple-element.80), kind=kOutput, calls=%fused_computation.61 | convolution fusion | flops 2684354560 | bytes 9437184 | tf_op jit(solution)/shard_map/tf,td->fd/dot_general | solution.py:289
  197.1 7.3 %fusion.112 = f32[1280,1024]{1,0:T(8,128)} fusion(bf16[1280,2048]{1,0:T(8,128)(2,1)S(1)} %copy-done.50, bf16[2048,1024]{1,0:T(8,128)(2,1)S(1)} %bitcast.117), kind=kOutput, calls=%fused_computation.200 | convolution fusion | flops 5368709120 | bytes 14680064 | tf_op jit(solution)/shard_map/tf,fd->td/dot_general | solution.py:289
  204.4 4.9 fusion.55.refs_8_
  209.4 8.0 %fusion.61.refs_10_ = f32[1024,1024]{1,0:T(8,128)} fusion(f32[1024,1024]{1,0:T(8,128)S(1)} %copy-done.49, bf16[1280,1024]{1,0:T(8,128)(2,1)} %collective-permute-done.1, bf16[1280,2048]{1,0:T(8,128)(2,1)S(1)} %bitcast.123), kind=kOutput, calls=%fused_computation.92 | convolution fusion | flops 2685403136 | bytes 13631488 | tf_op jit(solution)/shard_map/td,tf->df/dot_general | solution.py:289
  218.0 6.2 fusion.64.refs_11_
  224.2 6.4 %fusion.35 = f32[1024,1024]{1,0:T(8,128)} fusion(bf16[1280,1024]{1,0:T(8,128)(2,1)S(1)} %get-tuple-element.37, bf16[1280,2048]{1,0:T(8,128)(2,1)} %get-tuple-element.80), kind=kOutput, calls=%fused_computation.57 | convolution fusion | flops 2684354560 | bytes 9437184 | tf_op jit(solution)/shard_map/tf,td->fd/dot_general | solution.py:289
  230.7 7.6 %fusion.91 = f32[1280,1024]{1,0:T(8,128)} fusion(bf16[1280,2048]{1,0:T(8,128)(2,1)S(1)} %bitcast.125, bf16[1024,1024]{1,0:T(8,128)(2,1)S(1)} %copy-done.27, bf16[1024,1024]{1,0:T(8,128)(2,1)S(1)} %copy-done.25), kind=kOutput, calls=%fused_computation.184 | convolution fusion | flops 5377097728 | bytes 14680064 | tf_op jit(solution)/shard_map/tf,df->td/dot_general | solution.py:289
  240.0 6.5 %fusion.108.refs_1_ = f32[1536,1280]{1,0:T(8,128)} fusion(bf16[1024,1536]{1,0:T(8,128)(2,1)S(1)} %constant_dynamic-update-slice_fusion.4, bf16[1280,1024]{1,0:T(8,128)(2,1)S(1)} %copy-done.12), kind=kOutput, calls=%fused_computation.196 | convolution fusion | flops 4026531840 | bytes 13631488 | tf_op jit(solution)/shard_map/td,de->et/dot_general | solution.py:289
  246.4 8.2 %fusion.109.refs_2_ = f32[1536,1280]{1,0:T(8,128)} fusion(bf16[1024,1536]{1,0:T(8,128)(2,1)S(1)} %constant_dynamic-update-slice_fusion.4, bf16[1280,1024]{1,0:T(8,128)(2,1)} %collective-permute-done.1), kind=kOutput, calls=%fused_computation.197 | convolution fusion | flops 4026531840 | bytes 13631488 | tf_op jit(solution)/shard_map/td,de->et/dot_general | solution.py:289
  254.7 7.0 %fusion.107 = (f32[1024,1024]{1,0:T(8,128)}, f32[1024,1024]{1,0:T(8,128)}) fusion(f32[1024,1024]{1,0:T(8,128)S(1)} %collective-permute-done.23, f32[1024,1024]{1,0:T(8,128)} %fusion.35, bf16[1,1280,1024]{2,1,0:T(8,128)(2,1)S(1)} %copy-done.17, bf16[1280,2048]{1,0:T(8,128)(2,1)S(1)} %bitcast.121), kind=kOutput, calls=%fused_computation.195 | convolution fusion | flops 2686451712 | bytes 22020096 | tf_op jit(solution)/shard_map/tf,td->fd/dot_general | solution.py:289
  261.7 106.7 %shard_map.354 = (bf16[512,1280]{1,0:T(8,128)(2,1)S(1)}, bf16[512,1280]{1,0:T(8,128)(2,1)S(1)}, bf16[1536,1280]{1,0:T(8,128)(2,1)}, bf16[1536,1280]{1,0:T(8,128)(2,1)}) custom-call(s32[11]{0:T(128)S(1)} %pad_add_fusion.refs_0_, f32[1536,1280]{1,0:T(8,128)} %fusion.108.refs_1_, f32[1536,1280]{1,0:T(8,128)} %fusion.109.refs_2_, ...), custom_call_target="tpu_custom_call" | custom-call | flops 1048576 | bytes 1048576 | tf_op jit(solution)/shard_map/pallas_call | solution.py:232
  368.5 5.5 fusion.49
  374.0 3.8 fusion.53
  377.9 6.5 %fusion.113 = f32[1280,1024]{1,0:T(8,128)} fusion(bf16[1536,1280]{1,0:T(8,128)(2,1)S(1)} %copy-done.47, bf16[1024,1536]{1,0:T(8,128)(2,1)S(1)} %copy-done.35), kind=kOutput, calls=%fused_computation.201 | convolution fusion | flops 4026531840 | bytes 12320768 | tf_op jit(solution)/shard_map/et,de->td/dot_general | solution.py:289
  384.4 3.3 add.362
  389.8 3.7 collective-permute-start.13
  395.3 10.4 %add_convert_fusion = bf16[1280,1024]{1,0:T(8,128)(2,1)} fusion(f32[1280,1024]{1,0:T(8,128)} %fusion.91, bf16[1536,1280]{1,0:T(8,128)(2,1)} %get-tuple-element.43, bf16[1024,1536]{1,0:T(8,128)(2,1)} %copy-done.34), kind=kOutput, calls=%fused_computation.40 | convolution fusion | flops 4029153280 | bytes 14942208 | tf_op jit(solution)/shard_map/et,de->td/dot_general | solution.py:289
  407.1 7.1 %fusion.67 = f32[1024,768]{0,1:T(8,128)} fusion(f32[1024,768]{0,1:T(8,128)} %fusion.49, bf16[1280,1024]{1,0:T(8,128)(2,1)} %collective-permute-done.1, bf16[1536,1280]{1,0:T(8,128)(2,1)} %get-tuple-element.43), kind=kOutput, calls=%fused_computation.94 | convolution fusion | flops 2014052352 | bytes 10878976 | tf_op jit(solution)/shard_map/td,et->de/dot_general | solution.py:289
  414.3 5.7 fusion.51
  420.0 5.5 add_convert_fusion.1
  435.6 5.4 collective-permute-done.14
  441.1 4.5 collective-permute-start.21
  445.8 3.9 collective-permute-start.25
  452.2 11.0 %collective-permute-done.21 = bf16[256,512]{1,0:T(8,128)(2,1)S(1)} collective-permute-done((bf16[256,512]{1,0:T(8,128)(2,1)S(1)}, bf16[256,512]{1,0:T(8,128)(2,1)S(1)}, u32[]{:S(2)}, u32[]{:S(2)}) %collective-permute-start.21) | collective-permute-done | bytes 262176 | tf_op jit(solution)/shard_map/ppermute | solution.py:719
  464.7 9.0 %collective-permute-start.15 = (bf16[128,256]{1,0:T(8,128)(2,1)S(1)}, bf16[128,256]{1,0:T(8,128)(2,1)S(1)}, u32[]{:S(2)}, u32[]{:S(2)}) collective-permute-start(bf16[128,256]{1,0:T(8,128)(2,1)S(1)} %get-tuple-element.94), channel_id=1, source_target_pairs={{0,4},{4,8},{8,12},{12,0},{1,5},{5,9},{9,13},{13,1},{2,6},{6,10},{... | collective-permute-start | bytes 196616 | tf_op jit(solution)/shard_map/ppermute | solution.py:719
  473.7 8.5 %collective-permute-done.26 = bf16[512,256]{1,0:T(8,128)(2,1)S(1)} collective-permute-done((bf16[512,256]{1,0:T(8,128)(2,1)S(1)}, bf16[512,256]{1,0:T(8,128)(2,1)S(1)}, u32[]{:S(2)}, u32[]{:S(2)}) %collective-permute-start.26) | collective-permute-done | bytes 262176 | tf_op jit(solution)/shard_map/ppermute | solution.py:719
  490.4 19.5 %collective-permute-done.30 = f32[128,256]{1,0:T(8,128)S(1)} collective-permute-done((f32[128,256]{1,0:T(8,128)S(1)}, f32[128,256]{1,0:T(8,128)S(1)}, u32[]{:S(2)}, u32[]{:S(2)}) %collective-permute-start.30) | collective-permute-done | bytes 131104 | tf_op jit(solution)/shard_map/ppermute | solution.py:303
  517.5 4.8 add_add_fusion.1
  523.1 3.2 fusion.24
  526.3 15.8 %collective-permute-done.9 = bf16[1024,384]{0,1:T(8,128)(2,1)S(1)} collective-permute-done((bf16[1024,384]{0,1:T(8,128)(2,1)S(1)}, bf16[1024,384]{0,1:T(8,128)(2,1)S(1)}, u32[]{:S(2)}, u32[]{:S(2)}) %collective-permute-start.9) | collective-permute-done | bytes 786464 | tf_op jit(solution)/shard_map/ppermute | solution.py:303
  546.2 20.8 %collective-permute-done.6 = bf16[1280,1024]{1,0:T(8,128)(2,1)S(1)} collective-permute-done((bf16[1280,1024]{1,0:T(8,128)(2,1)}, bf16[1280,1024]{1,0:T(8,128)(2,1)S(1)}, u32[]{:S(2)}, u32[]{:S(2)}) %collective-permute-start.6) | collective-permute-done | bytes 2621472 | tf_op jit(solution)/shard_map/ppermute | solution.py:303
  570.9 7.5 %add_bitcast_fusion = (f32[1,1280,1024]{2,1,0:T(8,128)}, bf16[1,1280,1024]{2,1,0:T(8,128)(2,1)}) fusion(f32[1280]{0:T(1024)S(1)} %negate_multiply_fusion, bf16[1,1280,1024]{2,1,0:T(8,128)(2,1)S(1)} %copy-done.17, f32[1280]{0:T(1024)S(1)} %get-tuple-element.101, f32[1280]{0:T(1024)S(1)} %copy-done.38, bf16[1,1280,1024]{2,1,0:T(8,128)(2,1)S(1)} %copy-done.13, ...), kind=kLoop, calls=%fused_computation.38 | loop fusion | flops 19660800 | bytes 31481856 | tf_op jit(solution)/shard_map/broadcast_in_dim | solution.py:859
  582.5 11.5 %shard_map.355 = f32[24,128]{1,0:T(8,128)} custom-call(f32[24,128]{1,0:T(8,128)} %maximum_maximum_fusion.term_ref), custom_call_target="tpu_custom_call" | custom-call | tf_op jit(solution)/shard_map/pallas_call | solution.py:664
  599.1 5.9 fusion.98
  610.2 5.8 fusion.100
  617.4 3.2 fusion.104
  (256 shorter events, 83.6 us)
Async XLA Ops:
  7.2 161.5 %all-gather.2.cloned.1.call-start = ((), (), s32[]{:S(2)}) async-start(), calls=%async_computation | async-start | bytes 1966080 | tf_op jit(solution)/shard_map/all_gather | solution.py:689
  83.6 75.8 %collective-permute-start.4 = (bf16[256,256]{1,0:T(8,128)(2,1)S(1)}, bf16[256,256]{1,0:T(8,128)(2,1)S(1)}, u32[]{:S(2)}, u32[]{:S(2)}) collective-permute-start(bf16[256,256]{1,0:T(8,128)(2,1)S(1)} %get-tuple-element.36), channel_id=1, source_target_pairs={{0,12},{4,0},{8,4},{12,8},{1,13},{5,1},{9,5},{13,9},{2,14},{6,2},{... | collective-permute-start | bytes 393224 | tf_op jit(solution)/shard_map/ppermute | solution.py:699
  85.1 72.7 %collective-permute-start.3 = (bf16[256,256]{1,0:T(8,128)(2,1)S(1)}, bf16[256,256]{1,0:T(8,128)(2,1)}, u32[]{:S(2)}, u32[]{:S(2)}) collective-permute-start(bf16[256,256]{1,0:T(8,128)(2,1)S(1)} %get-tuple-element.36), channel_id=1, source_target_pairs={{0,8},{4,12},{8,0},{12,4},{1,9},{5,13},{9,1},{13,5},{2,10},{6,14},... | collective-permute-start | bytes 393224 | tf_op jit(solution)/shard_map/ppermute | solution.py:699
  85.6 70.7 %collective-permute-start.2 = (bf16[256,256]{1,0:T(8,128)(2,1)S(1)}, bf16[256,256]{1,0:T(8,128)(2,1)}, u32[]{:S(2)}, u32[]{:S(2)}) collective-permute-start(bf16[256,256]{1,0:T(8,128)(2,1)S(1)} %get-tuple-element.36), channel_id=1, source_target_pairs={{0,4},{4,8},{8,12},{12,0},{1,5},{5,9},{9,13},{13,1},{2,6},{6,10},{... | collective-permute-start | bytes 393224 | tf_op jit(solution)/shard_map/ppermute | solution.py:699
  86.2 85.5 %collective-permute-start.1 = (bf16[1280,1024]{1,0:T(8,128)(2,1)}, bf16[1280,1024]{1,0:T(8,128)(2,1)}, u32[]{:S(2)}, u32[]{:S(2)}) collective-permute-start(bf16[1280,1024]{1,0:T(8,128)(2,1)} %copy-done.10), channel_id=1, source_target_pairs={{0,16},{16,0},{1,17},{17,1},{2,18},{18,2},{3,19},{19,3},{4,20},{20... | collective-permute-start | bytes 7864328 | tf_op jit(solution)/shard_map/ppermute | solution.py:303
  91.8 25.6 %copy-start.24 = (bf16[1024,1024]{1,0:T(8,128)(2,1)}, bf16[1024,1024]{1,0:T(8,128)(2,1)S(1)}, u32[]{:S(2)}) copy-start(bf16[1024,1024]{1,0:T(8,128)(2,1)S(1)} %get-tuple-element.81) | copy-start | bytes 6291460
  91.8 25.6 %copy-start.26 = (bf16[1024,1024]{1,0:T(8,128)(2,1)}, bf16[1024,1024]{1,0:T(8,128)(2,1)S(1)}, u32[]{:S(2)}) copy-start(bf16[1024,1024]{1,0:T(8,128)(2,1)S(1)} %get-tuple-element.82) | copy-start | bytes 6291460
  160.1 2.1 collective-permute-start.5
  168.7 69.5 %collective-permute-start = (bf16[1024,768]{1,0:T(8,128)(2,1)}, bf16[1024,768]{1,0:T(8,128)(2,1)S(1)}, u32[]{:S(2)}, u32[]{:S(2)}) collective-permute-start(bf16[1024,768]{1,0:T(8,128)(2,1)} %all-gather.2.cloned.1.call-done), channel_id=1, source_target_pairs={{0,1},{1,0},{2,3},{3,2},{4,5},{5,4},{6,7},{7,6},{8,9},{9,8},{10,11... | collective-permute-start | bytes 4718600 | tf_op jit(solution)/shard_map/ppermute | solution.py:303
  209.4 21.3 %slice-start.10 = ((s8[5242880]{0:T(1024)(128)(4,1)}), s8[4194304]{0:T(1024)(128)(4,1)S(1)}, s32[]{:S(2)}) async-start(s8[5242880]{0:T(1024)(128)(4,1)} %bitcast.124), calls=%async_computation.11 | async-start | bytes 8388608
  217.4 167.0 %collective-permute-start.18 = (f32[1024,1024]{1,0:T(8,128)}, f32[1024,1024]{1,0:T(8,128)}, u32[]{:S(2)}, u32[]{:S(2)}) collective-permute-start(f32[1024,1024]{1,0:T(8,128)} %fusion.61.refs_10_), channel_id=1, source_target_pairs={{0,1},{1,0},{2,3},{3,2},{4,5},{5,4},{6,7},{7,6},{8,9},{9,8},{10,11... | collective-permute-start | bytes 12582920 | tf_op jit(solution)/shard_map/ppermute | solution.py:303
  217.9 36.8 %collective-permute-start.23 = (f32[1024,1024]{1,0:T(8,128)S(1)}, f32[1024,1024]{1,0:T(8,128)S(1)}, u32[]{:S(2)}, u32[]{:S(2)}) collective-permute-start(f32[1024,1024]{1,0:T(8,128)S(1)} %fusion.55.refs_8_), channel_id=1, source_target_pairs={{0,1},{1,0},{2,3},{3,2},{4,5},{5,4},{6,7},{7,6},{8,9},{9,8},{10,11... | collective-permute-start | bytes 12582920 | tf_op jit(solution)/shard_map/ppermute | solution.py:303
  387.8 38.5 %collective-permute-start.19 = (bf16[1024,512]{1,0:T(8,128)(2,1)S(1)}, bf16[1024,512]{1,0:T(8,128)(2,1)}, u32[]{:S(2)}, u32[]{:S(2)}) collective-permute-start(bf16[1024,512]{1,0:T(8,128)(2,1)S(1)} %dynamic-slice_convert_fusion.1), channel_id=1, source_target_pairs={{0,2},{1,3},{2,0},{3,1},{4,6},{5,7},{6,4},{7,5},{8,10},{9,11},{10,... | collective-permute-start | bytes 3145736 | tf_op jit(solution)/shard_map/ppermute | solution.py:303
  389.8 40.9 %collective-permute-start.13 = (f32[256,1024]{1,0:T(8,128)S(1)}, f32[256,1024]{1,0:T(8,128)S(1)}, u32[]{:S(2)}, u32[]{:S(2)}) collective-permute-start(f32[256,1024]{1,0:T(8,128)S(1)} %convolution_add_fusion), channel_id=1, source_target_pairs={{0,1},{1,0},{2,3},{3,2},{4,5},{5,4},{6,7},{7,6},{8,9},{9,8},{10,11... | collective-permute-start | bytes 3145736 | tf_op jit(solution)/shard_map/ppermute | solution.py:303
  393.6 40.2 %collective-permute-start.24 = (bf16[512,1024]{1,0:T(8,128)(2,1)S(1)}, bf16[512,1024]{1,0:T(8,128)(2,1)}, u32[]{:S(2)}, u32[]{:S(2)}) collective-permute-start(bf16[512,1024]{1,0:T(8,128)(2,1)S(1)} %dynamic-slice_convert_fusion), channel_id=1, source_target_pairs={{0,2},{1,3},{2,0},{3,1},{4,6},{5,7},{6,4},{7,5},{8,10},{9,11},{10,... | collective-permute-start | bytes 3145736 | tf_op jit(solution)/shard_map/ppermute | solution.py:303
  405.6 109.1 %collective-permute-start.7 = (bf16[1280,1024]{1,0:T(8,128)(2,1)}, bf16[1280,1024]{1,0:T(8,128)(2,1)S(1)}, u32[]{:S(2)}, u32[]{:S(2)}) collective-permute-start(bf16[1280,1024]{1,0:T(8,128)(2,1)} %add_convert_fusion), channel_id=1, source_target_pairs={{0,16},{16,0},{1,17},{17,1},{2,18},{18,2},{3,19},{19,3},{4,20},{20... | collective-permute-start | bytes 7864328 | tf_op jit(solution)/shard_map/ppermute | solution.py:303
  414.2 103.3 %collective-permute-start.8 = (f32[1024,768]{0,1:T(8,128)}, f32[1024,768]{0,1:T(8,128)}, u32[]{:S(2)}, u32[]{:S(2)}) collective-permute-start(f32[1024,768]{0,1:T(8,128)} %fusion.67), channel_id=1, source_target_pairs={{0,1},{1,0},{2,3},{3,2},{4,5},{5,4},{6,7},{7,6},{8,9},{9,8},{10,11... | collective-permute-start | bytes 9437192 | tf_op jit(solution)/shard_map/ppermute | solution.py:303
  428.2 17.6 %collective-permute-start.20 = (bf16[256,512]{1,0:T(8,128)(2,1)S(1)}, bf16[256,512]{1,0:T(8,128)(2,1)S(1)}, u32[]{:S(2)}, u32[]{:S(2)}) collective-permute-start(bf16[256,512]{1,0:T(8,128)(2,1)S(1)} %get-tuple-element.88), channel_id=1, source_target_pairs={{0,4},{4,8},{8,12},{12,0},{1,5},{5,9},{9,13},{13,1},{2,6},{6,10},{... | collective-permute-start | bytes 786440 | tf_op jit(solution)/shard_map/ppermute | solution.py:719
  430.7 19.0 %collective-permute-start.22 = (bf16[256,512]{1,0:T(8,128)(2,1)S(1)}, bf16[256,512]{1,0:T(8,128)(2,1)S(1)}, u32[]{:S(2)}, u32[]{:S(2)}) collective-permute-start(bf16[256,512]{1,0:T(8,128)(2,1)S(1)} %get-tuple-element.89), channel_id=1, source_target_pairs={{0,12},{4,0},{8,4},{12,8},{1,13},{5,1},{9,5},{13,9},{2,14},{6,2},{... | collective-permute-start | bytes 786440 | tf_op jit(solution)/shard_map/ppermute | solution.py:719
  432.1 82.6 %slice-start.2 = ((s8[5242880]{0:T(1024)(128)(4,1)}), s8[4194304]{0:T(1024)(128)(4,1)S(1)}, s32[]{:S(2)}) async-start(s8[5242880]{0:T(1024)(128)(4,1)} %bitcast.101), calls=%async_computation.3 | async-start | bytes 8388608
  433.8 7.3 %collective-permute-start.14 = (bf16[128,1024]{1,0:T(8,128)(2,1)S(1)}, bf16[128,1024]{1,0:T(8,128)(2,1)S(1)}, u32[]{:S(2)}, u32[]{:S(2)}) collective-permute-start(bf16[128,1024]{1,0:T(8,128)(2,1)S(1)} %dynamic-slice_convert_fusion.9), channel_id=1, source_target_pairs={{0,2},{1,3},{2,0},{3,1},{4,6},{5,7},{6,4},{7,5},{8,10},{9,11},{10,... | collective-permute-start | bytes 786440 | tf_op jit(solution)/shard_map/ppermute | solution.py:303
  441.1 22.1 %collective-permute-start.21 = (bf16[256,512]{1,0:T(8,128)(2,1)S(1)}, bf16[256,512]{1,0:T(8,128)(2,1)S(1)}, u32[]{:S(2)}, u32[]{:S(2)}) collective-permute-start(bf16[256,512]{1,0:T(8,128)(2,1)S(1)} %get-tuple-element.90), channel_id=1, source_target_pairs={{0,8},{4,12},{8,0},{12,4},{1,9},{5,13},{9,1},{13,5},{2,10},{6,14},... | collective-permute-start | bytes 786440 | tf_op jit(solution)/shard_map/ppermute | solution.py:719
  445.8 18.9 %collective-permute-start.25 = (bf16[512,256]{1,0:T(8,128)(2,1)S(1)}, bf16[512,256]{1,0:T(8,128)(2,1)S(1)}, u32[]{:S(2)}, u32[]{:S(2)}) collective-permute-start(bf16[512,256]{1,0:T(8,128)(2,1)S(1)} %get-tuple-element.85), channel_id=1, source_target_pairs={{0,4},{4,8},{8,12},{12,0},{1,5},{5,9},{9,13},{13,1},{2,6},{6,10},{... | collective-permute-start | bytes 786440 | tf_op jit(solution)/shard_map/ppermute | solution.py:719
  449.7 24.0 %collective-permute-start.27 = (bf16[512,256]{1,0:T(8,128)(2,1)S(1)}, bf16[512,256]{1,0:T(8,128)(2,1)S(1)}, u32[]{:S(2)}, u32[]{:S(2)}) collective-permute-start(bf16[512,256]{1,0:T(8,128)(2,1)S(1)} %get-tuple-element.86), channel_id=1, source_target_pairs={{0,12},{4,0},{8,4},{12,8},{1,13},{5,1},{9,5},{13,9},{2,14},{6,2},{... | collective-permute-start | bytes 786440 | tf_op jit(solution)/shard_map/ppermute | solution.py:719
  463.2 19.0 %collective-permute-start.26 = (bf16[512,256]{1,0:T(8,128)(2,1)S(1)}, bf16[512,256]{1,0:T(8,128)(2,1)S(1)}, u32[]{:S(2)}, u32[]{:S(2)}) collective-permute-start(bf16[512,256]{1,0:T(8,128)(2,1)S(1)} %get-tuple-element.87), channel_id=1, source_target_pairs={{0,8},{4,12},{8,0},{12,4},{1,9},{5,13},{9,1},{13,5},{2,10},{6,14},... | collective-permute-start | bytes 786440 | tf_op jit(solution)/shard_map/ppermute | solution.py:719
  463.2 51.5 %slice-start.3 = ((s8[5242880]{0:T(1024)(128)(4,1)}), s8[1048576]{0:T(1024)(128)(4,1)S(1)}, s32[]{:S(2)}) async-start(s8[5242880]{0:T(1024)(128)(4,1)} %bitcast.101), calls=%async_computation.4 | async-start | bytes 2097152
  464.7 18.3 %collective-permute-start.15 = (bf16[128,256]{1,0:T(8,128)(2,1)S(1)}, bf16[128,256]{1,0:T(8,128)(2,1)S(1)}, u32[]{:S(2)}, u32[]{:S(2)}) collective-permute-start(bf16[128,256]{1,0:T(8,128)(2,1)S(1)} %get-tuple-element.94), channel_id=1, source_target_pairs={{0,4},{4,8},{8,12},{12,0},{1,5},{5,9},{9,13},{13,1},{2,6},{6,10},{... | collective-permute-start | bytes 196616 | tf_op jit(solution)/shard_map/ppermute | solution.py:719
  473.7 9.5 %collective-permute-start.17 = (bf16[128,256]{1,0:T(8,128)(2,1)S(1)}, bf16[128,256]{1,0:T(8,128)(2,1)S(1)}, u32[]{:S(2)}, u32[]{:S(2)}) collective-permute-start(bf16[128,256]{1,0:T(8,128)(2,1)S(1)} %get-tuple-element.95), channel_id=1, source_target_pairs={{0,12},{4,0},{8,4},{12,8},{1,13},{5,1},{9,5},{13,9},{2,14},{6,2},{... | collective-permute-start | bytes 196616 | tf_op jit(solution)/shard_map/ppermute | solution.py:719
  482.2 5.2 collective-permute-start.16
  483.0 30.1 %collective-permute-start.32 = (f32[256,512]{1,0:T(8,128)S(1)}, f32[256,512]{1,0:T(8,128)S(1)}, u32[]{:S(2)}, u32[]{:S(2)}) collective-permute-start(f32[256,512]{1,0:T(8,128)S(1)} %get-tuple-element.73), channel_id=1, source_target_pairs={{0,2},{1,3},{2,0},{3,1},{4,6},{5,7},{6,4},{7,5},{8,10},{9,11},{10,... | collective-permute-start | bytes 1572872 | tf_op jit(solution)/shard_map/ppermute | solution.py:303
  483.2 28.7 %collective-permute-start.34 = (f32[512,256]{1,0:T(8,128)S(1)}, f32[512,256]{1,0:T(8,128)S(1)}, u32[]{:S(2)}, u32[]{:S(2)}) collective-permute-start(f32[512,256]{1,0:T(8,128)S(1)} %get-tuple-element.71), channel_id=1, source_target_pairs={{0,2},{1,3},{2,0},{3,1},{4,6},{5,7},{6,4},{7,5},{8,10},{9,11},{10,... | collective-permute-start | bytes 1572872 | tf_op jit(solution)/shard_map/ppermute | solution.py:303
  488.0 26.7 %slice-start = ((s8[5242880]{0:T(1024)(128)(4,1)}), s8[4194304]{0:T(1024)(128)(4,1)S(1)}, s32[]{:S(2)}) async-start(s8[5242880]{0:T(1024)(128)(4,1)} %bitcast.99), calls=%async_computation.1 | async-start | bytes 8388608
  488.0 26.7 %slice-start.1 = ((s8[5242880]{0:T(1024)(128)(4,1)}), s8[1048576]{0:T(1024)(128)(4,1)S(1)}, s32[]{:S(2)}) async-start(s8[5242880]{0:T(1024)(128)(4,1)} %bitcast.99), calls=%async_computation.2 | async-start | bytes 2097152
  488.0 21.9 %collective-permute-start.30 = (f32[128,256]{1,0:T(8,128)S(1)}, f32[128,256]{1,0:T(8,128)S(1)}, u32[]{:S(2)}, u32[]{:S(2)}) collective-permute-start(f32[128,256]{1,0:T(8,128)S(1)} %get-tuple-element.75), channel_id=1, source_target_pairs={{0,2},{1,3},{2,0},{3,1},{4,6},{5,7},{6,4},{7,5},{8,10},{9,11},{10,... | collective-permute-start | bytes 393224 | tf_op jit(solution)/shard_map/ppermute | solution.py:303
  490.3 24.4 %copy-start.13 = (bf16[1,1280,1024]{2,1,0:T(8,128)(2,1)S(1)}, bf16[1,1280,1024]{2,1,0:T(8,128)(2,1)}, u32[]{:S(2)}) copy-start(bf16[1,1280,1024]{2,1,0:T(8,128)(2,1)} %param.18) | copy-start | bytes 7864324
  490.3 24.4 %copy-start.38 = (f32[1280]{0:T(1024)S(1)}, f32[1280]{0:T(1024)}, u32[]{:S(2)}) copy-start(f32[1280]{0:T(1024)} %broadcast_multiply_fusion) | copy-start | bytes 15364
  490.3 24.4 %copy-start.39 = (f32[1,1024]{1,0:T(1,128)S(1)}, f32[1,1024]{1,0:T(1,128)}, u32[]{:S(2)}) copy-start(f32[1,1024]{1,0:T(1,128)} %slice.80) | copy-start | bytes 12292
  509.9 57.1 %collective-permute-start.6 = (bf16[1280,1024]{1,0:T(8,128)(2,1)}, bf16[1280,1024]{1,0:T(8,128)(2,1)S(1)}, u32[]{:S(2)}, u32[]{:S(2)}) collective-permute-start(bf16[1280,1024]{1,0:T(8,128)(2,1)} %add_convert_fusion.1), channel_id=1, source_target_pairs={{0,16},{16,0},{1,17},{17,1},{2,18},{18,2},{3,19},{19,3},{4,20},{20... | collective-permute-start | bytes 7864328 | tf_op jit(solution)/shard_map/ppermute | solution.py:303
  512.0 93.7 %collective-permute-start.31 = (f32[256,256]{1,0:T(8,128)}, f32[256,256]{1,0:T(8,128)}, u32[]{:S(2)}, u32[]{:S(2)}) collective-permute-start(f32[256,256]{1,0:T(8,128)} %maximum_select_fusion.8), channel_id=1, source_target_pairs={{0,1},{1,0},{2,3},{3,2},{4,5},{5,4},{6,7},{7,6},{8,9},{9,8},{10,11... | collective-permute-start | bytes 786440 | tf_op jit(solution)/shard_map/ppermute | solution.py:303
  513.0 86.1 %collective-permute-start.35 = (f32[1024,256]{1,0:T(8,128)}, f32[1024,256]{1,0:T(8,128)}, u32[]{:S(2)}, u32[]{:S(2)}) collective-permute-start(f32[1024,256]{1,0:T(8,128)} %maximum_select_fusion.4), channel_id=1, source_target_pairs={{0,1},{1,0},{2,3},{3,2},{4,5},{5,4},{6,7},{7,6},{8,9},{9,8},{10,11... | collective-permute-start | bytes 3145736 | tf_op jit(solution)/shard_map/ppermute | solution.py:303
  522.5 19.5 %collective-permute-start.9 = (bf16[1024,384]{0,1:T(8,128)(2,1)S(1)}, bf16[1024,384]{0,1:T(8,128)(2,1)S(1)}, u32[]{:S(2)}, u32[]{:S(2)}) collective-permute-start(bf16[1024,384]{0,1:T(8,128)(2,1)S(1)} %dynamic-slice_convert_fusion.2), channel_id=1, source_target_pairs={{0,2},{1,3},{2,0},{3,1},{4,6},{5,7},{6,4},{7,5},{8,10},{9,11},{10,... | collective-permute-start | bytes 2359304 | tf_op jit(solution)/shard_map/ppermute | solution.py:303
  542.4 36.0 %collective-permute-start.10 = (bf16[256,384]{0,1:T(8,128)(2,1)S(1)}, bf16[256,384]{0,1:T(8,128)(2,1)S(1)}, u32[]{:S(2)}, u32[]{:S(2)}) collective-permute-start(bf16[256,384]{0,1:T(8,128)(2,1)S(1)} %get-tuple-element.91), channel_id=1, source_target_pairs={{0,4},{4,8},{8,12},{12,0},{1,5},{5,9},{9,13},{13,1},{2,6},{6,10},{... | collective-permute-start | bytes 589832 | tf_op jit(solution)/shard_map/ppermute | solution.py:719
  544.9 33.5 %collective-permute-start.12 = (bf16[256,384]{0,1:T(8,128)(2,1)S(1)}, bf16[256,384]{0,1:T(8,128)(2,1)S(1)}, u32[]{:S(2)}, u32[]{:S(2)}) collective-permute-start(bf16[256,384]{0,1:T(8,128)(2,1)S(1)} %get-tuple-element.92), channel_id=1, source_target_pairs={{0,12},{4,0},{8,4},{12,8},{1,13},{5,1},{9,5},{13,9},{2,14},{6,2},{... | collective-permute-start | bytes 589832 | tf_op jit(solution)/shard_map/ppermute | solution.py:719
  568.5 10.0 %collective-permute-start.11 = (bf16[256,384]{0,1:T(8,128)(2,1)S(1)}, bf16[256,384]{0,1:T(8,128)(2,1)S(1)}, u32[]{:S(2)}, u32[]{:S(2)}) collective-permute-start(bf16[256,384]{0,1:T(8,128)(2,1)S(1)} %get-tuple-element.93), channel_id=1, source_target_pairs={{0,8},{4,12},{8,0},{12,4},{1,9},{5,13},{9,1},{13,5},{2,10},{6,14},... | collective-permute-start | bytes 589832 | tf_op jit(solution)/shard_map/ppermute | solution.py:719
  570.9 28.3 %copy-start.1 = (f32[2048,256]{1,0:T(8,128)S(1)}, f32[2048,256]{1,0:T(8,128)}, u32[]{:S(2)}) copy-start(f32[2048,256]{1,0:T(8,128)} %shrink_ref.1) | copy-start | bytes 6291460
  578.4 31.7 %collective-permute-start.33 = (f32[256,1024]{1,0:T(8,128)}, f32[256,1024]{1,0:T(8,128)}, u32[]{:S(2)}, u32[]{:S(2)}) collective-permute-start(f32[256,1024]{1,0:T(8,128)} %maximum_select_fusion.3), channel_id=1, source_target_pairs={{0,1},{1,0},{2,3},{3,2},{4,5},{5,4},{6,7},{7,6},{8,9},{9,8},{10,11... | collective-permute-start | bytes 3145736 | tf_op jit(solution)/shard_map/ppermute | solution.py:303
  598.0 11.9 %collective-permute-start.28 = (f32[256,384]{0,1:T(8,128)S(1)}, f32[256,384]{0,1:T(8,128)S(1)}, u32[]{:S(2)}, u32[]{:S(2)}) collective-permute-start(f32[256,384]{0,1:T(8,128)S(1)} %get-tuple-element.77), channel_id=1, source_target_pairs={{0,2},{1,3},{2,0},{3,1},{4,6},{5,7},{6,4},{7,5},{8,10},{9,11},{10,... | collective-permute-start | bytes 1179656 | tf_op jit(solution)/shard_map/ppermute | solution.py:303
  610.0 6.0 collective-permute-start.29
  (52 other events, 325.2 us)
Sparse Core Ops, SparseCore 0:
  86.4 37.0 all-gather.1

commit v4 on v3

--- a/solution.py
+++ b/solution.py
@@ -128,64 +128,83 @@
         queries = [query_ref[h, :, columns] for h in range(together)]
         backs = [back_ref[h, :, columns] for h in range(together)]
 
-        def scores(j, carry):
-            rows = stored(j)
-            allowed = (key_at >= start - j * BK) & (key_at <= own - j * BK)
+        def in_pairs(body, carry):
+            twos = lax.div(i + 1 - lowest, 2)
+            carry = lax.fori_loop(
+                0, twos, lambda n, c: body((lowest + 2 * n, lowest + 2 * n + 1), c), carry
+            )
+            return lax.fori_loop(lowest + 2 * twos, i + 1, lambda n, c: body((n,), c), carry)
+
+        def scores(group, carry):
+            made = []
+            for j in group:
+                rows = stored(j)
+                allowed = (key_at >= start - j * BK) & (key_at <= own - j * BK)
+                for h in range(together):
+                    raw = jnp.dot(
+                        key_ref[h, rows, :], queries[h], preferred_element_type=jnp.float32
+                    )
+                    share_grad = jnp.dot(
+                        value_ref[h, rows, :], backs[h], preferred_element_type=jnp.float32
+                    )
+                    masked = jnp.where(allowed, raw, masked_value)
+                    here = jnp.max(masked, axis=0, keepdims=True)
+                    shifted = jnp.exp(masked - here)
+                    shifted_ref[h, j] = shifted
+                    share_grad_ref[h, j] = share_grad
+                    top_ref[h, j] = here
+                    made.append(
+                        (
+                            here,
+                            jnp.sum(shifted, axis=0, keepdims=True),
+                            jnp.sum(shifted * share_grad, axis=0, keepdims=True),
+                        )
+                    )
             out = []
             for h in range(together):
                 top, total, inner = carry[h]
-                raw = jnp.dot(key_ref[h, rows, :], queries[h], preferred_element_type=jnp.float32)
-                share_grad = jnp.dot(
-                    value_ref[h, rows, :], backs[h], preferred_element_type=jnp.float32
-                )
-                masked = jnp.where(allowed, raw, masked_value)
-                here = jnp.max(masked, axis=0, keepdims=True)
-                shifted = jnp.exp(masked - here)
-                shifted_ref[h, j] = shifted
-                share_grad_ref[h, j] = share_grad
-                top_ref[h, j] = here
-                new = jnp.maximum(top, here)
-                old_by, here_by = jnp.exp(top - new), jnp.exp(here - new)
-                total = total * old_by + jnp.sum(shifted, axis=0, keepdims=True) * here_by
-                inner = (
-                    inner * old_by
-                    + jnp.sum(shifted * share_grad, axis=0, keepdims=True) * here_by
-                )
-                out.append((new, total, inner))
+                for here, here_total, here_inner in made[h::together]:
+                    new = jnp.maximum(top, here)
+                    old_by, here_by = jnp.exp(top - new), jnp.exp(here - new)
+                    total = total * old_by + here_total * here_by
+                    inner = inner * old_by + here_inner * here_by
+                    top = new
+                out.append((top, total, inner))
             return tuple(out)
 
         zero = jnp.zeros((1, BQ), jnp.float32)
         empty = (jnp.full((1, BQ), masked_value, jnp.float32), zero, zero)
-        stats = lax.fori_loop(lowest, i + 1, scores, (empty,) * together)
+        stats = in_pairs(scores, (empty,) * together)
         inverse = [1.0 / s[1] for s in stats]
         inners = [s[2] * r for s, r in zip(stats, inverse)]
 
-        def sums(j, carry):
-            rows = stored(j)
-            out = []
-            for h in range(together):
-                mixed, query_grad = carry[h]
-                by = jnp.exp(top_ref[h, j] - stats[h][0]) * inverse[h]
-                probs = shifted_ref[h, j] * by
-                shares = probs.astype(jnp.bfloat16)
-                score_grad = (probs * (share_grad_ref[h, j] - inners[h])).astype(jnp.bfloat16)
-                mixed = mixed + jnp.dot(
-                    value_columns_ref[h, :, rows], shares, preferred_element_type=jnp.float32
-                )
-                query_grad = query_grad + jnp.dot(
-                    key_columns_ref[h, :, rows], score_grad, preferred_element_type=jnp.float32
-                )
-                value_grad_ref[h, :, rows] += lax.dot_general(
-                    backs[h], shares, nt, preferred_element_type=jnp.float32
-                )
-                key_grad_ref[h, :, rows] += lax.dot_general(
-                    queries[h], score_grad, nt, preferred_element_type=jnp.float32
-                )
-                out.append((mixed, query_grad))
+        def sums(group, carry):
+            out = list(carry)
+            for j in group:
+                rows = stored(j)
+                for h in range(together):
+                    mixed, query_grad = out[h]
+                    by = jnp.exp(top_ref[h, j] - stats[h][0]) * inverse[h]
+                    probs = shifted_ref[h, j] * by
+                    shares = probs.astype(jnp.bfloat16)
+                    score_grad = (probs * (share_grad_ref[h, j] - inners[h])).astype(jnp.bfloat16)
+                    mixed = mixed + jnp.dot(
+                        value_columns_ref[h, :, rows], shares, preferred_element_type=jnp.float32
+                    )
+                    query_grad = query_grad + jnp.dot(
+                        key_columns_ref[h, :, rows], score_grad, preferred_element_type=jnp.float32
+                    )
+                    value_grad_ref[h, :, rows] += lax.dot_general(
+                        backs[h], shares, nt, preferred_element_type=jnp.float32
+                    )
+                    key_grad_ref[h, :, rows] += lax.dot_general(
+                        queries[h], score_grad, nt, preferred_element_type=jnp.float32
+                    )
+                    out[h] = (mixed, query_grad)
             return tuple(out)
 
         nothing = jnp.zeros((HD, BQ), jnp.float32)
-        results = lax.fori_loop(lowest, i + 1, sums, ((nothing, nothing),) * together)
+        results = in_pairs(sums, ((nothing, nothing),) * together)
         for h in range(together):
             back_ref[h, :, columns] = results[h][0].astype(jnp.bfloat16)
             query_grad_ref[h, :, columns] = results[h][1] * scale
@@ -303,12 +322,139 @@
     return lax.ppermute(array, axis, [(i, i ^ bit) for i in range(size)])
 
 
+def follow(array, *before):
+    return lax.optimization_barrier((array, *before))[0]
+
+
 def ordered(index, mine, other, axis):
     return jnp.where(
         index == 0,
         jnp.concatenate([mine, other], axis=axis),
         jnp.concatenate([other, mine], axis=axis),
     )
+
+
+UNITS = 512
+ROWS = 640
+
+
+def feed_kernel(
+    earlier,
+    hidden_ref,
+    back_ref,
+    expand_ref,
+    shrink_ref,
+    *refs,
+):
+    if earlier:
+        expand_before, shrink_before = refs[:2]
+        refs = refs[2:]
+    (
+        expand_grad,
+        shrink_grad,
+        hidden_part,
+        branch_part,
+        activated_ref,
+        lifted_grad_ref,
+        turned_ref,
+        hidden_sum,
+        branch_sum,
+    ) = refs
+    step, steps = pl.program_id(0), pl.num_programs(0)
+    tokens = hidden_ref.shape[0]
+    f32 = jnp.float32
+    nt = (((1,), (1,)), ((), ()))
+    tn = (((0,), (0,)), ((), ()))
+    slope = 0.7978845608028654
+
+    @pl.when(step == 0)
+    def _():
+        turned_ref[...] = hidden_ref[...].T
+
+    def block(at, first):
+        hidden = hidden_ref[at, :]
+        back = back_ref[at, :]
+        lifted = jnp.dot(hidden, expand_ref[...], preferred_element_type=f32)
+        active_grad = lax.dot_general(back, shrink_ref[...], nt, preferred_element_type=f32)
+        square = lifted * lifted
+        curve = jnp.tanh(slope * (lifted + 0.044715 * (square * lifted)))
+        rise = 0.5 * (1.0 + curve)
+        activated = (lifted * rise).astype(jnp.bfloat16)
+        bend = 0.5 * lifted * (1.0 - curve * curve) * (slope + (3.0 * 0.044715 * slope) * square)
+        lifted_grad = (active_grad * (rise + bend)).astype(jnp.bfloat16)
+        activated_ref[at, :] = activated
+        lifted_grad_ref[at, :] = lifted_grad
+        branch = jnp.dot(activated, shrink_ref[...], preferred_element_type=f32)
+        hidden_grad = lax.dot_general(lifted_grad, expand_ref[...], nt, preferred_element_type=f32)
+        if first:
+            branch_sum[at, :] = branch
+            hidden_sum[at, :] = hidden_grad
+        else:
+            branch_sum[at, :] += branch
+            hidden_sum[at, :] += hidden_grad
+
+    def blocks(first):
+        def one(i, _):
+            block(pl.ds(pl.multiple_of(i * ROWS, ROWS), ROWS), first)
+            return 0
+
+        lax.fori_loop(0, tokens // ROWS, one, 0)
+
+    @pl.when(step == 0)
+    def _():
+        blocks(True)
+
+    @pl.when(step > 0)
+    def _():
+        blocks(False)
+
+    made = lax.dot_general(activated_ref[...], back_ref[...], tn, preferred_element_type=f32)
+    shrink_grad[...] = made + shrink_before[...] if earlier else made
+    made = jnp.dot(turned_ref[...], lifted_grad_ref[...], preferred_element_type=f32)
+    expand_grad[...] = made + expand_before[...] if earlier else made
+
+    @pl.when(step == steps - 1)
+    def _():
+        hidden_part[...] = hidden_sum[...].astype(hidden_part.dtype)
+        branch_part[...] = branch_sum[...].astype(branch_part.dtype)
+
+
+def feed(hidden, back, expand, shrink, before, branch_type):
+    tokens, width = hidden.shape
+    units = 2 * expand.shape[2]
+    tile = min(UNITS, expand.shape[2])
+    steps = units // tile
+    low, f32 = jnp.bfloat16, jnp.float32
+    whole = pl.BlockSpec((tokens, width), lambda n: (0, 0), pipeline_mode=pl.Buffered(1))
+    columns = pl.BlockSpec((width, tile), lambda n: (0, n))
+    rows = pl.BlockSpec((tile, width), lambda n: (n, 0))
+    return pl.pallas_call(
+        partial(feed_kernel, bool(before)),
+        grid=(steps,),
+        in_specs=[
+            whole,
+            whole,
+            pl.BlockSpec((None, width, tile), lambda n: (n * 2 // steps, 0, n % (steps // 2))),
+            rows,
+        ]
+        + [columns, rows] * bool(before),
+        out_specs=[columns, rows, whole, whole],
+        out_shape=[
+            jax.ShapeDtypeStruct((width, units), f32),
+            jax.ShapeDtypeStruct((units, width), f32),
+            jax.ShapeDtypeStruct((tokens, width), f32),
+            jax.ShapeDtypeStruct((tokens, width), branch_type),
+        ],
+        scratch_shapes=[
+            pltpu.VMEM((tokens, tile), low),
+            pltpu.VMEM((tokens, tile), low),
+            pltpu.VMEM((width, tokens), low),
+            pltpu.VMEM((tokens, width), f32),
+            pltpu.VMEM((tokens, width), f32),
+        ],
+        compiler_params=pltpu.CompilerParams(vmem_limit_bytes=56 * 2**20),
+        cost_estimate=pl.CostEstimate(flops=2**20, bytes_accessed=2**20, transcendentals=0),
+    )(hidden, back, expand, shrink, *before)
 
 
 MESH = pl.DeviceIdType.MESH
@@ -701,12 +847,15 @@
             out = lax.dynamic_update_slice_in_dim(out, come, at * piece, depth)
         return jnp.concatenate([out, swap(out, "outer", 1)], axis=cut)
 
-    def total(self, own, sibling, cut, depth):
+    def pair_sum(self, own, sibling, cut):
         own = own + swap(sibling, "outer", 1)
         half = own.shape[cut] // 2
         keep = lax.dynamic_slice_in_dim(own, self.far * half, half, cut)
         send = lax.dynamic_slice_in_dim(own, (1 - self.far) * half, half, cut)
-        keep = keep + swap(send.astype(jnp.bfloat16), "outer", 2).astype(jnp.float32)
+        return keep, swap(send.astype(jnp.bfloat16), "outer", 2)
+
+    def line_sum(self, keep, come, depth):
+        keep = keep + come.astype(jnp.float32)
         piece = keep.shape[depth] // self.deep
 
         def part(at):
@@ -776,7 +925,6 @@
             cotangent[0],
         )
         backs = [cotangent[0], other_back]
-        expand = jnp.concatenate([expand[0], expand[1]], axis=1)
         shrink = shrink.reshape(-1, shrink.shape[2])
         project = plan.gather(project, 1, 0)
         mixing = plan.gather_few(mixing, 0, 1)
@@ -799,65 +947,104 @@
     def over_tokens(pattern, lefts, rights):
         return sum(product(pattern, left, right) for left, right in zip(lefts, rights))
 
-    def weight_sum(pattern, lefts, rights, cut, depth):
-        if not paired:
-            term = over_tokens(pattern, lefts, rights)
-            term = lax.psum_scatter(term, "dp", scatter_dimension=depth, tiled=True)
-            return lax.psum(term, "outer"), ()
+    def halves(pattern, lefts, rights, cut):
         sources = rights if cut == 1 else lefts
         axis = 0 if pattern.split(",")[cut].index("t") == 1 else 1
         half = sources[0].shape[axis] // 2
-
-        def term(near):
+        out = []
+        for near in (1, 0):
             chosen = [
                 lax.slice_in_dim(v, near * half, (near + 1) * half, axis=axis) for v in sources
             ]
-            return (
-                over_tokens(pattern, lefts, chosen)
-                if cut == 1
-                else over_tokens(pattern, chosen, rights)
+            pair = (lefts, chosen) if cut == 1 else (chosen, rights)
+            out.append(over_tokens(pattern, *pair))
+        return out
+
+    back_local = cotangent[0].astype(jnp.float32)
+    if paired:
+        *grads, hidden_own, branch_own = feed(
+            hiddens[0], backs[0], expand, shrink, (), jnp.float32
+        )
+        expand_grad, shrink_grad, hidden_other, branch_other = feed(
+            hiddens[1], backs[1], expand, shrink, grads, jnp.bfloat16
+        )
+        hidden_parts = [hidden_own, hidden_other]
+        half = expand_grad.shape[1] // 2
+        shrink_keep, shrink_come = plan.pair_sum(shrink_grad[:half], shrink_grad[half:], 0)
+        expand_keep, expand_come = plan.pair_sum(expand_grad[:, :half], expand_grad[:, half:], 1)
+        branch_come = swap(branch_other, "mp", 1)
+        mixing_other = swap(mixing, "mp", 1)
+        projected = [product("td,de->et", hidden, project) for hidden in hiddens]
+        mixed_backs = [product("td,fd->ft", back, mixing).astype(jnp.bfloat16) for back in backs]
+        mixed, projected_grads = attend(
+            projected,
+            mixed_backs,
+            begins,
+            cosine,
+            sine,
+            position,
+            (shrink_keep, expand_keep),
+        )
+        first_grad = follow(projected_grads[1], shrink_come, expand_come, branch_come)
+        sent = (hidden_parts[1] + product("et,de->td", first_grad, project)).astype(jnp.bfloat16)
+        hidden_come = swap(sent, "mp", 1)
+        projected_grads = [follow(v, sent) for v in projected_grads]
+        mixed = [follow(v, sent) for v in mixed]
+        mixed_come = swap(mixed[1], "mp", 1)
+        project_terms = halves("td,et->de", hiddens, projected_grads, 1)
+        project_sum = plan.line_sum(*plan.pair_sum(project_terms[1], project_terms[0], 1), 0)
+        mixing_terms = halves("ft,td->fd", mixed, backs, 0)
+        mixing_sum = plan.line_sum(*plan.pair_sum(mixing_terms[1], mixing_terms[0], 0), 1)
+        shrink_sum = plan.line_sum(shrink_keep, shrink_come, 1)
+        expand_sum = plan.line_sum(expand_keep, expand_come, 0)
+        hidden_grad = (
+            hidden_parts[0]
+            + product("et,de->td", projected_grads[0], project)
+            + hidden_come.astype(jnp.float32)
+        )
+        branch = (
+            branch_own
+            + branch_come.astype(jnp.float32)
+            + product("ft,fd->td", mixed[0], mixing)
+            + product("ft,fd->td", mixed_come, mixing_other)
+        )
+    else:
+        lifteds = [product("td,df->tf", hidden, expand) for hidden in hiddens]
+        activated = [gelu(lifted) for lifted in lifteds]
+        active_grads = [product("td,fd->tf", back, shrink) for back in backs]
+        lifted_grads = [gelu_both(a, b) for a, b in zip(lifteds, active_grads)]
+        hidden_parts = [product("tf,df->td", v, expand) for v in lifted_grads]
+        branch_parts = [product("tf,fd->td", v, shrink) for v in activated]
+        projected = [product("td,de->et", hidden, project) for hidden in hiddens]
+        mixed_backs = [product("td,fd->ft", back, mixing).astype(jnp.bfloat16) for back in backs]
+        mixed, projected_grads = attend(projected, mixed_backs, begins, cosine, sine, position)
+        project_sum, mixing_sum, expand_sum, shrink_sum = (
+            lax.psum(
+                lax.psum_scatter(
+                    over_tokens(pattern, lefts, rights),
+                    "dp",
+                    scatter_dimension=depth,
+                    tiled=True,
+                ),
+                "outer",
             )
-
-        sibling, own = term(1), term(0)
-        return plan.total(own, sibling, cut, depth), (sibling, own)
-
-    lifteds = [product("td,df->tf", hidden, expand) for hidden in hiddens]
-    activated = [gelu(lifted) for lifted in lifteds]
-    active_grads = [product("td,fd->tf", back, shrink) for back in backs]
-    lifted_grads = [gelu_both(a, b) for a, b in zip(lifteds, active_grads)]
-    shrink_sum, shrink_terms = weight_sum("tf,td->fd", activated, backs, 0, 1)
-    expand_sum, expand_terms = weight_sum("td,tf->df", hiddens, lifted_grads, 1, 0)
-    projected = [product("td,de->et", hidden, project) for hidden in hiddens]
-    mixed_backs = [product("td,fd->ft", back, mixing).astype(jnp.bfloat16) for back in backs]
-    mixed, projected_grads = attend(
-        projected,
-        mixed_backs,
-        begins,
-        cosine,
-        sine,
-        position,
-        (*shrink_terms, *expand_terms),
-    )
-    mixing_sum, _ = weight_sum("ft,td->fd", mixed, backs, 0, 1)
-    project_sum, _ = weight_sum("td,et->de", hiddens, projected_grads, 1, 0)
-    hidden_grads = [
-        product("et,de->td", a, project) + product("tf,df->td", b, expand)
-        for a, b in zip(projected_grads, lifted_grads)
-    ]
-    branches = [
-        product("ft,fd->td", a, mixing) + product("tf,fd->td", b, shrink)
-        for a, b in zip(mixed, activated)
-    ]
-
-    def over_positions(terms):
-        if paired:
-            other = swap(terms[1].astype(jnp.bfloat16), "mp", 1)
-            return terms[0] + other.astype(jnp.float32)
-        return lax.psum_scatter(terms[0], "mp", scatter_dimension=0, tiled=True)
-
-    rows_grad, gain_grad, bias_grad = norm_pull(over_positions(hidden_grads))
-    input_grad = (cotangent[0].astype(jnp.float32) + rows_grad)[None]
-    block_out = (rows_local + over_positions(branches)).astype(jnp.bfloat16)[None]
+            for pattern, lefts, rights, depth in (
+                ("td,et->de", hiddens, projected_grads, 0),
+                ("ft,td->fd", mixed, backs, 1),
+                ("td,tf->df", hiddens, lifted_grads, 0),
+                ("tf,td->fd", activated, backs, 1),
+            )
+        )
+        hidden_grad, branch = (
+            lax.psum_scatter(v, "mp", scatter_dimension=0, tiled=True)
+            for v in (
+                hidden_parts[0] + product("et,de->td", projected_grads[0], project),
+                branch_parts[0] + product("ft,fd->td", mixed[0], mixing),
+            )
+        )
+    rows_grad, gain_grad, bias_grad = norm_pull(hidden_grad)
+    input_grad = (back_local + rows_grad)[None]
+    block_out = (rows_local + branch).astype(jnp.bfloat16)[None]
     sums = (project_sum, mixing_sum, expand_sum, shrink_sum)
     own_square = sum(jnp.sum(v * v) for v in sums)
     if not paired:

time: 634 us -> 586 us (0.924)
  matrix products: 205 us -> 72.7 us
  Pallas kernels: 185 us -> 267 us
  starting transfers between devices: 47.7 us -> 32.3 us
  waiting for transfers between devices: 86.4 us -> 100 us
    dot_general x32 -> x16, matrix products: 205 us -> 72.7 us  [product(): return jnp.einsum(pattern, left, right, preferred_element_type=jnp.float32)]
    pallas_call x0 -> x2, Pallas kernels: none -> 93.5 us  [feed(): pl.pallas_call(partial(feed_kernel, bool(before)), grid=(steps,), in_spec...]
    ppermute x12, starting transfers between devices: 30 us -> 18 us  [line_sum(): lax.ppermute(part(target).astype(jnp.bfloat16), 'dp', pairs)]
    pallas_call x1, Pallas kernels: 107 us -> 95.9 us  [attend(): pl.pallas_call(partial(attend_kernel, together, parts, len(after)), grid_...]
    ppermute x12, waiting for transfers between devices: 22.7 us -> 30.4 us  [line_sum(): lax.ppermute(part(target).astype(jnp.bfloat16), 'dp', pairs)]
    broadcast_in_dim x1 -> x0, other arithmetic: 7.5 us -> none  [local(): input_grad = (cotangent[0].astype(jnp.float32) + rows_grad)[None]]
    slice x0 -> x2, local copies, waits for them, and re-layouts: none -> 7.34 us  [the longest x1 5.06 us: local(): shrink_grad[half:]]
    ppermute x21 -> x23, waiting for transfers between devices: 63.7 us -> 69.9 us  [swap(): return lax.ppermute(array, axis, [(i, i ^ bit) for i in range(size)])]
  transfers between devices with their start and end apart: 37 -> 39, of which waited for: 10 -> 13; matrix products, arithmetic and copies ran while one was open for 43% -> 20% of each run, Pallas kernels for 19% -> 34%
where the time goes in v4:
time: 586 us; the launch traced here: 579 us
  Pallas kernels  267 us (46%)
  waiting for transfers between devices  100 us (17%)
  matrix products  72.7 us (12%)
  other arithmetic  57.9 us (10%)
  starting transfers between devices  32.3 us (6%)
  local copies, waits for them, and re-layouts  28.4 us (5%)
  between operations  20.6 us (4%)
    pallas_call x1, Pallas kernels, attend(): pl.pallas_call(partial(attend_kernel, together, parts, len(after)), grid_...  95.9 us
    pallas_call x2, Pallas kernels, feed(): pl.pallas_call(partial(feed_kernel, bool(before)), grid=(steps,), in_spec...  93.5 us
    dot_general x16, matrix products, product(): return jnp.einsum(pattern, left, right, preferred_element_type=jnp.float32)  72.7 us
    ppermute x23, waiting for transfers between devices, swap(): return lax.ppermute(array, axis, [(i, i ^ bit) for i in range(size)])  69.9 us
    pallas_call x1, Pallas kernels, opening(): pl.pallas_call(opening_kernel, in_specs=[here() for _ in range(6)] + [pl....  68.1 us
    ppermute x12, waiting for transfers between devices, line_sum(): lax.ppermute(part(target).astype(jnp.bfloat16), 'dp', pairs)  30.4 us
    convert_element_type x5, other arithmetic, adam_update(): return (master_new, first_new, second_new, master_new.astype(jnp.bfloat16))  18.3 us
    ppermute x12, starting transfers between devices, line_sum(): lax.ppermute(part(target).astype(jnp.bfloat16), 'dp', pairs)  18 us
  transfers between devices with their start and end apart: 39, of which 13 were waited for; matrix products, arithmetic and copies ran while one was open for 20% of the time, Pallas kernels for 34%

profile of v4, /device:TPU:0, one launch (start us, length us, event | category | flops | bytes accessed | tf_op | source)
XLA Modules:
  0.0 579.1 jit_solution(8497264839108512057)
XLA Ops:
  7.3 3.2 copy.47.project_ref
  13.5 68.1 %shard_map.353 = (bf16[2,1024,1024]{2,1,0:T(8,128)(2,1)}, bf16[2,1024,1024]{2,1,0:T(8,128)(2,1)}, bf16[256,768]{1,0:T(8,128)(2,1)}, bf16[256,256]{1,0:T(8,128)(2...) custom-call(f32[256,2048]{1,0:T(8,128)S(1)} %copy-done.4, ...), custom_call_target="tpu_custom_call" | custom-call | bytes 1048576 | tf_op jit(solution)/shard_map/pallas_call | solution.py:720
  87.8 46.5 %shard_map.354 = (f32[1024,2048]{1,0:T(8,128)}, f32[2048,1024]{1,0:T(8,128)}, f32[1280,1024]{1,0:T(8,128)}, f32[1280,1024]{1,0:T(8,128)}) custom-call(bf16[1280,1024]{1,0:T(8,128)(2,1)} %get-tuple-element.47.hidden_ref, bf16[1280,1024]{1,0:T(8,128)(2,1)} %bitcast.57, bf16[2,1024,1024]{2,1,0:T(8,128)(2,1)} %get-tuple-element.48.expand_ref, ...), custom_call_target="tpu_custom_call" | custom-call | flops 1048576 | bytes 1048576 | tf_op jit(solution)/shard_map/pallas_call | solution.py:431
  134.7 6.3 %collective-permute-done.hidden_ref = bf16[1280,1024]{1,0:T(8,128)(2,1)S(1)} collective-permute-done((bf16[1280,1024]{1,0:T(8,128)(2,1)}, bf16[1280,1024]{1,0:T(8,128)(2,1)S(1)}, u32[]{:S(2)}, u32[]{:S(2)}) %collective-permute-start) | collective-permute-done | bytes 2621472 | tf_op jit(solution)/shard_map/ppermute | solution.py:322
  142.5 47.0 %shard_map.355 = (f32[1024,2048]{1,0:T(8,128)}, f32[2048,1024]{1,0:T(8,128)}, f32[1280,1024]{1,0:T(8,128)}, bf16[1280,1024]{1,0:T(8,128)(2,1)}) custom-call(bf16[1280,1024]{1,0:T(8,128)(2,1)} %copy-done.19, bf16[1280,1024]{1,0:T(8,128)(2,1)} %copy-done, bf16[2,1024,1024]{2,1,0:T(8,128)(2,1)} %get-tuple-element.48.expand_ref, bf16[2048,1024]{1,0:T(8,128)(2,1)} %bitcast.59, ...), custom_call_target="tpu_custom_call" | custom-call | flops 1048576 | bytes 1048576 | tf_op jit(solution)/shard_map/pallas_call | solution.py:431
  189.5 5.1 slice.53
  195.6 2.3 slice.55
  204.0 5.6 collective-permute-done.6
  209.5 2.2 pad_maximum_fusion
  211.8 2.9 convolution_convert_fusion.refs_4_
  214.7 2.7 convolution_convert_fusion.1.refs_3_
  218.4 9.9 %fusion.55.refs_1_ = f32[1536,1280]{1,0:T(8,128)} fusion(bf16[1024,1536]{1,0:T(8,128)(2,1)S(1)} %constant_dynamic-update-slice_fusion.4, bf16[1280,1024]{1,0:T(8,128)(2,1)} %get-tuple-element.47.hidden_ref), kind=kOutput, calls=%fused_computation.143 | convolution fusion | flops 4026531840 | bytes 13631488 | tf_op jit(solution)/shard_map/td,de->et/dot_general | solution.py:308
  228.3 4.8 slice_add_fusion.1
  235.0 3.2 slice_add_fusion
  239.1 9.4 %fusion.56.refs_2_ = f32[1536,1280]{1,0:T(8,128)} fusion(bf16[1024,1536]{1,0:T(8,128)(2,1)} %copy-done.30, bf16[1280,1024]{1,0:T(8,128)(2,1)S(1)} %copy-done.20), kind=kOutput, calls=%fused_computation.144 | convolution fusion | flops 4026531840 | bytes 13631488 | tf_op jit(solution)/shard_map/td,de->et/dot_general | solution.py:308
  248.4 11.1 %collective-permute-done.9 = bf16[512,1024]{1,0:T(8,128)(2,1)} collective-permute-done((bf16[512,1024]{1,0:T(8,128)(2,1)S(1)}, bf16[512,1024]{1,0:T(8,128)(2,1)}, u32[]{:S(2)}, u32[]{:S(2)}) %collective-permute-start.9) | collective-permute-done | bytes 1048608 | tf_op jit(solution)/shard_map/ppermute | solution.py:322
  259.6 3.9 convert_add_fusion.2
  263.5 17.3 %collective-permute-done.10 = bf16[1024,512]{1,0:T(8,128)(2,1)S(1)} collective-permute-done((bf16[1024,512]{1,0:T(8,128)(2,1)S(1)}, bf16[1024,512]{1,0:T(8,128)(2,1)S(1)}, u32[]{:S(2)}, u32[]{:S(2)}) %collective-permute-start.10) | collective-permute-done | bytes 1048608 | tf_op jit(solution)/shard_map/ppermute | solution.py:322
  282.7 95.9 %shard_map.356 = (bf16[512,1280]{1,0:T(8,128)(2,1)S(1)}, bf16[512,1280]{1,0:T(8,128)(2,1)S(1)}, bf16[1536,1280]{1,0:T(8,128)(2,1)}, bf16[1536,1280]{1,0:T(8,128)(2,1)}) custom-call(s32[11]{0:T(128)S(1)} %pad_add_fusion.refs_0_, f32[1536,1280]{1,0:T(8,128)} %fusion.55.refs_1_, f32[1536,1280]{1,0:T(8,128)} %fusion.56.refs_2_, ...), custom_call_target="tpu_custom_call" | custom-call | flops 1048576 | bytes 1048576 | tf_op jit(solution)/shard_map/pallas_call | solution.py:251
  378.6 7.6 %fusion.57 = f32[1280,1024]{1,0:T(8,128)S(1)} fusion(bf16[1536,1280]{1,0:T(8,128)(2,1)} %get-tuple-element.70, bf16[1024,1536]{1,0:T(8,128)(2,1)} %copy-done.30), kind=kOutput, calls=%fused_computation.145 | convolution fusion | flops 4026531840 | bytes 12320768 | tf_op jit(solution)/shard_map/et,de->td/dot_general | solution.py:308
  386.2 2.4 add_convert_fusion
  388.6 4.7 fusion.16
  393.3 4.1 fusion.20
  397.4 4.5 fusion.58
  403.9 3.7 collective-permute-start.29
  410.8 3.9 fusion.18
  415.6 3.9 fusion.22
  421.0 14.0 %collective-permute-done.28 = bf16[512,256]{1,0:T(8,128)(2,1)S(1)} collective-permute-done((bf16[512,256]{1,0:T(8,128)(2,1)S(1)}, bf16[512,256]{1,0:T(8,128)(2,1)S(1)}, u32[]{:S(2)}, u32[]{:S(2)}) %collective-permute-start.28) | collective-permute-done | bytes 262176 | tf_op jit(solution)/shard_map/ppermute | solution.py:868
  435.9 10.4 %collective-permute-done.25 = bf16[256,512]{1,0:T(8,128)(2,1)S(1)} collective-permute-done((bf16[256,512]{1,0:T(8,128)(2,1)S(1)}, bf16[256,512]{1,0:T(8,128)(2,1)S(1)}, u32[]{:S(2)}, u32[]{:S(2)}) %collective-permute-start.25) | collective-permute-done | bytes 262176 | tf_op jit(solution)/shard_map/ppermute | solution.py:868
  446.3 5.0 collective-permute-done.26
  452.9 5.3 fusion.42
  458.1 3.0 collective-permute-done.36
  461.1 2.0 collective-permute-start.22
  463.2 2.2 collective-permute-start.23
  472.0 3.3 collective-permute-done.32
  477.5 4.1 fusion.4
  481.7 2.7 add_add_fusion.1
  485.1 3.2 fusion.7
  488.4 16.2 %collective-permute-done.15 = bf16[1024,384]{0,1:T(8,128)(2,1)S(1)} collective-permute-done((bf16[1024,384]{0,1:T(8,128)(2,1)S(1)}, bf16[1024,384]{0,1:T(8,128)(2,1)S(1)}, u32[]{:S(2)}, u32[]{:S(2)}) %collective-permute-start.15) | collective-permute-done | bytes 786464 | tf_op jit(solution)/shard_map/ppermute | solution.py:322
  507.0 3.4 collective-permute-start.17
  510.4 6.0 %collective-permute-done.11 = bf16[512,1280]{1,0:T(8,128)(2,1)S(1)} collective-permute-done((bf16[512,1280]{1,0:T(8,128)(2,1)S(1)}, bf16[512,1280]{1,0:T(8,128)(2,1)S(1)}, u32[]{:S(2)}, u32[]{:S(2)}) %collective-permute-start.11) | collective-permute-done | bytes 1310752 | tf_op jit(solution)/shard_map/ppermute | solution.py:322
  516.4 3.2 collective-permute-start.18
  519.6 10.4 %add_bitcast_fusion = (f32[1,1280,1024]{2,1,0:T(8,128)}, bf16[1,1280,1024]{2,1,0:T(8,128)(2,1)}) fusion(f32[1280]{0:T(1024)S(1)} %negate_multiply_fusion, bf16[1,1280,1024]{2,1,0:T(8,128)(2,1)S(1)} %copy-done.11, f32[1280]{0:T(1024)S(1)} %get-tuple-element.127, f32[1280]{0:T(1024)S(1)} %broadcast_multiply_fusion, bf16[1,1280,1024]{2,1,0:T(8,128)(2,1)S(1)} %copy-done.10, ...), kind=kOutput, calls=%fused_computation.13 | convolution fusion | flops 1363148800 | bytes 33841152 | tf_op jit(solution)/shard_map/ft,fd->td/dot_general | solution.py:308
  534.2 9.3 %shard_map.357 = f32[24,128]{1,0:T(8,128)} custom-call(f32[24,128]{1,0:T(8,128)} %maximum_maximum_fusion.term_ref), custom_call_target="tpu_custom_call" | custom-call | tf_op jit(solution)/shard_map/pallas_call | solution.py:810
  549.3 5.9 %fusion.46 = (bf16[2048,256]{1,0:T(8,128)(2,1)}, f32[2048,256]{1,0:T(8,128)}, f32[2048,256]{1,0:T(8,128)}, f32[2048,256]{1,0:T(8,128)}) fusion(f32[2048,256]{1,0:T(8,128)S(1)} %copy-done.3, f32[1024,256]{1,0:T(8,128)} %maximum_select_fusion.4, f32[1024,256]{1,0:T(8,128)} %collective-permute-done.37, pred[]{:T(512)S(6)} %eq.6, f32[]{:T(128)S(6)} %div.128, ...), kind=kLoop, calls=%fused_computation.138 | loop fusion | flops 10485760 | bytes 15728645 | tf_op jit(solution)/shard_map/convert_element_type | solution.py:304
  557.2 2.8 fusion.50
  560.3 5.7 fusion.48
  567.4 3.3 fusion.52
  (206 shorter events, 55.0 us)
Async XLA Ops:
  7.2 196.1 %all-gather.2.cloned.1.call-start = ((), (), s32[]{:S(2)}) async-start(), calls=%async_computation | async-start | bytes 1966080 | tf_op jit(solution)/shard_map/all_gather | solution.py:835
  13.5 74.0 %copy-start.34 = (s32[1,12]{1,0:T(1,128)S(1)}, s32[1,12]{1,0:T(1,128)}, u32[]{:S(2)}) copy-start(s32[1,12]{1,0:T(1,128)} %param.20) | copy-start | bytes 148
  83.0 57.9 %collective-permute-start = (bf16[1280,1024]{1,0:T(8,128)(2,1)}, bf16[1280,1024]{1,0:T(8,128)(2,1)S(1)}, u32[]{:S(2)}, u32[]{:S(2)}) collective-permute-start(bf16[1280,1024]{1,0:T(8,128)(2,1)} %get-tuple-element.47.hidden_ref), channel_id=1, source_target_pairs={{0,16},{16,0},{1,17},{17,1},{2,18},{18,2},{3,19},{19,3},{4,20},{20... | collective-permute-start | bytes 7864328 | tf_op jit(solution)/shard_map/ppermute | solution.py:322
  83.6 115.4 %collective-permute-start.3 = (bf16[256,256]{1,0:T(8,128)(2,1)S(1)}, bf16[256,256]{1,0:T(8,128)(2,1)}, u32[]{:S(2)}, u32[]{:S(2)}) collective-permute-start(bf16[256,256]{1,0:T(8,128)(2,1)S(1)} %get-tuple-element.56), channel_id=1, source_target_pairs={{0,4},{4,8},{8,12},{12,0},{1,5},{5,9},{9,13},{13,1},{2,6},{6,10},{... | collective-permute-start | bytes 393224 | tf_op jit(solution)/shard_map/ppermute | solution.py:845
  84.2 116.4 %collective-permute-start.4 = (bf16[256,256]{1,0:T(8,128)(2,1)S(1)}, bf16[256,256]{1,0:T(8,128)(2,1)}, u32[]{:S(2)}, u32[]{:S(2)}) collective-permute-start(bf16[256,256]{1,0:T(8,128)(2,1)S(1)} %get-tuple-element.56), channel_id=1, source_target_pairs={{0,8},{4,12},{8,0},{12,4},{1,9},{5,13},{9,1},{13,5},{2,10},{6,14},... | collective-permute-start | bytes 393224 | tf_op jit(solution)/shard_map/ppermute | solution.py:845
  85.7 116.4 %collective-permute-start.5 = (bf16[256,256]{1,0:T(8,128)(2,1)S(1)}, bf16[256,256]{1,0:T(8,128)(2,1)S(1)}, u32[]{:S(2)}, u32[]{:S(2)}) collective-permute-start(bf16[256,256]{1,0:T(8,128)(2,1)S(1)} %get-tuple-element.56), channel_id=1, source_target_pairs={{0,12},{4,0},{8,4},{12,8},{1,13},{5,1},{9,5},{13,9},{2,14},{6,2},{... | collective-permute-start | bytes 393224 | tf_op jit(solution)/shard_map/ppermute | solution.py:845
  87.8 46.5 %copy-start.9 = (bf16[1,1280,1024]{2,1,0:T(8,128)(2,1)S(1)}, bf16[1,1280,1024]{2,1,0:T(8,128)(2,1)}, u32[]{:S(2)}) copy-start(bf16[1,1280,1024]{2,1,0:T(8,128)(2,1)} %param.18) | copy-start | bytes 7864324
  194.5 33.8 %collective-permute-start.7 = (f32[1024,1024]{1,0:T(8,128)}, f32[1024,1024]{1,0:T(8,128)}, u32[]{:S(2)}, u32[]{:S(2)}) collective-permute-start(f32[1024,1024]{1,0:T(8,128)} %slice.53), channel_id=1, source_target_pairs={{0,1},{1,0},{2,3},{3,2},{4,5},{5,4},{6,7},{7,6},{8,9},{9,8},{10,11... | collective-permute-start | bytes 12582920 | tf_op jit(solution)/shard_map/ppermute | solution.py:322
  197.9 37.1 %collective-permute-start.8 = (f32[1024,1024]{1,0:T(8,128)}, f32[1024,1024]{1,0:T(8,128)}, u32[]{:S(2)}, u32[]{:S(2)}) collective-permute-start(f32[1024,1024]{1,0:T(8,128)} %slice.55), channel_id=1, source_target_pairs={{0,1},{1,0},{2,3},{3,2},{4,5},{5,4},{6,7},{7,6},{8,9},{9,8},{10,11... | collective-permute-start | bytes 12582920 | tf_op jit(solution)/shard_map/ppermute | solution.py:322
  202.8 6.7 %collective-permute-start.6 = (bf16[256,1024]{1,0:T(8,128)(2,1)}, bf16[256,1024]{1,0:T(8,128)(2,1)}, u32[]{:S(2)}, u32[]{:S(2)}) collective-permute-start(bf16[256,1024]{1,0:T(8,128)(2,1)} %constant_dynamic-update-slice_fusion), channel_id=1, source_target_pairs={{0,1},{1,0},{2,3},{3,2},{4,5},{5,4},{6,7},{7,6},{8,9},{9,8},{10,11... | collective-permute-start | bytes 1572872 | tf_op jit(solution)/shard_map/ppermute | solution.py:322
  203.3 14.9 %collective-permute-start.2 = (bf16[1024,768]{1,0:T(8,128)(2,1)}, bf16[1024,768]{1,0:T(8,128)(2,1)S(1)}, u32[]{:S(2)}, u32[]{:S(2)}) collective-permute-start(bf16[1024,768]{1,0:T(8,128)(2,1)} %all-gather.2.cloned.1.call-done), channel_id=1, source_target_pairs={{0,1},{1,0},{2,3},{3,2},{4,5},{5,4},{6,7},{7,6},{8,9},{9,8},{10,11... | collective-permute-start | bytes 4718600 | tf_op jit(solution)/shard_map/ppermute | solution.py:322
  217.6 161.0 %collective-permute-start.1 = (bf16[1280,1024]{1,0:T(8,128)(2,1)}, bf16[1280,1024]{1,0:T(8,128)(2,1)}, u32[]{:S(2)}, u32[]{:S(2)}) collective-permute-start(bf16[1280,1024]{1,0:T(8,128)(2,1)} %get-tuple-element.54), channel_id=1, source_target_pairs={{0,16},{16,0},{1,17},{17,1},{2,18},{18,2},{3,19},{19,3},{4,20},{20... | collective-permute-start | bytes 7864328 | tf_op jit(solution)/shard_map/ppermute | solution.py:322
  218.2 16.7 %slice-start = ((s8[8388608]{0:T(1024)(128)(4,1)}), s8[4194304]{0:T(1024)(128)(4,1)S(1)}, s32[]{:S(2)}) async-start(s8[8388608]{0:T(1024)(128)(4,1)} %bitcast.60), calls=%async_computation.1 | async-start | bytes 8388608
  218.4 16.6 %slice-start.1 = ((s8[8388608]{0:T(1024)(128)(4,1)}), s8[4194304]{0:T(1024)(128)(4,1)S(1)}, s32[]{:S(2)}) async-start(s8[8388608]{0:T(1024)(128)(4,1)} %bitcast.60), calls=%async_computation.2 | async-start | bytes 8388608
  233.4 26.2 %collective-permute-start.9 = (bf16[512,1024]{1,0:T(8,128)(2,1)S(1)}, bf16[512,1024]{1,0:T(8,128)(2,1)}, u32[]{:S(2)}, u32[]{:S(2)}) collective-permute-start(bf16[512,1024]{1,0:T(8,128)(2,1)S(1)} %dynamic-slice_convert_fusion.1), channel_id=1, source_target_pairs={{0,2},{1,3},{2,0},{3,1},{4,6},{5,7},{6,4},{7,5},{8,10},{9,11},{10,... | collective-permute-start | bytes 3145736 | tf_op jit(solution)/shard_map/ppermute | solution.py:322
  238.3 42.5 %collective-permute-start.10 = (bf16[1024,512]{1,0:T(8,128)(2,1)S(1)}, bf16[1024,512]{1,0:T(8,128)(2,1)S(1)}, u32[]{:S(2)}, u32[]{:S(2)}) collective-permute-start(bf16[1024,512]{1,0:T(8,128)(2,1)S(1)} %dynamic-slice_convert_fusion), channel_id=1, source_target_pairs={{0,2},{1,3},{2,0},{3,1},{4,6},{5,7},{6,4},{7,5},{8,10},{9,11},{10,... | collective-permute-start | bytes 3145736 | tf_op jit(solution)/shard_map/ppermute | solution.py:322
  282.7 103.5 %slice-start.2 = ((s8[5242880]{0:T(1024)(128)(4,1)}), s8[1048576]{0:T(1024)(128)(4,1)S(1)}, s32[]{:S(2)}) async-start(s8[5242880]{0:T(1024)(128)(4,1)} %bitcast.63), calls=%async_computation.3 | async-start | bytes 2097152
  402.0 74.1 %collective-permute-start.13 = (bf16[1280,1024]{1,0:T(8,128)(2,1)}, bf16[1280,1024]{1,0:T(8,128)(2,1)S(1)}, u32[]{:S(2)}, u32[]{:S(2)}) collective-permute-start(bf16[1280,1024]{1,0:T(8,128)(2,1)} %add_convert_fusion), channel_id=1, source_target_pairs={{0,16},{16,0},{1,17},{17,1},{2,18},{18,2},{3,19},{19,3},{4,20},{20... | collective-permute-start | bytes 7864328 | tf_op jit(solution)/shard_map/ppermute | solution.py:322
  403.8 15.8 %collective-permute-start.27 = (bf16[512,256]{1,0:T(8,128)(2,1)S(1)}, bf16[512,256]{1,0:T(8,128)(2,1)S(1)}, u32[]{:S(2)}, u32[]{:S(2)}) collective-permute-start(bf16[512,256]{1,0:T(8,128)(2,1)S(1)} %get-tuple-element.111), channel_id=1, source_target_pairs={{0,4},{4,8},{8,12},{12,0},{1,5},{5,9},{9,13},{13,1},{2,6},{6,10},{... | collective-permute-start | bytes 786440 | tf_op jit(solution)/shard_map/ppermute | solution.py:868
  403.8 31.2 %collective-permute-start.28 = (bf16[512,256]{1,0:T(8,128)(2,1)S(1)}, bf16[512,256]{1,0:T(8,128)(2,1)S(1)}, u32[]{:S(2)}, u32[]{:S(2)}) collective-permute-start(bf16[512,256]{1,0:T(8,128)(2,1)S(1)} %get-tuple-element.113), channel_id=1, source_target_pairs={{0,8},{4,12},{8,0},{12,4},{1,9},{5,13},{9,1},{13,5},{2,10},{6,14},... | collective-permute-start | bytes 786440 | tf_op jit(solution)/shard_map/ppermute | solution.py:868
  403.9 31.1 %collective-permute-start.29 = (bf16[512,256]{1,0:T(8,128)(2,1)S(1)}, bf16[512,256]{1,0:T(8,128)(2,1)S(1)}, u32[]{:S(2)}, u32[]{:S(2)}) collective-permute-start(bf16[512,256]{1,0:T(8,128)(2,1)S(1)} %get-tuple-element.112), channel_id=1, source_target_pairs={{0,12},{4,0},{8,4},{12,8},{1,13},{5,1},{9,5},{13,9},{2,14},{6,2},{... | collective-permute-start | bytes 786440 | tf_op jit(solution)/shard_map/ppermute | solution.py:868
  409.4 10.8 %collective-permute-start.19 = (f32[256,1024]{1,0:T(8,128)S(1)}, f32[256,1024]{1,0:T(8,128)S(1)}, u32[]{:S(2)}, u32[]{:S(2)}) collective-permute-start(f32[256,1024]{1,0:T(8,128)S(1)} %convolution_add_fusion), channel_id=1, source_target_pairs={{0,1},{1,0},{2,3},{3,2},{4,5},{5,4},{6,7},{7,6},{8,9},{9,8},{10,11... | collective-permute-start | bytes 3145736 | tf_op jit(solution)/shard_map/ppermute | solution.py:322
  419.5 15.5 %collective-permute-start.24 = (bf16[256,512]{1,0:T(8,128)(2,1)S(1)}, bf16[256,512]{1,0:T(8,128)(2,1)S(1)}, u32[]{:S(2)}, u32[]{:S(2)}) collective-permute-start(bf16[256,512]{1,0:T(8,128)(2,1)S(1)} %get-tuple-element.114), channel_id=1, source_target_pairs={{0,4},{4,8},{8,12},{12,0},{1,5},{5,9},{9,13},{13,1},{2,6},{6,10},{... | collective-permute-start | bytes 786440 | tf_op jit(solution)/shard_map/ppermute | solution.py:868
  420.1 61.5 %collective-permute-start.14 = (f32[1024,768]{0,1:T(8,128)}, f32[1024,768]{0,1:T(8,128)}, u32[]{:S(2)}, u32[]{:S(2)}) collective-permute-start(f32[1024,768]{0,1:T(8,128)} %fusion.22), channel_id=1, source_target_pairs={{0,1},{1,0},{2,3},{3,2},{4,5},{5,4},{6,7},{7,6},{8,9},{9,8},{10,11... | collective-permute-start | bytes 9437192 | tf_op jit(solution)/shard_map/ppermute | solution.py:322
  435.0 11.3 %collective-permute-start.25 = (bf16[256,512]{1,0:T(8,128)(2,1)S(1)}, bf16[256,512]{1,0:T(8,128)(2,1)S(1)}, u32[]{:S(2)}, u32[]{:S(2)}) collective-permute-start(bf16[256,512]{1,0:T(8,128)(2,1)S(1)} %get-tuple-element.116), channel_id=1, source_target_pairs={{0,8},{4,12},{8,0},{12,4},{1,9},{5,13},{9,1},{13,5},{2,10},{6,14},... | collective-permute-start | bytes 786440 | tf_op jit(solution)/shard_map/ppermute | solution.py:868
  435.0 16.3 %collective-permute-start.26 = (bf16[256,512]{1,0:T(8,128)(2,1)S(1)}, bf16[256,512]{1,0:T(8,128)(2,1)S(1)}, u32[]{:S(2)}, u32[]{:S(2)}) collective-permute-start(bf16[256,512]{1,0:T(8,128)(2,1)S(1)} %get-tuple-element.115), channel_id=1, source_target_pairs={{0,12},{4,0},{8,4},{12,8},{1,13},{5,1},{9,5},{13,9},{2,14},{6,2},{... | collective-permute-start | bytes 786440 | tf_op jit(solution)/shard_map/ppermute | solution.py:868
  435.1 17.0 %collective-permute-start.20 = (bf16[128,1024]{1,0:T(8,128)(2,1)S(1)}, bf16[128,1024]{1,0:T(8,128)(2,1)S(1)}, u32[]{:S(2)}, u32[]{:S(2)}) collective-permute-start(bf16[128,1024]{1,0:T(8,128)(2,1)S(1)} %dynamic-slice_convert_fusion.9), channel_id=1, source_target_pairs={{0,2},{1,3},{2,0},{3,1},{4,6},{5,7},{6,4},{7,5},{8,10},{9,11},{10,... | collective-permute-start | bytes 786440 | tf_op jit(solution)/shard_map/ppermute | solution.py:322
  446.3 14.9 %collective-permute-start.36 = (f32[512,256]{1,0:T(8,128)S(1)}, f32[512,256]{1,0:T(8,128)S(1)}, u32[]{:S(2)}, u32[]{:S(2)}) collective-permute-start(f32[512,256]{1,0:T(8,128)S(1)} %get-tuple-element.97), channel_id=1, source_target_pairs={{0,2},{1,3},{2,0},{3,1},{4,6},{5,7},{6,4},{7,5},{8,10},{9,11},{10,... | collective-permute-start | bytes 1572872 | tf_op jit(solution)/shard_map/ppermute | solution.py:322
  452.0 18.3 %collective-permute-start.34 = (f32[256,512]{1,0:T(8,128)S(1)}, f32[256,512]{1,0:T(8,128)S(1)}, u32[]{:S(2)}, u32[]{:S(2)}) collective-permute-start(f32[256,512]{1,0:T(8,128)S(1)} %get-tuple-element.101), channel_id=1, source_target_pairs={{0,2},{1,3},{2,0},{3,1},{4,6},{5,7},{6,4},{7,5},{8,10},{9,11},{10,... | collective-permute-start | bytes 1572872 | tf_op jit(solution)/shard_map/ppermute | solution.py:322
  452.2 25.3 %slice-start.4 = ((s8[5242880]{0:T(1024)(128)(4,1)}), s8[4194304]{0:T(1024)(128)(4,1)S(1)}, s32[]{:S(2)}) async-start(s8[5242880]{0:T(1024)(128)(4,1)} %bitcast.65), calls=%async_computation.5 | async-start | bytes 8388608
  452.2 25.3 %slice-start.5 = ((s8[5242880]{0:T(1024)(128)(4,1)}), s8[1048576]{0:T(1024)(128)(4,1)S(1)}, s32[]{:S(2)}) async-start(s8[5242880]{0:T(1024)(128)(4,1)} %bitcast.65), calls=%async_computation.6 | async-start | bytes 2097152
  452.2 11.0 %collective-permute-start.21 = (bf16[128,256]{1,0:T(8,128)(2,1)S(1)}, bf16[128,256]{1,0:T(8,128)(2,1)S(1)}, u32[]{:S(2)}, u32[]{:S(2)}) collective-permute-start(bf16[128,256]{1,0:T(8,128)(2,1)S(1)} %get-tuple-element.120), channel_id=1, source_target_pairs={{0,4},{4,8},{8,12},{12,0},{1,5},{5,9},{9,13},{13,1},{2,6},{6,10},{... | collective-permute-start | bytes 196616 | tf_op jit(solution)/shard_map/ppermute | solution.py:868
  458.1 19.4 %copy-start.10 = (bf16[1,1280,1024]{2,1,0:T(8,128)(2,1)S(1)}, bf16[1,1280,1024]{2,1,0:T(8,128)(2,1)}, u32[]{:S(2)}) copy-start(bf16[1,1280,1024]{2,1,0:T(8,128)(2,1)} %param.18) | copy-start | bytes 7864324
  461.1 5.3 collective-permute-start.22
  463.2 5.0 collective-permute-start.23
  466.5 40.6 %collective-permute-start.12 = (bf16[512,1024]{1,0:T(8,128)(2,1)S(1)}, bf16[512,1024]{1,0:T(8,128)(2,1)S(1)}, u32[]{:S(2)}, u32[]{:S(2)}) collective-permute-start(bf16[512,1024]{1,0:T(8,128)(2,1)S(1)} %copy-done.29), channel_id=1, source_target_pairs={{0,16},{16,0},{1,17},{17,1},{2,18},{18,2},{3,19},{19,3},{4,20},{20... | collective-permute-start | bytes 3145736 | tf_op jit(solution)/shard_map/ppermute | solution.py:322
  468.2 48.2 %collective-permute-start.11 = (bf16[512,1280]{1,0:T(8,128)(2,1)S(1)}, bf16[512,1280]{1,0:T(8,128)(2,1)S(1)}, u32[]{:S(2)}, u32[]{:S(2)}) collective-permute-start(bf16[512,1280]{1,0:T(8,128)(2,1)S(1)} %get-tuple-element.65), channel_id=1, source_target_pairs={{0,16},{16,0},{1,17},{17,1},{2,18},{18,2},{3,19},{19,3},{4,20},{20... | collective-permute-start | bytes 3932168 | tf_op jit(solution)/shard_map/ppermute | solution.py:322
  470.3 5.0 collective-permute-start.32
  475.3 74.0 %collective-permute-start.37 = (f32[1024,256]{1,0:T(8,128)}, f32[1024,256]{1,0:T(8,128)}, u32[]{:S(2)}, u32[]{:S(2)}) collective-permute-start(f32[1024,256]{1,0:T(8,128)} %maximum_select_fusion.4), channel_id=1, source_target_pairs={{0,1},{1,0},{2,3},{3,2},{4,5},{5,4},{6,7},{7,6},{8,9},{9,8},{10,11... | collective-permute-start | bytes 3145736 | tf_op jit(solution)/shard_map/ppermute | solution.py:322
  476.0 84.2 %collective-permute-start.35 = (f32[256,1024]{1,0:T(8,128)}, f32[256,1024]{1,0:T(8,128)}, u32[]{:S(2)}, u32[]{:S(2)}) collective-permute-start(f32[256,1024]{1,0:T(8,128)} %maximum_select_fusion.3), channel_id=1, source_target_pairs={{0,1},{1,0},{2,3},{3,2},{4,5},{5,4},{6,7},{7,6},{8,9},{9,8},{10,11... | collective-permute-start | bytes 3145736 | tf_op jit(solution)/shard_map/ppermute | solution.py:322
  484.6 20.0 %collective-permute-start.15 = (bf16[1024,384]{0,1:T(8,128)(2,1)S(1)}, bf16[1024,384]{0,1:T(8,128)(2,1)S(1)}, u32[]{:S(2)}, u32[]{:S(2)}) collective-permute-start(bf16[1024,384]{0,1:T(8,128)(2,1)S(1)} %dynamic-slice_convert_fusion.2), channel_id=1, source_target_pairs={{0,2},{1,3},{2,0},{3,1},{4,6},{5,7},{6,4},{7,5},{8,10},{9,11},{10,... | collective-permute-start | bytes 2359304 | tf_op jit(solution)/shard_map/ppermute | solution.py:322
  505.0 25.0 %collective-permute-start.16 = (bf16[256,384]{0,1:T(8,128)(2,1)S(1)}, bf16[256,384]{0,1:T(8,128)(2,1)S(1)}, u32[]{:S(2)}, u32[]{:S(2)}) collective-permute-start(bf16[256,384]{0,1:T(8,128)(2,1)S(1)} %get-tuple-element.117), channel_id=1, source_target_pairs={{0,4},{4,8},{8,12},{12,0},{1,5},{5,9},{9,13},{13,1},{2,6},{6,10},{... | collective-permute-start | bytes 589832 | tf_op jit(solution)/shard_map/ppermute | solution.py:868
  507.0 23.1 %collective-permute-start.17 = (bf16[256,384]{0,1:T(8,128)(2,1)S(1)}, bf16[256,384]{0,1:T(8,128)(2,1)S(1)}, u32[]{:S(2)}, u32[]{:S(2)}) collective-permute-start(bf16[256,384]{0,1:T(8,128)(2,1)S(1)} %get-tuple-element.119), channel_id=1, source_target_pairs={{0,8},{4,12},{8,0},{12,4},{1,9},{5,13},{9,1},{13,5},{2,10},{6,14},... | collective-permute-start | bytes 589832 | tf_op jit(solution)/shard_map/ppermute | solution.py:868
  516.4 13.8 %collective-permute-start.18 = (bf16[256,384]{0,1:T(8,128)(2,1)S(1)}, bf16[256,384]{0,1:T(8,128)(2,1)S(1)}, u32[]{:S(2)}, u32[]{:S(2)}) collective-permute-start(bf16[256,384]{0,1:T(8,128)(2,1)S(1)} %get-tuple-element.118), channel_id=1, source_target_pairs={{0,12},{4,0},{8,4},{12,8},{1,13},{5,1},{9,5},{13,9},{2,14},{6,2},{... | collective-permute-start | bytes 589832 | tf_op jit(solution)/shard_map/ppermute | solution.py:868
  519.6 29.7 %copy-start.3 = (f32[2048,256]{1,0:T(8,128)S(1)}, f32[2048,256]{1,0:T(8,128)}, u32[]{:S(2)}) copy-start(f32[2048,256]{1,0:T(8,128)} %shrink_ref.1) | copy-start | bytes 6291460
  530.0 25.8 %collective-permute-start.33 = (f32[256,256]{1,0:T(8,128)}, f32[256,256]{1,0:T(8,128)}, u32[]{:S(2)}, u32[]{:S(2)}) collective-permute-start(f32[256,256]{1,0:T(8,128)} %maximum_select_fusion.8), channel_id=1, source_target_pairs={{0,1},{1,0},{2,3},{3,2},{4,5},{5,4},{6,7},{7,6},{8,9},{9,8},{10,11... | collective-permute-start | bytes 786440 | tf_op jit(solution)/shard_map/ppermute | solution.py:322
  547.5 12.5 %collective-permute-start.30 = (f32[256,384]{0,1:T(8,128)S(1)}, f32[256,384]{0,1:T(8,128)S(1)}, u32[]{:S(2)}, u32[]{:S(2)}) collective-permute-start(f32[256,384]{0,1:T(8,128)S(1)} %get-tuple-element.107), channel_id=1, source_target_pairs={{0,2},{1,3},{2,0},{3,1},{4,6},{5,7},{6,4},{7,5},{8,10},{9,11},{10,... | collective-permute-start | bytes 1179656 | tf_op jit(solution)/shard_map/ppermute | solution.py:322
  560.1 5.9 %collective-permute-start.31 = (f32[256,768]{0,1:T(8,128)S(1)}, f32[256,768]{0,1:T(8,128)S(1)}, u32[]{:S(2)}, u32[]{:S(2)}) collective-permute-start(f32[256,768]{0,1:T(8,128)S(1)} %maximum_select_fusion.6), channel_id=1, source_target_pairs={{0,1},{1,0},{2,3},{3,2},{4,5},{5,4},{6,7},{7,6},{8,9},{9,8},{10,11... | collective-permute-start | bytes 2359304 | tf_op jit(solution)/shard_map/ppermute | solution.py:322
  (34 other events, 162.4 us)
Sparse Core Ops, SparseCore 0:
  83.7 39.2 all-gather.1

commit v5 on v4

--- a/solution.py
+++ b/solution.py
@@ -587,14 +587,11 @@
     for w in range(2):
         for copy in own_copies(w):
             copy.start()
-    heads = project_ref.shape[1] // 2
-    units = mixing_ref.shape[0] // 2
-    project_out[...] = project_ref[
-        :, pl.ds(pl.multiple_of(near * heads, heads), heads)
-    ].astype(jnp.bfloat16)
-    mixing_out[...] = mixing_ref[
-        pl.ds(pl.multiple_of(near * units, units), units), :
-    ].astype(jnp.bfloat16)
+    for source, target in ((project_ref, project_out), (mixing_ref, mixing_out)):
+        units = target.shape[0]
+        target[...] = source[pl.ds(pl.multiple_of(near * units, units), units), :].astype(
+            jnp.bfloat16
+        )
     norm_all[0] = norm_low[...]
     for copy in norm_copies:
         copy.wait()
@@ -726,7 +723,7 @@
         out_shape=[
             jax.ShapeDtypeStruct((2, rows * deep, units // 2), low),
             jax.ShapeDtypeStruct((2, units // 2, rows * deep), low),
-            jax.ShapeDtypeStruct((project.shape[0], project.shape[1] // 2), low),
+            jax.ShapeDtypeStruct((project.shape[0] // 2, project.shape[1]), low),
             jax.ShapeDtypeStruct((mixing.shape[0] // 2, mixing.shape[1]), low),
             jax.ShapeDtypeStruct((8, rows * deep), jnp.float32),
             jax.ShapeDtypeStruct(inputs.shape, low),
@@ -755,6 +752,331 @@
     )(expand, shrink, project, mixing, norm, inputs, back)
 
 
+def closing_kernel(
+    later,
+    project_hbm,
+    *refs,
+):
+    sources = (project_hbm, *refs[:9])
+    part_own, part_other, gain_ref = refs[9:12]
+    input_grad, norm_grad, project_share, mixing_share = refs[12 + later : 16 + later]
+    refs = refs[16 + later :]
+    held = refs[:10]
+    (
+        part_in,
+        total_ref,
+        sent_ref,
+        come_ref,
+        out_ref,
+        project_sib,
+        project_land,
+        project_own,
+        mixing_sib,
+        mixing_land,
+        mixing_own,
+        project_far,
+        project_come,
+        mixing_far,
+        mixing_come,
+        project_line,
+        project_lands,
+        mixing_line,
+        mixing_lands,
+        held_sem,
+        part_sem,
+        out_sem,
+        row_send,
+        row_recv,
+        near_send,
+        near_recv,
+        far_send,
+        far_recv,
+        line_send,
+        line_recv,
+    ) = refs[10:]
+    (
+        project,
+        grads_other,
+        grads_own,
+        hidden_other,
+        hidden_own,
+        mixed_other,
+        mixed_own,
+        back_other,
+        back_own,
+        inputs,
+    ) = held
+    low, f32 = jnp.bfloat16, jnp.float32
+    tn = (((0,), (0,)), ((), ()))
+    place, deep = lax.axis_index("dp"), 4
+    outer = lax.axis_index("outer")
+    far, near = outer // 2, outer % 2
+    row_id = {"mp": 1 - lax.axis_index("mp")}
+    far_id = {"outer": (outer + 2) % 4}
+    near_id = {"outer": outer + 1 - 2 * near}
+
+    copies = [
+        pltpu.make_async_copy(source, target, held_sem.at[n])
+        for n, (source, target) in enumerate(zip(sources, held))
+    ]
+    for copy in copies:
+        copy.start()
+    barrier = pltpu.get_barrier_semaphore()
+    for device in (row_id, far_id, near_id):
+        pl.semaphore_signal(barrier, inc=1, device_id=device, device_id_type=MESH)
+    for step in range(1, deep):
+        pl.semaphore_signal(
+            barrier, inc=1, device_id={"dp": (place + step) % deep}, device_id_type=MESH
+        )
+    height = 256
+    tokens, width = hidden_own.shape
+    blocks = tokens // height
+    at = [slice(n * height, (n + 1) * height) for n in range(blocks)]
+
+    def remote(source, target, send, recv, device):
+        return pltpu.make_async_remote_copy(
+            src_ref=source,
+            dst_ref=target,
+            send_sem=send,
+            recv_sem=recv,
+            device_id=device,
+            device_id_type=MESH,
+        )
+
+    loads = [
+        pltpu.make_async_copy(source.at[at[n]], part_in.at[(k * blocks + n) % 2], part_sem.at[(k * blocks + n) % 2])
+        for k, source in enumerate((part_other, part_own))
+        for n in range(blocks)
+    ]
+    loads[0].start()
+    loads[1].start()
+
+    copies[0].wait()
+    copies[1].wait()
+    pl.semaphore_wait(barrier, deep + 2)
+    row_copies = []
+    for n in range(blocks):
+        made = lax.dot_general(grads_other[:, at[n]], project[...], tn, preferred_element_type=f32)
+        loads[n].wait()
+        sent_ref[at[n], :] = (part_in[n % 2] + made).astype(low)
+        loads[n + 2].start()
+        copy = remote(
+            sent_ref.at[at[n]], come_ref.at[at[n]], row_send.at[n], row_recv.at[n], row_id
+        )
+        copy.start()
+        row_copies.append(copy)
+
+    for n in range(2, 9):
+        copies[n].wait()
+    half = project_own.shape[0]
+    few = mixing_own.shape[0]
+    near_copies = []
+    for n in range(half // height):
+        rows = slice(half + n * height, half + (n + 1) * height)
+        project_sib[at[n], :] = jnp.dot(
+            grads_own[rows, :], hidden_own[...], preferred_element_type=f32
+        ) + jnp.dot(grads_other[rows, :], hidden_other[...], preferred_element_type=f32)
+        near_copies.append(
+            remote(
+                project_sib.at[at[n]],
+                project_land.at[at[n]],
+                near_send.at[n],
+                near_recv.at[n],
+                near_id,
+            )
+        )
+        near_copies[-1].start()
+    mixing_sib[...] = jnp.dot(
+        mixed_own[few:, :], back_own[...], preferred_element_type=f32
+    ) + jnp.dot(mixed_other[few:, :], back_other[...], preferred_element_type=f32)
+    near_copies.append(
+        remote(mixing_sib, mixing_land, near_send.at[3], near_recv.at[3], near_id)
+    )
+    near_copies[-1].start()
+    for n in range(half // height):
+        made = jnp.dot(
+            grads_own[at[n], :], hidden_own[...], preferred_element_type=f32
+        ) + jnp.dot(grads_other[at[n], :], hidden_other[...], preferred_element_type=f32)
+        near_copies[n].wait()
+        project_own[at[n], :] = made + project_land[at[n], :]
+
+    def to_far(own, send, come, n):
+        size = send.shape[0]
+        send[...] = own[pl.ds(pl.multiple_of((1 - far) * size, size), size), :].astype(low)
+        copy = remote(send, come, far_send.at[n], far_recv.at[n], far_id)
+        copy.start()
+        return copy
+
+    far_copies = [to_far(project_own, project_far, project_come, 0)]
+    made = jnp.dot(mixed_own[:few, :], back_own[...], preferred_element_type=f32) + jnp.dot(
+        mixed_other[:few, :], back_other[...], preferred_element_type=f32
+    )
+    near_copies[3].wait()
+    mixing_own[...] = made + mixing_land[...]
+    far_copies.append(to_far(mixing_own, mixing_far, mixing_come, 1))
+
+    for n in range(blocks):
+        made = lax.dot_general(grads_own[:, at[n]], project[...], tn, preferred_element_type=f32)
+        loads[blocks + n].wait()
+        total_ref[at[n], :] = part_in[(blocks + n) % 2] + made
+        if n + 2 < blocks:
+            loads[blocks + n + 2].start()
+
+    line_copies = []
+    for k, (own, come, line, lands) in enumerate(
+        (
+            (project_own, project_come, project_line, project_lands),
+            (mixing_own, mixing_come, mixing_line, mixing_lands),
+        )
+    ):
+        size = come.shape[0]
+        keep = pl.ds(pl.multiple_of(far * size, size), size)
+        far_copies[k].wait()
+        own[keep, :] = own[keep, :] + come[...].astype(f32)
+        piece = width // deep
+        for step in range(1, deep):
+            target = (place + step) % deep
+            line[step] = own[keep, pl.ds(pl.multiple_of(target * piece, piece), piece)].astype(low)
+            copy = remote(
+                line.at[step],
+                lands.at[step],
+                line_send.at[k, step],
+                line_recv.at[k, step],
+                {"dp": target},
+            )
+            copy.start()
+            line_copies.append(copy)
+
+    copies[9].wait()
+    gain = gain_ref[0:1]
+    gain_sum = jnp.zeros((1, width), f32)
+    bias_sum = jnp.zeros((1, width), f32)
+    out_copies = []
+    for n in range(blocks):
+        row_copies[n].wait()
+        if n >= 2:
+            out_copies[n - 2].wait()
+
+        def some(i, carry):
+            gain_sum, bias_sum = carry
+            small = 64
+            rows = pl.ds(pl.multiple_of(n * height + i * small, small), small)
+            x = inputs[rows, :].astype(f32)
+            mean = jnp.mean(x, axis=1, keepdims=True)
+            centred = x - mean
+            spread = jnp.mean(centred * centred, axis=1, keepdims=True)
+            inverse = lax.rsqrt(spread + norm_epsilon)
+            normed = centred * inverse
+            grad = total_ref[rows, :] + come_ref[rows, :].astype(f32)
+            scaled = grad * gain
+            middle = jnp.mean(scaled, axis=1, keepdims=True)
+            along = jnp.mean(scaled * normed, axis=1, keepdims=True)
+            result = inverse * (scaled - middle - normed * along)
+            out_ref[n % 2, pl.ds(pl.multiple_of(i * small, small), small), :] = (
+                back_own[rows, :].astype(f32) + result
+            )
+            gain_sum = gain_sum + jnp.sum(grad * normed, axis=0, keepdims=True)
+            bias_sum = bias_sum + jnp.sum(grad, axis=0, keepdims=True)
+            return gain_sum, bias_sum
+
+        gain_sum, bias_sum = lax.fori_loop(0, height // 64, some, (gain_sum, bias_sum))
+        out_copies.append(
+            pltpu.make_async_copy(out_ref.at[n % 2], input_grad.at[at[n]], out_sem.at[n % 2])
+        )
+        out_copies[-1].start()
+    norm_grad[...] = jnp.zeros_like(norm_grad)
+    norm_grad[0:1] = gain_sum
+    norm_grad[1:2] = bias_sum
+    for copy in line_copies:
+        copy.wait()
+    for own, lands, share in (
+        (project_own, project_lands, project_share),
+        (mixing_own, mixing_lands, mixing_share),
+    ):
+        size, piece = share.shape
+        result = own[
+            pl.ds(pl.multiple_of(far * size, size), size),
+            pl.ds(pl.multiple_of(place * piece, piece), piece),
+        ]
+        for step in range(1, deep):
+            result = result + lands[step].astype(f32)
+        share[...] = result
+    for copy in out_copies[-2:]:
+        copy.wait()
+
+
+def closing(project, grads, hiddens, mixed, backs, inputs, parts, gain, after):
+    deep = 4
+    low, f32 = jnp.bfloat16, jnp.float32
+    tokens, width = inputs.shape
+    half, few = grads[0].shape[0] // 2, mixed[0].shape[0] // 2
+    piece = width // deep
+    anywhere = pl.BlockSpec(memory_space=pl.ANY)
+    here = lambda: pl.BlockSpec(memory_space=pltpu.VMEM)
+    held = (
+        project,
+        grads[1],
+        grads[0],
+        hiddens[1],
+        hiddens[0],
+        mixed[1],
+        mixed[0],
+        backs[1],
+        backs[0],
+        inputs,
+    )
+    sem = pltpu.SemaphoreType.DMA
+    space = pltpu.VMEM
+    return pl.pallas_call(
+        partial(closing_kernel, len(after)),
+        in_specs=[anywhere] * 12 + [here()] + [anywhere] * len(after),
+        out_specs=[anywhere, here(), here(), here()],
+        out_shape=[
+            jax.ShapeDtypeStruct((tokens, width), f32),
+            jax.ShapeDtypeStruct((8, width), f32),
+            jax.ShapeDtypeStruct((half // 2, piece), f32),
+            jax.ShapeDtypeStruct((few // 2, piece), f32),
+        ],
+        scratch_shapes=[space(v.shape, v.dtype) for v in held]
+        + [
+            space((2, 256, width), f32),
+            space((tokens, width), f32),
+            space((tokens, width), low),
+            space((tokens, width), low),
+            space((2, 256, width), f32),
+            space((half, width), f32),
+            space((half, width), f32),
+            space((half, width), f32),
+            space((few, width), f32),
+            space((few, width), f32),
+            space((few, width), f32),
+            space((half // 2, width), low),
+            space((half // 2, width), low),
+            space((few // 2, width), low),
+            space((few // 2, width), low),
+            space((deep, half // 2, piece), low),
+            space((deep, half // 2, piece), low),
+            space((deep, few // 2, piece), low),
+            space((deep, few // 2, piece), low),
+            sem((len(held),)),
+            sem((2,)),
+            sem((2,)),
+            sem((tokens // 256,)),
+            sem((tokens // 256,)),
+            sem((4,)),
+            sem((4,)),
+            sem((2,)),
+            sem((2,)),
+            sem((2, deep)),
+            sem((2, deep)),
+        ],
+        compiler_params=pltpu.CompilerParams(
+            collective_id=3, has_side_effects=True, vmem_limit_bytes=62 * 2**20
+        ),
+        cost_estimate=pl.CostEstimate(flops=2**20, bytes_accessed=2**20, transcendentals=0),
+    )(*held, *parts, gain, *after)
+
+
 def total_kernel(term_ref, out_ref, first, second, first_send, first_recv, second_send, second_recv):
     split, outers, deep = first.shape[0] // 4, 4, second.shape[0]
     plane = split * outers
@@ -852,7 +1174,8 @@
         half = own.shape[cut] // 2
         keep = lax.dynamic_slice_in_dim(own, self.far * half, half, cut)
         send = lax.dynamic_slice_in_dim(own, (1 - self.far) * half, half, cut)
-        return keep, swap(send.astype(jnp.bfloat16), "outer", 2)
+        send = send.astype(jnp.bfloat16)
+        return keep, swap(send, "outer", 2), send
 
     def line_sum(self, keep, come, depth):
         keep = keep + come.astype(jnp.float32)
@@ -906,10 +1229,10 @@
     )
     position = lax.axis_index("mp")
     count = width * split
-    project_flat = project_master.reshape(project_master.shape[0], heads_here * 3 * HD)
+    project_flat = project_master.transpose(1, 2, 0).reshape(heads_here * 3 * HD, -1)
     mixing_flat = mixing_master.reshape(heads_here * HD, mixing_master.shape[2])
     masters = (project_flat, mixing_flat, expand_master, shrink_master)
-    cuts, depths = (1, 0, 1, 0), (0, 1, 0, 1)
+    cuts, depths = (0, 0, 1, 0), (1, 1, 0, 1)
     rows_local = inputs[0].astype(jnp.float32)
     begins, places = layout(lengths[0], count)
     cosine, sine = turns(places)
@@ -926,10 +1249,8 @@
         )
         backs = [cotangent[0], other_back]
         shrink = shrink.reshape(-1, shrink.shape[2])
-        project = plan.gather(project, 1, 0)
+        project = plan.gather(project, 0, 1)
         mixing = plan.gather_few(mixing, 0, 1)
-        gain, bias = norm_weight[0], norm_weight[1]
-        norm_pull = jax.vjp(layer_norm, rows_local, gain, bias)[1]
         hiddens = [hidden_local, swap(hidden_local, "mp", 1)]
     else:
         norm_weight = lax.all_gather(norm_master.astype(jnp.bfloat16), "dp", axis=1, tiled=True)
@@ -947,19 +1268,6 @@
     def over_tokens(pattern, lefts, rights):
         return sum(product(pattern, left, right) for left, right in zip(lefts, rights))
 
-    def halves(pattern, lefts, rights, cut):
-        sources = rights if cut == 1 else lefts
-        axis = 0 if pattern.split(",")[cut].index("t") == 1 else 1
-        half = sources[0].shape[axis] // 2
-        out = []
-        for near in (1, 0):
-            chosen = [
-                lax.slice_in_dim(v, near * half, (near + 1) * half, axis=axis) for v in sources
-            ]
-            pair = (lefts, chosen) if cut == 1 else (chosen, rights)
-            out.append(over_tokens(pattern, *pair))
-        return out
-
     back_local = cotangent[0].astype(jnp.float32)
     if paired:
         *grads, hidden_own, branch_own = feed(
@@ -970,11 +1278,13 @@
         )
         hidden_parts = [hidden_own, hidden_other]
         half = expand_grad.shape[1] // 2
-        shrink_keep, shrink_come = plan.pair_sum(shrink_grad[:half], shrink_grad[half:], 0)
-        expand_keep, expand_come = plan.pair_sum(expand_grad[:, :half], expand_grad[:, half:], 1)
+        shrink_keep, shrink_come, shrink_sent = plan.pair_sum(shrink_grad[:half], shrink_grad[half:], 0)
+        expand_keep, expand_come, expand_sent = plan.pair_sum(
+            expand_grad[:, :half], expand_grad[:, half:], 1
+        )
         branch_come = swap(branch_other, "mp", 1)
         mixing_other = swap(mixing, "mp", 1)
-        projected = [product("td,de->et", hidden, project) for hidden in hiddens]
+        projected = [product("td,ed->et", hidden, project) for hidden in hiddens]
         mixed_backs = [product("td,fd->ft", back, mixing).astype(jnp.bfloat16) for back in backs]
         mixed, projected_grads = attend(
             projected,
@@ -983,25 +1293,23 @@
             cosine,
             sine,
             position,
-            (shrink_keep, expand_keep),
-        )
-        first_grad = follow(projected_grads[1], shrink_come, expand_come, branch_come)
-        sent = (hidden_parts[1] + product("et,de->td", first_grad, project)).astype(jnp.bfloat16)
-        hidden_come = swap(sent, "mp", 1)
-        projected_grads = [follow(v, sent) for v in projected_grads]
-        mixed = [follow(v, sent) for v in mixed]
-        mixed_come = swap(mixed[1], "mp", 1)
-        project_terms = halves("td,et->de", hiddens, projected_grads, 1)
-        project_sum = plan.line_sum(*plan.pair_sum(project_terms[1], project_terms[0], 1), 0)
-        mixing_terms = halves("ft,td->fd", mixed, backs, 0)
-        mixing_sum = plan.line_sum(*plan.pair_sum(mixing_terms[1], mixing_terms[0], 0), 1)
+            (shrink_sent, expand_sent),
+        )
+        input_grad, norm_terms, project_sum, mixing_sum = closing(
+            project,
+            projected_grads,
+            hiddens,
+            mixed,
+            backs,
+            inputs[0],
+            (hidden_own, hidden_other),
+            norm_weight,
+            (shrink_come, expand_come, branch_come),
+        )
+        norm_terms = norm_terms[:2]
+        mixed_come = swap(follow(mixed[1], norm_terms), "mp", 1)
         shrink_sum = plan.line_sum(shrink_keep, shrink_come, 1)
         expand_sum = plan.line_sum(expand_keep, expand_come, 0)
-        hidden_grad = (
-            hidden_parts[0]
-            + product("et,de->td", projected_grads[0], project)
-            + hidden_come.astype(jnp.float32)
-        )
         branch = (
             branch_own
             + branch_come.astype(jnp.float32)
@@ -1015,7 +1323,7 @@
         lifted_grads = [gelu_both(a, b) for a, b in zip(lifteds, active_grads)]
         hidden_parts = [product("tf,df->td", v, expand) for v in lifted_grads]
         branch_parts = [product("tf,fd->td", v, shrink) for v in activated]
-        projected = [product("td,de->et", hidden, project) for hidden in hiddens]
+        projected = [product("td,ed->et", hidden, project) for hidden in hiddens]
         mixed_backs = [product("td,fd->ft", back, mixing).astype(jnp.bfloat16) for back in backs]
         mixed, projected_grads = attend(projected, mixed_backs, begins, cosine, sine, position)
         project_sum, mixing_sum, expand_sum, shrink_sum = (
@@ -1029,7 +1337,7 @@
                 "outer",
             )
             for pattern, lefts, rights, depth in (
-                ("td,et->de", hiddens, projected_grads, 0),
+                ("et,td->ed", projected_grads, hiddens, 1),
                 ("ft,td->fd", mixed, backs, 1),
                 ("td,tf->df", hiddens, lifted_grads, 0),
                 ("tf,td->fd", activated, backs, 1),
@@ -1038,19 +1346,20 @@
         hidden_grad, branch = (
             lax.psum_scatter(v, "mp", scatter_dimension=0, tiled=True)
             for v in (
-                hidden_parts[0] + product("et,de->td", projected_grads[0], project),
+                hidden_parts[0] + product("et,ed->td", projected_grads[0], project),
                 branch_parts[0] + product("ft,fd->td", mixed[0], mixing),
             )
         )
-    rows_grad, gain_grad, bias_grad = norm_pull(hidden_grad)
-    input_grad = (back_local + rows_grad)[None]
+        rows_grad, gain_grad, bias_grad = norm_pull(hidden_grad)
+        input_grad = back_local + rows_grad
+        norm_terms = jnp.stack([gain_grad, bias_grad])
+    input_grad = input_grad[None]
     block_out = (rows_local + branch).astype(jnp.bfloat16)[None]
     sums = (project_sum, mixing_sum, expand_sum, shrink_sum)
     own_square = sum(jnp.sum(v * v) for v in sums)
     if not paired:
         own_square = own_square / lax.axis_size("outer")
-    norm_terms = jnp.concatenate([gain_grad, bias_grad, jnp.full((D,), own_square)])
-    norm_terms = norm_terms.reshape(-1, 128)
+    norm_terms = jnp.concatenate([norm_terms, jnp.full((1, D), own_square)]).reshape(-1, 128)
     if paired:
         norm_all = total_over_all(norm_terms, split, deep)
     else:
@@ -1062,12 +1371,9 @@
     norm_gradient = lax.dynamic_slice_in_dim(
         norm_full, lax.axis_index("dp") * (D // deep), D // deep, 1
     )
-    gradients = [
-        (plan.spread(v, cut) if paired else v).reshape(master.shape)
-        for v, cut, master in zip(
-            sums, cuts, (project_master, mixing_master, expand_master, shrink_master)
-        )
-    ]
+    gradients = [plan.spread(v, cut) if paired else v for v, cut in zip(sums, cuts)]
+    gradients[0] = gradients[0].reshape(heads_here, 3 * HD, -1).transpose(2, 0, 1)
+    gradients[1] = gradients[1].reshape(mixing_master.shape)
     states = (
         (project_master, project_first, project_second, D ** (-0.5)),
         (mixing_master, mixing_first, mixing_second, (D // 32) ** (-0.5)),

time: 586 us -> 539 us (0.920)
  Pallas kernels: 267 us -> 347 us
  waiting for transfers between devices: 100 us -> 21.1 us
  matrix products: 72.7 us -> 37 us
  other arithmetic: 57.9 us -> 42.6 us
    pallas_call x0 -> x1, Pallas kernels: none -> 78.1 us  [closing(): pl.pallas_call(partial(closing_kernel, len(after)), in_specs=[anywhere] *...]
    ppermute x23 -> x18, waiting for transfers between devices: 69.9 us -> 13.1 us  [swap(): return lax.ppermute(array, axis, [(i, i ^ bit) for i in range(size)])]
    dot_general x16 -> x6, matrix products: 72.7 us -> 37 us  [product(): return jnp.einsum(pattern, left, right, preferred_element_type=jnp.float32)]
    ppermute x12 -> x6, waiting for transfers between devices: 30.4 us -> 7.91 us  [line_sum(): lax.ppermute(part(target).astype(jnp.bfloat16), 'dp', pairs)]
    ppermute x23 -> x18, starting transfers between devices: 10.4 us -> 21.6 us  [swap(): return lax.ppermute(array, axis, [(i, i ^ bit) for i in range(size)])]
    ppermute x12 -> x6, starting transfers between devices: 18 us -> 7.34 us  [line_sum(): lax.ppermute(part(target).astype(jnp.bfloat16), 'dp', pairs)]
    pallas_call x1, Pallas kernels: 9.34 us -> 17.5 us  [total_over_all(): pl.pallas_call(total_kernel, in_specs=[pl.BlockSpec(memory_space=pltpu.VM...]
    reduce_sum x3 -> x0, other arithmetic: 7.74 us -> none  [the longest x1 4.14 us: layer_norm(): spread = jnp.mean(centred * centred, axis=1, keepdims=True)]
  transfers between devices with their start and end apart: 39 -> 28, of which waited for: 13 -> 6; matrix products, arithmetic and copies ran while one was open for 20% -> 17% of each run, Pallas kernels for 34% -> 53%
where the time goes in v5:
time: 539 us; the launch traced here: 531 us
  Pallas kernels  347 us (64%)
  other arithmetic  42.6 us (8%)
  matrix products  37 us (7%)
  starting transfers between devices  32.8 us (6%)
  local copies, waits for them, and re-layouts  30.7 us (6%)
  waiting for transfers between devices  21.1 us (4%)
  between operations  20.1 us (4%)
    pallas_call x2, Pallas kernels, feed(): pl.pallas_call(partial(feed_kernel, bool(before)), grid=(steps,), in_spec...  92.4 us
    pallas_call x1, Pallas kernels, attend(): pl.pallas_call(partial(attend_kernel, together, parts, len(after)), grid_...  91.9 us
    pallas_call x1, Pallas kernels, closing(): pl.pallas_call(partial(closing_kernel, len(after)), in_specs=[anywhere] *...  78.1 us
    pallas_call x1, Pallas kernels, opening(): pl.pallas_call(opening_kernel, in_specs=[here() for _ in range(6)] + [pl....  67.2 us
    dot_general x6, matrix products, product(): return jnp.einsum(pattern, left, right, preferred_element_type=jnp.float32)  37 us
    ppermute x18, starting transfers between devices, swap(): return lax.ppermute(array, axis, [(i, i ^ bit) for i in range(size)])  21.6 us
    pallas_call x1, Pallas kernels, total_over_all(): pl.pallas_call(total_kernel, in_specs=[pl.BlockSpec(memory_space=pltpu.VM...  17.5 us
    unnamed x104, local copies, waits for them, and re-layouts  16 us
  transfers between devices with their start and end apart: 28, of which 6 were waited for; matrix products, arithmetic and copies ran while one was open for 17% of the time, Pallas kernels for 53%

profile of v5, /device:TPU:0, one launch (start us, length us, event | category | flops | bytes accessed | tf_op | source)
XLA Modules:
  0.0 531.5 jit_solution(12254402794571155027)
XLA Ops:
  7.2 1.6 copy-done.4
  8.8 1.6 copy-done.6
  10.4 1.4 copy-done.8
  13.6 67.2 %shard_map.353 = (bf16[2,1024,1024]{2,1,0:T(8,128)(2,1)}, bf16[2,1024,1024]{2,1,0:T(8,128)(2,1)}, bf16[768,256]{1,0:T(8,128)(2,1)}, bf16[256,256]{1,0:T(8,128)(2...) custom-call(f32[256,2048]{1,0:T(8,128)S(1)} %copy-done.6, ...), custom_call_target="tpu_custom_call" | custom-call | bytes 1048576 | tf_op jit(solution)/shard_map/pallas_call | solution.py:717
  80.8 1.5 copy-done.2
  84.1 1.5 collective-permute-start.4
  85.6 1.7 collective-permute-start.5
  87.3 45.7 %shard_map.354 = (f32[1024,2048]{1,0:T(8,128)}, f32[2048,1024]{1,0:T(8,128)}, f32[1280,1024]{1,0:T(8,128)}, f32[1280,1024]{1,0:T(8,128)}) custom-call(bf16[1280,1024]{1,0:T(8,128)(2,1)} %copy-done, bf16[1280,1024]{1,0:T(8,128)(2,1)} %bitcast.33, bf16[2,1024,1024]{2,1,0:T(8,128)(2,1)} %get-tuple-element.47.expand_ref, bf16[2048,1024]{1,0:T(8,128)(2,1)} %bitcast.35), custom_call_target="tpu_custom_call" | custom-call | flops 1048576 | bytes 1048576 | tf_op jit(solution)/shard_map/pallas_call | solution.py:431
  133.0 7.7 %collective-permute-done.hidden_ref.refs_2_ = bf16[1280,1024]{1,0:T(8,128)(2,1)} collective-permute-done((bf16[1280,1024]{1,0:T(8,128)(2,1)S(1)}, bf16[1280,1024]{1,0:T(8,128)(2,1)}, u32[]{:S(2)}, u32[]{:S(2)}) %collective-permute-start) | collective-permute-done | bytes 2621472 | tf_op jit(solution)/shard_map/ppermute | solution.py:322
  140.7 46.7 %shard_map.355 = (f32[1024,2048]{1,0:T(8,128)}, f32[2048,1024]{1,0:T(8,128)}, f32[1280,1024]{1,0:T(8,128)}, bf16[1280,1024]{1,0:T(8,128)(2,1)}) custom-call(bf16[1280,1024]{1,0:T(8,128)(2,1)} %collective-permute-done.hidden_ref.refs_2_, bf16[1280,1024]{1,0:T(8,128)(2,1)} %copy-done.2, bf16[2,1024,1024]{2,1,0:T(8,128)(2,1)} %get-tuple-element.47.expand_ref, ...), custom_call_target="tpu_custom_call" | custom-call | flops 1048576 | bytes 1048576 | tf_op jit(solution)/shard_map/pallas_call | solution.py:431
  187.5 4.7 slice.30
  193.1 4.8 slice.32
  201.4 1.4 multiply_sine_fusion
  202.8 4.2 collective-permute-done.6
  207.0 2.1 pad_maximum_fusion
  209.6 3.9 convolution_convert_fusion.refs_4_
  213.5 3.8 convolution_convert_fusion.1.refs_3_
  217.4 1.3 collective-permute-start.1
  219.2 6.4 %fusion.24.refs_1_ = f32[1536,1280]{1,0:T(8,128)} fusion(bf16[1536,1024]{1,0:T(8,128)(2,1)S(1)} %constant_dynamic-update-slice_fusion.project_hbm, bf16[1280,1024]{1,0:T(8,128)(2,1)S(1)} %copy-done.1), kind=kOutput, calls=%fused_computation.86 | convolution fusion | flops 4026531840 | bytes 13631488 | tf_op jit(solution)/shard_map/td,ed->et/dot_general | solution.py:308
  225.6 4.8 slice_add_fusion.1
  230.6 1.6 collective-permute-start.11
  232.2 3.1 slice_add_fusion
  236.1 8.9 %fusion.25.refs_2_ = f32[1536,1280]{1,0:T(8,128)} fusion(bf16[1536,1024]{1,0:T(8,128)(2,1)S(1)} %constant_dynamic-update-slice_fusion.project_hbm, bf16[1280,1024]{1,0:T(8,128)(2,1)} %collective-permute-done.hidden_ref.refs_2_), kind=kOutput, calls=%fused_computation.87 | convolution fusion | flops 4026531840 | bytes 13631488 | tf_op jit(solution)/shard_map/td,ed->et/dot_general | solution.py:308
  245.0 91.9 %shard_map.356 = (bf16[512,1280]{1,0:T(8,128)(2,1)S(1)}, bf16[512,1280]{1,0:T(8,128)(2,1)}, bf16[1536,1280]{1,0:T(8,128)(2,1)}, bf16[1536,1280]{1,0:T(8,128)(2,1)}) custom-call(s32[11]{0:T(128)S(1)} %pad_add_fusion.refs_0_, f32[1536,1280]{1,0:T(8,128)} %fusion.24.refs_1_, f32[1536,1280]{1,0:T(8,128)} %fusion.25.refs_2_, ...), custom_call_target="tpu_custom_call" | custom-call | flops 1048576 | bytes 1048576 | tf_op jit(solution)/shard_map/pallas_call | solution.py:251
  336.9 1.3 collective-permute-start.9
  338.2 5.0 fusion.12
  345.7 1.5 collective-permute-start.17
  348.3 78.1 %shard_map.357 = (f32[1280,1024]{1,0:T(8,128)}, f32[8,1024]{1,0:T(8,128)}, f32[384,256]{1,0:T(8,128)}, f32[128,256]{1,0:T(8,128)}) custom-call(bf16[1536,1024]{1,0:T(8,128)(2,1)} %copy-done.20, bf16[1536,1280]{1,0:T(8,128)(2,1)} %get-tuple-element.60.refs_0_, bf16[1536,1280]{1,0:T(8,128)(2,1)} %get-tuple-element.61.refs_1_, ...), custom_call_target="tpu_custom_call" | custom-call | flops 1048576 | bytes 1048576 | tf_op jit(solution)/shard_map/pallas_call | solution.py:1030
  426.4 4.7 collective-permute-start.21
  431.0 1.9 convert_add_fusion.1
  437.0 2.1 collective-permute-start.13
  439.6 2.3 collective-permute-done.18
  441.9 2.7 collective-permute-start.15
  444.6 1.7 maximum_select_fusion.7
  446.3 2.0 multiply_reduce_fusion
  448.4 7.2 %collective-permute-start.19 = (f32[384,256]{1,0:T(8,128)S(1)}, f32[384,256]{1,0:T(8,128)}, u32[]{:S(2)}, u32[]{:S(2)}) collective-permute-start(f32[384,256]{1,0:T(8,128)S(1)} %copy-done.32), channel_id=1, source_target_pairs={{0,2},{1,3},{2,0},{3,1},{4,6},{5,7},{6,4},{7,5},{8,10},{9,11},{10,... | collective-permute-start | bytes 1179656 | tf_op jit(solution)/shard_map/ppermute | solution.py:322
  455.5 3.5 collective-permute-done.14
  459.0 2.2 collective-permute-done.15
  461.1 2.6 multiply_reduce_fusion.1
  465.0 2.1 collective-permute-start.23
  467.2 9.1 %fusion = bf16[1,1280,1024]{2,1,0:T(8,128)(2,1)} fusion(f32[1280,1024]{1,0:T(8,128)} %fusion.12, f32[1280,1024]{1,0:T(8,128)} %get-tuple-element.49, bf16[1280,1024]{1,0:T(8,128)(2,1)} %copy-done.19, bf16[1,1280,1024]{2,1,0:T(8,128)(2,1)S(1)} %copy-done.16, bf16[512,1280]{1,0:T(8,128)(2,1)} %collective-permute-done.9, ...), kind=kOutput, calls=%fused_computation.7 | convolution fusion | flops 1351352320 | bytes 20709376 | tf_op jit(solution)/shard_map/ft,fd->td/dot_general | solution.py:308
  476.9 17.5 %shard_map.358 = f32[24,128]{1,0:T(8,128)} custom-call(f32[24,128]{1,0:T(8,128)} %reshape.93.term_ref), custom_call_target="tpu_custom_call" | custom-call | tf_op jit(solution)/shard_map/pallas_call | solution.py:1132
  503.6 1.5 fusion.19
  505.1 1.5 maximum_select_fusion.3
  508.5 3.3 fusion.21
  513.3 3.6 fusion.15
  516.9 3.8 fusion.17
  520.7 2.4 copy.47
  (174 shorter events, 28.6 us)
Async XLA Ops:
  7.2 193.8 %all-gather.2.cloned.1.call-start = ((), (), s32[]{:S(2)}) async-start(), calls=%async_computation | async-start | bytes 1966080 | tf_op jit(solution)/shard_map/all_gather | solution.py:1157
  82.9 57.8 %collective-permute-start = (bf16[1280,1024]{1,0:T(8,128)(2,1)S(1)}, bf16[1280,1024]{1,0:T(8,128)(2,1)}, u32[]{:S(2)}, u32[]{:S(2)}) collective-permute-start(bf16[1280,1024]{1,0:T(8,128)(2,1)S(1)} %get-tuple-element.46.hidden_ref.refs_3_), channel_id=1, source_target_pairs={{0,16},{16,0},{1,17},{17,1},{2,18},{18,2},{3,19},{19,3},{4,20},{20... | collective-permute-start | bytes 7864328 | tf_op jit(solution)/shard_map/ppermute | solution.py:322
  83.4 116.4 %collective-permute-start.3 = (bf16[256,256]{1,0:T(8,128)(2,1)S(1)}, bf16[256,256]{1,0:T(8,128)(2,1)}, u32[]{:S(2)}, u32[]{:S(2)}) collective-permute-start(bf16[256,256]{1,0:T(8,128)(2,1)S(1)} %get-tuple-element.55), channel_id=1, source_target_pairs={{0,4},{4,8},{8,12},{12,0},{1,5},{5,9},{9,13},{13,1},{2,6},{6,10},{... | collective-permute-start | bytes 393224 | tf_op jit(solution)/shard_map/ppermute | solution.py:1167
  84.1 116.7 %collective-permute-start.4 = (bf16[256,256]{1,0:T(8,128)(2,1)S(1)}, bf16[256,256]{1,0:T(8,128)(2,1)S(1)}, u32[]{:S(2)}, u32[]{:S(2)}) collective-permute-start(bf16[256,256]{1,0:T(8,128)(2,1)S(1)} %get-tuple-element.55), channel_id=1, source_target_pairs={{0,8},{4,12},{8,0},{12,4},{1,9},{5,13},{9,1},{13,5},{2,10},{6,14},... | collective-permute-start | bytes 393224 | tf_op jit(solution)/shard_map/ppermute | solution.py:1167
  85.6 115.2 %collective-permute-start.5 = (bf16[256,256]{1,0:T(8,128)(2,1)S(1)}, bf16[256,256]{1,0:T(8,128)(2,1)S(1)}, u32[]{:S(2)}, u32[]{:S(2)}) collective-permute-start(bf16[256,256]{1,0:T(8,128)(2,1)S(1)} %get-tuple-element.55), channel_id=1, source_target_pairs={{0,12},{4,0},{8,4},{12,8},{1,13},{5,1},{9,5},{13,9},{2,14},{6,2},{... | collective-permute-start | bytes 393224 | tf_op jit(solution)/shard_map/ppermute | solution.py:1167
  192.2 33.4 %collective-permute-start.7 = (f32[1024,1024]{1,0:T(8,128)}, f32[1024,1024]{1,0:T(8,128)}, u32[]{:S(2)}, u32[]{:S(2)}) collective-permute-start(f32[1024,1024]{1,0:T(8,128)} %slice.30), channel_id=1, source_target_pairs={{0,1},{1,0},{2,3},{3,2},{4,5},{5,4},{6,7},{7,6},{8,9},{9,8},{10,11... | collective-permute-start | bytes 12582920 | tf_op jit(solution)/shard_map/ppermute | solution.py:322
  197.9 11.7 %copy-start.3 = (bf16[1280,1024]{1,0:T(8,128)(2,1)S(1)}, bf16[1280,1024]{1,0:T(8,128)(2,1)}, u32[]{:S(2)}) copy-start(bf16[1280,1024]{1,0:T(8,128)(2,1)} %copy-done.2) | copy-start | bytes 7864324
  197.9 34.3 %collective-permute-start.8 = (f32[1024,1024]{1,0:T(8,128)}, f32[1024,1024]{1,0:T(8,128)}, u32[]{:S(2)}, u32[]{:S(2)}) collective-permute-start(f32[1024,1024]{1,0:T(8,128)} %slice.32), channel_id=1, source_target_pairs={{0,1},{1,0},{2,3},{3,2},{4,5},{5,4},{6,7},{7,6},{8,9},{9,8},{10,11... | collective-permute-start | bytes 12582920 | tf_op jit(solution)/shard_map/ppermute | solution.py:322
  200.8 6.2 %collective-permute-start.6 = (bf16[256,1024]{1,0:T(8,128)(2,1)S(1)}, bf16[256,1024]{1,0:T(8,128)(2,1)}, u32[]{:S(2)}, u32[]{:S(2)}) collective-permute-start(bf16[256,1024]{1,0:T(8,128)(2,1)S(1)} %constant_dynamic-update-slice_fusion.2), channel_id=1, source_target_pairs={{0,1},{1,0},{2,3},{3,2},{4,5},{5,4},{6,7},{7,6},{8,9},{9,8},{10,11... | collective-permute-start | bytes 1572872 | tf_op jit(solution)/shard_map/ppermute | solution.py:322
  201.0 17.8 %collective-permute-start.2 = (bf16[768,1024]{1,0:T(8,128)(2,1)}, bf16[768,1024]{1,0:T(8,128)(2,1)S(1)}, u32[]{:S(2)}, u32[]{:S(2)}) collective-permute-start(bf16[768,1024]{1,0:T(8,128)(2,1)} %all-gather.2.cloned.1.call-done), channel_id=1, source_target_pairs={{0,1},{1,0},{2,3},{3,2},{4,5},{5,4},{6,7},{7,6},{8,9},{9,8},{10,11... | collective-permute-start | bytes 4718600 | tf_op jit(solution)/shard_map/ppermute | solution.py:322
  209.1 256.0 %collective-permute-start.10 = (bf16[512,1024]{1,0:T(8,128)(2,1)}, bf16[512,1024]{1,0:T(8,128)(2,1)}, u32[]{:S(2)}, u32[]{:S(2)}) collective-permute-start(bf16[512,1024]{1,0:T(8,128)(2,1)} %pad_maximum_fusion), channel_id=1, source_target_pairs={{0,16},{16,0},{1,17},{17,1},{2,18},{18,2},{3,19},{19,3},{4,20},{20... | collective-permute-start | bytes 3145736 | tf_op jit(solution)/shard_map/ppermute | solution.py:322
  217.4 128.3 %collective-permute-start.1 = (bf16[1280,1024]{1,0:T(8,128)(2,1)}, bf16[1280,1024]{1,0:T(8,128)(2,1)S(1)}, u32[]{:S(2)}, u32[]{:S(2)}) collective-permute-start(bf16[1280,1024]{1,0:T(8,128)(2,1)} %get-tuple-element.53), channel_id=1, source_target_pairs={{0,16},{16,0},{1,17},{17,1},{2,18},{18,2},{3,19},{19,3},{4,20},{20... | collective-permute-start | bytes 7864328 | tf_op jit(solution)/shard_map/ppermute | solution.py:322
  218.8 13.4 %slice-start = ((s8[8388608]{0:T(1024)(128)(4,1)}), s8[4194304]{0:T(1024)(128)(4,1)S(1)}, s32[]{:S(2)}) async-start(s8[8388608]{0:T(1024)(128)(4,1)} %bitcast.37), calls=%async_computation.1 | async-start | bytes 8388608
  219.2 16.9 %copy-start.20 = (bf16[1536,1024]{1,0:T(8,128)(2,1)}, bf16[1536,1024]{1,0:T(8,128)(2,1)S(1)}, u32[]{:S(2)}) copy-start(bf16[1536,1024]{1,0:T(8,128)(2,1)S(1)} %constant_dynamic-update-slice_fusion.project_hbm) | copy-start | bytes 9437188
  219.2 13.0 %slice-start.1 = ((s8[8388608]{0:T(1024)(128)(4,1)}), s8[4194304]{0:T(1024)(128)(4,1)S(1)}, s32[]{:S(2)}) async-start(s8[8388608]{0:T(1024)(128)(4,1)} %bitcast.37), calls=%async_computation.2 | async-start | bytes 8388608
  230.6 112.6 %collective-permute-start.11 = (bf16[512,1024]{1,0:T(8,128)(2,1)S(1)}, bf16[512,1024]{1,0:T(8,128)(2,1)S(1)}, u32[]{:S(2)}, u32[]{:S(2)}) collective-permute-start(bf16[512,1024]{1,0:T(8,128)(2,1)S(1)} %dynamic-slice_convert_fusion.1.refs_8_), channel_id=1, source_target_pairs={{0,2},{1,3},{2,0},{3,1},{4,6},{5,7},{6,4},{7,5},{8,10},{9,11},{10,... | collective-permute-start | bytes 3145736 | tf_op jit(solution)/shard_map/ppermute | solution.py:322
  235.3 9.6 %copy-start.18 = (f32[1024,1024]{1,0:T(8,128)}, f32[1024,1024]{1,0:T(8,128)S(1)}, u32[]{:S(2)}) copy-start(f32[1024,1024]{1,0:T(8,128)S(1)} %slice_add_fusion) | copy-start | bytes 12582916
  235.5 111.7 %collective-permute-start.12 = (bf16[1024,512]{1,0:T(8,128)(2,1)S(1)}, bf16[1024,512]{1,0:T(8,128)(2,1)S(1)}, u32[]{:S(2)}, u32[]{:S(2)}) collective-permute-start(bf16[1024,512]{1,0:T(8,128)(2,1)S(1)} %dynamic-slice_convert_fusion.refs_9_), channel_id=1, source_target_pairs={{0,2},{1,3},{2,0},{3,1},{4,6},{5,7},{6,4},{7,5},{8,10},{9,11},{10,... | collective-permute-start | bytes 3145736 | tf_op jit(solution)/shard_map/ppermute | solution.py:322
  336.9 6.3 %copy-start.10 = (bf16[512,1280]{1,0:T(8,128)(2,1)}, bf16[512,1280]{1,0:T(8,128)(2,1)S(1)}, u32[]{:S(2)}) copy-start(bf16[512,1280]{1,0:T(8,128)(2,1)S(1)} %get-tuple-element.58.refs_5_) | copy-start | bytes 3932164
  336.9 130.2 %collective-permute-start.9 = (bf16[512,1280]{1,0:T(8,128)(2,1)}, bf16[512,1280]{1,0:T(8,128)(2,1)}, u32[]{:S(2)}, u32[]{:S(2)}) collective-permute-start(bf16[512,1280]{1,0:T(8,128)(2,1)} %get-tuple-element.59.refs_4_), channel_id=1, source_target_pairs={{0,16},{16,0},{1,17},{17,1},{2,18},{18,2},{3,19},{19,3},{4,20},{20... | collective-permute-start | bytes 3932168 | tf_op jit(solution)/shard_map/ppermute | solution.py:322
  345.2 91.8 %collective-permute-start.16 = (bf16[512,256]{1,0:T(8,128)(2,1)}, bf16[512,256]{1,0:T(8,128)(2,1)}, u32[]{:S(2)}, u32[]{:S(2)}) collective-permute-start(bf16[512,256]{1,0:T(8,128)(2,1)} %get-tuple-element.93), channel_id=1, source_target_pairs={{0,4},{4,8},{8,12},{12,0},{1,5},{5,9},{9,13},{13,1},{2,6},{6,10},{... | collective-permute-start | bytes 786440 | tf_op jit(solution)/shard_map/ppermute | solution.py:1191
  345.7 93.3 %collective-permute-start.17 = (bf16[512,256]{1,0:T(8,128)(2,1)}, bf16[512,256]{1,0:T(8,128)(2,1)}, u32[]{:S(2)}, u32[]{:S(2)}) collective-permute-start(bf16[512,256]{1,0:T(8,128)(2,1)} %get-tuple-element.95), channel_id=1, source_target_pairs={{0,8},{4,12},{8,0},{12,4},{1,9},{5,13},{9,1},{13,5},{2,10},{6,14},... | collective-permute-start | bytes 786440 | tf_op jit(solution)/shard_map/ppermute | solution.py:1191
  348.3 82.8 %copy-start.25 = (bf16[1024,512]{1,0:T(8,128)(2,1)S(1)}, bf16[1024,512]{1,0:T(8,128)(2,1)}, u32[]{:S(2)}) copy-start(bf16[1024,512]{1,0:T(8,128)(2,1)} %copy-done.24) | copy-start | bytes 3145732
  426.4 7.8 %copy-start.37 = (f32[128,256]{1,0:T(8,128)S(1)}, f32[128,256]{1,0:T(8,128)}, u32[]{:S(2)}) copy-start(f32[128,256]{1,0:T(8,128)} %get-tuple-element.68) | copy-start | bytes 393220
  426.4 8.5 %copy-start.32 = (f32[384,256]{1,0:T(8,128)S(1)}, f32[384,256]{1,0:T(8,128)}, u32[]{:S(2)}) copy-start(f32[384,256]{1,0:T(8,128)} %get-tuple-element.67) | copy-start | bytes 1179652
  426.4 7.8 %collective-permute-start.21 = (f32[128,256]{1,0:T(8,128)}, f32[128,256]{1,0:T(8,128)S(1)}, u32[]{:S(2)}, u32[]{:S(2)}) collective-permute-start(f32[128,256]{1,0:T(8,128)} %get-tuple-element.68), channel_id=1, source_target_pairs={{0,2},{1,3},{2,0},{3,1},{4,6},{5,7},{6,4},{7,5},{8,10},{9,11},{10,... | collective-permute-start | bytes 393224 | tf_op jit(solution)/shard_map/ppermute | solution.py:322
  433.0 9.0 %copy-start.22 = (f32[1024,512]{1,0:T(8,128)}, f32[1024,512]{1,0:T(8,128)S(1)}, u32[]{:S(2)}) copy-start(f32[1024,512]{1,0:T(8,128)S(1)} %convert_add_fusion.1) | copy-start | bytes 6291460
  433.0 11.7 %copy-start.38 = (f32[128,256]{1,0:T(8,128)S(1)}, f32[128,256]{1,0:T(8,128)}, u32[]{:S(2)}) copy-start(f32[128,256]{1,0:T(8,128)} %get-tuple-element.68) | copy-start | bytes 393220
  434.2 7.7 %collective-permute-start.18 = (bf16[512,256]{1,0:T(8,128)(2,1)}, bf16[512,256]{1,0:T(8,128)(2,1)S(1)}, u32[]{:S(2)}, u32[]{:S(2)}) collective-permute-start(bf16[512,256]{1,0:T(8,128)(2,1)} %get-tuple-element.94), channel_id=1, source_target_pairs={{0,12},{4,0},{8,4},{12,8},{1,13},{5,1},{9,5},{13,9},{2,14},{6,2},{... | collective-permute-start | bytes 786440 | tf_op jit(solution)/shard_map/ppermute | solution.py:1191
  437.0 11.4 %collective-permute-start.13 = (bf16[256,512]{1,0:T(8,128)(2,1)S(1)}, bf16[256,512]{1,0:T(8,128)(2,1)S(1)}, u32[]{:S(2)}, u32[]{:S(2)}) collective-permute-start(bf16[256,512]{1,0:T(8,128)(2,1)S(1)} %get-tuple-element.96), channel_id=1, source_target_pairs={{0,4},{4,8},{8,12},{12,0},{1,5},{5,9},{9,13},{13,1},{2,6},{6,10},{... | collective-permute-start | bytes 786440 | tf_op jit(solution)/shard_map/ppermute | solution.py:1191
  439.1 19.9 %collective-permute-start.14 = (bf16[256,512]{1,0:T(8,128)(2,1)S(1)}, bf16[256,512]{1,0:T(8,128)(2,1)S(1)}, u32[]{:S(2)}, u32[]{:S(2)}) collective-permute-start(bf16[256,512]{1,0:T(8,128)(2,1)S(1)} %get-tuple-element.98), channel_id=1, source_target_pairs={{0,8},{4,12},{8,0},{12,4},{1,9},{5,13},{9,1},{13,5},{2,10},{6,14},... | collective-permute-start | bytes 786440 | tf_op jit(solution)/shard_map/ppermute | solution.py:1191
  441.9 25.2 %copy-start.16 = (bf16[1,1280,1024]{2,1,0:T(8,128)(2,1)S(1)}, bf16[1,1280,1024]{2,1,0:T(8,128)(2,1)}, u32[]{:S(2)}) copy-start(bf16[1,1280,1024]{2,1,0:T(8,128)(2,1)} %param.18) | copy-start | bytes 7864324
  441.9 19.2 %collective-permute-start.15 = (bf16[256,512]{1,0:T(8,128)(2,1)S(1)}, bf16[256,512]{1,0:T(8,128)(2,1)S(1)}, u32[]{:S(2)}, u32[]{:S(2)}) collective-permute-start(bf16[256,512]{1,0:T(8,128)(2,1)S(1)} %get-tuple-element.97), channel_id=1, source_target_pairs={{0,12},{4,0},{8,4},{12,8},{1,13},{5,1},{9,5},{13,9},{2,14},{6,2},{... | collective-permute-start | bytes 786440 | tf_op jit(solution)/shard_map/ppermute | solution.py:1191
  448.4 50.0 %collective-permute-start.19 = (f32[384,256]{1,0:T(8,128)S(1)}, f32[384,256]{1,0:T(8,128)}, u32[]{:S(2)}, u32[]{:S(2)}) collective-permute-start(f32[384,256]{1,0:T(8,128)S(1)} %copy-done.32), channel_id=1, source_target_pairs={{0,2},{1,3},{2,0},{3,1},{4,6},{5,7},{6,4},{7,5},{8,10},{9,11},{10,... | collective-permute-start | bytes 1179656 | tf_op jit(solution)/shard_map/ppermute | solution.py:322
  459.0 41.4 %collective-permute-start.22 = (f32[256,256]{1,0:T(8,128)}, f32[256,256]{1,0:T(8,128)}, u32[]{:S(2)}, u32[]{:S(2)}) collective-permute-start(f32[256,256]{1,0:T(8,128)} %maximum_select_fusion.7), channel_id=1, source_target_pairs={{0,1},{1,0},{2,3},{3,2},{4,5},{5,4},{6,7},{7,6},{8,9},{9,8},{10,11... | collective-permute-start | bytes 786440 | tf_op jit(solution)/shard_map/ppermute | solution.py:322
  461.1 40.6 %collective-permute-start.25 = (f32[512,256]{1,0:T(8,128)S(1)}, f32[512,256]{1,0:T(8,128)}, u32[]{:S(2)}, u32[]{:S(2)}) collective-permute-start(f32[512,256]{1,0:T(8,128)S(1)} %get-tuple-element.90), channel_id=1, source_target_pairs={{0,2},{1,3},{2,0},{3,1},{4,6},{5,7},{6,4},{7,5},{8,10},{9,11},{10,... | collective-permute-start | bytes 1572872 | tf_op jit(solution)/shard_map/ppermute | solution.py:322
  465.0 40.0 %collective-permute-start.23 = (f32[256,512]{1,0:T(8,128)}, f32[256,512]{1,0:T(8,128)}, u32[]{:S(2)}, u32[]{:S(2)}) collective-permute-start(f32[256,512]{1,0:T(8,128)} %get-tuple-element.92), channel_id=1, source_target_pairs={{0,2},{1,3},{2,0},{3,1},{4,6},{5,7},{6,4},{7,5},{8,10},{9,11},{10,... | collective-permute-start | bytes 1572872 | tf_op jit(solution)/shard_map/ppermute | solution.py:322
  467.1 9.1 %copy-start.42 = (f32[8,1024]{1,0:T(8,128)S(1)}, f32[8,1024]{1,0:T(8,128)}, u32[]{:S(2)}) copy-start(f32[8,1024]{1,0:T(8,128)} %get-tuple-element.66) | copy-start | bytes 98308
  467.1 9.1 %copy-start.45 = (pred[3]{0:T(512)(128)(4,1)S(1)}, pred[3]{0:T(512)(128)(4,1)}, u32[]{:S(2)}) copy-start(pred[3]{0:T(512)(128)(4,1)} %constant.144.clone.1) | copy-start | bytes 13
  467.1 32.6 %copy-start.15 = (f32[2,256]{1,0:T(2,128)S(1)}, f32[2,256]{1,0:T(2,128)}, u32[]{:S(2)}) copy-start(f32[2,256]{1,0:T(2,128)} %norm_ref.1) | copy-start | bytes 6148
  467.1 32.6 %copy-start.43 = (f32[2,256]{1,0:T(2,128)S(1)}, f32[2,256]{1,0:T(2,128)}, u32[]{:S(2)}) copy-start(f32[2,256]{1,0:T(2,128)} %param.34) | copy-start | bytes 6148
  467.1 32.6 %copy-start.44 = (f32[2,256]{1,0:T(2,128)S(1)}, f32[2,256]{1,0:T(2,128)}, u32[]{:S(2)}) copy-start(f32[2,256]{1,0:T(2,128)} %param.35) | copy-start | bytes 6148
  498.3 5.2 copy-start.12
  498.3 5.2 copy-start.35
  499.7 7.0 %collective-permute-start.20 = (f32[768,256]{1,0:T(8,128)S(1)}, f32[768,256]{1,0:T(8,128)S(1)}, u32[]{:S(2)}, u32[]{:S(2)}) collective-permute-start(f32[768,256]{1,0:T(8,128)S(1)} %maximum_select_fusion.5), channel_id=1, source_target_pairs={{0,1},{1,0},{2,3},{3,2},{4,5},{5,4},{6,7},{7,6},{8,9},{9,8},{10,11... | collective-permute-start | bytes 2359304 | tf_op jit(solution)/shard_map/ppermute | solution.py:322
  503.0 8.8 %collective-permute-start.26 = (f32[1024,256]{1,0:T(8,128)S(1)}, f32[1024,256]{1,0:T(8,128)S(1)}, u32[]{:S(2)}, u32[]{:S(2)}) collective-permute-start(f32[1024,256]{1,0:T(8,128)S(1)} %maximum_select_fusion.4), channel_id=1, source_target_pairs={{0,1},{1,0},{2,3},{3,2},{4,5},{5,4},{6,7},{7,6},{8,9},{9,8},{10,11... | collective-permute-start | bytes 3145736 | tf_op jit(solution)/shard_map/ppermute | solution.py:322
  506.6 10.3 %collective-permute-start.24 = (f32[256,1024]{1,0:T(8,128)S(1)}, f32[256,1024]{1,0:T(8,128)S(1)}, u32[]{:S(2)}, u32[]{:S(2)}) collective-permute-start(f32[256,1024]{1,0:T(8,128)S(1)} %maximum_select_fusion.3), channel_id=1, source_target_pairs={{0,1},{1,0},{2,3},{3,2},{4,5},{5,4},{6,7},{7,6},{8,9},{9,8},{10,11... | collective-permute-start | bytes 3145736 | tf_op jit(solution)/shard_map/ppermute | solution.py:322
  513.3 7.4 %slice-start.2 = ((s8[5242880]{0:T(1024)(128)(4,1)}), s8[1048576]{0:T(1024)(128)(4,1)S(1)}, s32[]{:S(2)}) async-start(s8[5242880]{0:T(1024)(128)(4,1)} %bitcast.40), calls=%async_computation.3 | async-start | bytes 2097152
  (31 other events, 82.0 us)
Sparse Core Ops, SparseCore 0:
  83.6 41.6 all-gather.1

commit v6 on v5

--- a/solution.py
+++ b/solution.py
@@ -326,50 +326,82 @@
     return lax.optimization_barrier((array, *before))[0]
 
 
-def ordered(index, mine, other, axis):
-    return jnp.where(
-        index == 0,
-        jnp.concatenate([mine, other], axis=axis),
-        jnp.concatenate([other, mine], axis=axis),
-    )
-
-
-UNITS = 512
 ROWS = 640
 
 
-def feed_kernel(
-    earlier,
-    hidden_ref,
-    back_ref,
-    expand_ref,
-    shrink_ref,
-    *refs,
-):
-    if earlier:
-        expand_before, shrink_before = refs[:2]
-        refs = refs[2:]
-    (
-        expand_grad,
-        shrink_grad,
-        hidden_part,
-        branch_part,
-        activated_ref,
-        lifted_grad_ref,
-        turned_ref,
-        hidden_sum,
-        branch_sum,
-    ) = refs
+MESH = pl.DeviceIdType.MESH
+
+
+def feed_kernel(exchange, hidden_ref, back_ref, expand_ref, shrink_ref, *refs):
     step, steps = pl.program_id(0), pl.num_programs(0)
+    f32 = jnp.float32
+    if exchange:
+        (
+            expand_before,
+            shrink_before,
+            keep_ref,
+            away_ref,
+            land_hbm,
+            hidden_part,
+            branch_part,
+            activated_ref,
+            lifted_grad_ref,
+            hidden_sum,
+            branch_sum,
+            send_ref,
+            land_ref,
+            near_send,
+            near_recv,
+            load_sem,
+        ) = refs
+        outer = lax.axis_index("outer")
+        far, near = outer // 2, outer % 2
+        near_id = {"outer": outer + 1 - 2 * near}
+
+        def near_copy(tile, k):
+            return pltpu.make_async_remote_copy(
+                src_ref=send_ref.at[k],
+                dst_ref=land_hbm.at[tile, k],
+                send_sem=near_send.at[tile, k],
+                recv_sem=near_recv.at[tile, k],
+                device_id=near_id,
+                device_id_type=MESH,
+            )
+
+        def load(tile, k):
+            return pltpu.make_async_copy(land_hbm.at[tile, k], land_ref.at[k], load_sem.at[k])
+
+        @pl.when(step == 0)
+        def _():
+            barrier = pltpu.get_barrier_semaphore()
+            pl.semaphore_signal(
+                barrier, inc=1, device_id=near_id, device_id_type=MESH
+            )
+            pl.semaphore_wait(barrier, 1)
+
+        for tile in range(2):
+
+            @pl.when(step == 2 + tile)
+            def _(tile=tile):
+                for k in range(2):
+                    near_copy(tile, k).wait_recv()
+                    load(tile, k).start()
+
+    else:
+        (
+            expand_grad,
+            shrink_grad,
+            hidden_part,
+            branch_part,
+            activated_ref,
+            lifted_grad_ref,
+            hidden_sum,
+            branch_sum,
+        ) = refs
     tokens = hidden_ref.shape[0]
-    f32 = jnp.float32
     nt = (((1,), (1,)), ((), ()))
     tn = (((0,), (0,)), ((), ()))
     slope = 0.7978845608028654
-
-    @pl.when(step == 0)
-    def _():
-        turned_ref[...] = hidden_ref[...].T
 
     def block(at, first):
         hidden = hidden_ref[at, :]
@@ -408,10 +440,41 @@
     def _():
         blocks(False)
 
-    made = lax.dot_general(activated_ref[...], back_ref[...], tn, preferred_element_type=f32)
-    shrink_grad[...] = made + shrink_before[...] if earlier else made
-    made = jnp.dot(turned_ref[...], lifted_grad_ref[...], preferred_element_type=f32)
-    expand_grad[...] = made + expand_before[...] if earlier else made
+    def gradient(k):
+        made_of = ((activated_ref, back_ref), (lifted_grad_ref, hidden_ref))[k]
+        made = lax.dot_general(made_of[0][...], made_of[1][...], tn, preferred_element_type=f32)
+        return made + (shrink_before, expand_before)[k][...] if exchange else made
+
+    if not exchange:
+        shrink_grad[...] = gradient(0)
+        expand_grad[...] = gradient(1)
+    else:
+        for tile in range(2):
+
+            @pl.when(step == tile)
+            def _(tile=tile):
+                for k in range(2):
+                    if tile:
+                        near_copy(tile - 1, k).wait_send()
+                    send_ref[k] = gradient(k)
+                    near_copy(tile, k).start()
+
+            @pl.when(step == 2 + tile)
+            def _(tile=tile):
+                for k in range(2):
+                    load(tile, k).wait()
+                    total = gradient(k) + land_ref[k]
+
+                    @pl.when(far == tile)
+                    def _():
+                        keep_ref[k] = total
+
+                    @pl.when(far != tile)
+                    def _():
+                        away_ref[k] = total.astype(jnp.bfloat16)
+
+                    if tile == 0:
+                        near_copy(1, k).wait_send()
 
     @pl.when(step == steps - 1)
     def _():
@@ -422,42 +485,65 @@
 def feed(hidden, back, expand, shrink, before, branch_type):
     tokens, width = hidden.shape
     units = 2 * expand.shape[2]
-    tile = min(UNITS, expand.shape[2])
-    steps = units // tile
+    steps = 4
+    tile = units // steps
+    exchange = bool(before)
     low, f32 = jnp.bfloat16, jnp.float32
+    turn = steps // 2 if exchange else 0
     whole = pl.BlockSpec((tokens, width), lambda n: (0, 0), pipeline_mode=pl.Buffered(1))
-    columns = pl.BlockSpec((width, tile), lambda n: (0, n))
-    rows = pl.BlockSpec((tile, width), lambda n: (n, 0))
+    rows = pl.BlockSpec((tile, width), lambda n: ((n + turn) % steps, 0))
+    quarter = pl.BlockSpec((2, tile, width), lambda n: (0, 0, 0), pipeline_mode=pl.Buffered(1))
+    columns = pl.BlockSpec(
+        (None, width, tile),
+        lambda n: ((n + turn) % steps // 2, 0, (n + turn) % 2),
+    )
+    grads = jax.ShapeDtypeStruct((units, width), f32)
+    sem = pltpu.SemaphoreType.DMA
     return pl.pallas_call(
-        partial(feed_kernel, bool(before)),
+        partial(feed_kernel, exchange),
         grid=(steps,),
-        in_specs=[
-            whole,
-            whole,
-            pl.BlockSpec((None, width, tile), lambda n: (n * 2 // steps, 0, n % (steps // 2))),
-            rows,
-        ]
-        + [columns, rows] * bool(before),
-        out_specs=[columns, rows, whole, whole],
-        out_shape=[
-            jax.ShapeDtypeStruct((width, units), f32),
-            jax.ShapeDtypeStruct((units, width), f32),
+        in_specs=[whole, whole, columns, rows] + [rows, rows] * exchange,
+        out_specs=(
+            [quarter, quarter, pl.BlockSpec(memory_space=pl.ANY)] if exchange else [rows, rows]
+        )
+        + [whole, whole],
+        out_shape=(
+            [
+                jax.ShapeDtypeStruct((2, tile, width), f32),
+                jax.ShapeDtypeStruct((2, tile, width), low),
+                jax.ShapeDtypeStruct((2, 2, tile, width), f32),
+            ]
+            if exchange
+            else [grads, grads]
+        )
+        + [
             jax.ShapeDtypeStruct((tokens, width), f32),
             jax.ShapeDtypeStruct((tokens, width), branch_type),
         ],
         scratch_shapes=[
             pltpu.VMEM((tokens, tile), low),
             pltpu.VMEM((tokens, tile), low),
-            pltpu.VMEM((width, tokens), low),
             pltpu.VMEM((tokens, width), f32),
             pltpu.VMEM((tokens, width), f32),
-        ],
-        compiler_params=pltpu.CompilerParams(vmem_limit_bytes=56 * 2**20),
+        ]
+        + [
+            pltpu.VMEM((2, tile, width), f32),
+            pltpu.VMEM((2, tile, width), f32),
+            sem((2, 2)),
+            sem((2, 2)),
+            sem((2,)),
+        ]
+        * exchange,
+        compiler_params=pltpu.CompilerParams(
+            vmem_limit_bytes=60 * 2**20,
+            **(dict(collective_id=4, has_side_effects=True) if exchange else {}),
+        ),
         cost_estimate=pl.CostEstimate(flops=2**20, bytes_accessed=2**20, transcendentals=0),
     )(hidden, back, expand, shrink, *before)
 
 
-MESH = pl.DeviceIdType.MESH
+def most_of(tokens):
+    return tokens * 4 // 5 // 16 * 16
 
 
 def opening_kernel(
@@ -569,7 +655,14 @@
         return out
 
     start_own(0)
-    row_copy = remote(back_ref, other_back, row_sem.at[0], row_sem.at[1], row_id)
+    most = most_of(back_ref.shape[0])
+    row_copy = remote(
+        back_ref.at[slice(0, most)],
+        other_back.at[slice(0, most)],
+        row_sem.at[0],
+        row_sem.at[1],
+        row_id,
+    )
     row_copy.start()
     norm_copies = []
     for step in range(1, deep):
@@ -758,20 +851,18 @@
     *refs,
 ):
     sources = (project_hbm, *refs[:9])
-    part_own, part_other, gain_ref = refs[9:12]
-    input_grad, norm_grad, project_share, mixing_share = refs[12 + later : 16 + later]
-    refs = refs[16 + later :]
+    part_own, part_other, feed_keep, feed_come, gain_ref = refs[9:14]
+    input_grad, small_sum, mixed_come = refs[14 + later : 17 + later]
+    full_refs = refs[17 + later : 21 + later]
+    refs = refs[21 + later :]
     held = refs[:10]
     (
         part_in,
         total_ref,
         sent_ref,
         come_ref,
-        out_ref,
-        project_sib,
         project_land,
         project_own,
-        mixing_sib,
         mixing_land,
         mixing_own,
         project_far,
@@ -782,11 +873,34 @@
         project_lands,
         mixing_line,
         mixing_lands,
+        feed_in,
+        feed_line,
+        feed_lands,
+        feed_share,
+        expand_share,
+        project_share,
+        mixing_share,
+        small_ref,
+        plane_lands,
+        deep_lands,
         held_sem,
         part_sem,
         out_sem,
+        feed_sem,
+        feed_send,
+        feed_recv,
+        spread_sem,
+        spread_far_send,
+        spread_far_recv,
+        spread_near_send,
+        spread_near_recv,
+        plane_send,
+        plane_recv,
+        deep_send,
+        deep_recv,
         row_send,
         row_recv,
+        mixed_sem,
         near_send,
         near_recv,
         far_send,
@@ -808,7 +922,7 @@
     ) = held
     low, f32 = jnp.bfloat16, jnp.float32
     tn = (((0,), (0,)), ((), ()))
-    place, deep = lax.axis_index("dp"), 4
+    place, deep, outers = lax.axis_index("dp"), 4, 4
     outer = lax.axis_index("outer")
     far, near = outer // 2, outer % 2
     row_id = {"mp": 1 - lax.axis_index("mp")}
@@ -819,11 +933,18 @@
         pltpu.make_async_copy(source, target, held_sem.at[n])
         for n, (source, target) in enumerate(zip(sources, held))
     ]
-    for copy in copies:
+    for copy in copies[:2]:
         copy.start()
     barrier = pltpu.get_barrier_semaphore()
-    for device in (row_id, far_id, near_id):
-        pl.semaphore_signal(barrier, inc=1, device_id=device, device_id_type=MESH)
+    plane = 2 * outers
+    me = lax.axis_index("mp") * outers + outer
+
+    def plane_id(step):
+        other = (me + step) % plane
+        return {"mp": other // outers, "outer": other % outers}
+
+    for step in range(1, plane):
+        pl.semaphore_signal(barrier, inc=1, device_id=plane_id(step), device_id_type=MESH)
     for step in range(1, deep):
         pl.semaphore_signal(
             barrier, inc=1, device_id={"dp": (place + step) % deep}, device_id_type=MESH
@@ -850,10 +971,27 @@
     ]
     loads[0].start()
     loads[1].start()
+    for copy in copies[2:]:
+        copy.start()
+    quarter = feed_keep.shape[1]
+    feed_copies = [
+        (
+            pltpu.make_async_copy(
+                feed_keep.at[k],
+                total_ref.at[slice(k * quarter, (k + 1) * quarter)],
+                feed_sem.at[k],
+            ),
+            pltpu.make_async_copy(feed_come.at[k], feed_in.at[k], feed_sem.at[2 + k]),
+        )
+        for k in range(2)
+    ]
+    for pair in feed_copies:
+        for copy in pair:
+            copy.start()
 
     copies[0].wait()
     copies[1].wait()
-    pl.semaphore_wait(barrier, deep + 2)
+    pl.semaphore_wait(barrier, plane + deep - 2)
     row_copies = []
     for n in range(blocks):
         made = lax.dot_general(grads_other[:, at[n]], project[...], tn, preferred_element_type=f32)
@@ -866,19 +1004,50 @@
         copy.start()
         row_copies.append(copy)
 
-    for n in range(2, 9):
+    copies[5].wait()
+    mixed_copy = remote(mixed_other, mixed_come, mixed_sem.at[0], mixed_sem.at[1], row_id)
+    mixed_copy.start()
+
+    piece = width // deep
+
+    def columns(place):
+        return pl.ds(pl.multiple_of(place * piece, piece), piece)
+
+    line_copies = []
+    for k in range(2):
+        for copy in feed_copies[k]:
+            copy.wait()
+        rows = slice(k * quarter, (k + 1) * quarter)
+        for step in range(1, deep):
+            target = (place + step) % deep
+            feed_line[k, step - 1] = (
+                total_ref[rows, columns(target)] + feed_in[k, :, columns(target)].astype(f32)
+            ).astype(low)
+            line_copies.append(
+                remote(
+                    feed_line.at[k, step - 1],
+                    feed_lands.at[k, step - 1],
+                    feed_send.at[k, step - 1],
+                    feed_recv.at[k, step - 1],
+                    {"dp": target},
+                )
+            )
+            line_copies[-1].start()
+        feed_share[k] = total_ref[rows, columns(place)] + feed_in[k, :, columns(place)].astype(f32)
+
+    for n in (2, 3, 4, 6, 7, 8):
         copies[n].wait()
     half = project_own.shape[0]
     few = mixing_own.shape[0]
     near_copies = []
     for n in range(half // height):
         rows = slice(half + n * height, half + (n + 1) * height)
-        project_sib[at[n], :] = jnp.dot(
+        total_ref[at[n], :] = jnp.dot(
             grads_own[rows, :], hidden_own[...], preferred_element_type=f32
         ) + jnp.dot(grads_other[rows, :], hidden_other[...], preferred_element_type=f32)
         near_copies.append(
             remote(
-                project_sib.at[at[n]],
+                total_ref.at[at[n]],
                 project_land.at[at[n]],
                 near_send.at[n],
                 near_recv.at[n],
@@ -886,11 +1055,17 @@
             )
         )
         near_copies[-1].start()
-    mixing_sib[...] = jnp.dot(
+    total_ref[half : half + few, :] = jnp.dot(
         mixed_own[few:, :], back_own[...], preferred_element_type=f32
     ) + jnp.dot(mixed_other[few:, :], back_other[...], preferred_element_type=f32)
     near_copies.append(
-        remote(mixing_sib, mixing_land, near_send.at[3], near_recv.at[3], near_id)
+        remote(
+            total_ref.at[slice(half, half + few)],
+            mixing_land,
+            near_send.at[3],
+            near_recv.at[3],
+            near_id,
+        )
     )
     near_copies[-1].start()
     for n in range(half // height):
@@ -922,7 +1097,6 @@
         if n + 2 < blocks:
             loads[blocks + n + 2].start()
 
-    line_copies = []
     for k, (own, come, line, lands) in enumerate(
         (
             (project_own, project_come, project_line, project_lands),
@@ -933,26 +1107,75 @@
         keep = pl.ds(pl.multiple_of(far * size, size), size)
         far_copies[k].wait()
         own[keep, :] = own[keep, :] + come[...].astype(f32)
-        piece = width // deep
         for step in range(1, deep):
             target = (place + step) % deep
-            line[step] = own[keep, pl.ds(pl.multiple_of(target * piece, piece), piece)].astype(low)
+            line[step - 1] = own[keep, columns(target)].astype(low)
             copy = remote(
-                line.at[step],
-                lands.at[step],
-                line_send.at[k, step],
-                line_recv.at[k, step],
+                line.at[step - 1],
+                lands.at[step - 1],
+                line_send.at[k, step - 1],
+                line_recv.at[k, step - 1],
                 {"dp": target},
             )
             copy.start()
             line_copies.append(copy)
 
+    shares = (feed_share.at[0], expand_share, project_share, mixing_share)
+
+    def place_in(k, near, far):
+        if k == 1:
+            return full_refs[k].at[:, pl.ds(pl.multiple_of((2 * near + far) * quarter, quarter), quarter)]
+        size = shares[k].shape[0]
+        return full_refs[k].at[pl.ds(pl.multiple_of((2 * near + far) * size, size), size)]
+
+    def spread(k):
+        if k < 2:
+            result, lands = feed_share[k], feed_lands.at[k]
+        else:
+            own, lands = ((project_own, project_lands), (mixing_own, mixing_lands))[k - 2]
+            size = shares[k].shape[0]
+            result = own[pl.ds(pl.multiple_of(far * size, size), size), columns(place)]
+        for copy in line_copies[3 * k : 3 * k + 3]:
+            copy.wait()
+        for step in range(1, deep):
+            result = result + lands[step - 1].astype(f32)
+        shares[k][...] = result.T if k == 1 else result
+        here = place_in(k, near, far)
+        copies = [
+            pltpu.make_async_copy(shares[k], here, spread_sem.at[k]),
+            remote(shares[k], here, spread_far_send.at[k], spread_far_recv.at[k], far_id),
+            remote(shares[k], here, spread_near_send.at[k, 0], spread_near_recv.at[k, 0], near_id),
+        ]
+        for copy in copies:
+            copy.start()
+        return copies, jnp.sum(result * result)
+
+    def pass_on(k, copies):
+        copies[1].wait()
+        there = place_in(k, near, 1 - far)
+        copy = remote(
+            there, there, spread_near_send.at[k, 1], spread_near_recv.at[k, 1], near_id
+        )
+        copy.start()
+        return copy
+
     copies[9].wait()
     gain = gain_ref[0:1]
     gain_sum = jnp.zeros((1, width), f32)
     bias_sum = jnp.zeros((1, width), f32)
-    out_copies = []
+    out_copies, spreads, passed = [], [], []
+    square = jnp.float32(0.0)
     for n in range(blocks):
+        if n == blocks - 2:
+            for k in range(2):
+                copies, more = spread(k)
+                spreads.append(copies)
+                square = square + more
+        if n == blocks - 1:
+            for k in range(2, 4):
+                copies, more = spread(k)
+                spreads.append(copies)
+                square = square + more
         row_copies[n].wait()
         if n >= 2:
             out_copies[n - 2].wait()
@@ -972,7 +1195,7 @@
             middle = jnp.mean(scaled, axis=1, keepdims=True)
             along = jnp.mean(scaled * normed, axis=1, keepdims=True)
             result = inverse * (scaled - middle - normed * along)
-            out_ref[n % 2, pl.ds(pl.multiple_of(i * small, small), small), :] = (
+            part_in[n % 2, pl.ds(pl.multiple_of(i * small, small), small), :] = (
                 back_own[rows, :].astype(f32) + result
             )
             gain_sum = gain_sum + jnp.sum(grad * normed, axis=0, keepdims=True)
@@ -981,36 +1204,51 @@
 
         gain_sum, bias_sum = lax.fori_loop(0, height // 64, some, (gain_sum, bias_sum))
         out_copies.append(
-            pltpu.make_async_copy(out_ref.at[n % 2], input_grad.at[at[n]], out_sem.at[n % 2])
+            pltpu.make_async_copy(part_in.at[n % 2], input_grad.at[at[n]], out_sem.at[n % 2])
         )
         out_copies[-1].start()
-    norm_grad[...] = jnp.zeros_like(norm_grad)
-    norm_grad[0:1] = gain_sum
-    norm_grad[1:2] = bias_sum
-    for copy in line_copies:
-        copy.wait()
-    for own, lands, share in (
-        (project_own, project_lands, project_share),
-        (mixing_own, mixing_lands, mixing_share),
-    ):
-        size, piece = share.shape
-        result = own[
-            pl.ds(pl.multiple_of(far * size, size), size),
-            pl.ds(pl.multiple_of(place * piece, piece), piece),
-        ]
-        for step in range(1, deep):
-            result = result + lands[step].astype(f32)
-        share[...] = result
+    for k in range(4):
+        passed.append(pass_on(k, spreads[k]))
+
+    small_ref[...] = jnp.full(small_ref.shape, square)
+    small_ref[0:1] = gain_sum
+    small_ref[1:2] = bias_sum
+
+    def everywhere(lands, send, recv, size, index, device):
+        copies = []
+        for step in range(1, size):
+            copy = remote(small_ref, lands.at[step], send.at[step], recv.at[step], device(step))
+            copy.start()
+            copies.append(copy)
+        lands[0] = small_ref[...]
+        for copy in copies:
+            copy.wait()
+        total = lands[index]
+        for at in range(1, size):
+            total = total + lands[(index + size - at) % size]
+        small_ref[...] = total
+
+    everywhere(plane_lands, plane_send, plane_recv, plane, me, plane_id)
+    everywhere(
+        deep_lands, deep_send, deep_recv, deep, place, lambda step: {"dp": (place + step) % deep}
+    )
+    small_sum[...] = small_ref[...]
+    for k in range(4):
+        spreads[k][0].wait()
+        spreads[k][2].wait()
+        passed[k].wait()
+    mixed_copy.wait()
     for copy in out_copies[-2:]:
         copy.wait()
 
 
-def closing(project, grads, hiddens, mixed, backs, inputs, parts, gain, after):
+def closing(project, grads, hiddens, mixed, backs, inputs, parts, feeds, gain, after):
     deep = 4
     low, f32 = jnp.bfloat16, jnp.float32
     tokens, width = inputs.shape
     half, few = grads[0].shape[0] // 2, mixed[0].shape[0] // 2
     piece = width // deep
+    quarter = feeds[0].shape[1]
     anywhere = pl.BlockSpec(memory_space=pl.ANY)
     here = lambda: pl.BlockSpec(memory_space=pltpu.VMEM)
     held = (
@@ -1029,13 +1267,21 @@
     space = pltpu.VMEM
     return pl.pallas_call(
         partial(closing_kernel, len(after)),
-        in_specs=[anywhere] * 12 + [here()] + [anywhere] * len(after),
-        out_specs=[anywhere, here(), here(), here()],
+        in_specs=[anywhere] * 14 + [here()] + [anywhere] * len(after),
+        out_specs=[anywhere, here()] + [anywhere] * 5,
         out_shape=[
             jax.ShapeDtypeStruct((tokens, width), f32),
             jax.ShapeDtypeStruct((8, width), f32),
-            jax.ShapeDtypeStruct((half // 2, piece), f32),
-            jax.ShapeDtypeStruct((few // 2, piece), f32),
+            jax.ShapeDtypeStruct(mixed[1].shape, low),
+        ]
+        + [
+            jax.ShapeDtypeStruct(shape, f32)
+            for shape in (
+                (4 * quarter, piece),
+                (piece, 4 * quarter),
+                (2 * half, piece),
+                (2 * few, piece),
+            )
         ],
         scratch_shapes=[space(v.shape, v.dtype) for v in held]
         + [
@@ -1043,26 +1289,46 @@
             space((tokens, width), f32),
             space((tokens, width), low),
             space((tokens, width), low),
-            space((2, 256, width), f32),
             space((half, width), f32),
             space((half, width), f32),
-            space((half, width), f32),
-            space((few, width), f32),
             space((few, width), f32),
             space((few, width), f32),
             space((half // 2, width), low),
             space((half // 2, width), low),
             space((few // 2, width), low),
             space((few // 2, width), low),
-            space((deep, half // 2, piece), low),
-            space((deep, half // 2, piece), low),
-            space((deep, few // 2, piece), low),
-            space((deep, few // 2, piece), low),
+            space((deep - 1, half // 2, piece), low),
+            space((deep - 1, half // 2, piece), low),
+            space((deep - 1, few // 2, piece), low),
+            space((deep - 1, few // 2, piece), low),
+            space((2, quarter, width), low),
+            space((2, deep - 1, quarter, piece), low),
+            space((2, deep - 1, quarter, piece), low),
+            space((2, quarter, piece), f32),
+            space((piece, quarter), f32),
+            space((half // 2, piece), f32),
+            space((few // 2, piece), f32),
+            space((8, width), f32),
+            space((8, 8, width), f32),
+            space((deep, 8, width), f32),
             sem((len(held),)),
             sem((2,)),
             sem((2,)),
+            sem((4,)),
+            sem((2, deep - 1)),
+            sem((2, deep - 1)),
+            sem((4,)),
+            sem((4,)),
+            sem((4,)),
+            sem((4, 2)),
+            sem((4, 2)),
+            sem((8,)),
+            sem((8,)),
+            sem((deep,)),
+            sem((deep,)),
             sem((tokens // 256,)),
             sem((tokens // 256,)),
+            sem((2,)),
             sem((4,)),
             sem((4,)),
             sem((2,)),
@@ -1074,128 +1340,36 @@
             collective_id=3, has_side_effects=True, vmem_limit_bytes=62 * 2**20
         ),
         cost_estimate=pl.CostEstimate(flops=2**20, bytes_accessed=2**20, transcendentals=0),
-    )(*held, *parts, gain, *after)
-
-
-def total_kernel(term_ref, out_ref, first, second, first_send, first_recv, second_send, second_recv):
-    split, outers, deep = first.shape[0] // 4, 4, second.shape[0]
-    plane = split * outers
-    place = lax.axis_index("dp")
-    me = lax.axis_index("mp") * outers + lax.axis_index("outer")
-
-    def plane_id(step):
-        other = (me + step) % plane
-        return {"mp": other // outers, "outer": other % outers}
-
-    def line_id(step):
-        return {"dp": (place + step) % deep}
-
-    barrier = pltpu.get_barrier_semaphore()
-    for step in range(1, plane):
-        pl.semaphore_signal(barrier, inc=1, device_id=plane_id(step), device_id_type=MESH)
-    for step in range(1, deep):
-        pl.semaphore_signal(barrier, inc=1, device_id=line_id(step), device_id_type=MESH)
-    pl.semaphore_wait(barrier, plane + deep - 2)
-
-    def exchange(source, slots, send, recv, size, device):
-        copies = []
-        for step in range(1, size):
-            copy = pltpu.make_async_remote_copy(
-                src_ref=source,
-                dst_ref=slots.at[step],
-                send_sem=send.at[step],
-                recv_sem=recv.at[step],
-                device_id=device(step),
-                device_id_type=MESH,
-            )
-            copy.start()
-            copies.append(copy)
-        slots[0] = source[...]
-        for copy in copies:
-            copy.wait()
-
-    exchange(term_ref, first, first_send, first_recv, plane, plane_id)
-    total = first[me]
-    for at in range(1, plane):
-        total = total + first[(me + plane - at) % plane]
-    out_ref[...] = total
-    exchange(out_ref, second, second_send, second_recv, deep, line_id)
-    total = second[place]
-    for at in range(1, deep):
-        total = total + second[(place + deep - at) % deep]
-    out_ref[...] = total
-
-
-def total_over_all(term, split, deep):
-    plane = split * 4
-    sem = pltpu.SemaphoreType.DMA
-    return pl.pallas_call(
-        total_kernel,
-        in_specs=[pl.BlockSpec(memory_space=pltpu.VMEM)],
-        out_specs=pl.BlockSpec(memory_space=pltpu.VMEM),
-        out_shape=jax.ShapeDtypeStruct(term.shape, term.dtype),
-        scratch_shapes=[
-            pltpu.VMEM((plane, *term.shape), term.dtype),
-            pltpu.VMEM((deep, *term.shape), term.dtype),
-            sem((plane,)),
-            sem((plane,)),
-            sem((deep,)),
-            sem((deep,)),
-        ],
-        compiler_params=pltpu.CompilerParams(collective_id=2, has_side_effects=True),
-    )(term)
+    )(*held, *parts, *feeds, gain, *after)
 
 
 class Paired:
     def __init__(self):
-        outer = lax.axis_index("outer")
-        self.far, self.near = outer // 2, outer % 2
         self.place = lax.axis_index("dp")
         self.deep = lax.axis_size("dp")
 
     def gather(self, own, cut, depth):
-        own = lax.all_gather(own, "dp", axis=depth, tiled=True)
-        return jnp.concatenate([own, swap(own, "outer", 1)], axis=cut)
-
-    def gather_few(self, own, cut, depth):
+        return lax.all_gather(own, "dp", axis=depth, tiled=True)
+
+    def gather_few(self, own):
+        size = self.deep
+        return [
+            lax.ppermute(own, "dp", [(i, (i + step) % size) for i in range(size)])
+            for step in range(1, size)
+        ]
+
+    def placed(self, own, come, depth):
         wide = list(own.shape)
         piece = wide[depth]
         wide[depth] *= self.deep
         out = jnp.zeros(wide, own.dtype)
-        for step in range(self.deep):
-            pairs = [(i, (i + step) % self.deep) for i in range(self.deep)]
-            come = lax.ppermute(own, "dp", pairs) if step else own
+        for step, one in enumerate([own, *come]):
             at = lax.rem(self.place - step + self.deep, self.deep)
-            out = lax.dynamic_update_slice_in_dim(out, come, at * piece, depth)
-        return jnp.concatenate([out, swap(out, "outer", 1)], axis=cut)
-
-    def pair_sum(self, own, sibling, cut):
-        own = own + swap(sibling, "outer", 1)
-        half = own.shape[cut] // 2
-        keep = lax.dynamic_slice_in_dim(own, self.far * half, half, cut)
-        send = lax.dynamic_slice_in_dim(own, (1 - self.far) * half, half, cut)
-        send = send.astype(jnp.bfloat16)
-        return keep, swap(send, "outer", 2), send
-
-    def line_sum(self, keep, come, depth):
-        keep = keep + come.astype(jnp.float32)
-        piece = keep.shape[depth] // self.deep
-
-        def part(at):
-            return lax.dynamic_slice_in_dim(keep, at * piece, piece, depth)
-
-        result = part(self.place)
-        for step in range(1, self.deep):
-            target = lax.rem(self.place + step, self.deep)
-            pairs = [(i, (i + step) % self.deep) for i in range(self.deep)]
-            result = result + lax.ppermute(
-                part(target).astype(jnp.bfloat16), "dp", pairs
-            ).astype(jnp.float32)
-        return result
-
-    def spread(self, share, cut):
-        pair = ordered(self.far, share, swap(share, "outer", 2), cut)
-        return ordered(self.near, pair, swap(pair, "outer", 1), cut)
+            out = lax.dynamic_update_slice_in_dim(out, one, at * piece, depth)
+        return out
+
+    def paired(self, half, cut):
+        return jnp.concatenate([half, swap(half, "outer", 1)], axis=cut)
 
 
 def local(
@@ -1232,7 +1406,7 @@
     project_flat = project_master.transpose(1, 2, 0).reshape(heads_here * 3 * HD, -1)
     mixing_flat = mixing_master.reshape(heads_here * HD, mixing_master.shape[2])
     masters = (project_flat, mixing_flat, expand_master, shrink_master)
-    cuts, depths = (0, 0, 1, 0), (1, 1, 0, 1)
+    depths = (1, 1, 0, 1)
     rows_local = inputs[0].astype(jnp.float32)
     begins, places = layout(lengths[0], count)
     cosine, sine = turns(places)
@@ -1247,10 +1421,14 @@
             inputs[0],
             cotangent[0],
         )
+        most = most_of(width)
+        other_back = lax.dynamic_update_slice(
+            other_back, swap(cotangent[0, most:], "mp", 1), (most, 0)
+        )
         backs = [cotangent[0], other_back]
         shrink = shrink.reshape(-1, shrink.shape[2])
-        project = plan.gather(project, 0, 1)
-        mixing = plan.gather_few(mixing, 0, 1)
+        project_half = plan.gather(project, 0, 1)
+        mixing_come = plan.gather_few(mixing)
         hiddens = [hidden_local, swap(hidden_local, "mp", 1)]
     else:
         norm_weight = lax.all_gather(norm_master.astype(jnp.bfloat16), "dp", axis=1, tiled=True)
@@ -1273,15 +1451,13 @@
         *grads, hidden_own, branch_own = feed(
             hiddens[0], backs[0], expand, shrink, (), jnp.float32
         )
-        expand_grad, shrink_grad, hidden_other, branch_other = feed(
+        project = plan.paired(follow(project_half, branch_own), 0)
+        mixing_come = [follow(v, branch_own) for v in mixing_come]
+        mixing = plan.paired(plan.placed(mixing, mixing_come, 1), 0)
+        feed_keep, feed_away, _, hidden_other, branch_other = feed(
             hiddens[1], backs[1], expand, shrink, grads, jnp.bfloat16
         )
-        hidden_parts = [hidden_own, hidden_other]
-        half = expand_grad.shape[1] // 2
-        shrink_keep, shrink_come, shrink_sent = plan.pair_sum(shrink_grad[:half], shrink_grad[half:], 0)
-        expand_keep, expand_come, expand_sent = plan.pair_sum(
-            expand_grad[:, :half], expand_grad[:, half:], 1
-        )
+        feed_come = swap(feed_away, "outer", 2)
         branch_come = swap(branch_other, "mp", 1)
         mixing_other = swap(mixing, "mp", 1)
         projected = [product("td,ed->et", hidden, project) for hidden in hiddens]
@@ -1293,9 +1469,9 @@
             cosine,
             sine,
             position,
-            (shrink_sent, expand_sent),
-        )
-        input_grad, norm_terms, project_sum, mixing_sum = closing(
+            (feed_away, branch_other),
+        )
+        input_grad, small_sum, mixed_come, shrink_sum, expand_sum, project_sum, mixing_sum = closing(
             project,
             projected_grads,
             hiddens,
@@ -1303,17 +1479,15 @@
             backs,
             inputs[0],
             (hidden_own, hidden_other),
+            (feed_keep, feed_come),
             norm_weight,
-            (shrink_come, expand_come, branch_come),
-        )
-        norm_terms = norm_terms[:2]
-        mixed_come = swap(follow(mixed[1], norm_terms), "mp", 1)
-        shrink_sum = plan.line_sum(shrink_keep, shrink_come, 1)
-        expand_sum = plan.line_sum(expand_keep, expand_come, 0)
+            (branch_come,),
+        )
+        mixed_own = follow(mixed[0], small_sum)
         branch = (
             branch_own
             + branch_come.astype(jnp.float32)
-            + product("ft,fd->td", mixed[0], mixing)
+            + product("ft,fd->td", mixed_own, mixing)
             + product("ft,fd->td", mixed_come, mixing_other)
         )
     else:
@@ -1356,22 +1530,18 @@
     input_grad = input_grad[None]
     block_out = (rows_local + branch).astype(jnp.bfloat16)[None]
     sums = (project_sum, mixing_sum, expand_sum, shrink_sum)
-    own_square = sum(jnp.sum(v * v) for v in sums)
     if not paired:
-        own_square = own_square / lax.axis_size("outer")
-    norm_terms = jnp.concatenate([norm_terms, jnp.full((1, D), own_square)]).reshape(-1, 128)
-    if paired:
-        norm_all = total_over_all(norm_terms, split, deep)
-    else:
-        norm_all = lax.psum(norm_terms, ("mp", "dp", "outer"))
-    norm_all = norm_all.reshape(3, D)
-    norm_full = norm_all[:2]
-    grad_norm = jnp.sqrt(norm_all[2, 0] + jnp.sum(norm_full * norm_full))
+        own_square = sum(jnp.sum(v * v) for v in sums) / lax.axis_size("outer")
+        small_sum = lax.psum(
+            jnp.concatenate([norm_terms, jnp.full((1, D), own_square)]), ("mp", "dp", "outer")
+        )
+    norm_full = small_sum[:2]
+    grad_norm = jnp.sqrt(small_sum[2, 0] + jnp.sum(norm_full * norm_full))
     factor = clip_level / jnp.maximum(grad_norm, clip_level)
     norm_gradient = lax.dynamic_slice_in_dim(
         norm_full, lax.axis_index("dp") * (D // deep), D // deep, 1
     )
-    gradients = [plan.spread(v, cut) if paired else v for v, cut in zip(sums, cuts)]
+    gradients = list(sums)
     gradients[0] = gradients[0].reshape(heads_here, 3 * HD, -1).transpose(2, 0, 1)
     gradients[1] = gradients[1].reshape(mixing_master.shape)
     states = (

time: 539 us -> 477 us (0.88)
  starting transfers between devices: 32.8 us -> 10.4 us
  other arithmetic: 42.6 us -> 25 us
  matrix products: 37 us -> 29.1 us
  waiting for transfers between devices: 21.1 us -> 13.8 us
  local copies, waits for them, and re-layouts: 30.7 us -> 24 us
    pallas_call x1, Pallas kernels: 78.1 us -> 102 us  [closing(): pl.pallas_call(partial(closing_kernel, len(after)), in_specs=[anywhere] *...]
    pallas_call x3 -> x2, Pallas kernels: 110 us -> 94.2 us  [feed(): pl.pallas_call(partial(feed_kernel, exchange), grid=(steps,), in_specs=[w...]
    ppermute x18 -> x7, starting transfers between devices: 21.6 us -> 6.54 us  [swap(): return lax.ppermute(array, axis, [(i, i ^ bit) for i in range(size)])]
    add x4 -> x0, other arithmetic: 10.3 us -> none  [the longest x2 7.94 us: pair_sum(): own = own + swap(sibling, 'outer', 1)]
    pallas_call x1, Pallas kernels: 67.2 us -> 58.3 us  [opening(): pl.pallas_call(opening_kernel, in_specs=[here() for _ in range(6)] + [pl....]
    slice x4 -> x1, local copies, waits for them, and re-layouts: 10 us -> 1.19 us  [local(): grad_norm = jnp.sqrt(small_sum[2, 0] + jnp.sum(norm_full * norm_full))]
    ppermute x9 -> x3, waiting for transfers between devices: 7.92 us -> 0.01 us  [gather_few(): lax.ppermute(own, 'dp', [(i, (i + step) % size) for i in range(size)])]
    dot_general x6, matrix products: 37 us -> 29.1 us  [product(): return jnp.einsum(pattern, left, right, preferred_element_type=jnp.float32)]
  transfers between devices with their start and end apart: 28 -> 11, of which waited for: 6 -> 1; matrix products, arithmetic and copies ran while one was open for 17% -> 12% of each run, Pallas kernels for 53% -> 62%
where the time goes in v6:
time: 477 us; the launch traced here: 469 us
  Pallas kernels  349 us (73%)
  matrix products  29.1 us (6%)
  other arithmetic  25 us (5%)
  local copies, waits for them, and re-layouts  24 us (5%)
  between operations  17.5 us (4%)
  waiting for transfers between devices  13.8 us (3%)
  starting transfers between devices  10.4 us (2%)
    pallas_call x1, Pallas kernels, closing(): pl.pallas_call(partial(closing_kernel, len(after)), in_specs=[anywhere] *...  102 us
    pallas_call x1, Pallas kernels, attend(): pl.pallas_call(partial(attend_kernel, together, parts, len(after)), grid_...  95 us
    pallas_call x2, Pallas kernels, feed(): pl.pallas_call(partial(feed_kernel, exchange), grid=(steps,), in_specs=[w...  94.2 us
    pallas_call x1, Pallas kernels, opening(): pl.pallas_call(opening_kernel, in_specs=[here() for _ in range(6)] + [pl....  58.3 us
    dot_general x6, matrix products, product(): return jnp.einsum(pattern, left, right, preferred_element_type=jnp.float32)  29.1 us
    convert_element_type x5, other arithmetic, adam_update(): return (master_new, first_new, second_new, master_new.astype(jnp.bfloat16))  16.3 us
    unnamed x80, local copies, waits for them, and re-layouts  16.3 us
    ppermute x7, waiting for transfers between devices, swap(): return lax.ppermute(array, axis, [(i, i ^ bit) for i in range(size)])  13.7 us
  transfers between devices with their start and end apart: 11, of which 1 were waited for; matrix products, arithmetic and copies ran while one was open for 12% of the time, Pallas kernels for 62%

profile of v6, /device:TPU:0, one launch (start us, length us, event | category | flops | bytes accessed | tf_op | source)
XLA Modules:
  0.0 468.9 jit_solution(2977786164791628111)
XLA Ops:
  7.2 1.6 copy-done.4
  8.8 1.6 copy-done.6
  10.4 1.4 copy-done.8
  11.8 1.0 copy-done.12
  12.9 0.7 copy-done.16
  13.6 58.3 %shard_map.353 = (bf16[2,1024,1024]{2,1,0:T(8,128)(2,1)}, bf16[2,1024,1024]{2,1,0:T(8,128)(2,1)}, bf16[768,256]{1,0:T(8,128)(2,1)}, bf16[256,256]{1,0:T(8,128)(2...) custom-call(f32[256,2048]{1,0:T(8,128)S(1)} %copy-done.6, ...), custom_call_target="tpu_custom_call" | custom-call | bytes 1048576 | tf_op jit(solution)/shard_map/pallas_call | solution.py:810
  71.8 1.5 copy-done.2
  73.3 0.6 copy-done.15
  74.0 1.8 collective-permute-start
  75.8 3.1 collective-permute-start.5
  78.9 0.7 collective-permute-start.6
  79.6 1.9 slice_bitcast_fusion
  82.0 0.6 subtract_convert_fusion
  82.6 44.9 %shard_map.354 = (f32[2048,1024]{1,0:T(8,128)}, f32[2048,1024]{1,0:T(8,128)}, f32[1280,1024]{1,0:T(8,128)}, f32[1280,1024]{1,0:T(8,128)}) custom-call(bf16[1280,1024]{1,0:T(8,128)(2,1)} %copy-done, bf16[1280,1024]{1,0:T(8,128)(2,1)} %bitcast.33, bf16[2,1024,1024]{2,1,0:T(8,128)(2,1)} %get-tuple-element.55.expand_ref, bf16[2048,1024]{1,0:T(8,128)(2,1)} %bitcast.37), custom_call_target="tpu_custom_call" | custom-call | flops 1048576 | bytes 1048576 | tf_op jit(solution)/shard_map/pallas_call | solution.py:502
  127.7 0.9 constant_dynamic-update-slice_fusion.2
  128.8 0.5 collective-permute-start.3
  129.2 1.4 multiply_sine_fusion
  130.8 13.7 %collective-permute-done.1 = bf16[256,1024]{1,0:T(8,128)(2,1)} collective-permute-done((bf16[256,1024]{1,0:T(8,128)(2,1)}, bf16[256,1024]{1,0:T(8,128)(2,1)}, u32[]{:S(2)}, u32[]{:S(2)}) %collective-permute-start.1) | collective-permute-done | bytes 524320 | tf_op jit(solution)/shard_map/ppermute | solution.py:322
  144.5 1.9 constant_dynamic-update-slice_fusion.6.back_ref.refs_6_
  146.4 2.1 pad_maximum_fusion
  148.5 1.7 collective-permute-start.9
  150.2 49.2 %shard_map.355 = (f32[2,512,1024]{2,1,0:T(8,128)}, bf16[2,512,1024]{2,1,0:T(8,128)(2,1)}, f32[2,2,512,1024]{3,2,1,0:T(8,128)}, f32[1280,1024]{1,0:T(8,128)}, bf16[1280,1024]{1,0:T(8,128)(2,1)}) custom-call(bf16[1280,1024]{1,0:T(8,128)(2,1)} %collective-permute-done.hidden_ref.refs_2_, ...), custom_call_target="tpu_custom_call" | custom-call | flops 1048576 | bytes 1048576 | tf_op jit(solution)/shard_map/pallas_call | solution.py:502
  199.9 2.8 convolution_convert_fusion.refs_4_
  202.7 2.8 convolution_convert_fusion.1.refs_3_
  205.5 1.8 collective-permute-start.8
  207.5 1.7 constant_dynamic-update-slice_fusion.project_hbm
  209.1 0.5 copy-done.1
  209.6 6.4 %fusion.19.refs_1_ = f32[1536,1280]{1,0:T(8,128)} fusion(bf16[1536,1024]{1,0:T(8,128)(2,1)S(1)} %constant_dynamic-update-slice_fusion.project_hbm, bf16[1280,1024]{1,0:T(8,128)(2,1)S(1)} %copy-done.1), kind=kOutput, calls=%fused_computation.58 | convolution fusion | flops 4026531840 | bytes 13631488 | tf_op jit(solution)/shard_map/td,ed->et/dot_general | solution.py:308
  216.1 8.1 %fusion.20.refs_2_ = f32[1536,1280]{1,0:T(8,128)} fusion(bf16[1536,1024]{1,0:T(8,128)(2,1)S(1)} %constant_dynamic-update-slice_fusion.project_hbm, bf16[1280,1024]{1,0:T(8,128)(2,1)} %collective-permute-done.hidden_ref.refs_2_), kind=kOutput, calls=%fused_computation.59 | convolution fusion | flops 4026531840 | bytes 13631488 | tf_op jit(solution)/shard_map/td,ed->et/dot_general | solution.py:308
  224.2 95.0 %shard_map.356 = (bf16[512,1280]{1,0:T(8,128)(2,1)S(1)}, bf16[512,1280]{1,0:T(8,128)(2,1)S(1)}, bf16[1536,1280]{1,0:T(8,128)(2,1)}, bf16[1536,1280]{1,0:T(8,128)(2,1)}) custom-call(s32[11]{0:T(128)S(1)} %pad_add_fusion.refs_0_, f32[1536,1280]{1,0:T(8,128)} %fusion.19.refs_1_, f32[1536,1280]{1,0:T(8,128)} %fusion.20.refs_2_, ...), custom_call_target="tpu_custom_call" | custom-call | flops 1048576 | bytes 1048576 | tf_op jit(solution)/shard_map/pallas_call | solution.py:251
  319.2 1.0 copy-done.10
  320.3 1.1 copy-done.14
  321.3 101.6 %shard_map.357 = (f32[1280,1024]{1,0:T(8,128)}, f32[8,1024]{1,0:T(8,128)}, bf16[512,1280]{1,0:T(8,128)(2,1)}, f32[2048,256]{1,0:T(8,128)}, f32[256,2048]{1,0:T(8...) custom-call(bf16[1536,1024]{1,0:T(8,128)(2,1)} %copy-done.20, bf16[1536,1280]{1,0:T(8,128)(2,1)} %get-tuple-element.70.refs_0_, ...), custom_call_target="tpu_custom_call" | custom-call | flops 1048576 | bytes 1048576 | tf_op jit(solution)/shard_map/pallas_call | solution.py:1268
  423.0 1.4 fusion.18
  424.3 1.2 slice.14
  426.9 1.2 broadcast_multiply_fusion.1
  428.2 1.7 broadcast_multiply_fusion
  429.9 6.4 %fusion.10 = (bf16[2048,256]{1,0:T(8,128)(2,1)}, f32[2048,256]{1,0:T(8,128)}, f32[2048,256]{1,0:T(8,128)}, f32[2048,256]{1,0:T(8,128)}) fusion(f32[2048,256]{1,0:T(8,128)S(1)} %copy-done.5, f32[2048,256]{1,0:T(8,128)} %get-tuple-element.84, f32[]{:T(128)S(6)} %div.94, f32[2048,256]{1,0:T(8,128)S(1)} %copy-done.21, f32[2048,256]{1,0:T(8,128)} %param.32), kind=kLoop, calls=%fused_computation.53 | loop fusion | flops 8912896 | bytes 15728644 | tf_op jit(solution)/shard_map/convert_element_type | solution.py:304
  436.3 1.5 fusion.14
  437.8 0.5 copy-done.9
  438.3 0.5 copy-done.27
  438.9 3.3 fusion.16
  442.2 2.8 fusion.7
  445.0 0.6 fusion.8
  445.6 4.5 fusion.12
  450.2 1.0 copy-done.19
  451.8 6.3 %fusion = bf16[1,1280,1024]{2,1,0:T(8,128)(2,1)} fusion(f32[1280,1024]{1,0:T(8,128)S(1)} %fusion.7, f32[1280,1024]{1,0:T(8,128)S(1)} %bitcast.41, bf16[1280,1024]{1,0:T(8,128)(2,1)} %collective-permute-done.2.refs_14_, bf16[1,1280,1024]{2,1,0:T(8,128)(2,1)S(1)} %copy-done.19, bf16[512,1280]{1,0:T(8,128)(2,1)S(1)} %copy-done.29, ...), kind=kOutput, calls=%fused_computation.5 | convolution fusion | flops 1351352320 | bytes 20709376 | tf_op jit(solution)/shard_map/ft,fd->td/dot_general | solution.py:308
  458.1 2.4 copy.48
  (95 shorter events, 2.2 us)
Async XLA Ops:
  7.2 121.6 %all-gather.2.cloned.1.call-start = ((), (), s32[]{:S(2)}) async-start(), calls=%async_computation | async-start | bytes 1966080 | tf_op jit(solution)/shard_map/all_gather | solution.py:1352
  7.2 1.6 copy-start.4
  8.8 1.6 copy-start.6
  10.4 1.4 copy-start.8
  11.8 1.0 copy-start.12
  13.6 68.2 %copy-start.34 = (s32[1,12]{1,0:T(1,128)S(1)}, s32[1,12]{1,0:T(1,128)}, u32[]{:S(2)}) copy-start(s32[1,12]{1,0:T(1,128)} %param.20) | copy-start | bytes 148
  71.8 1.5 copy-start.2
  73.9 8.7 %copy-start = (bf16[1280,1024]{1,0:T(8,128)(2,1)}, bf16[1280,1024]{1,0:T(8,128)(2,1)S(1)}, u32[]{:S(2)}) copy-start(bf16[1280,1024]{1,0:T(8,128)(2,1)S(1)} %get-tuple-element.54.hidden_ref.refs_3_) | copy-start | bytes 7864324
  74.0 76.3 %collective-permute-start = (bf16[1280,1024]{1,0:T(8,128)(2,1)S(1)}, bf16[1280,1024]{1,0:T(8,128)(2,1)}, u32[]{:S(2)}, u32[]{:S(2)}) collective-permute-start(bf16[1280,1024]{1,0:T(8,128)(2,1)S(1)} %get-tuple-element.54.hidden_ref.refs_3_), channel_id=1, source_target_pairs={{0,16},{16,0},{1,17},{17,1},{2,18},{18,2},{3,19},{19,3},{4,20},{20... | collective-permute-start | bytes 7864328 | tf_op jit(solution)/shard_map/ppermute | solution.py:322
  75.8 51.9 %collective-permute-start.4 = (bf16[256,256]{1,0:T(8,128)(2,1)S(1)}, bf16[256,256]{1,0:T(8,128)(2,1)S(1)}, u32[]{:S(2)}, u32[]{:S(2)}) collective-permute-start(bf16[256,256]{1,0:T(8,128)(2,1)S(1)} %get-tuple-element.64), channel_id=1, source_target_pairs={{0,4},{4,8},{8,12},{12,0},{1,5},{5,9},{9,13},{13,1},{2,6},{6,10},{... | collective-permute-start | bytes 393224 | tf_op jit(solution)/shard_map/ppermute | solution.py:1357
  75.8 51.9 %collective-permute-start.5 = (bf16[256,256]{1,0:T(8,128)(2,1)S(1)}, bf16[256,256]{1,0:T(8,128)(2,1)S(1)}, u32[]{:S(2)}, u32[]{:S(2)}) collective-permute-start(bf16[256,256]{1,0:T(8,128)(2,1)S(1)} %get-tuple-element.64), channel_id=1, source_target_pairs={{0,8},{4,12},{8,0},{12,4},{1,9},{5,13},{9,1},{13,5},{2,10},{6,14},... | collective-permute-start | bytes 393224 | tf_op jit(solution)/shard_map/ppermute | solution.py:1357
  78.9 48.8 %collective-permute-start.6 = (bf16[256,256]{1,0:T(8,128)(2,1)S(1)}, bf16[256,256]{1,0:T(8,128)(2,1)}, u32[]{:S(2)}, u32[]{:S(2)}) collective-permute-start(bf16[256,256]{1,0:T(8,128)(2,1)S(1)} %get-tuple-element.64), channel_id=1, source_target_pairs={{0,12},{4,0},{8,4},{12,8},{1,13},{5,1},{9,5},{13,9},{2,14},{6,2},{... | collective-permute-start | bytes 393224 | tf_op jit(solution)/shard_map/ppermute | solution.py:1357
  81.5 63.0 %collective-permute-start.1 = (bf16[256,1024]{1,0:T(8,128)(2,1)}, bf16[256,1024]{1,0:T(8,128)(2,1)}, u32[]{:S(2)}, u32[]{:S(2)}) collective-permute-start(bf16[256,1024]{1,0:T(8,128)(2,1)} %slice_bitcast_fusion), channel_id=1, source_target_pairs={{0,16},{16,0},{1,17},{17,1},{2,18},{18,2},{3,19},{19,3},{4,20},{20... | collective-permute-start | bytes 1572872 | tf_op jit(solution)/shard_map/ppermute | solution.py:322
  128.6 17.7 %collective-permute-start.7 = (bf16[256,1024]{1,0:T(8,128)(2,1)S(1)}, bf16[256,1024]{1,0:T(8,128)(2,1)}, u32[]{:S(2)}, u32[]{:S(2)}) collective-permute-start(bf16[256,1024]{1,0:T(8,128)(2,1)S(1)} %constant_dynamic-update-slice_fusion.2), channel_id=1, source_target_pairs={{0,1},{1,0},{2,3},{3,2},{4,5},{5,4},{6,7},{7,6},{8,9},{9,8},{10,11... | collective-permute-start | bytes 1572872 | tf_op jit(solution)/shard_map/ppermute | solution.py:322
  128.8 78.7 %collective-permute-start.3 = (bf16[768,1024]{1,0:T(8,128)(2,1)}, bf16[768,1024]{1,0:T(8,128)(2,1)}, u32[]{:S(2)}, u32[]{:S(2)}) collective-permute-start(bf16[768,1024]{1,0:T(8,128)(2,1)} %all-gather.2.cloned.1.call-done), channel_id=1, source_target_pairs={{0,1},{1,0},{2,3},{3,2},{4,5},{5,4},{6,7},{7,6},{8,9},{9,8},{10,11... | collective-permute-start | bytes 4718600 | tf_op jit(solution)/shard_map/ppermute | solution.py:322
  148.5 301.7 %collective-permute-start.9 = (bf16[512,1024]{1,0:T(8,128)(2,1)}, bf16[512,1024]{1,0:T(8,128)(2,1)}, u32[]{:S(2)}, u32[]{:S(2)}) collective-permute-start(bf16[512,1024]{1,0:T(8,128)(2,1)} %pad_maximum_fusion), channel_id=1, source_target_pairs={{0,16},{16,0},{1,17},{17,1},{2,18},{18,2},{3,19},{19,3},{4,20},{20... | collective-permute-start | bytes 3145736 | tf_op jit(solution)/shard_map/ppermute | solution.py:322
  150.2 49.6 %copy-start.3 = (bf16[1280,1024]{1,0:T(8,128)(2,1)S(1)}, bf16[1280,1024]{1,0:T(8,128)(2,1)}, u32[]{:S(2)}) copy-start(bf16[1280,1024]{1,0:T(8,128)(2,1)} %constant_dynamic-update-slice_fusion.6.back_ref.refs_6_) | copy-start | bytes 7864324
  199.5 3.2 copy-start.18
  199.5 121.9 %collective-permute-start.2 = (bf16[1280,1024]{1,0:T(8,128)(2,1)}, bf16[1280,1024]{1,0:T(8,128)(2,1)}, u32[]{:S(2)}, u32[]{:S(2)}) collective-permute-start(bf16[1280,1024]{1,0:T(8,128)(2,1)} %get-tuple-element.61.refs_9_), channel_id=1, source_target_pairs={{0,16},{16,0},{1,17},{17,1},{2,18},{18,2},{3,19},{19,3},{4,20},{20... | collective-permute-start | bytes 7864328 | tf_op jit(solution)/shard_map/ppermute | solution.py:322
  202.7 2.8 copy-start.25
  202.7 4.6 copy-start.26
  205.5 115.9 %collective-permute-start.8 = (bf16[2,512,1024]{2,1,0:T(8,128)(2,1)S(1)}, bf16[2,512,1024]{2,1,0:T(8,128)(2,1)}, u32[]{:S(2)}, u32[]{:S(2)}) collective-permute-start(bf16[2,512,1024]{2,1,0:T(8,128)(2,1)S(1)} %copy-done.25), channel_id=1, source_target_pairs={{0,2},{1,3},{2,0},{3,1},{4,6},{5,7},{6,4},{7,5},{8,10},{9,11},{10,... | collective-permute-start | bytes 6291464 | tf_op jit(solution)/shard_map/ppermute | solution.py:322
  207.4 2.2 copy-start.1
  209.6 6.4 %copy-start.20 = (bf16[1536,1024]{1,0:T(8,128)(2,1)}, bf16[1536,1024]{1,0:T(8,128)(2,1)S(1)}, u32[]{:S(2)}) copy-start(bf16[1536,1024]{1,0:T(8,128)(2,1)S(1)} %constant_dynamic-update-slice_fusion.project_hbm) | copy-start | bytes 9437188
  319.2 1.1 copy-start.10
  320.3 1.1 copy-start.14
  426.9 2.9 copy-start.5
  426.9 2.9 copy-start.21
  429.9 6.4 %copy-start.13 = (f32[8,64,256]{2,1,0:T(8,128)S(1)}, f32[8,64,256]{2,1,0:T(8,128)}, u32[]{:S(2)}) copy-start(f32[8,64,256]{2,1,0:T(8,128)} %param.24) | copy-start | bytes 1572868
  429.9 6.4 %copy-start.30 = (f32[8,64,256]{2,1,0:T(8,128)S(1)}, f32[8,64,256]{2,1,0:T(8,128)}, u32[]{:S(2)}) copy-start(f32[8,64,256]{2,1,0:T(8,128)} %param.25) | copy-start | bytes 1572868
  429.9 6.4 %copy-start.31 = (f32[8,64,256]{2,1,0:T(8,128)S(1)}, f32[8,64,256]{2,1,0:T(8,128)}, u32[]{:S(2)}) copy-start(f32[8,64,256]{2,1,0:T(8,128)} %param.26) | copy-start | bytes 1572868
  429.9 7.9 %copy-start.28 = (f32[256,8,192]{0,2,1:T(8,128)S(1)}, f32[256,8,192]{0,2,1:T(8,128)}, u32[]{:S(2)}) copy-start(f32[256,8,192]{0,2,1:T(8,128)} %param.23) | copy-start | bytes 4718596
  436.3 2.0 copy-start.9
  436.3 2.5 copy-start.27
  438.8 3.3 copy-start.11
  438.8 6.7 %copy-start.24 = (f32[256,2048]{1,0:T(8,128)S(1)}, f32[256,2048]{1,0:T(8,128)}, u32[]{:S(2)}) copy-start(f32[256,2048]{1,0:T(8,128)} %get-tuple-element.83) | copy-start | bytes 6291460
  442.1 2.8 copy-start.17
  442.1 2.8 copy-start.32
  442.1 2.8 copy-start.33
  442.1 3.5 copy-start.7
  442.1 3.4 copy-start.22
  442.2 3.4 copy-start.23
  445.6 4.6 slice-start
  445.6 5.6 %copy-start.19 = (bf16[1,1280,1024]{2,1,0:T(8,128)(2,1)S(1)}, bf16[1,1280,1024]{2,1,0:T(8,128)(2,1)}, u32[]{:S(2)}) copy-start(bf16[1,1280,1024]{2,1,0:T(8,128)(2,1)} %param.18) | copy-start | bytes 7864324
  445.6 5.8 %slice-start.1 = ((s8[5242880]{0:T(1024)(128)(4,1)}), s8[1048576]{0:T(1024)(128)(4,1)S(1)}, s32[]{:S(2)}) async-start(s8[5242880]{0:T(1024)(128)(4,1)} %bitcast.40), calls=%async_computation.2 | async-start | bytes 2097152
  445.6 6.2 %copy-start.29 = (bf16[512,1280]{1,0:T(8,128)(2,1)S(1)}, bf16[512,1280]{1,0:T(8,128)(2,1)}, u32[]{:S(2)}) copy-start(bf16[512,1280]{1,0:T(8,128)(2,1)} %get-tuple-element.79) | copy-start | bytes 3932164
  450.2 7.9 %slice-start.2 = ((s8[5242880]{0:T(1024)(128)(4,1)}), s8[4194304]{0:T(1024)(128)(4,1)S(1)}, s32[]{:S(2)}) async-start(s8[5242880]{0:T(1024)(128)(4,1)} %bitcast.42), calls=%async_computation.3 | async-start | bytes 8388608
  451.8 6.3 %slice-start.3 = ((s8[5242880]{0:T(1024)(128)(4,1)}), s8[1048576]{0:T(1024)(128)(4,1)S(1)}, s32[]{:S(2)}) async-start(s8[5242880]{0:T(1024)(128)(4,1)} %bitcast.42), calls=%async_computation.4 | async-start | bytes 2097152
  (2 other events, 1.3 us)
Sparse Core Ops, SparseCore 0:
  74.1 44.0 all-gather.1

commit v7 on v6

--- a/solution.py
+++ b/solution.py
@@ -73,7 +73,6 @@
     turn = facts[blocks]
     half = ROT // 2
     scale = HD ** (-0.5)
-    nt = (((1,), (1,)), ((), ()))
 
     def place_of(part):
         if parts == 1:
@@ -127,6 +126,8 @@
         lowest = facts[i]
         queries = [query_ref[h, :, columns] for h in range(together)]
         backs = [back_ref[h, :, columns] for h in range(together)]
+        query_rows = [queries[h].T for h in range(together)]
+        back_rows = [backs[h].T for h in range(together)]
 
         def in_pairs(body, carry):
             twos = lax.div(i + 1 - lowest, 2)
@@ -194,11 +195,11 @@
                     query_grad = query_grad + jnp.dot(
                         key_columns_ref[h, :, rows], score_grad, preferred_element_type=jnp.float32
                     )
-                    value_grad_ref[h, :, rows] += lax.dot_general(
-                        backs[h], shares, nt, preferred_element_type=jnp.float32
+                    value_grad_ref[h, rows, :] += jnp.dot(
+                        shares, back_rows[h], preferred_element_type=jnp.float32
                     )
-                    key_grad_ref[h, :, rows] += lax.dot_general(
-                        queries[h], score_grad, nt, preferred_element_type=jnp.float32
+                    key_grad_ref[h, rows, :] += jnp.dot(
+                        score_grad, query_rows[h], preferred_element_type=jnp.float32
                     )
                     out[h] = (mixed, query_grad)
             return tuple(out)
@@ -215,13 +216,13 @@
         columns = slice(part * width, (part + 1) * width)
         cosine, sine = cos_ref[:, place_of(part)], sin_ref[:, place_of(part)]
 
-        def turned_back(ref, h):
-            first, second = ref[h, :half, columns], ref[h, half:ROT, columns]
+        def turned_back(grad):
+            first, second = grad[:half], grad[half:ROT]
             return jnp.concatenate(
                 [
                     first * cosine + second * sine,
                     second * cosine - first * sine,
-                    ref[h, ROT:, columns],
+                    grad[ROT:],
                 ],
                 axis=0,
             ).astype(jnp.bfloat16)
@@ -229,11 +230,11 @@
         for h in range(together):
             base = h * 3 * HD
             mixed_refs[part][h * HD : (h + 1) * HD] = back_ref[h, :, columns]
-            grad_refs[part][base : base + HD] = turned_back(query_grad_ref, h)
-            grad_refs[part][base + HD : base + 2 * HD] = turned_back(key_grad_ref, h)
-            grad_refs[part][base + 2 * HD : base + 3 * HD] = value_grad_ref[h, :, columns].astype(
-                jnp.bfloat16
-            )
+            grad_refs[part][base : base + HD] = turned_back(query_grad_ref[h, :, columns])
+            grad_refs[part][base + HD : base + 2 * HD] = turned_back(key_grad_ref[h, columns, :].T)
+            grad_refs[part][base + 2 * HD : base + 3 * HD] = value_grad_ref[
+                h, columns, :
+            ].T.astype(jnp.bfloat16)
 
 
 def attend(projected, back, begins, cosine, sine, offset, after=()):
@@ -266,8 +267,8 @@
                 pltpu.VMEM((together, count, HD), jnp.bfloat16),
                 pltpu.VMEM((together, HD, count), jnp.bfloat16),
                 pltpu.VMEM((together, HD, count), jnp.float32),
-                pltpu.VMEM((together, HD, count), jnp.float32),
-                pltpu.VMEM((together, HD, count), jnp.float32),
+                pltpu.VMEM((together, count, HD), jnp.float32),
+                pltpu.VMEM((together, count, HD), jnp.float32),
                 pltpu.VMEM((together, blocks, BK, BQ), jnp.float32),
                 pltpu.VMEM((together, blocks, BK, BQ), jnp.float32),
                 pltpu.VMEM((together, blocks, 1, BQ), jnp.float32),
@@ -332,13 +333,12 @@
 MESH = pl.DeviceIdType.MESH
 
 
-def feed_kernel(exchange, hidden_ref, back_ref, expand_ref, shrink_ref, *refs):
+def feed_kernel(exchange, later, hidden_ref, back_ref, expand_ref, shrink_ref, *refs):
     step, steps = pl.program_id(0), pl.num_programs(0)
     f32 = jnp.float32
     if exchange:
+        expand_before, shrink_before = refs[:2]
         (
-            expand_before,
-            shrink_before,
             keep_ref,
             away_ref,
             land_hbm,
@@ -353,7 +353,7 @@
             near_send,
             near_recv,
             load_sem,
-        ) = refs
+        ) = refs[2 + later :]
         outer = lax.axis_index("outer")
         far, near = outer // 2, outer % 2
         near_id = {"outer": outer + 1 - 2 * near}
@@ -482,7 +482,7 @@
         branch_part[...] = branch_sum[...].astype(branch_part.dtype)
 
 
-def feed(hidden, back, expand, shrink, before, branch_type):
+def feed(hidden, back, expand, shrink, before, branch_type, after=()):
     tokens, width = hidden.shape
     units = 2 * expand.shape[2]
     steps = 4
@@ -500,9 +500,11 @@
     grads = jax.ShapeDtypeStruct((units, width), f32)
     sem = pltpu.SemaphoreType.DMA
     return pl.pallas_call(
-        partial(feed_kernel, exchange),
+        partial(feed_kernel, exchange, len(after)),
         grid=(steps,),
-        in_specs=[whole, whole, columns, rows] + [rows, rows] * exchange,
+        in_specs=[whole, whole, columns, rows]
+        + [rows, rows] * exchange
+        + [pl.BlockSpec(memory_space=pl.ANY)] * len(after),
         out_specs=(
             [quarter, quarter, pl.BlockSpec(memory_space=pl.ANY)] if exchange else [rows, rows]
         )
@@ -539,32 +541,33 @@
             **(dict(collective_id=4, has_side_effects=True) if exchange else {}),
         ),
         cost_estimate=pl.CostEstimate(flops=2**20, bytes_accessed=2**20, transcendentals=0),
-    )(hidden, back, expand, shrink, *before)
-
-
-def most_of(tokens):
-    return tokens * 4 // 5 // 16 * 16
+    )(hidden, back, expand, shrink, *before, *after)
 
 
 def opening_kernel(
+    expand_hbm,
+    shrink_hbm,
+    project_hbm,
+    mixing_hbm,
+    inputs_hbm,
+    norm_ref,
+    back_ref,
+    expand_out,
+    shrink_out,
+    later_out,
+    norm_out,
+    hidden_ref,
+    other_back,
     expand_ref,
     shrink_ref,
     project_ref,
     mixing_ref,
-    norm_ref,
     inputs_ref,
-    back_ref,
-    expand_out,
-    shrink_out,
-    project_out,
-    mixing_out,
-    norm_out,
-    hidden_ref,
-    other_back,
     expand_low,
     shrink_low,
     norm_low,
     norm_all,
+    load_sem,
     own_sem,
     norm_send,
     norm_recv,
@@ -585,6 +588,20 @@
     half = expand_ref.shape[1] // 2
     part = half // 2
 
+    loads = [
+        pltpu.make_async_copy(source, target, load_sem.at[n])
+        for n, (source, target) in enumerate(
+            (
+                (expand_hbm, expand_ref),
+                (shrink_hbm, shrink_ref),
+                (project_hbm, project_ref),
+                (mixing_hbm, mixing_ref),
+                (inputs_hbm, inputs_ref),
+            )
+        )
+    ]
+    loads[0].start()
+    loads[1].start()
     barrier = pltpu.get_barrier_semaphore()
     for step in range(1, deep):
         pl.semaphore_signal(
@@ -595,7 +612,8 @@
     row_id = {"mp": 1 - lax.axis_index("mp")}
     pl.semaphore_signal(barrier, inc=1, device_id=row_id, device_id_type=MESH)
 
-    expand_low[...] = expand_ref[...].astype(jnp.bfloat16)
+    for load in loads[2:]:
+        load.start()
     norm_low[...] = jnp.zeros_like(norm_low)
     norm_low[0:2] = norm_ref[...].astype(jnp.bfloat16).astype(jnp.float32)
     pl.semaphore_wait(barrier, deep + 2)
@@ -654,16 +672,11 @@
             out.append(pltpu.make_async_copy(*pair, own_sem.at[w, which]))
         return out
 
+    row_copy = remote(back_ref, other_back, row_sem.at[0], row_sem.at[1], row_id)
+    row_copy.start()
+    loads[0].wait()
+    expand_low[...] = expand_ref[...].astype(jnp.bfloat16)
     start_own(0)
-    most = most_of(back_ref.shape[0])
-    row_copy = remote(
-        back_ref.at[slice(0, most)],
-        other_back.at[slice(0, most)],
-        row_sem.at[0],
-        row_sem.at[1],
-        row_id,
-    )
-    row_copy.start()
     norm_copies = []
     for step in range(1, deep):
         copy = remote(
@@ -675,16 +688,21 @@
         )
         copy.start()
         norm_copies.append(copy)
+    loads[1].wait()
     shrink_low[...] = shrink_ref[...].astype(jnp.bfloat16)
     start_own(1)
     for w in range(2):
         for copy in own_copies(w):
             copy.start()
-    for source, target in ((project_ref, project_out), (mixing_ref, mixing_out)):
-        units = target.shape[0]
-        target[...] = source[pl.ds(pl.multiple_of(near * units, units), units), :].astype(
-            jnp.bfloat16
-        )
+    for load in loads[2:]:
+        load.wait()
+    first = 0
+    for source in (project_ref, mixing_ref):
+        units = source.shape[0] // 2
+        later_out[first : first + units] = source[
+            pl.ds(pl.multiple_of(near * units, units), units), :
+        ].astype(jnp.bfloat16)
+        first += units
     norm_all[0] = norm_low[...]
     for copy in norm_copies:
         copy.wait()
@@ -801,32 +819,70 @@
                         to_near(w, way, step, other).wait_recv()
 
 
+def project_kernel(hidden_ref, back_ref, own_ref, sibling_ref, projected_ref, mixed_back_ref):
+    nt = (((1,), (1,)), ((), ()))
+    cut = own_ref.shape[0] * 3 // 4
+    few = own_ref.shape[0] - cut
+    for n, weights in enumerate((own_ref, sibling_ref)):
+        projected_ref[n * cut : (n + 1) * cut] = lax.dot_general(
+            weights[:cut], hidden_ref[...], nt, preferred_element_type=jnp.float32
+        )
+        mixed_back_ref[n * few : (n + 1) * few] = lax.dot_general(
+            weights[cut:], back_ref[...], nt, preferred_element_type=jnp.float32
+        ).astype(jnp.bfloat16)
+
+
+def project_all(hidden, back, own, sibling):
+    tokens, width = hidden.shape
+    cut = own.shape[0] * 3 // 4
+    rows = pl.BlockSpec((256, width), lambda n: (n, 0))
+    whole = pl.BlockSpec(own.shape, lambda n: (0, 0), pipeline_mode=pl.Buffered(1))
+    columns = lambda height: pl.BlockSpec((height, 256), lambda n: (0, n))
+    return pl.pallas_call(
+        project_kernel,
+        grid=(tokens // 256,),
+        in_specs=[rows, rows, whole, whole],
+        out_specs=[columns(2 * cut), columns(2 * (own.shape[0] - cut))],
+        out_shape=[
+            jax.ShapeDtypeStruct((2 * cut, tokens), jnp.float32),
+            jax.ShapeDtypeStruct((2 * (own.shape[0] - cut), tokens), jnp.bfloat16),
+        ],
+        compiler_params=pltpu.CompilerParams(vmem_limit_bytes=60 * 2**20),
+        cost_estimate=pl.CostEstimate(flops=2**20, bytes_accessed=2**20, transcendentals=0),
+    )(hidden, back, own, sibling)
+
+
 def opening(expand, shrink, project, mixing, norm, inputs, back):
     deep = 4
     here = lambda: pl.BlockSpec(memory_space=pltpu.VMEM)
     rows, units = expand.shape
+    later = project.shape[0] + mixing.shape[0]
     low = jnp.bfloat16
     sem = pltpu.SemaphoreType.DMA
     return pl.pallas_call(
         opening_kernel,
-        in_specs=[here() for _ in range(6)] + [pl.BlockSpec(memory_space=pl.ANY)],
+        in_specs=[pl.BlockSpec(memory_space=pl.ANY)] * 5
+        + [here(), pl.BlockSpec(memory_space=pl.ANY)],
         out_specs=[pl.BlockSpec(memory_space=pl.ANY)] * 2
-        + [here() for _ in range(4)]
+        + [here() for _ in range(3)]
         + [pl.BlockSpec(memory_space=pl.ANY)],
         out_shape=[
             jax.ShapeDtypeStruct((2, rows * deep, units // 2), low),
             jax.ShapeDtypeStruct((2, units // 2, rows * deep), low),
-            jax.ShapeDtypeStruct((project.shape[0] // 2, project.shape[1]), low),
-            jax.ShapeDtypeStruct((mixing.shape[0] // 2, mixing.shape[1]), low),
+            jax.ShapeDtypeStruct((later // 2, project.shape[1]), low),
             jax.ShapeDtypeStruct((8, rows * deep), jnp.float32),
             jax.ShapeDtypeStruct(inputs.shape, low),
             jax.ShapeDtypeStruct(back.shape, low),
         ],
         scratch_shapes=[
+            pltpu.VMEM(v.shape, v.dtype) for v in (expand, shrink, project, mixing, inputs)
+        ]
+        + [
             pltpu.VMEM(expand.shape, low),
             pltpu.VMEM(shrink.shape, low),
             pltpu.VMEM((8, norm.shape[1]), jnp.float32),
             pltpu.VMEM((deep, 8, norm.shape[1]), jnp.float32),
+            sem((5,)),
             sem((2, 2)),
             sem((deep,)),
             sem((deep,)),
@@ -839,18 +895,19 @@
             sem((2,)),
         ],
         compiler_params=pltpu.CompilerParams(
-            collective_id=1, has_side_effects=True, vmem_limit_bytes=40 * 2**20
+            collective_id=1, has_side_effects=True, vmem_limit_bytes=60 * 2**20
         ),
         cost_estimate=pl.CostEstimate(flops=0, bytes_accessed=2**20, transcendentals=0),
-    )(expand, shrink, project, mixing, norm, inputs, back)
+    )(expand, shrink, project, mixing, inputs, norm, back)
 
 
 def closing_kernel(
     later,
-    project_hbm,
+    own_weights,
+    sibling_weights,
     *refs,
 ):
-    sources = (project_hbm, *refs[:9])
+    sources = (own_weights, *refs[:9])
     part_own, part_other, feed_keep, feed_come, gain_ref = refs[9:14]
     input_grad, small_sum, mixed_come = refs[14 + later : 17 + later]
     full_refs = refs[17 + later : 21 + later]
@@ -884,6 +941,7 @@
         plane_lands,
         deep_lands,
         held_sem,
+        half_sem,
         part_sem,
         out_sem,
         feed_sem,
@@ -932,8 +990,17 @@
     copies = [
         pltpu.make_async_copy(source, target, held_sem.at[n])
         for n, (source, target) in enumerate(zip(sources, held))
+        if n
     ]
-    for copy in copies[:2]:
+    copies.insert(0, None)
+    cut = project.shape[0] // 2
+    halves = [
+        pltpu.make_async_copy(
+            source.at[slice(0, cut)], project.at[slice(n * cut, (n + 1) * cut)], half_sem.at[n]
+        )
+        for n, source in enumerate((own_weights, sibling_weights))
+    ]
+    for copy in (*halves, copies[1]):
         copy.start()
     barrier = pltpu.get_barrier_semaphore()
     plane = 2 * outers
@@ -989,8 +1056,8 @@
         for copy in pair:
             copy.start()
 
-    copies[0].wait()
-    copies[1].wait()
+    for copy in (*halves, copies[1]):
+        copy.wait()
     pl.semaphore_wait(barrier, plane + deep - 2)
     row_copies = []
     for n in range(blocks):
@@ -1242,7 +1309,7 @@
         copy.wait()
 
 
-def closing(project, grads, hiddens, mixed, backs, inputs, parts, feeds, gain, after):
+def closing(weights, grads, hiddens, mixed, backs, inputs, parts, feeds, gain, after):
     deep = 4
     low, f32 = jnp.bfloat16, jnp.float32
     tokens, width = inputs.shape
@@ -1252,7 +1319,7 @@
     anywhere = pl.BlockSpec(memory_space=pl.ANY)
     here = lambda: pl.BlockSpec(memory_space=pltpu.VMEM)
     held = (
-        project,
+        jax.ShapeDtypeStruct(grads[0].shape[:1] + (width,), low),
         grads[1],
         grads[0],
         hiddens[1],
@@ -1267,7 +1334,7 @@
     space = pltpu.VMEM
     return pl.pallas_call(
         partial(closing_kernel, len(after)),
-        in_specs=[anywhere] * 14 + [here()] + [anywhere] * len(after),
+        in_specs=[anywhere] * 15 + [here()] + [anywhere] * len(after),
         out_specs=[anywhere, here()] + [anywhere] * 5,
         out_shape=[
             jax.ShapeDtypeStruct((tokens, width), f32),
@@ -1314,6 +1381,7 @@
             sem((len(held),)),
             sem((2,)),
             sem((2,)),
+            sem((2,)),
             sem((4,)),
             sem((2, deep - 1)),
             sem((2, deep - 1)),
@@ -1340,36 +1408,7 @@
             collective_id=3, has_side_effects=True, vmem_limit_bytes=62 * 2**20
         ),
         cost_estimate=pl.CostEstimate(flops=2**20, bytes_accessed=2**20, transcendentals=0),
-    )(*held, *parts, *feeds, gain, *after)
-
-
-class Paired:
-    def __init__(self):
-        self.place = lax.axis_index("dp")
-        self.deep = lax.axis_size("dp")
-
-    def gather(self, own, cut, depth):
-        return lax.all_gather(own, "dp", axis=depth, tiled=True)
-
-    def gather_few(self, own):
-        size = self.deep
-        return [
-            lax.ppermute(own, "dp", [(i, (i + step) % size) for i in range(size)])
-            for step in range(1, size)
-        ]
-
-    def placed(self, own, come, depth):
-        wide = list(own.shape)
-        piece = wide[depth]
-        wide[depth] *= self.deep
-        out = jnp.zeros(wide, own.dtype)
-        for step, one in enumerate([own, *come]):
-            at = lax.rem(self.place - step + self.deep, self.deep)
-            out = lax.dynamic_update_slice_in_dim(out, one, at * piece, depth)
-        return out
-
-    def paired(self, half, cut):
-        return jnp.concatenate([half, swap(half, "outer", 1)], axis=cut)
+    )(*weights, *held[1:], *parts, *feeds, gain, *after)
 
 
 def local(
@@ -1411,8 +1450,7 @@
     begins, places = layout(lengths[0], count)
     cosine, sine = turns(places)
     if paired:
-        plan = Paired()
-        expand, shrink, project, mixing, norm_weight, hidden_local, other_back = opening(
+        expand, shrink, later, norm_weight, hidden_local, other_back = opening(
             expand_master,
             shrink_master,
             project_flat,
@@ -1421,14 +1459,9 @@
             inputs[0],
             cotangent[0],
         )
-        most = most_of(width)
-        other_back = lax.dynamic_update_slice(
-            other_back, swap(cotangent[0, most:], "mp", 1), (most, 0)
-        )
         backs = [cotangent[0], other_back]
         shrink = shrink.reshape(-1, shrink.shape[2])
-        project_half = plan.gather(project, 0, 1)
-        mixing_come = plan.gather_few(mixing)
+        later = lax.all_gather(later, "dp", axis=1, tiled=True)
         hiddens = [hidden_local, swap(hidden_local, "mp", 1)]
     else:
         norm_weight = lax.all_gather(norm_master.astype(jnp.bfloat16), "dp", axis=1, tiled=True)
@@ -1451,17 +1484,19 @@
         *grads, hidden_own, branch_own = feed(
             hiddens[0], backs[0], expand, shrink, (), jnp.float32
         )
-        project = plan.paired(follow(project_half, branch_own), 0)
-        mixing_come = [follow(v, branch_own) for v in mixing_come]
-        mixing = plan.paired(plan.placed(mixing, mixing_come, 1), 0)
+        later = follow(later, branch_own)
+        later = [later, swap(later, "outer", 1)]
+        cut = later[0].shape[0] * 3 // 4
+        mixing = jnp.concatenate([v[cut:] for v in later])
+        own_columns = project_all(hiddens[0], backs[0], *later)
         feed_keep, feed_away, _, hidden_other, branch_other = feed(
-            hiddens[1], backs[1], expand, shrink, grads, jnp.bfloat16
+            hiddens[1], backs[1], expand, follow(shrink, *own_columns), grads, jnp.bfloat16
         )
         feed_come = swap(feed_away, "outer", 2)
         branch_come = swap(branch_other, "mp", 1)
         mixing_other = swap(mixing, "mp", 1)
-        projected = [product("td,ed->et", hidden, project) for hidden in hiddens]
-        mixed_backs = [product("td,fd->ft", back, mixing).astype(jnp.bfloat16) for back in backs]
+        other_columns = project_all(hiddens[1], backs[1], *later)
+        projected, mixed_backs = zip(own_columns, other_columns)
         mixed, projected_grads = attend(
             projected,
             mixed_backs,
@@ -1472,7 +1507,7 @@
             (feed_away, branch_other),
         )
         input_grad, small_sum, mixed_come, shrink_sum, expand_sum, project_sum, mixing_sum = closing(
-            project,
+            later,
             projected_grads,
             hiddens,
             mixed,

time: 477 us -> 466 us (0.977)
  Pallas kernels: 349 us -> 388 us
  matrix products: 29.1 us -> 7.76 us
  waiting for transfers between devices: 13.8 us -> 4.54 us
  local copies, waits for them, and re-layouts: 24 us -> 14.9 us
  starting transfers between devices: 10.4 us -> 4.35 us
  other arithmetic: 25 us -> 20.1 us
    pallas_call x3 -> x5, Pallas kernels: 152 us -> 195 us  [the longest x2 105 us: feed(): pl.pallas_call(partial(feed_kernel, exchange, len(after)), grid=(steps,),...]
    dot_general x6 -> x2, matrix products: 29.1 us -> 7.76 us  [product(): return jnp.einsum(pattern, left, right, preferred_element_type=jnp.float32)]
    pallas_call x1, Pallas kernels: 95 us -> 77.2 us  [attend(): pl.pallas_call(partial(attend_kernel, together, parts, len(after)), grid_...]
    pallas_call x1, Pallas kernels: 102 us -> 116 us  [closing(): pl.pallas_call(partial(closing_kernel, len(after)), in_specs=[anywhere] *...]
    ppermute x7 -> x5, waiting for transfers between devices: 13.7 us -> 4.5 us  [swap(): return lax.ppermute(array, axis, [(i, i ^ bit) for i in range(size)])]
    unnamed x80 -> x61, local copies, waits for them, and re-layouts: 16.3 us -> 11.4 us
  transfers between devices with their start and end apart: 11 -> 6, of which waited for: 1 -> 1; matrix products, arithmetic and copies ran while one was open for 12% -> 5% of each run, Pallas kernels for 62% -> 57%
where the time goes in v7:
time: 466 us; the launch traced here: 457 us
  Pallas kernels  388 us (83%)
  other arithmetic  20.1 us (4%)
  between operations  17 us (4%)
  local copies, waits for them, and re-layouts  14.9 us (3%)
  matrix products  7.76 us (2%)
    pallas_call x1, Pallas kernels, closing(): pl.pallas_call(partial(closing_kernel, len(after)), in_specs=[anywhere] *...  116 us
    pallas_call x2, Pallas kernels, feed(): pl.pallas_call(partial(feed_kernel, exchange, len(after)), grid=(steps,),...  105 us
    pallas_call x1, Pallas kernels, attend(): pl.pallas_call(partial(attend_kernel, together, parts, len(after)), grid_...  77.2 us
    pallas_call x1, Pallas kernels, opening(): pl.pallas_call(opening_kernel, in_specs=[pl.BlockSpec(memory_space=pl.ANY...  67.2 us
    pallas_call x2, Pallas kernels, project_all(): pl.pallas_call(project_kernel, grid=(tokens // 256,), in_specs=[rows, row...  22.9 us
    convert_element_type x5, other arithmetic, adam_update(): return (master_new, first_new, second_new, master_new.astype(jnp.bfloat16))  13.9 us
    unnamed x61, local copies, waits for them, and re-layouts  11.4 us
  transfers between devices with their start and end apart: 6, of which 1 were waited for; matrix products, arithmetic and copies ran while one was open for 5% of the time, Pallas kernels for 57%

profile of v7, /device:TPU:0, one launch (start us, length us, event | category | flops | bytes accessed | tf_op | source)
XLA Modules:
  0.0 457.1 jit_solution(8762853131070642995)
XLA Ops:
  7.2 0.0 all-gather.2.cloned.1.call-start
  7.2 67.2 %shard_map.353 = (bf16[2,1024,1024]{2,1,0:T(8,128)(2,1)}, bf16[2,1024,1024]{2,1,0:T(8,128)(2,1)}, bf16[1024,256]{1,0:T(8,128)(2,1)}, f32[8,1024]{1,0:T(8,128)}, ...) custom-call(f32[256,2048]{1,0:T(8,128)} %expand_hbm.1, f32[2048,256]{1,0:T(8,128)} %shrink_hbm.1, ...), custom_call_target="tpu_custom_call" | custom-call | bytes 1048576 | tf_op jit(solution)/shard_map/pallas_call | solution.py:862
  74.5 0.0 all-gather.2.cloned.1.call-update
  74.5 0.6 collective-permute-start
  75.1 44.8 %shard_map.354 = (f32[2048,1024]{1,0:T(8,128)}, f32[2048,1024]{1,0:T(8,128)}, f32[1280,1024]{1,0:T(8,128)}, f32[1280,1024]{1,0:T(8,128)}) custom-call(bf16[1280,1024]{1,0:T(8,128)(2,1)} %get-tuple-element.55.hidden_ref.refs_3_, bf16[1280,1024]{1,0:T(8,128)(2,1)} %bitcast.22, bf16[2,1024,1024]{2,1,0:T(8,128)(2,1)} %get-tuple-element.56.expand_ref, ...), custom_call_target="tpu_custom_call" | custom-call | flops 1048576 | bytes 1048576 | tf_op jit(solution)/shard_map/pallas_call | solution.py:502
  119.9 0.0 all-gather.2.cloned.1.call-done.own_ref.own_weights
  120.0 0.1 collective-permute-start.1
  120.0 4.5 collective-permute-done.1.sibling_ref.sibling_weights
  124.5 11.5 %shard_map.355 = (f32[1536,1280]{1,0:T(8,128)}, bf16[512,1280]{1,0:T(8,128)(2,1)}) custom-call(bf16[1280,1024]{1,0:T(8,128)(2,1)} %get-tuple-element.55.hidden_ref.refs_3_, bf16[1280,1024]{1,0:T(8,128)(2,1)} %bitcast.23, bf16[1024,1024]{1,0:T(8,128)(2,1)} %all-gather.2.cloned.1.call-done.own_ref.own_weights, ...), custom_call_target="tpu_custom_call" | custom-call | flops 1048576 | bytes 1048576 | tf_op jit(solution)/shard_map/pallas_call | solution.py:841
  136.0 1.5 copy-done.6
  137.5 60.5 %shard_map.356 = (f32[2,512,1024]{2,1,0:T(8,128)}, bf16[2,512,1024]{2,1,0:T(8,128)(2,1)}, f32[2,2,512,1024]{3,2,1,0:T(8,128)}, f32[1280,1024]{1,0:T(8,128)}, bf16[1280,1024]{1,0:T(8,128)(2,1)}) custom-call(bf16[1280,1024]{1,0:T(8,128)(2,1)} %copy-done.6, bf16[1280,1024]{1,0:T(8,128)(2,1)} %get-tuple-element.59.back_ref.refs_6_, ...), custom_call_target="tpu_custom_call" | custom-call | flops 1048576 | bytes 1048576 | tf_op jit(solution)/shard_map/pallas_call | solution.py:502
  198.0 1.6 collective-permute-start.2
  199.6 1.5 collective-permute-start.3
  201.1 0.1 select_reduce_fusion.1
  201.2 0.1 select_reduce_fusion
  201.4 0.1 slice.15
  201.5 0.1 pad_add_fusion.refs_0_
  201.6 0.6 multiply_sine_fusion
  202.2 1.1 slice.16
  203.3 1.1 slice.20
  204.4 1.1 pad_maximum_fusion
  205.5 0.5 collective-permute-start.4
  206.0 11.4 %shard_map.357 = (f32[1536,1280]{1,0:T(8,128)}, bf16[512,1280]{1,0:T(8,128)(2,1)}) custom-call(bf16[1280,1024]{1,0:T(8,128)(2,1)} %copy-done.6, bf16[1280,1024]{1,0:T(8,128)(2,1)} %get-tuple-element.59.back_ref.refs_6_, bf16[1024,1024]{1,0:T(8,128)(2,1)} %all-gather.2.cloned.1.call-done.own_ref.own_weights, ...), custom_call_target="tpu_custom_call" | custom-call | flops 1048576 | bytes 1048576 | tf_op jit(solution)/shard_map/pallas_call | solution.py:841
  217.5 1.3 copy-done.4
  218.8 77.2 %shard_map.358 = (bf16[512,1280]{1,0:T(8,128)(2,1)S(1)}, bf16[512,1280]{1,0:T(8,128)(2,1)S(1)}, bf16[1536,1280]{1,0:T(8,128)(2,1)}, bf16[1536,1280]{1,0:T(8,128)(2,1)}) custom-call(s32[11]{0:T(128)S(1)} %pad_add_fusion.refs_0_, f32[1536,1280]{1,0:T(8,128)} %get-tuple-element.62.refs_1_, f32[1536,1280]{1,0:T(8,128)} %get-tuple-element.68.refs_2_, ...), custom_call_target="tpu_custom_call" | custom-call | flops 1048576 | bytes 1048576 | tf_op jit(solution)/shard_map/pallas_call | solution.py:252
  296.0 1.1 copy-done
  297.1 1.1 copy-done.3
  298.1 115.8 %shard_map.359 = (f32[1280,1024]{1,0:T(8,128)}, f32[8,1024]{1,0:T(8,128)}, bf16[512,1280]{1,0:T(8,128)(2,1)}, f32[2048,256]{1,0:T(8,128)}, f32[256,2048]{1,0:T(8...) custom-call(bf16[1024,1024]{1,0:T(8,128)(2,1)} %all-gather.2.cloned.1.call-done.own_ref.own_weights, ...), custom_call_target="tpu_custom_call" | custom-call | flops 1048576 | bytes 1048576 | tf_op jit(solution)/shard_map/pallas_call | solution.py:1335
  413.9 1.4 fusion.17
  415.3 1.2 slice.18
  417.8 1.2 broadcast_multiply_fusion.1
  419.0 1.7 broadcast_multiply_fusion
  420.7 1.6 fusion.6
  422.3 0.1 copy-done.7
  422.4 0.6 copy-done.10
  423.0 0.6 copy-done.11
  423.6 4.1 fusion.9
  427.8 1.5 fusion.13
  429.3 0.5 copy-done.9
  429.8 0.5 copy-done.17
  430.4 3.4 fusion.15
  433.7 0.6 fusion.7
  434.4 0.8 copy-done.13
  435.2 0.6 copy-done.14
  435.8 4.3 fusion.11
  440.1 0.3 copy-done.19
  440.4 6.2 %fusion = bf16[1,1280,1024]{2,1,0:T(8,128)(2,1)} fusion(f32[1280,1024]{1,0:T(8,128)S(1)} %fusion.6, f32[1280,1024]{1,0:T(8,128)S(1)} %bitcast.32, bf16[1280,1024]{1,0:T(8,128)(2,1)} %collective-permute-done.2.refs_14_, bf16[1,1280,1024]{2,1,0:T(8,128)(2,1)S(1)} %copy-done.5, bf16[512,1280]{1,0:T(8,128)(2,1)S(1)} %copy-done.19, ...), kind=kOutput, calls=%fused_computation.3 | convolution fusion | flops 1351352320 | bytes 20709376 | tf_op jit(solution)/shard_map/ft,fd->td/dot_general | solution.py:309
  446.6 2.4 copy.42
  (58 shorter events, 0.2 us)
Async XLA Ops:
  7.2 112.8 %all-gather.2.cloned.1.call-start = ((), (), s32[]{:S(2)}) async-start(), calls=%async_computation | async-start | bytes 2621440 | tf_op jit(solution)/shard_map/all_gather | solution.py:1464
  74.5 61.5 %collective-permute-start = (bf16[1280,1024]{1,0:T(8,128)(2,1)}, bf16[1280,1024]{1,0:T(8,128)(2,1)S(1)}, u32[]{:S(2)}, u32[]{:S(2)}) collective-permute-start(bf16[1280,1024]{1,0:T(8,128)(2,1)} %get-tuple-element.55.hidden_ref.refs_3_), channel_id=1, source_target_pairs={{0,16},{16,0},{1,17},{17,1},{2,18},{18,2},{3,19},{19,3},{4,20},{20... | collective-permute-start | bytes 7864328 | tf_op jit(solution)/shard_map/ppermute | solution.py:323
  120.0 4.6 collective-permute-start.1
  136.0 1.5 copy-start.6
  137.5 63.6 %copy-start.25 = (s32[1,12]{1,0:T(1,128)S(1)}, s32[1,12]{1,0:T(1,128)}, u32[]{:S(2)}) copy-start(s32[1,12]{1,0:T(1,128)} %param.20) | copy-start | bytes 148
  198.0 100.1 %collective-permute-start.2 = (bf16[1280,1024]{1,0:T(8,128)(2,1)}, bf16[1280,1024]{1,0:T(8,128)(2,1)}, u32[]{:S(2)}, u32[]{:S(2)}) collective-permute-start(bf16[1280,1024]{1,0:T(8,128)(2,1)} %get-tuple-element.67.refs_9_), channel_id=1, source_target_pairs={{0,16},{16,0},{1,17},{17,1},{2,18},{18,2},{3,19},{19,3},{4,20},{20... | collective-permute-start | bytes 7864328 | tf_op jit(solution)/shard_map/ppermute | solution.py:323
  199.6 98.5 %collective-permute-start.3 = (bf16[2,512,1024]{2,1,0:T(8,128)(2,1)}, bf16[2,512,1024]{2,1,0:T(8,128)(2,1)}, u32[]{:S(2)}, u32[]{:S(2)}) collective-permute-start(bf16[2,512,1024]{2,1,0:T(8,128)(2,1)} %get-tuple-element.70.refs_8_), channel_id=1, source_target_pairs={{0,2},{1,3},{2,0},{3,1},{4,6},{5,7},{6,4},{7,5},{8,10},{9,11},{10,... | collective-permute-start | bytes 6291464 | tf_op jit(solution)/shard_map/ppermute | solution.py:323
  205.5 12.0 %copy-start.2 = (bf16[512,1280]{1,0:T(8,128)(2,1)S(1)}, bf16[512,1280]{1,0:T(8,128)(2,1)}, u32[]{:S(2)}) copy-start(bf16[512,1280]{1,0:T(8,128)(2,1)} %get-tuple-element.63.refs_3_) | copy-start | bytes 3932164
  205.5 234.6 %collective-permute-start.4 = (bf16[512,1024]{1,0:T(8,128)(2,1)}, bf16[512,1024]{1,0:T(8,128)(2,1)}, u32[]{:S(2)}, u32[]{:S(2)}) collective-permute-start(bf16[512,1024]{1,0:T(8,128)(2,1)} %pad_maximum_fusion), channel_id=1, source_target_pairs={{0,16},{16,0},{1,17},{17,1},{2,18},{18,2},{3,19},{19,3},{4,20},{20... | collective-permute-start | bytes 3145736 | tf_op jit(solution)/shard_map/ppermute | solution.py:323
  217.4 1.3 copy-start.4
  296.0 1.1 copy-start
  297.0 1.1 copy-start.3
  417.8 2.9 copy-start.1
  419.0 3.3 copy-start.15
  420.7 1.7 copy-start.7
  420.7 2.3 copy-start.10
  420.7 2.9 copy-start.11
  423.6 4.1 copy-start.16
  423.6 4.2 copy-start.20
  423.6 4.2 copy-start.21
  423.6 5.7 %copy-start.18 = (f32[256,8,192]{0,2,1:T(8,128)S(1)}, f32[256,8,192]{0,2,1:T(8,128)}, u32[]{:S(2)}) copy-start(f32[256,8,192]{0,2,1:T(8,128)} %param.23) | copy-start | bytes 4718596
  427.8 2.0 copy-start.9
  427.8 2.5 copy-start.17
  430.3 3.4 copy-start.22
  430.3 3.4 copy-start.23
  430.3 3.4 copy-start.24
  430.3 4.0 copy-start.8
  430.3 4.0 copy-start.12
  430.3 4.9 %copy-start.13 = (f32[256,2048]{1,0:T(8,128)S(1)}, f32[256,2048]{1,0:T(8,128)}, u32[]{:S(2)}) copy-start(f32[256,2048]{1,0:T(8,128)} %param.29) | copy-start | bytes 6291460
  430.4 5.4 %copy-start.14 = (f32[256,2048]{1,0:T(8,128)S(1)}, f32[256,2048]{1,0:T(8,128)}, u32[]{:S(2)}) copy-start(f32[256,2048]{1,0:T(8,128)} %get-tuple-element.85) | copy-start | bytes 6291460
  434.4 5.7 %slice-start = ((s8[5242880]{0:T(1024)(128)(4,1)}), s8[4194304]{0:T(1024)(128)(4,1)S(1)}, s32[]{:S(2)}) async-start(s8[5242880]{0:T(1024)(128)(4,1)} %bitcast.31), calls=%async_computation.1 | async-start | bytes 8388608
  435.8 4.3 copy-start.5
  435.8 4.3 slice-start.1
  435.8 4.6 %copy-start.19 = (bf16[512,1280]{1,0:T(8,128)(2,1)S(1)}, bf16[512,1280]{1,0:T(8,128)(2,1)}, u32[]{:S(2)}) copy-start(bf16[512,1280]{1,0:T(8,128)(2,1)} %get-tuple-element.81) | copy-start | bytes 3932164
  440.1 6.5 %slice-start.2 = ((s8[5242880]{0:T(1024)(128)(4,1)}), s8[4194304]{0:T(1024)(128)(4,1)S(1)}, s32[]{:S(2)}) async-start(s8[5242880]{0:T(1024)(128)(4,1)} %bitcast.33), calls=%async_computation.3 | async-start | bytes 8388608
  440.4 6.2 %slice-start.3 = ((s8[5242880]{0:T(1024)(128)(4,1)}), s8[1048576]{0:T(1024)(128)(4,1)S(1)}, s32[]{:S(2)}) async-start(s8[5242880]{0:T(1024)(128)(4,1)} %bitcast.33), calls=%async_computation.4 | async-start | bytes 2097152
Sparse Core Ops, SparseCore 0:
  74.6 44.4 all-gather.1

commit v8 on v7

--- a/solution.py
+++ b/solution.py
@@ -993,6 +993,21 @@
         if n
     ]
     copies.insert(0, None)
+    quarter = feed_keep.shape[1]
+    feed_copies = [
+        (
+            pltpu.make_async_copy(
+                feed_keep.at[k],
+                total_ref.at[slice(k * quarter, (k + 1) * quarter)],
+                feed_sem.at[k],
+            ),
+            pltpu.make_async_copy(feed_come.at[k], feed_in.at[k], feed_sem.at[2 + k]),
+        )
+        for k in range(2)
+    ]
+    for pair in feed_copies:
+        for copy in pair:
+            copy.start()
     cut = project.shape[0] // 2
     halves = [
         pltpu.make_async_copy(
@@ -1040,40 +1055,7 @@
     loads[1].start()
     for copy in copies[2:]:
         copy.start()
-    quarter = feed_keep.shape[1]
-    feed_copies = [
-        (
-            pltpu.make_async_copy(
-                feed_keep.at[k],
-                total_ref.at[slice(k * quarter, (k + 1) * quarter)],
-                feed_sem.at[k],
-            ),
-            pltpu.make_async_copy(feed_come.at[k], feed_in.at[k], feed_sem.at[2 + k]),
-        )
-        for k in range(2)
-    ]
-    for pair in feed_copies:
-        for copy in pair:
-            copy.start()
-
-    for copy in (*halves, copies[1]):
-        copy.wait()
     pl.semaphore_wait(barrier, plane + deep - 2)
-    row_copies = []
-    for n in range(blocks):
-        made = lax.dot_general(grads_other[:, at[n]], project[...], tn, preferred_element_type=f32)
-        loads[n].wait()
-        sent_ref[at[n], :] = (part_in[n % 2] + made).astype(low)
-        loads[n + 2].start()
-        copy = remote(
-            sent_ref.at[at[n]], come_ref.at[at[n]], row_send.at[n], row_recv.at[n], row_id
-        )
-        copy.start()
-        row_copies.append(copy)
-
-    copies[5].wait()
-    mixed_copy = remote(mixed_other, mixed_come, mixed_sem.at[0], mixed_sem.at[1], row_id)
-    mixed_copy.start()
 
     piece = width // deep
 
@@ -1102,6 +1084,30 @@
             line_copies[-1].start()
         feed_share[k] = total_ref[rows, columns(place)] + feed_in[k, :, columns(place)].astype(f32)
 
+    for copy in (*halves, copies[1]):
+        copy.wait()
+    row_copies = []
+    for n in range(blocks):
+        made = lax.dot_general(grads_other[:, at[n]], project[...], tn, preferred_element_type=f32)
+        loads[n].wait()
+        sent_ref[at[n], :] = (part_in[n % 2] + made).astype(low)
+        loads[n + 2].start()
+        copy = remote(
+            sent_ref.at[at[n]], come_ref.at[at[n]], row_send.at[n], row_recv.at[n], row_id
+        )
+        copy.start()
+        row_copies.append(copy)
+
+    copies[5].wait()
+    mixed_copy = remote(
+        mixed_other.at[slice(0, mixed_come.shape[0])],
+        mixed_come,
+        mixed_sem.at[0],
+        mixed_sem.at[1],
+        row_id,
+    )
+    mixed_copy.start()
+
     for n in (2, 3, 4, 6, 7, 8):
         copies[n].wait()
     half = project_own.shape[0]
@@ -1274,7 +1280,7 @@
             pltpu.make_async_copy(part_in.at[n % 2], input_grad.at[at[n]], out_sem.at[n % 2])
         )
         out_copies[-1].start()
-    for k in range(4):
+    for k in range(2):
         passed.append(pass_on(k, spreads[k]))
 
     small_ref[...] = jnp.full(small_ref.shape, square)
@@ -1299,7 +1305,13 @@
     everywhere(
         deep_lands, deep_send, deep_recv, deep, place, lambda step: {"dp": (place + step) % deep}
     )
+    for k in range(2, 4):
+        passed.append(pass_on(k, spreads[k]))
+    small = small_ref[0:2]
+    norm = jnp.sqrt(small_ref[2:3] + jnp.sum(small * small))
     small_sum[...] = small_ref[...]
+    small_sum[2:3] = norm
+    small_sum[3:4] = clip_level / jnp.maximum(norm, clip_level)
     for k in range(4):
         spreads[k][0].wait()
         spreads[k][2].wait()
@@ -1339,7 +1351,7 @@
         out_shape=[
             jax.ShapeDtypeStruct((tokens, width), f32),
             jax.ShapeDtypeStruct((8, width), f32),
-            jax.ShapeDtypeStruct(mixed[1].shape, low),
+            jax.ShapeDtypeStruct((few, tokens), low),
         ]
         + [
             jax.ShapeDtypeStruct(shape, f32)
@@ -1519,11 +1531,14 @@
             (branch_come,),
         )
         mixed_own = follow(mixed[0], small_sum)
+        few = mixed_come.shape[0]
+        mixed_last = swap(follow(mixed[1], small_sum)[few:], "mp", 1)
         branch = (
             branch_own
             + branch_come.astype(jnp.float32)
             + product("ft,fd->td", mixed_own, mixing)
-            + product("ft,fd->td", mixed_come, mixing_other)
+            + product("ft,fd->td", mixed_come, mixing_other[:few])
+            + product("ft,fd->td", mixed_last, mixing_other[few:])
         )
     else:
         lifteds = [product("td,df->tf", hidden, expand) for hidden in hiddens]
@@ -1570,9 +1585,12 @@
         small_sum = lax.psum(
             jnp.concatenate([norm_terms, jnp.full((1, D), own_square)]), ("mp", "dp", "outer")
         )
+        square = small_sum[2, 0] + jnp.sum(small_sum[:2] * small_sum[:2])
+        grad_norm = jnp.sqrt(square)
+        factor = clip_level / jnp.maximum(grad_norm, clip_level)
+    else:
+        grad_norm, factor = small_sum[2, 0], small_sum[3, 0]
     norm_full = small_sum[:2]
-    grad_norm = jnp.sqrt(small_sum[2, 0] + jnp.sum(norm_full * norm_full))
-    factor = clip_level / jnp.maximum(grad_norm, clip_level)
     norm_gradient = lax.dynamic_slice_in_dim(
         norm_full, lax.axis_index("dp") * (D // deep), D // deep, 1
     )

time: 466 us -> 449 us (0.964)
  Pallas kernels: 388 us -> 373 us
    pallas_call x1, Pallas kernels: 116 us -> 101 us  [closing(): pl.pallas_call(partial(closing_kernel, len(after)), in_specs=[anywhere] *...]
    pallas_call x2, Pallas kernels: 105 us -> 93.1 us  [feed(): pl.pallas_call(partial(feed_kernel, exchange, len(after)), grid=(steps,),...]
    pallas_call x1, Pallas kernels: 77.2 us -> 88.3 us  [attend(): pl.pallas_call(partial(attend_kernel, together, parts, len(after)), grid_...]
    unnamed x61 -> x63, local copies, waits for them, and re-layouts: 11.4 us -> 8.62 us
  transfers between devices with their start and end apart: 6 -> 7, of which waited for: 1 -> 1; matrix products, arithmetic and copies ran while one was open for 5% -> 7% of each run, Pallas kernels for 57% -> 58%
where the time goes in v8:
time: 449 us; the launch traced here: 442 us
  Pallas kernels  373 us (83%)
  other arithmetic  22.6 us (5%)
  between operations  14.6 us (3%)
  local copies, waits for them, and re-layouts  13.8 us (3%)
  matrix products  8.66 us (2%)
  starting transfers between devices  5.35 us (1%)
  waiting for transfers between devices  4.54 us (1%)
    pallas_call x1, Pallas kernels, closing(): pl.pallas_call(partial(closing_kernel, len(after)), in_specs=[anywhere] *...  101 us
    pallas_call x2, Pallas kernels, feed(): pl.pallas_call(partial(feed_kernel, exchange, len(after)), grid=(steps,),...  93.1 us
    pallas_call x1, Pallas kernels, attend(): pl.pallas_call(partial(attend_kernel, together, parts, len(after)), grid_...  88.3 us
    pallas_call x1, Pallas kernels, opening(): pl.pallas_call(opening_kernel, in_specs=[pl.BlockSpec(memory_space=pl.ANY...  67.2 us
    pallas_call x2, Pallas kernels, project_all(): pl.pallas_call(project_kernel, grid=(tokens // 256,), in_specs=[rows, row...  22.9 us
    convert_element_type x5, other arithmetic, adam_update(): return (master_new, first_new, second_new, master_new.astype(jnp.bfloat16))  16.4 us
  transfers between devices with their start and end apart: 7, of which 1 were waited for; matrix products, arithmetic and copies ran while one was open for 7% of the time, Pallas kernels for 58%

profile of v8, /device:TPU:0, one launch (start us, length us, event | category | flops | bytes accessed | tf_op | source)
XLA Modules:
  0.0 442.2 jit_solution(8038019662879987271)
XLA Ops:
  7.2 0.0 all-gather.2.cloned.1.call-start
  7.2 67.2 %shard_map.353 = (bf16[2,1024,1024]{2,1,0:T(8,128)(2,1)}, bf16[2,1024,1024]{2,1,0:T(8,128)(2,1)}, bf16[1024,256]{1,0:T(8,128)(2,1)}, f32[8,1024]{1,0:T(8,128)}, ...) custom-call(f32[256,2048]{1,0:T(8,128)} %expand_hbm.1, f32[2048,256]{1,0:T(8,128)} %shrink_hbm.1, ...), custom_call_target="tpu_custom_call" | custom-call | bytes 1048576 | tf_op jit(solution)/shard_map/pallas_call | solution.py:862
  74.5 0.0 all-gather.2.cloned.1.call-update
  74.5 0.6 collective-permute-start
  75.1 44.8 %shard_map.354 = (f32[2048,1024]{1,0:T(8,128)}, f32[2048,1024]{1,0:T(8,128)}, f32[1280,1024]{1,0:T(8,128)}, f32[1280,1024]{1,0:T(8,128)}) custom-call(bf16[1280,1024]{1,0:T(8,128)(2,1)} %get-tuple-element.56.hidden_ref.refs_3_, bf16[1280,1024]{1,0:T(8,128)(2,1)} %bitcast.23, bf16[2,1024,1024]{2,1,0:T(8,128)(2,1)} %get-tuple-element.57.expand_ref, ...), custom_call_target="tpu_custom_call" | custom-call | flops 1048576 | bytes 1048576 | tf_op jit(solution)/shard_map/pallas_call | solution.py:502
  119.9 0.0 all-gather.2.cloned.1.call-done.own_ref.own_weights
  119.9 0.1 collective-permute-start.1
  120.0 4.5 %collective-permute-done.1.sibling_ref.sibling_weights = bf16[1024,1024]{1,0:T(8,128)(2,1)} collective-permute-done((bf16[1024,1024]{1,0:T(8,128)(2,1)}, bf16[1024,1024]{1,0:T(8,128)(2,1)}, u32[]{:S(2)}, u32[]{:S(2)}) %collective-permute-start.1) | collective-permute-done | bytes 2097184 | tf_op jit(solution)/shard_map/ppermute | solution.py:323
  124.5 11.5 %shard_map.355 = (f32[1536,1280]{1,0:T(8,128)}, bf16[512,1280]{1,0:T(8,128)(2,1)}) custom-call(bf16[1280,1024]{1,0:T(8,128)(2,1)} %get-tuple-element.56.hidden_ref.refs_3_, bf16[1280,1024]{1,0:T(8,128)(2,1)} %bitcast.24, bf16[1024,1024]{1,0:T(8,128)(2,1)} %all-gather.2.cloned.1.call-done.own_ref.own_weights, ...), custom_call_target="tpu_custom_call" | custom-call | flops 1048576 | bytes 1048576 | tf_op jit(solution)/shard_map/pallas_call | solution.py:841
  136.0 1.5 copy-done.7
  137.5 48.2 %shard_map.356 = (f32[2,512,1024]{2,1,0:T(8,128)}, bf16[2,512,1024]{2,1,0:T(8,128)(2,1)}, f32[2,2,512,1024]{3,2,1,0:T(8,128)}, f32[1280,1024]{1,0:T(8,128)}, bf16[1280,1024]{1,0:T(8,128)(2,1)}) custom-call(bf16[1280,1024]{1,0:T(8,128)(2,1)} %copy-done.7, bf16[1280,1024]{1,0:T(8,128)(2,1)} %get-tuple-element.60.back_ref.refs_6_, ...), custom_call_target="tpu_custom_call" | custom-call | flops 1048576 | bytes 1048576 | tf_op jit(solution)/shard_map/pallas_call | solution.py:502
  185.8 1.6 collective-permute-start.2
  187.3 1.5 collective-permute-start.3
  188.9 0.1 select_reduce_fusion.1
  189.0 0.1 select_reduce_fusion
  189.1 0.1 slice.27
  189.3 0.1 pad_add_fusion.refs_0_
  189.3 0.6 multiply_sine_fusion
  190.0 1.1 slice.28
  191.1 1.1 slice.36
  192.2 1.0 pad_maximum_fusion
  193.2 0.5 collective-permute-start.4
  193.7 11.4 %shard_map.357 = (f32[1536,1280]{1,0:T(8,128)}, bf16[512,1280]{1,0:T(8,128)(2,1)}) custom-call(bf16[1280,1024]{1,0:T(8,128)(2,1)} %copy-done.7, bf16[1280,1024]{1,0:T(8,128)(2,1)} %get-tuple-element.60.back_ref.refs_6_, bf16[1024,1024]{1,0:T(8,128)(2,1)} %all-gather.2.cloned.1.call-done.own_ref.own_weights, ...), custom_call_target="tpu_custom_call" | custom-call | flops 1048576 | bytes 1048576 | tf_op jit(solution)/shard_map/pallas_call | solution.py:841
  205.2 0.0 copy-start.5
  205.2 1.3 copy-done.5
  206.5 88.3 %shard_map.358 = (bf16[512,1280]{1,0:T(8,128)(2,1)S(1)}, bf16[512,1280]{1,0:T(8,128)(2,1)S(1)}, bf16[1536,1280]{1,0:T(8,128)(2,1)}, bf16[1536,1280]{1,0:T(8,128)(2,1)}) custom-call(s32[11]{0:T(128)S(1)} %pad_add_fusion.refs_0_, f32[1536,1280]{1,0:T(8,128)} %get-tuple-element.63.refs_1_, f32[1536,1280]{1,0:T(8,128)} %get-tuple-element.69.refs_2_, ...), custom_call_target="tpu_custom_call" | custom-call | flops 1048576 | bytes 1048576 | tf_op jit(solution)/shard_map/pallas_call | solution.py:252
  294.8 1.1 copy-done
  295.9 1.1 copy-done.2
  296.9 101.2 %shard_map.359 = (f32[1280,1024]{1,0:T(8,128)}, f32[8,1024]{1,0:T(8,128)}, bf16[256,1280]{1,0:T(8,128)(2,1)}, f32[2048,256]{1,0:T(8,128)}, f32[256,2048]{1,0:T(8...) custom-call(bf16[1024,1024]{1,0:T(8,128)(2,1)} %all-gather.2.cloned.1.call-done.own_ref.own_weights, ...), custom_call_target="tpu_custom_call" | custom-call | flops 1048576 | bytes 1048576 | tf_op jit(solution)/shard_map/pallas_call | solution.py:1347
  398.1 0.8 slice.34
  398.9 1.3 fusion.23
  400.1 1.8 broadcast_multiply_fusion.1
  402.0 0.0 copy-start.1
  402.0 2.3 broadcast_multiply_fusion
  404.3 0.9 slice.31
  405.1 1.0 collective-permute-start.5
  406.2 1.6 fusion.12
  407.8 0.4 copy-done.12
  408.1 0.0 copy-start.14
  408.2 4.8 %fusion.15 = (bf16[2048,256]{1,0:T(8,128)(2,1)}, f32[2048,256]{1,0:T(8,128)}, f32[2048,256]{1,0:T(8,128)}, f32[2048,256]{1,0:T(8,128)}) fusion(f32[2048,256]{1,0:T(8,128)S(1)} %copy-done.8, f32[2048,256]{1,0:T(8,128)S(1)} %copy-done.16, f32[]{:T(128)} %bitcast.10, f32[2048,256]{1,0:T(8,128)S(1)} %copy-done.11, f32[2048,256]{1,0:T(8,128)S(1)} %copy-done.12), kind=kLoop, calls=%fused_computation.45 | loop fusion | flops 8912896 | bytes 15728644 | tf_op jit(solution)/shard_map/convert_element_type | solution.py:305
  413.0 1.5 fusion.19
  414.5 0.9 copy-done.9
  415.4 4.9 %fusion.17 = (bf16[256,2048]{1,0:T(8,128)(2,1)}, f32[256,2048]{1,0:T(8,128)}, f32[256,2048]{1,0:T(8,128)}, f32[256,2048]{1,0:T(8,128)}) fusion(f32[256,2048]{1,0:T(8,128)S(1)} %copy-done.9, f32[256,2048]{1,0:T(8,128)S(1)} %copy-done.15, f32[]{:T(128)} %bitcast.10, f32[256,2048]{1,0:T(8,128)S(1)} %copy-done.13, f32[256,2048]{1,0:T(8,128)S(1)} %copy-done.14), kind=kLoop, calls=%fused_computation.46 | loop fusion | flops 8912896 | bytes 15728644 | tf_op jit(solution)/shard_map/convert_element_type | solution.py:305
  420.3 2.1 fusion.9
  422.4 1.9 fusion.13
  424.4 3.4 fusion.21
  427.8 5.0 %fusion = bf16[1,1280,1024]{2,1,0:T(8,128)(2,1)} fusion(f32[1280,1024]{1,0:T(8,128)S(1)} %fusion.9, f32[1280,1024]{1,0:T(8,128)S(1)} %fusion.12, f32[1280,1024]{1,0:T(8,128)S(1)} %bitcast.36, bf16[1280,1024]{1,0:T(8,128)(2,1)} %collective-permute-done.2.refs_14_, bf16[256,1280]{1,0:T(8,128)(2,1)S(1)} %collective-permute-done.5, ...), kind=kOutput, calls=%fused_computation.3 | convolution fusion | flops 681574400 | bytes 24772608 | tf_op jit(solution)/shard_map/ft,fd->td/dot_general | solution.py:309
  432.8 2.4 copy.42
  (64 shorter events, 0.2 us)
Async XLA Ops:
  7.2 112.7 %all-gather.2.cloned.1.call-start = ((), (), s32[]{:S(2)}) async-start(), calls=%async_computation | async-start | bytes 2621440 | tf_op jit(solution)/shard_map/all_gather | solution.py:1476
  74.5 61.5 %collective-permute-start = (bf16[1280,1024]{1,0:T(8,128)(2,1)}, bf16[1280,1024]{1,0:T(8,128)(2,1)S(1)}, u32[]{:S(2)}, u32[]{:S(2)}) collective-permute-start(bf16[1280,1024]{1,0:T(8,128)(2,1)} %get-tuple-element.56.hidden_ref.refs_3_), channel_id=1, source_target_pairs={{0,16},{16,0},{1,17},{17,1},{2,18},{18,2},{3,19},{19,3},{4,20},{20... | collective-permute-start | bytes 7864328 | tf_op jit(solution)/shard_map/ppermute | solution.py:323
  119.9 4.6 %collective-permute-start.1 = (bf16[1024,1024]{1,0:T(8,128)(2,1)}, bf16[1024,1024]{1,0:T(8,128)(2,1)}, u32[]{:S(2)}, u32[]{:S(2)}) collective-permute-start(bf16[1024,1024]{1,0:T(8,128)(2,1)} %all-gather.2.cloned.1.call-done.own_ref.own_weights), channel_id=1, source_target_pairs={{0,1},{1,0},{2,3},{3,2},{4,5},{5,4},{6,7},{7,6},{8,9},{9,8},{10,11... | collective-permute-start | bytes 6291464 | tf_op jit(solution)/shard_map/ppermute | solution.py:323
  136.0 1.5 copy-start.7
  137.5 51.4 %copy-start.26 = (s32[1,12]{1,0:T(1,128)S(1)}, s32[1,12]{1,0:T(1,128)}, u32[]{:S(2)}) copy-start(s32[1,12]{1,0:T(1,128)} %param.20) | copy-start | bytes 148
  185.8 111.2 %collective-permute-start.2 = (bf16[1280,1024]{1,0:T(8,128)(2,1)}, bf16[1280,1024]{1,0:T(8,128)(2,1)}, u32[]{:S(2)}, u32[]{:S(2)}) collective-permute-start(bf16[1280,1024]{1,0:T(8,128)(2,1)} %get-tuple-element.68.refs_9_), channel_id=1, source_target_pairs={{0,16},{16,0},{1,17},{17,1},{2,18},{18,2},{3,19},{19,3},{4,20},{20... | collective-permute-start | bytes 7864328 | tf_op jit(solution)/shard_map/ppermute | solution.py:323
  187.3 109.6 %collective-permute-start.3 = (bf16[2,512,1024]{2,1,0:T(8,128)(2,1)}, bf16[2,512,1024]{2,1,0:T(8,128)(2,1)}, u32[]{:S(2)}, u32[]{:S(2)}) collective-permute-start(bf16[2,512,1024]{2,1,0:T(8,128)(2,1)} %get-tuple-element.71.refs_8_), channel_id=1, source_target_pairs={{0,2},{1,3},{2,0},{3,1},{4,6},{5,7},{6,4},{7,5},{8,10},{9,11},{10,... | collective-permute-start | bytes 6291464 | tf_op jit(solution)/shard_map/ppermute | solution.py:323
  193.2 11.9 %copy-start.4 = (bf16[512,1280]{1,0:T(8,128)(2,1)S(1)}, bf16[512,1280]{1,0:T(8,128)(2,1)}, u32[]{:S(2)}) copy-start(bf16[512,1280]{1,0:T(8,128)(2,1)} %get-tuple-element.64.refs_3_) | copy-start | bytes 3932164
  193.2 227.0 %collective-permute-start.4 = (bf16[512,1024]{1,0:T(8,128)(2,1)}, bf16[512,1024]{1,0:T(8,128)(2,1)}, u32[]{:S(2)}, u32[]{:S(2)}) collective-permute-start(bf16[512,1024]{1,0:T(8,128)(2,1)} %pad_maximum_fusion), channel_id=1, source_target_pairs={{0,16},{16,0},{1,17},{17,1},{2,18},{18,2},{3,19},{19,3},{4,20},{20... | collective-permute-start | bytes 3145736 | tf_op jit(solution)/shard_map/ppermute | solution.py:323
  205.2 1.3 copy-start.5
  294.8 1.1 copy-start
  295.9 1.1 copy-start.2
  400.1 4.1 copy-start.3
  402.0 4.2 copy-start.1
  404.3 3.5 copy-start.16
  405.1 2.6 copy-start.8
  405.1 2.6 copy-start.11
  405.1 3.0 copy-start.12
  405.1 22.6 %collective-permute-start.5 = (bf16[256,1280]{1,0:T(8,128)(2,1)}, bf16[256,1280]{1,0:T(8,128)(2,1)S(1)}, u32[]{:S(2)}, u32[]{:S(2)}) collective-permute-start(bf16[256,1280]{1,0:T(8,128)(2,1)} %slice.31), channel_id=1, source_target_pairs={{0,16},{16,0},{1,17},{17,1},{2,18},{18,2},{3,19},{19,3},{4,20},{20... | collective-permute-start | bytes 1966088 | tf_op jit(solution)/shard_map/ppermute | solution.py:323
  408.1 4.8 %copy-start.17 = (f32[8,64,256]{2,1,0:T(8,128)S(1)}, f32[8,64,256]{2,1,0:T(8,128)}, u32[]{:S(2)}) copy-start(f32[8,64,256]{2,1,0:T(8,128)} %param.24) | copy-start | bytes 1572868
  408.1 4.8 %copy-start.21 = (f32[8,64,256]{2,1,0:T(8,128)S(1)}, f32[8,64,256]{2,1,0:T(8,128)}, u32[]{:S(2)}) copy-start(f32[8,64,256]{2,1,0:T(8,128)} %param.25) | copy-start | bytes 1572868
  408.1 4.9 %copy-start.22 = (f32[8,64,256]{2,1,0:T(8,128)S(1)}, f32[8,64,256]{2,1,0:T(8,128)}, u32[]{:S(2)}) copy-start(f32[8,64,256]{2,1,0:T(8,128)} %param.26) | copy-start | bytes 1572868
  408.1 6.3 %copy-start.13 = (f32[256,2048]{1,0:T(8,128)S(1)}, f32[256,2048]{1,0:T(8,128)}, u32[]{:S(2)}) copy-start(f32[256,2048]{1,0:T(8,128)} %param.28) | copy-start | bytes 6291460
  408.1 6.3 %copy-start.14 = (f32[256,2048]{1,0:T(8,128)S(1)}, f32[256,2048]{1,0:T(8,128)}, u32[]{:S(2)}) copy-start(f32[256,2048]{1,0:T(8,128)} %param.29) | copy-start | bytes 6291460
  408.1 6.3 %copy-start.15 = (f32[256,2048]{1,0:T(8,128)S(1)}, f32[256,2048]{1,0:T(8,128)}, u32[]{:S(2)}) copy-start(f32[256,2048]{1,0:T(8,128)} %get-tuple-element.87) | copy-start | bytes 6291460
  413.0 2.4 copy-start.9
  415.4 4.9 %copy-start.18 = (bf16[256,1280]{1,0:T(8,128)(2,1)S(1)}, bf16[256,1280]{1,0:T(8,128)(2,1)}, u32[]{:S(2)}) copy-start(bf16[256,1280]{1,0:T(8,128)(2,1)} %get-tuple-element.82) | copy-start | bytes 1966084
  420.3 2.1 copy-start.23
  420.3 2.2 copy-start.24
  420.3 2.1 copy-start.25
  420.3 4.0 copy-start.10
  420.3 4.0 copy-start.19
  420.3 4.0 copy-start.20
  420.3 7.4 %slice-start.2 = ((s8[5242880]{0:T(1024)(128)(4,1)}), s8[4194304]{0:T(1024)(128)(4,1)S(1)}, s32[]{:S(2)}) async-start(s8[5242880]{0:T(1024)(128)(4,1)} %bitcast.35), calls=%async_computation.3 | async-start | bytes 8388608
  424.3 3.4 copy-start.6
  424.3 3.4 slice-start.3
  424.4 8.4 %slice-start = ((s8[5242880]{0:T(1024)(128)(4,1)}), s8[1048576]{0:T(1024)(128)(4,1)S(1)}, s32[]{:S(2)}) async-start(s8[5242880]{0:T(1024)(128)(4,1)} %bitcast.32), calls=%async_computation.1 | async-start | bytes 2097152
  427.7 5.1 %slice-start.1 = ((s8[5242880]{0:T(1024)(128)(4,1)}), s8[4194304]{0:T(1024)(128)(4,1)S(1)}, s32[]{:S(2)}) async-start(s8[5242880]{0:T(1024)(128)(4,1)} %bitcast.32), calls=%async_computation.2 | async-start | bytes 8388608
Sparse Core Ops, SparseCore 0:
  74.6 44.4 all-gather.1

commit v9 on v8

--- a/solution.py
+++ b/solution.py
@@ -1053,8 +1053,6 @@
     ]
     loads[0].start()
     loads[1].start()
-    for copy in copies[2:]:
-        copy.start()
     pl.semaphore_wait(barrier, plane + deep - 2)
 
     piece = width // deep
@@ -1086,6 +1084,8 @@
 
     for copy in (*halves, copies[1]):
         copy.wait()
+    for copy in copies[2:]:
+        copy.start()
     row_copies = []
     for n in range(blocks):
         made = lax.dot_general(grads_other[:, at[n]], project[...], tn, preferred_element_type=f32)
@@ -1597,6 +1597,7 @@
     gradients = list(sums)
     gradients[0] = gradients[0].reshape(heads_here, 3 * HD, -1).transpose(2, 0, 1)
     gradients[1] = gradients[1].reshape(mixing_master.shape)
+    gradients[:2] = lax.optimization_barrier(gradients[:2])
     states = (
         (project_master, project_first, project_second, D ** (-0.5)),
         (mixing_master, mixing_first, mixing_second, (D // 32) ** (-0.5)),

time: 449 us -> 449 us (level)
  no operation moved by 1% of the time
where the time goes in v9:
time: 449 us; the launch traced here: 440 us
  Pallas kernels  372 us (83%)
  other arithmetic  19.6 us (4%)
  local copies, waits for them, and re-layouts  14.6 us (3%)
  between operations  14.6 us (3%)
  matrix products  10 us (2%)
  starting transfers between devices  4.73 us (1%)
  waiting for transfers between devices  4.54 us (1%)
    pallas_call x1, Pallas kernels, closing(): pl.pallas_call(partial(closing_kernel, len(after)), in_specs=[anywhere] *...  100 us
    pallas_call x2, Pallas kernels, feed(): pl.pallas_call(partial(feed_kernel, exchange, len(after)), grid=(steps,),...  93 us
    pallas_call x1, Pallas kernels, attend(): pl.pallas_call(partial(attend_kernel, together, parts, len(after)), grid_...  88.4 us
    pallas_call x1, Pallas kernels, opening(): pl.pallas_call(opening_kernel, in_specs=[pl.BlockSpec(memory_space=pl.ANY...  67.2 us
    pallas_call x2, Pallas kernels, project_all(): pl.pallas_call(project_kernel, grid=(tokens // 256,), in_specs=[rows, row...  22.8 us
    convert_element_type x5, other arithmetic, adam_update(): return (master_new, first_new, second_new, master_new.astype(jnp.bfloat16))  17.6 us
    dot_general x3, matrix products, product(): return jnp.einsum(pattern, left, right, preferred_element_type=jnp.float32)  10 us
  transfers between devices with their start and end apart: 7, of which 1 were waited for; matrix products, arithmetic and copies ran while one was open for 7% of the time, Pallas kernels for 58%

profile of v9, /device:TPU:0, one launch (start us, length us, event | category | flops | bytes accessed | tf_op | source)
XLA Modules:
  0.0 439.9 jit_solution(13793844594973538294)
XLA Ops:
  7.2 0.0 all-gather.2.cloned.1.call-start
  7.2 67.2 %shard_map.353 = (bf16[2,1024,1024]{2,1,0:T(8,128)(2,1)}, bf16[2,1024,1024]{2,1,0:T(8,128)(2,1)}, bf16[1024,256]{1,0:T(8,128)(2,1)}, f32[8,1024]{1,0:T(8,128)}, ...) custom-call(f32[256,2048]{1,0:T(8,128)} %expand_hbm.1, f32[2048,256]{1,0:T(8,128)} %shrink_hbm.1, ...), custom_call_target="tpu_custom_call" | custom-call | bytes 1048576 | tf_op jit(solution)/shard_map/pallas_call | solution.py:862
  74.5 0.0 all-gather.2.cloned.1.call-update
  74.5 0.6 collective-permute-start
  75.1 44.8 %shard_map.354 = (f32[2048,1024]{1,0:T(8,128)}, f32[2048,1024]{1,0:T(8,128)}, f32[1280,1024]{1,0:T(8,128)}, f32[1280,1024]{1,0:T(8,128)}) custom-call(bf16[1280,1024]{1,0:T(8,128)(2,1)} %get-tuple-element.58.hidden_ref.refs_3_, bf16[1280,1024]{1,0:T(8,128)(2,1)} %bitcast.23, bf16[2,1024,1024]{2,1,0:T(8,128)(2,1)} %get-tuple-element.59.expand_ref, ...), custom_call_target="tpu_custom_call" | custom-call | flops 1048576 | bytes 1048576 | tf_op jit(solution)/shard_map/pallas_call | solution.py:502
  119.9 0.0 all-gather.2.cloned.1.call-done.own_ref.own_weights
  119.9 0.1 collective-permute-start.1
  120.0 4.5 %collective-permute-done.1.sibling_ref.sibling_weights = bf16[1024,1024]{1,0:T(8,128)(2,1)} collective-permute-done((bf16[1024,1024]{1,0:T(8,128)(2,1)}, bf16[1024,1024]{1,0:T(8,128)(2,1)}, u32[]{:S(2)}, u32[]{:S(2)}) %collective-permute-start.1) | collective-permute-done | bytes 2097184 | tf_op jit(solution)/shard_map/ppermute | solution.py:323
  124.5 11.4 %shard_map.355 = (f32[1536,1280]{1,0:T(8,128)}, bf16[512,1280]{1,0:T(8,128)(2,1)}) custom-call(bf16[1280,1024]{1,0:T(8,128)(2,1)} %get-tuple-element.58.hidden_ref.refs_3_, bf16[1280,1024]{1,0:T(8,128)(2,1)} %bitcast.24, bf16[1024,1024]{1,0:T(8,128)(2,1)} %all-gather.2.cloned.1.call-done.own_ref.own_weights, ...), custom_call_target="tpu_custom_call" | custom-call | flops 1048576 | bytes 1048576 | tf_op jit(solution)/shard_map/pallas_call | solution.py:841
  135.9 1.5 copy-done.6
  137.4 48.2 %shard_map.356 = (f32[2,512,1024]{2,1,0:T(8,128)}, bf16[2,512,1024]{2,1,0:T(8,128)(2,1)}, f32[2,2,512,1024]{3,2,1,0:T(8,128)}, f32[1280,1024]{1,0:T(8,128)}, bf16[1280,1024]{1,0:T(8,128)(2,1)}) custom-call(bf16[1280,1024]{1,0:T(8,128)(2,1)} %copy-done.6, bf16[1280,1024]{1,0:T(8,128)(2,1)} %get-tuple-element.62.back_ref.refs_6_, ...), custom_call_target="tpu_custom_call" | custom-call | flops 1048576 | bytes 1048576 | tf_op jit(solution)/shard_map/pallas_call | solution.py:502
  185.7 1.6 collective-permute-start.2
  187.2 1.5 collective-permute-start.3
  188.8 0.1 select_reduce_fusion.1
  188.9 0.1 select_reduce_fusion
  189.0 0.1 slice.27
  189.1 0.1 pad_add_fusion.refs_0_
  189.2 0.6 multiply_sine_fusion
  189.9 1.1 slice.28
  191.0 1.1 slice.36
  192.1 0.8 copy-done.10
  192.8 1.0 pad_maximum_fusion
  193.9 0.5 collective-permute-start.4
  194.4 11.4 %shard_map.357 = (f32[1536,1280]{1,0:T(8,128)}, bf16[512,1280]{1,0:T(8,128)(2,1)}) custom-call(bf16[1280,1024]{1,0:T(8,128)(2,1)} %copy-done.6, bf16[1280,1024]{1,0:T(8,128)(2,1)} %get-tuple-element.62.back_ref.refs_6_, bf16[1024,1024]{1,0:T(8,128)(2,1)} %all-gather.2.cloned.1.call-done.own_ref.own_weights, ...), custom_call_target="tpu_custom_call" | custom-call | flops 1048576 | bytes 1048576 | tf_op jit(solution)/shard_map/pallas_call | solution.py:841
  205.8 1.3 copy-done.4
  207.1 88.4 %shard_map.358 = (bf16[512,1280]{1,0:T(8,128)(2,1)S(1)}, bf16[512,1280]{1,0:T(8,128)(2,1)S(1)}, bf16[1536,1280]{1,0:T(8,128)(2,1)}, bf16[1536,1280]{1,0:T(8,128)(2,1)}) custom-call(s32[11]{0:T(128)S(1)} %pad_add_fusion.refs_0_, f32[1536,1280]{1,0:T(8,128)} %get-tuple-element.65.refs_1_, f32[1536,1280]{1,0:T(8,128)} %get-tuple-element.71.refs_2_, ...), custom_call_target="tpu_custom_call" | custom-call | flops 1048576 | bytes 1048576 | tf_op jit(solution)/shard_map/pallas_call | solution.py:252
  295.5 1.1 copy-done
  296.6 1.1 copy-done.2
  297.6 100.3 %shard_map.359 = (f32[1280,1024]{1,0:T(8,128)}, f32[8,1024]{1,0:T(8,128)}, bf16[256,1280]{1,0:T(8,128)(2,1)}, f32[2048,256]{1,0:T(8,128)}, f32[256,2048]{1,0:T(8...) custom-call(bf16[1024,1024]{1,0:T(8,128)(2,1)} %all-gather.2.cloned.1.call-done.own_ref.own_weights, ...), custom_call_target="tpu_custom_call" | custom-call | flops 1048576 | bytes 1048576 | tf_op jit(solution)/shard_map/pallas_call | solution.py:1347
  398.0 0.8 slice.34
  398.7 1.3 fusion.23
  400.0 2.1 slice.31
  402.1 0.4 collective-permute-start.5
  402.5 2.8 fusion.12
  405.3 0.0 copy-start.17
  405.3 0.0 copy-start.22
  405.4 0.0 copy-start.14
  405.4 4.9 %fusion.15 = (bf16[2048,256]{1,0:T(8,128)(2,1)}, f32[2048,256]{1,0:T(8,128)}, f32[2048,256]{1,0:T(8,128)}, f32[2048,256]{1,0:T(8,128)}) fusion(f32[2048,256]{1,0:T(8,128)S(1)} %copy-done.7, f32[2048,256]{1,0:T(8,128)S(1)} %copy-done.16, f32[]{:T(128)} %bitcast.10, f32[2048,256]{1,0:T(8,128)S(1)} %copy-done.11, f32[2048,256]{1,0:T(8,128)S(1)} %copy-done.12), kind=kLoop, calls=%fused_computation.43 | loop fusion | flops 8912896 | bytes 15728644 | tf_op jit(solution)/shard_map/convert_element_type | solution.py:305
  410.4 2.3 fusion.19
  412.7 5.0 %fusion.17 = (bf16[256,2048]{1,0:T(8,128)(2,1)}, f32[256,2048]{1,0:T(8,128)}, f32[256,2048]{1,0:T(8,128)}, f32[256,2048]{1,0:T(8,128)}) fusion(f32[256,2048]{1,0:T(8,128)S(1)} %copy-done.8, f32[256,2048]{1,0:T(8,128)S(1)} %copy-done.15, f32[]{:T(128)} %bitcast.10, f32[256,2048]{1,0:T(8,128)S(1)} %copy-done.13, f32[256,2048]{1,0:T(8,128)S(1)} %copy-done.14), kind=kLoop, calls=%fused_computation.44 | loop fusion | flops 8912896 | bytes 15728644 | tf_op jit(solution)/shard_map/convert_element_type | solution.py:305
  417.7 0.0 copy-start.26
  417.7 0.0 copy-start.27
  417.8 0.0 copy-start.20
  417.8 2.1 fusion.9
  419.9 1.3 fusion.13
  421.3 4.1 fusion.21
  425.4 5.2 %fusion = bf16[1,1280,1024]{2,1,0:T(8,128)(2,1)} fusion(f32[1280,1024]{1,0:T(8,128)S(1)} %fusion.9, f32[1280,1024]{1,0:T(8,128)S(1)} %fusion.12, f32[1280,1024]{1,0:T(8,128)S(1)} %bitcast.35, bf16[1280,1024]{1,0:T(8,128)(2,1)} %collective-permute-done.2.refs_14_, bf16[256,1280]{1,0:T(8,128)(2,1)} %collective-permute-done.5, ...), kind=kOutput, calls=%fused_computation.3 | convolution fusion | flops 681574400 | bytes 24772608 | tf_op jit(solution)/shard_map/ft,fd->td/dot_general | solution.py:309
  430.6 2.4 copy.42
  (66 shorter events, 0.2 us)
Async XLA Ops:
  7.2 112.7 %all-gather.2.cloned.1.call-start = ((), (), s32[]{:S(2)}) async-start(), calls=%async_computation | async-start | bytes 2621440 | tf_op jit(solution)/shard_map/all_gather | solution.py:1476
  74.5 61.4 %collective-permute-start = (bf16[1280,1024]{1,0:T(8,128)(2,1)}, bf16[1280,1024]{1,0:T(8,128)(2,1)S(1)}, u32[]{:S(2)}, u32[]{:S(2)}) collective-permute-start(bf16[1280,1024]{1,0:T(8,128)(2,1)} %get-tuple-element.58.hidden_ref.refs_3_), channel_id=1, source_target_pairs={{0,16},{16,0},{1,17},{17,1},{2,18},{18,2},{3,19},{19,3},{4,20},{20... | collective-permute-start | bytes 7864328 | tf_op jit(solution)/shard_map/ppermute | solution.py:323
  119.9 4.6 %collective-permute-start.1 = (bf16[1024,1024]{1,0:T(8,128)(2,1)}, bf16[1024,1024]{1,0:T(8,128)(2,1)}, u32[]{:S(2)}, u32[]{:S(2)}) collective-permute-start(bf16[1024,1024]{1,0:T(8,128)(2,1)} %all-gather.2.cloned.1.call-done.own_ref.own_weights), channel_id=1, source_target_pairs={{0,1},{1,0},{2,3},{3,2},{4,5},{5,4},{6,7},{7,6},{8,9},{9,8},{10,11... | collective-permute-start | bytes 6291464 | tf_op jit(solution)/shard_map/ppermute | solution.py:323
  135.9 1.5 copy-start.6
  137.4 51.3 %copy-start.28 = (s32[1,12]{1,0:T(1,128)S(1)}, s32[1,12]{1,0:T(1,128)}, u32[]{:S(2)}) copy-start(s32[1,12]{1,0:T(1,128)} %param.20) | copy-start | bytes 148
  185.7 112.0 %collective-permute-start.2 = (bf16[1280,1024]{1,0:T(8,128)(2,1)}, bf16[1280,1024]{1,0:T(8,128)(2,1)}, u32[]{:S(2)}, u32[]{:S(2)}) collective-permute-start(bf16[1280,1024]{1,0:T(8,128)(2,1)} %get-tuple-element.70.refs_9_), channel_id=1, source_target_pairs={{0,16},{16,0},{1,17},{17,1},{2,18},{18,2},{3,19},{19,3},{4,20},{20... | collective-permute-start | bytes 7864328 | tf_op jit(solution)/shard_map/ppermute | solution.py:323
  187.2 110.4 %collective-permute-start.3 = (bf16[2,512,1024]{2,1,0:T(8,128)(2,1)}, bf16[2,512,1024]{2,1,0:T(8,128)(2,1)}, u32[]{:S(2)}, u32[]{:S(2)}) collective-permute-start(bf16[2,512,1024]{2,1,0:T(8,128)(2,1)} %get-tuple-element.73.refs_8_), channel_id=1, source_target_pairs={{0,2},{1,3},{2,0},{3,1},{4,6},{5,7},{6,4},{7,5},{8,10},{9,11},{10,... | collective-permute-start | bytes 6291464 | tf_op jit(solution)/shard_map/ppermute | solution.py:323
  192.0 0.8 copy-start.10
  193.9 11.9 %copy-start.3 = (bf16[512,1280]{1,0:T(8,128)(2,1)S(1)}, bf16[512,1280]{1,0:T(8,128)(2,1)}, u32[]{:S(2)}) copy-start(bf16[512,1280]{1,0:T(8,128)(2,1)} %get-tuple-element.66.refs_3_) | copy-start | bytes 3932164
  193.9 223.8 %collective-permute-start.4 = (bf16[512,1024]{1,0:T(8,128)(2,1)}, bf16[512,1024]{1,0:T(8,128)(2,1)}, u32[]{:S(2)}, u32[]{:S(2)}) collective-permute-start(bf16[512,1024]{1,0:T(8,128)(2,1)} %pad_maximum_fusion), channel_id=1, source_target_pairs={{0,16},{16,0},{1,17},{17,1},{2,18},{18,2},{3,19},{19,3},{4,20},{20... | collective-permute-start | bytes 3145736 | tf_op jit(solution)/shard_map/ppermute | solution.py:323
  205.8 1.3 copy-start.4
  295.5 1.1 copy-start
  296.6 1.1 copy-start.2
  297.6 104.9 %copy-start.1 = (bf16[512,1280]{1,0:T(8,128)(2,1)S(1)}, bf16[512,1280]{1,0:T(8,128)(2,1)}, u32[]{:S(2)}) copy-start(bf16[512,1280]{1,0:T(8,128)(2,1)} %copy-done) | copy-start | bytes 3932164
  400.0 5.3 %copy-start.16 = (f32[2048,256]{1,0:T(8,128)S(1)}, f32[2048,256]{1,0:T(8,128)}, u32[]{:S(2)}) copy-start(f32[2048,256]{1,0:T(8,128)} %get-tuple-element.92) | copy-start | bytes 6291460
  402.1 3.2 copy-start.7
  402.1 3.2 copy-start.11
  402.1 3.2 copy-start.12
  402.1 23.2 %collective-permute-start.5 = (bf16[256,1280]{1,0:T(8,128)(2,1)}, bf16[256,1280]{1,0:T(8,128)(2,1)}, u32[]{:S(2)}, u32[]{:S(2)}) collective-permute-start(bf16[256,1280]{1,0:T(8,128)(2,1)} %slice.31), channel_id=1, source_target_pairs={{0,16},{16,0},{1,17},{17,1},{2,18},{18,2},{3,19},{19,3},{4,20},{20... | collective-permute-start | bytes 1966088 | tf_op jit(solution)/shard_map/ppermute | solution.py:323
  405.3 5.0 %copy-start.17 = (f32[8,64,256]{2,1,0:T(8,128)S(1)}, f32[8,64,256]{2,1,0:T(8,128)}, u32[]{:S(2)}) copy-start(f32[8,64,256]{2,1,0:T(8,128)} %param.24) | copy-start | bytes 1572868
  405.3 5.0 %copy-start.22 = (f32[8,64,256]{2,1,0:T(8,128)S(1)}, f32[8,64,256]{2,1,0:T(8,128)}, u32[]{:S(2)}) copy-start(f32[8,64,256]{2,1,0:T(8,128)} %param.25) | copy-start | bytes 1572868
  405.4 5.0 %copy-start.23 = (f32[8,64,256]{2,1,0:T(8,128)S(1)}, f32[8,64,256]{2,1,0:T(8,128)}, u32[]{:S(2)}) copy-start(f32[8,64,256]{2,1,0:T(8,128)} %param.26) | copy-start | bytes 1572868
  405.4 5.0 %copy-start.24 = (f32[512,256]{1,0:T(8,128)S(1)}, f32[512,256]{1,0:T(8,128)}, u32[]{:S(2)}) copy-start(f32[512,256]{1,0:T(8,128)} %get-tuple-element.88) | copy-start | bytes 1572868
  405.4 7.3 %copy-start.13 = (f32[256,2048]{1,0:T(8,128)S(1)}, f32[256,2048]{1,0:T(8,128)}, u32[]{:S(2)}) copy-start(f32[256,2048]{1,0:T(8,128)} %param.28) | copy-start | bytes 6291460
  405.4 7.3 %copy-start.14 = (f32[256,2048]{1,0:T(8,128)S(1)}, f32[256,2048]{1,0:T(8,128)}, u32[]{:S(2)}) copy-start(f32[256,2048]{1,0:T(8,128)} %param.29) | copy-start | bytes 6291460
  405.4 7.3 %copy-start.15 = (f32[256,2048]{1,0:T(8,128)S(1)}, f32[256,2048]{1,0:T(8,128)}, u32[]{:S(2)}) copy-start(f32[256,2048]{1,0:T(8,128)} %get-tuple-element.91) | copy-start | bytes 6291460
  410.4 2.3 copy-start.8
  412.7 5.0 %copy-start.18 = (bf16[256,1280]{1,0:T(8,128)(2,1)S(1)}, bf16[256,1280]{1,0:T(8,128)(2,1)}, u32[]{:S(2)}) copy-start(bf16[256,1280]{1,0:T(8,128)(2,1)} %get-tuple-element.84) | copy-start | bytes 1966084
  412.7 12.6 %slice-start.2 = ((s8[5242880]{0:T(1024)(128)(4,1)}), s8[4194304]{0:T(1024)(128)(4,1)S(1)}, s32[]{:S(2)}) async-start(s8[5242880]{0:T(1024)(128)(4,1)} %bitcast.34), calls=%async_computation.3 | async-start | bytes 8388608
  417.7 2.2 copy-start.25
  417.7 2.2 copy-start.26
  417.7 2.2 copy-start.27
  417.7 3.5 copy-start.9
  417.7 3.5 copy-start.19
  417.8 3.5 copy-start.20
  417.8 3.5 copy-start.21
  417.8 7.6 %slice-start.3 = ((s8[5242880]{0:T(1024)(128)(4,1)}), s8[1048576]{0:T(1024)(128)(4,1)S(1)}, s32[]{:S(2)}) async-start(s8[5242880]{0:T(1024)(128)(4,1)} %bitcast.34), calls=%async_computation.4 | async-start | bytes 2097152
  421.2 4.1 copy-start.5
  421.2 9.3 %slice-start = ((s8[5242880]{0:T(1024)(128)(4,1)}), s8[4194304]{0:T(1024)(128)(4,1)S(1)}, s32[]{:S(2)}) async-start(s8[5242880]{0:T(1024)(128)(4,1)} %bitcast.31), calls=%async_computation.1 | async-start | bytes 8388608
  425.3 5.2 %slice-start.1 = ((s8[5242880]{0:T(1024)(128)(4,1)}), s8[1048576]{0:T(1024)(128)(4,1)S(1)}, s32[]{:S(2)}) async-start(s8[5242880]{0:T(1024)(128)(4,1)} %bitcast.31), calls=%async_computation.2 | async-start | bytes 2097152
Sparse Core Ops, SparseCore 0:
  74.6 44.4 all-gather.1

commit v10 on v9

--- a/solution.py
+++ b/solution.py
@@ -1351,7 +1351,7 @@
         out_shape=[
             jax.ShapeDtypeStruct((tokens, width), f32),
             jax.ShapeDtypeStruct((8, width), f32),
-            jax.ShapeDtypeStruct((few, tokens), low),
+            jax.ShapeDtypeStruct((few // 2, tokens), low),
         ]
         + [
             jax.ShapeDtypeStruct(shape, f32)

time: 449 us -> 451 us (level)
  no operation moved by 1% of the time
where the time goes in v10:
time: 451 us; the launch traced here: 442 us
  Pallas kernels  372 us (82%)
  other arithmetic  22 us (5%)
  between operations  14.7 us (3%)
  local copies, waits for them, and re-layouts  13.6 us (3%)
  matrix products  9.67 us (2%)
  starting transfers between devices  5.69 us (1%)
  waiting for transfers between devices  4.54 us (1%)
    pallas_call x1, Pallas kernels, closing(): pl.pallas_call(partial(closing_kernel, len(after)), in_specs=[anywhere] *...  101 us
    pallas_call x2, Pallas kernels, feed(): pl.pallas_call(partial(feed_kernel, exchange, len(after)), grid=(steps,),...  93 us
    pallas_call x1, Pallas kernels, attend(): pl.pallas_call(partial(attend_kernel, together, parts, len(after)), grid_...  88.4 us
    pallas_call x1, Pallas kernels, opening(): pl.pallas_call(opening_kernel, in_specs=[pl.BlockSpec(memory_space=pl.ANY...  67.2 us
    pallas_call x2, Pallas kernels, project_all(): pl.pallas_call(project_kernel, grid=(tokens // 256,), in_specs=[rows, row...  22.9 us
    convert_element_type x5, other arithmetic, adam_update(): return (master_new, first_new, second_new, master_new.astype(jnp.bfloat16))  20 us
    dot_general x3, matrix products, product(): return jnp.einsum(pattern, left, right, preferred_element_type=jnp.float32)  9.67 us
  transfers between devices with their start and end apart: 7, of which 1 were waited for; matrix products, arithmetic and copies ran while one was open for 7% of the time, Pallas kernels for 58%

profile of v10, /device:TPU:0, one launch (start us, length us, event | category | flops | bytes accessed | tf_op | source)
XLA Modules:
  0.0 442.4 jit_solution(8560147801223999973)
XLA Ops:
  7.2 0.0 all-gather.2.cloned.1.call-start
  7.2 67.2 %shard_map.353 = (bf16[2,1024,1024]{2,1,0:T(8,128)(2,1)}, bf16[2,1024,1024]{2,1,0:T(8,128)(2,1)}, bf16[1024,256]{1,0:T(8,128)(2,1)}, f32[8,1024]{1,0:T(8,128)}, ...) custom-call(f32[256,2048]{1,0:T(8,128)} %expand_hbm.1, f32[2048,256]{1,0:T(8,128)} %shrink_hbm.1, ...), custom_call_target="tpu_custom_call" | custom-call | bytes 1048576 | tf_op jit(solution)/shard_map/pallas_call | solution.py:862
  74.5 0.0 all-gather.2.cloned.1.call-update
  74.5 0.6 collective-permute-start
  75.1 44.8 %shard_map.354 = (f32[2048,1024]{1,0:T(8,128)}, f32[2048,1024]{1,0:T(8,128)}, f32[1280,1024]{1,0:T(8,128)}, f32[1280,1024]{1,0:T(8,128)}) custom-call(bf16[1280,1024]{1,0:T(8,128)(2,1)} %get-tuple-element.58.hidden_ref.refs_3_, bf16[1280,1024]{1,0:T(8,128)(2,1)} %bitcast.23, bf16[2,1024,1024]{2,1,0:T(8,128)(2,1)} %get-tuple-element.59.expand_ref, ...), custom_call_target="tpu_custom_call" | custom-call | flops 1048576 | bytes 1048576 | tf_op jit(solution)/shard_map/pallas_call | solution.py:502
  119.9 0.0 all-gather.2.cloned.1.call-done.own_ref.own_weights
  119.9 0.1 collective-permute-start.1
  120.0 4.5 %collective-permute-done.1.sibling_ref.sibling_weights = bf16[1024,1024]{1,0:T(8,128)(2,1)} collective-permute-done((bf16[1024,1024]{1,0:T(8,128)(2,1)}, bf16[1024,1024]{1,0:T(8,128)(2,1)}, u32[]{:S(2)}, u32[]{:S(2)}) %collective-permute-start.1) | collective-permute-done | bytes 2097184 | tf_op jit(solution)/shard_map/ppermute | solution.py:323
  124.5 11.4 %shard_map.355 = (f32[1536,1280]{1,0:T(8,128)}, bf16[512,1280]{1,0:T(8,128)(2,1)}) custom-call(bf16[1280,1024]{1,0:T(8,128)(2,1)} %get-tuple-element.58.hidden_ref.refs_3_, bf16[1280,1024]{1,0:T(8,128)(2,1)} %bitcast.24, bf16[1024,1024]{1,0:T(8,128)(2,1)} %all-gather.2.cloned.1.call-done.own_ref.own_weights, ...), custom_call_target="tpu_custom_call" | custom-call | flops 1048576 | bytes 1048576 | tf_op jit(solution)/shard_map/pallas_call | solution.py:841
  136.0 1.5 copy-done.7
  137.4 48.2 %shard_map.356 = (f32[2,512,1024]{2,1,0:T(8,128)}, bf16[2,512,1024]{2,1,0:T(8,128)(2,1)}, f32[2,2,512,1024]{3,2,1,0:T(8,128)}, f32[1280,1024]{1,0:T(8,128)}, bf16[1280,1024]{1,0:T(8,128)(2,1)}) custom-call(bf16[1280,1024]{1,0:T(8,128)(2,1)} %copy-done.7, bf16[1280,1024]{1,0:T(8,128)(2,1)} %get-tuple-element.62.back_ref.refs_6_, ...), custom_call_target="tpu_custom_call" | custom-call | flops 1048576 | bytes 1048576 | tf_op jit(solution)/shard_map/pallas_call | solution.py:502
  185.6 1.6 collective-permute-start.2
  187.2 1.5 collective-permute-start.3
  188.7 0.1 select_reduce_fusion.1
  188.8 0.1 select_reduce_fusion
  189.0 0.1 slice.27
  189.1 0.1 pad_add_fusion.refs_0_
  189.2 0.6 multiply_sine_fusion
  189.8 1.1 slice.28
  190.9 1.1 slice.36
  192.0 0.0 copy-start.11
  192.0 0.8 copy-done.11
  192.8 1.0 pad_maximum_fusion
  193.8 0.5 collective-permute-start.4
  194.4 11.5 %shard_map.357 = (f32[1536,1280]{1,0:T(8,128)}, bf16[512,1280]{1,0:T(8,128)(2,1)}) custom-call(bf16[1280,1024]{1,0:T(8,128)(2,1)} %copy-done.7, bf16[1280,1024]{1,0:T(8,128)(2,1)} %get-tuple-element.62.back_ref.refs_6_, bf16[1024,1024]{1,0:T(8,128)(2,1)} %all-gather.2.cloned.1.call-done.own_ref.own_weights, ...), custom_call_target="tpu_custom_call" | custom-call | flops 1048576 | bytes 1048576 | tf_op jit(solution)/shard_map/pallas_call | solution.py:841
  205.9 0.0 copy-start.5
  205.9 1.3 copy-done.5
  207.2 88.4 %shard_map.358 = (bf16[512,1280]{1,0:T(8,128)(2,1)S(1)}, bf16[512,1280]{1,0:T(8,128)(2,1)S(1)}, bf16[1536,1280]{1,0:T(8,128)(2,1)}, bf16[1536,1280]{1,0:T(8,128)(2,1)}) custom-call(s32[11]{0:T(128)S(1)} %pad_add_fusion.refs_0_, f32[1536,1280]{1,0:T(8,128)} %get-tuple-element.65.refs_1_, f32[1536,1280]{1,0:T(8,128)} %get-tuple-element.71.refs_2_, ...), custom_call_target="tpu_custom_call" | custom-call | flops 1048576 | bytes 1048576 | tf_op jit(solution)/shard_map/pallas_call | solution.py:252
  295.6 1.1 copy-done
  296.6 1.1 copy-done.2
  297.7 100.7 %shard_map.359 = (f32[1280,1024]{1,0:T(8,128)}, f32[8,1024]{1,0:T(8,128)}, bf16[128,1280]{1,0:T(8,128)(2,1)}, f32[2048,256]{1,0:T(8,128)}, f32[256,2048]{1,0:T(8...) custom-call(bf16[1024,1024]{1,0:T(8,128)(2,1)} %all-gather.2.cloned.1.call-done.own_ref.own_weights, ...), custom_call_target="tpu_custom_call" | custom-call | flops 1048576 | bytes 1048576 | tf_op jit(solution)/shard_map/pallas_call | solution.py:1347
  398.4 0.9 slice.34
  399.3 1.3 fusion.23
  400.6 1.0 slice.31
  401.6 1.4 collective-permute-start.5
  403.0 1.6 fusion.12
  404.5 0.0 copy-start.18
  404.6 0.0 copy-start.13
  404.6 0.0 copy-start.14
  404.6 4.2 fusion.21
  408.8 2.3 fusion.19
  411.2 4.8 %fusion.15 = (bf16[2048,256]{1,0:T(8,128)(2,1)}, f32[2048,256]{1,0:T(8,128)}, f32[2048,256]{1,0:T(8,128)}, f32[2048,256]{1,0:T(8,128)}) fusion(f32[2048,256]{1,0:T(8,128)S(1)} %copy-done.8, f32[2048,256]{1,0:T(8,128)S(1)} %copy-done.17, f32[]{:T(128)} %bitcast.10, f32[2048,256]{1,0:T(8,128)S(1)} %copy-done.13, f32[2048,256]{1,0:T(8,128)S(1)} %copy-done.14), kind=kLoop, calls=%fused_computation.43 | loop fusion | flops 8912896 | bytes 15728644 | tf_op jit(solution)/shard_map/convert_element_type | solution.py:305
  416.0 0.0 copy-start.9
  416.1 2.0 fusion.9
  418.1 1.8 fusion.13
  419.9 7.0 %fusion.17 = (bf16[256,2048]{1,0:T(8,128)(2,1)}, f32[256,2048]{1,0:T(8,128)}, f32[256,2048]{1,0:T(8,128)}, f32[256,2048]{1,0:T(8,128)}) fusion(f32[256,2048]{1,0:T(8,128)S(1)} %copy-done.9, f32[256,2048]{1,0:T(8,128)} %get-tuple-element.91, f32[]{:T(128)} %bitcast.10, f32[256,2048]{1,0:T(8,128)S(1)} %copy-done.15, f32[256,2048]{1,0:T(8,128)S(1)} %copy-done.16), kind=kLoop, calls=%fused_computation.44 | loop fusion | flops 8912896 | bytes 15728644 | tf_op jit(solution)/shard_map/convert_element_type | solution.py:305
  426.9 6.2 %fusion = bf16[1,1280,1024]{2,1,0:T(8,128)(2,1)} fusion(f32[1280,1024]{1,0:T(8,128)S(1)} %fusion.9, f32[1280,1024]{1,0:T(8,128)S(1)} %fusion.12, f32[1280,1024]{1,0:T(8,128)S(1)} %bitcast.35, bf16[1280,1024]{1,0:T(8,128)(2,1)} %collective-permute-done.2.refs_14_, bf16[384,1280]{1,0:T(8,128)(2,1)} %collective-permute-done.5, ...), kind=kOutput, calls=%fused_computation.3 | convolution fusion | flops 1017118720 | bytes 25362432 | tf_op jit(solution)/shard_map/ft,fd->td/dot_general | solution.py:309
  433.0 2.4 copy.42
  (68 shorter events, 0.2 us)
Async XLA Ops:
  7.2 112.8 %all-gather.2.cloned.1.call-start = ((), (), s32[]{:S(2)}) async-start(), calls=%async_computation | async-start | bytes 2621440 | tf_op jit(solution)/shard_map/all_gather | solution.py:1476
  74.5 61.4 %collective-permute-start = (bf16[1280,1024]{1,0:T(8,128)(2,1)}, bf16[1280,1024]{1,0:T(8,128)(2,1)S(1)}, u32[]{:S(2)}, u32[]{:S(2)}) collective-permute-start(bf16[1280,1024]{1,0:T(8,128)(2,1)} %get-tuple-element.58.hidden_ref.refs_3_), channel_id=1, source_target_pairs={{0,16},{16,0},{1,17},{17,1},{2,18},{18,2},{3,19},{19,3},{4,20},{20... | collective-permute-start | bytes 7864328 | tf_op jit(solution)/shard_map/ppermute | solution.py:323
  119.9 4.6 %collective-permute-start.1 = (bf16[1024,1024]{1,0:T(8,128)(2,1)}, bf16[1024,1024]{1,0:T(8,128)(2,1)}, u32[]{:S(2)}, u32[]{:S(2)}) collective-permute-start(bf16[1024,1024]{1,0:T(8,128)(2,1)} %all-gather.2.cloned.1.call-done.own_ref.own_weights), channel_id=1, source_target_pairs={{0,1},{1,0},{2,3},{3,2},{4,5},{5,4},{6,7},{7,6},{8,9},{9,8},{10,11... | collective-permute-start | bytes 6291464 | tf_op jit(solution)/shard_map/ppermute | solution.py:323
  135.9 1.5 copy-start.7
  137.4 51.3 %copy-start.29 = (s32[1,12]{1,0:T(1,128)S(1)}, s32[1,12]{1,0:T(1,128)}, u32[]{:S(2)}) copy-start(s32[1,12]{1,0:T(1,128)} %param.20) | copy-start | bytes 148
  185.6 112.0 %collective-permute-start.2 = (bf16[1280,1024]{1,0:T(8,128)(2,1)}, bf16[1280,1024]{1,0:T(8,128)(2,1)}, u32[]{:S(2)}, u32[]{:S(2)}) collective-permute-start(bf16[1280,1024]{1,0:T(8,128)(2,1)} %get-tuple-element.70.refs_9_), channel_id=1, source_target_pairs={{0,16},{16,0},{1,17},{17,1},{2,18},{18,2},{3,19},{19,3},{4,20},{20... | collective-permute-start | bytes 7864328 | tf_op jit(solution)/shard_map/ppermute | solution.py:323
  187.2 110.5 %collective-permute-start.3 = (bf16[2,512,1024]{2,1,0:T(8,128)(2,1)}, bf16[2,512,1024]{2,1,0:T(8,128)(2,1)}, u32[]{:S(2)}, u32[]{:S(2)}) collective-permute-start(bf16[2,512,1024]{2,1,0:T(8,128)(2,1)} %get-tuple-element.73.refs_8_), channel_id=1, source_target_pairs={{0,2},{1,3},{2,0},{3,1},{4,6},{5,7},{6,4},{7,5},{8,10},{9,11},{10,... | collective-permute-start | bytes 6291464 | tf_op jit(solution)/shard_map/ppermute | solution.py:323
  192.0 0.8 copy-start.11
  193.8 12.0 %copy-start.4 = (bf16[512,1280]{1,0:T(8,128)(2,1)S(1)}, bf16[512,1280]{1,0:T(8,128)(2,1)}, u32[]{:S(2)}) copy-start(bf16[512,1280]{1,0:T(8,128)(2,1)} %get-tuple-element.66.refs_3_) | copy-start | bytes 3932164
  193.8 222.2 %collective-permute-start.4 = (bf16[512,1024]{1,0:T(8,128)(2,1)}, bf16[512,1024]{1,0:T(8,128)(2,1)}, u32[]{:S(2)}, u32[]{:S(2)}) collective-permute-start(bf16[512,1024]{1,0:T(8,128)(2,1)} %pad_maximum_fusion), channel_id=1, source_target_pairs={{0,16},{16,0},{1,17},{17,1},{2,18},{18,2},{3,19},{19,3},{4,20},{20... | collective-permute-start | bytes 3145736 | tf_op jit(solution)/shard_map/ppermute | solution.py:323
  205.9 1.3 copy-start.5
  295.6 1.1 copy-start
  296.6 1.1 copy-start.2
  297.7 102.9 %copy-start.3 = (bf16[512,1280]{1,0:T(8,128)(2,1)S(1)}, bf16[512,1280]{1,0:T(8,128)(2,1)}, u32[]{:S(2)}) copy-start(bf16[512,1280]{1,0:T(8,128)(2,1)} %copy-done.2) | copy-start | bytes 3932164
  398.4 4.6 %copy-start.1 = (bf16[512,1280]{1,0:T(8,128)(2,1)S(1)}, bf16[512,1280]{1,0:T(8,128)(2,1)}, u32[]{:S(2)}) copy-start(bf16[512,1280]{1,0:T(8,128)(2,1)} %copy-done) | copy-start | bytes 3932164
  398.4 4.6 %copy-start.12 = (bf16[256,1024]{1,0:T(8,128)(2,1)S(1)}, bf16[256,1024]{1,0:T(8,128)(2,1)}, u32[]{:S(2)}) copy-start(bf16[256,1024]{1,0:T(8,128)(2,1)} %copy-done.11) | copy-start | bytes 1572868
  401.6 2.9 copy-start.10
  401.6 2.9 copy-start.19
  401.6 3.0 copy-start.20
  401.6 3.0 copy-start.21
  401.6 25.3 %collective-permute-start.5 = (bf16[384,1280]{1,0:T(8,128)(2,1)}, bf16[384,1280]{1,0:T(8,128)(2,1)}, u32[]{:S(2)}, u32[]{:S(2)}) collective-permute-start(bf16[384,1280]{1,0:T(8,128)(2,1)} %slice.31), channel_id=1, source_target_pairs={{0,16},{16,0},{1,17},{17,1},{2,18},{18,2},{3,19},{19,3},{4,20},{20... | collective-permute-start | bytes 2949128 | tf_op jit(solution)/shard_map/ppermute | solution.py:323
  404.5 4.2 copy-start.18
  404.6 4.2 copy-start.23
  404.6 4.2 copy-start.24
  404.6 4.2 copy-start.25
  404.6 6.6 %copy-start.13 = (f32[2048,256]{1,0:T(8,128)S(1)}, f32[2048,256]{1,0:T(8,128)}, u32[]{:S(2)}) copy-start(f32[2048,256]{1,0:T(8,128)} %param.31) | copy-start | bytes 6291460
  404.6 6.5 %copy-start.14 = (f32[2048,256]{1,0:T(8,128)S(1)}, f32[2048,256]{1,0:T(8,128)}, u32[]{:S(2)}) copy-start(f32[2048,256]{1,0:T(8,128)} %param.32) | copy-start | bytes 6291460
  404.6 6.5 %copy-start.17 = (f32[2048,256]{1,0:T(8,128)S(1)}, f32[2048,256]{1,0:T(8,128)}, u32[]{:S(2)}) copy-start(f32[2048,256]{1,0:T(8,128)} %get-tuple-element.92) | copy-start | bytes 6291460
  408.8 2.4 copy-start.8
  411.2 4.8 %copy-start.22 = (bf16[128,1280]{1,0:T(8,128)(2,1)S(1)}, bf16[128,1280]{1,0:T(8,128)(2,1)}, u32[]{:S(2)}) copy-start(bf16[128,1280]{1,0:T(8,128)(2,1)} %get-tuple-element.84) | copy-start | bytes 983044
  411.2 8.7 %copy-start.16 = (f32[256,2048]{1,0:T(8,128)S(1)}, f32[256,2048]{1,0:T(8,128)}, u32[]{:S(2)}) copy-start(f32[256,2048]{1,0:T(8,128)} %param.29) | copy-start | bytes 6291460
  416.0 2.0 copy-start.26
  416.0 2.0 copy-start.27
  416.0 2.0 copy-start.28
  416.0 3.8 copy-start.9
  416.0 3.8 copy-start.15
  416.1 10.8 %slice-start.2 = ((s8[5242880]{0:T(1024)(128)(4,1)}), s8[4194304]{0:T(1024)(128)(4,1)S(1)}, s32[]{:S(2)}) async-start(s8[5242880]{0:T(1024)(128)(4,1)} %bitcast.34), calls=%async_computation.3 | async-start | bytes 8388608
  419.9 7.0 %copy-start.6 = (bf16[1,1280,1024]{2,1,0:T(8,128)(2,1)S(1)}, bf16[1,1280,1024]{2,1,0:T(8,128)(2,1)}, u32[]{:S(2)}) copy-start(bf16[1,1280,1024]{2,1,0:T(8,128)(2,1)} %param.18) | copy-start | bytes 7864324
  419.9 7.0 %slice-start.3 = ((s8[5242880]{0:T(1024)(128)(4,1)}), s8[1048576]{0:T(1024)(128)(4,1)S(1)}, s32[]{:S(2)}) async-start(s8[5242880]{0:T(1024)(128)(4,1)} %bitcast.34), calls=%async_computation.4 | async-start | bytes 2097152
  419.9 13.2 %slice-start = ((s8[5242880]{0:T(1024)(128)(4,1)}), s8[1048576]{0:T(1024)(128)(4,1)S(1)}, s32[]{:S(2)}) async-start(s8[5242880]{0:T(1024)(128)(4,1)} %bitcast.31), calls=%async_computation.1 | async-start | bytes 2097152
  426.8 6.2 %slice-start.1 = ((s8[5242880]{0:T(1024)(128)(4,1)}), s8[4194304]{0:T(1024)(128)(4,1)S(1)}, s32[]{:S(2)}) async-start(s8[5242880]{0:T(1024)(128)(4,1)} %bitcast.31), calls=%async_computation.2 | async-start | bytes 8388608
Sparse Core Ops, SparseCore 0:
  74.6 44.4 all-gather.1
